TPU v7x, 32 devices: a whole 2x2x4 slice. The times are simulated.
32 devices in a mesh: rep: 2 (over x), node: 2 (over core), local: 8 (over z, y).
Axes of the slice: x: 2, y: 2, z: 4, core: 2. Of those that a mesh axis runs over, the one named last changes fastest.
Arguments:
- tokens: bfloat16 [1024, 3584], P(('rep', 'node', 'local')), parts along dimension 0, may hold values from -6 to 6
- expert_ids: int32 [1024, 8], P(('rep', 'node', 'local')), parts along dimension 0, may hold values from 0 to 15, all different within a row; in each aligned block of 32 rows (0 to 31, 32 to 63, ...) at most 32 rows name the same one
- route_weights: bfloat16 [1024, 8], P(('rep', 'node', 'local')), parts along dimension 0, may hold values from 0.099609375 to 1
- w_up: bfloat16 [16, 3584, 1024], P(('node', 'local')), may hold values from -0.09375 to 0.09375
- w_down: bfloat16 [16, 1024, 3584], P(('node', 'local')), may hold values from -0.1875 to 0.1875
Outputs:
- mixed: bfloat16 [1024, 3584], P(('rep', 'node', 'local')), parts along dimension 0
There are 2 independent parts, one for each index of `rep`. A program takes and returns all parts, laid end to end along the dimension named above; an argument that names none is the same for every part. Nothing has to cross between parts.
Inputs may be any that keep to these rules, and one draw needn't show every extreme that they name: `expert_ids`: the 8 experts of a token differ; in each aligned block of 32 rows (the rows of one device) no expert is named by more than 32 rows.
All inputs are finite; a program needn't handle non-finite values.
Results may differ from a plain program's by a relative error of at most 0.0058.
Values may be sent and summed in bfloat16 or wider, within the bound.
No kernel may reach another device: no remote copies, remote signals or barrier semaphores. Data moves between devices by JAX's collectives and lax.ppermute only.
A program may use at most 64 MiB of HBM per device.

v0:
```python
import jax
import jax.numpy as jnp
from jax import lax
from jax.sharding import PartitionSpec as P


def place_rows(targets, groups, width):
    onehot = (targets[:, None] == jnp.arange(groups, dtype=jnp.int32)[None, :]).astype(jnp.int32)
    before = jnp.cumsum(onehot, axis=0) - onehot
    rank = jnp.sum(before * onehot, axis=1)
    return jnp.where(targets >= 0, targets * width + rank, groups * width)


def per_device(tokens, expert_ids, route_weights, w_up, w_down):
    up_matrix = w_up[0]
    down_matrix = w_down[0]
    rows = tokens.shape[0]
    top = expert_ids.shape[1]
    width_d = tokens.shape[1]
    experts = lax.axis_size(("node", "local"))
    most = max(4, 2 * rows * top // experts)
    slot = place_rows(expert_ids.reshape(-1), experts, most)
    source = tokens[jnp.arange(rows * top, dtype=jnp.int32) // top]
    buffer = jnp.zeros((experts * most, width_d), jnp.bfloat16).at[slot].set(source, mode="drop")
    buffer = buffer.reshape(experts, most, width_d)
    received = lax.all_to_all(buffer, ("node", "local"), split_axis=0, concat_axis=0, tiled=True)
    shape = received.shape
    flat = received.reshape(-1, shape[-1])
    hidden = jax.nn.silu(jnp.dot(flat, up_matrix, preferred_element_type=jnp.float32)).astype(
        jnp.bfloat16
    )
    answer = jnp.dot(hidden, down_matrix, preferred_element_type=jnp.float32).astype(jnp.bfloat16)
    done = answer.reshape(shape)
    returned = lax.all_to_all(
        done, ("node", "local"), split_axis=0, concat_axis=0, tiled=True
    ).reshape(experts * most, width_d)
    picked = returned[jnp.minimum(slot, experts * most - 1)].reshape(rows, top, width_d)
    mixed = jnp.einsum("tk,tkd->td", route_weights, picked, preferred_element_type=jnp.float32)
    return mixed.astype(jnp.bfloat16)


def solution(mesh):
    placed = (
        P(("rep", "node", "local"), None),
        P(("rep", "node", "local"), None),
        P(("rep", "node", "local"), None),
        P(("node", "local"), None, None),
        P(("node", "local"), None, None),
    )
    return jax.shard_map(
        per_device,
        mesh=mesh,
        in_specs=placed,
        out_specs=P(("rep", "node", "local"), None),
        check_vma=False,
    )
```

profile of v0, /device:TPU:0, one launch (start us, length us, event | category | flops | bytes accessed | tf_op | source)
XLA Modules:
  0.0 212.5 jit_solution(13505756013356486724)
XLA Ops:
  0.0 0.0 copy-start
  0.0 0.8 copy.8
  0.8 0.1 eq.29
  0.9 0.1 eq.25
  1.0 0.7 broadcast_multiply_fusion
  1.7 0.7 broadcast_compare_fusion
  2.4 0.6 reduce-window.6
  3.0 0.2 slice_reduce_fusion
  3.2 0.1 copy.7
  3.3 0.1 mul.25
  3.4 0.1 copy.6
  3.5 0.1 ge.18
  3.6 0.1 fusion.18
  3.7 0.0 copy-done
  3.7 10.9 %scatter_custom_fusion = bf16[512,3584]{1,0:T(8,128)(2,1)} fusion(s32[256]{0:T(256)S(1)} %bitcast.55, bf16[32,3584]{1,0:T(8,128)(2,1)S(1)} %copy-done, s32[1024]{0:T(1024)S(1)} %pad_clamp_fusion.1, bf16[]{:T(256)} %constant.26.clone.1), kind=kCustom, calls=%fused_computation.11 | custom fusion | bytes 3670018 | tf_op jit(solution)/shard_map/scatter | solution.py:24
  14.6 90.7 %all_to_all.10 = bf16[16,32,3584]{2,1,0:T(8,128)(2,1)} all-to-all(bf16[16,32,3584]{2,1,0:T(8,128)(2,1)} %bitcast.48), channel_id=1, replica_groups=mesh['rep'=2,'node'=2,'local'=8] {'node','local'}, dimensions={0} | all-to-all | bytes 7340032 | tf_op jit(solution)/shard_map/all_to_all | solution.py:26
  105.3 16.0 %fusion.4 = bf16[512,3584]{1,0:T(8,128)(2,1)} fusion(bf16[1,1024,3584]{2,1,0:T(8,128)(2,1)} %param.9, bf16[512,3584]{1,0:T(8,128)(2,1)} %bitcast.50, bf16[1,3584,1024]{2,1,0:T(8,128)(2,1)} %param.8), kind=kOutput, calls=%fused_computation.7 | convolution fusion | flops 7520649216 | bytes 22020096 | tf_op jit(solution)/shard_map/dot_general | solution.py:32
  121.3 0.0 copy-start.1
  121.3 4.6 %all-to-all-start.1 = ((bf16[16,32,3584]{2,1,0:T(8,128)(2,1)}), bf16[16,32,3584]{2,1,0:T(8,128)(2,1)}, u32[]{:S(2)}, u32[]{:S(2)}) async-start(bf16[16,32,3584]{2,1,0:T(8,128)(2,1)} %bitcast.49), calls=%async_computation.1 | async-start | bytes 7340032 | tf_op jit(solution)/shard_map/all_to_all | solution.py:34
  125.9 0.0 copy-done.1
  125.9 0.1 copy.11
  126.0 79.1 %all-to-all-done.1 = bf16[16,32,3584]{2,1,0:T(8,128)(2,1)} async-done(((bf16[16,32,3584]{2,1,0:T(8,128)(2,1)}), bf16[16,32,3584]{2,1,0:T(8,128)(2,1)}, u32[]{:S(2)}, u32[]{:S(2)}) %all-to-all-start.1) | async-done | bytes 3670048 | tf_op jit(solution)/shard_map/all_to_all | solution.py:34
  205.1 6.0 %gather_fusion = bf16[256,3584]{1,0:T(8,128)(2,1)S(1)} fusion(bf16[512,3584]{1,0:T(8,128)(2,1)} %bitcast.9, s32[1024]{0:T(1024)S(1)} %pad_clamp_fusion), kind=kCustom, calls=%fused_computation.1 | custom fusion | bytes 3671040 | tf_op jit(solution)/shard_map/gather | solution.py:37
  211.1 0.6 fusion.7
  211.8 0.7 copy.16
  (7 shorter events, 0.1 us)
Async XLA Ops:
  0.0 3.7 %copy-start = (bf16[32,3584]{1,0:T(8,128)(2,1)S(1)}, bf16[32,3584]{1,0:T(8,128)(2,1)}, u32[]{:S(2)}) copy-start(bf16[32,3584]{1,0:T(8,128)(2,1)} %param.5) | copy-start | bytes 688132
  121.3 4.6 %copy-start.1 = (bf16[32,8]{0,1:T(8,128)(2,1)S(1)}, bf16[32,8]{0,1:T(8,128)(2,1)}, u32[]{:S(2)}) copy-start(bf16[32,8]{0,1:T(8,128)(2,1)} %param.7) | copy-start | bytes 1540
  121.3 83.8 %all-to-all-start.1 = ((bf16[16,32,3584]{2,1,0:T(8,128)(2,1)}), bf16[16,32,3584]{2,1,0:T(8,128)(2,1)}, u32[]{:S(2)}, u32[]{:S(2)}) async-start(bf16[16,32,3584]{2,1,0:T(8,128)(2,1)} %bitcast.49), calls=%async_computation.1 | async-start | bytes 7340032 | tf_op jit(solution)/shard_map/all_to_all | solution.py:34
where the time goes:
time: 215 us; the launch traced here: 212 us
  blocking collectives  90.7 us (42%)
  waiting for transfers between devices  79.1 us (37%)
  local copies, waits for them, and re-layouts  19.3 us (9%)
  matrix products  16.6 us (8%)
  starting transfers between devices  4.63 us (2%)
    all_to_all x1, blocking collectives, per_device(): lax.all_to_all(buffer, ('node', 'local'), split_axis=0, concat_axis=0, ti...  90.7 us
    all_to_all x1, waiting for transfers between devices, per_device(): lax.all_to_all(done, ('node', 'local'), split_axis=0, concat_axis=0, tile...  79.1 us
    dot_general x1, matrix products, per_device(): jnp.dot(hidden, down_matrix, preferred_element_type=jnp.float32)  16 us
    scatter x1, local copies, waits for them, and re-layouts, per_device(): jnp.zeros((experts * most, width_d), jnp.bfloat16).at[slot]  10.9 us
    gather x1, local copies, waits for them, and re-layouts, per_device(): returned[jnp.minimum(slot, experts * most - 1)].reshape(rows, top, width_d)  6.04 us
    all_to_all x1, starting transfers between devices, per_device(): lax.all_to_all(done, ('node', 'local'), split_axis=0, concat_axis=0, tile...  4.63 us
  transfers between devices with their start and end apart: 1, of which 1 were waited for; matrix products, arithmetic and copies ran while one was open for 0% of the time, Pallas kernels for 0%

commit v1 on v0

v1 whole, which is shorter than its diff:
```python
import jax
import jax.numpy as jnp
from jax import lax
from jax.sharding import PartitionSpec as P


def per_device(tokens, expert_ids, route_weights, w_up, w_down):
    axes = ("node", "local")
    mine = lax.axis_index(axes)
    everyone = lax.all_gather(tokens, axes, tiled=True)
    ids = lax.all_gather(expert_ids, axes, tiled=True)
    weights = lax.all_gather(route_weights, axes, tiled=True)
    scale = jnp.sum(jnp.where(ids == mine, weights.astype(jnp.float32), 0.0), axis=1)
    hidden = jax.nn.silu(jnp.dot(everyone, w_up[0], preferred_element_type=jnp.float32)).astype(jnp.bfloat16)
    answer = jnp.dot(hidden, w_down[0], preferred_element_type=jnp.float32)
    part = (answer * scale[:, None]).astype(jnp.bfloat16)
    return lax.psum_scatter(part, axes, scatter_dimension=0, tiled=True)


def solution(mesh):
    placed = (
        P(("rep", "node", "local"), None),
        P(("rep", "node", "local"), None),
        P(("rep", "node", "local"), None),
        P(("node", "local"), None, None),
        P(("node", "local"), None, None),
    )
    return jax.shard_map(
        per_device,
        mesh=mesh,
        in_specs=placed,
        out_specs=P(("rep", "node", "local"), None),
        check_vma=False,
    )
```

time: 215 us -> 162 us (0.75); the launches traced: 212 us -> 162 us
  blocking collectives: 90.7 us -> 64.1 us
  local copies, waits for them, and re-layouts: 19.3 us -> 0.08 us
  between operations: 0.07 us -> 13.4 us
  waiting for transfers between devices: 79.1 us -> 69 us
  starting transfers between devices: 4.63 us -> 0.04 us
    all_to_all x1 -> x0, blocking collectives: 90.7 us -> none  [per_device(): lax.all_to_all(buffer, ('node', 'local'), split_axis=0, concat_axis=0, ti...]
    all_to_all x1 -> x0, waiting for transfers between devices: 79.1 us -> none  [per_device(): lax.all_to_all(done, ('node', 'local'), split_axis=0, concat_axis=0, tile...]
    reduce_scatter x0 -> x1, waiting for transfers between devices: none -> 68.2 us  [per_device(): return lax.psum_scatter(part, axes, scatter_dimension=0, tiled=True)]
    all_gather x0 -> x2, blocking collectives: none -> 64.1 us  [the longest x1 34.7 us: per_device(): weights = lax.all_gather(route_weights, axes, tiled=True)]
    scatter x1 -> x0, local copies, waits for them, and re-layouts: 10.9 us -> none  [per_device(): jnp.zeros((experts * most, width_d), jnp.bfloat16).at[slot]]
    gather x1 -> x0, local copies, waits for them, and re-layouts: 6.04 us -> none  [per_device(): returned[jnp.minimum(slot, experts * most - 1)].reshape(rows, top, width_d)]
    all_to_all x1 -> x0, starting transfers between devices: 4.63 us -> none  [per_device(): lax.all_to_all(done, ('node', 'local'), split_axis=0, concat_axis=0, tile...]
    dot_general x2 -> x1, matrix products: 16.6 us -> 15 us  [per_device(): answer = jnp.dot(hidden, w_down[0], preferred_element_type=jnp.float32)]
  transfers between devices with their start and end apart: 1 -> 2, of which waited for: 1 -> 1; matrix products, arithmetic and copies ran while one was open for 0% -> 0% of each run, Pallas kernels for 0% -> 0%
where the time goes in v1:
time: 162 us
  waiting for transfers between devices  69 us (43%)
  blocking collectives  64.1 us (40%)
  matrix products  15 us (9%)
  between operations  13.4 us (8%)
    reduce_scatter x1, waiting for transfers between devices, per_device(): return lax.psum_scatter(part, axes, scatter_dimension=0, tiled=True)  68.2 us
    all_gather x1, blocking collectives, per_device(): weights = lax.all_gather(route_weights, axes, tiled=True)  34.7 us
    all_gather x1, blocking collectives, per_device(): ids = lax.all_gather(expert_ids, axes, tiled=True)  29.4 us
    dot_general x1, matrix products, per_device(): answer = jnp.dot(hidden, w_down[0], preferred_element_type=jnp.float32)  15 us
  transfers between devices with their start and end apart: 2, of which 1 were waited for; matrix products, arithmetic and copies ran while one was open for 0% of the time, Pallas kernels for 0%

profile of v1, /device:TPU:0, one launch (start us, length us, event | category | flops | bytes accessed | tf_op | source)
XLA Modules:
  0.0 161.6 jit_solution(12459005864058008529)
XLA Ops:
  6.5 0.0 all-gather.4.cloned.1.call-start
  6.5 0.7 all-gather.4.cloned.1.call-update
  7.3 0.0 reduce-scatter.2.cloned.1.call-start
  7.3 34.7 %all-gather.1 = bf16[16,32,8]{1,2,0:T(8,128)(2,1)S(1)} all-gather(bf16[1,32,8]{1,2,0:T(8,128)(2,1)} %bitcast.16), channel_id=1, replica_groups=mesh['rep'=2,'node'=2,'local'=8] {'node','local'}, dimensions={0}, use_global_device_ids=true | all-gather | bytes 8704 | tf_op jit(solution)/shard_map/all_gather | solution.py:12
  42.0 29.4 %all-gather = s32[16,32,8]{1,2,0:T(8,128)S(1)} all-gather(s32[1,32,8]{1,2,0:T(8,128)} %bitcast.15), channel_id=1, replica_groups=mesh['rep'=2,'node'=2,'local'=8] {'node','local'}, dimensions={0}, use_global_device_ids=true | all-gather | bytes 17408 | tf_op jit(solution)/shard_map/all_gather | solution.py:11
  71.5 0.1 reshape.10
  71.6 0.0 all-gather.4.cloned.1.call-done
  71.6 15.0 %multiply_convert_fusion = bf16[512,3584]{1,0:T(8,128)(2,1)} fusion(bf16[1,1024,3584]{2,1,0:T(8,128)(2,1)} %param.9, f32[512]{0:T(512)S(1)} %reshape.10, bf16[512,3584]{1,0:T(8,128)(2,1)} %all-gather.4.cloned.1.call-done, bf16[1,3584,1024]{2,1,0:T(8,128)(2,1)} %param.8), kind=kOutput, calls=%fused_computation.4 | convolution fusion | flops 7522484224 | bytes 22022144 | tf_op jit(solution)/shard_map/dot_general | solution.py:15
  86.6 0.0 reduce-scatter.2.cloned.1.call-update
  86.6 68.2 %reduce-scatter.2.cloned.1.call-done = bf16[32,3584]{1,0:T(8,128)(2,1)} async-done(((bf16[512,3584]{1,0:T(8,128)(2,1)}), bf16[32,3584]{1,0:T(8,128)(2,1)}) %reduce-scatter.2.cloned.1.call-update) | async-done | bytes 229392 | tf_op jit(solution)/shard_map/reduce_scatter | solution.py:17
  (1 shorter events, 0.0 us)
Async XLA Ops:
  6.5 65.0 %all-gather.4.cloned.1.call-start = ((), (), s32[]{:S(2)}) async-start(), calls=%async_computation.1 | async-start | bytes 3899392 | tf_op jit(solution)/shard_map/all_gather | solution.py:10
  7.3 147.6 %reduce-scatter.2.cloned.1.call-start = ((), (), s32[]{:S(2)}) async-start(), calls=%async_computation.2 | async-start | bytes 3899392 | tf_op jit(solution)/shard_map/reduce_scatter | solution.py:17
Sparse Core Ops, SparseCore 0:
  9.6 51.6 all-gather.3
  86.7 68.0 reduce-scatter.1

commit v2 on v1

v2 whole, which is shorter than its diff:
```python
import jax
import jax.numpy as jnp
from jax import lax
from jax.sharding import PartitionSpec as P

BOTH = ("node", "local")
LANES = 128


def gather_plan(tokens, expert_ids, route_weights, w_up, w_down):
    mine = lax.axis_index(BOTH)
    everyone = lax.all_gather(tokens, BOTH, tiled=True)
    ids = lax.all_gather(expert_ids, BOTH, tiled=True)
    weights = lax.all_gather(route_weights, BOTH, tiled=True)
    scale = jnp.sum(jnp.where(ids == mine, weights.astype(jnp.float32), 0.0), axis=1)
    hidden = jax.nn.silu(jnp.dot(everyone, w_up[0], preferred_element_type=jnp.float32)).astype(jnp.bfloat16)
    answer = jnp.dot(hidden, w_down[0], preferred_element_type=jnp.float32)
    part = (answer * scale[:, None]).astype(jnp.bfloat16)
    return lax.psum_scatter(part, BOTH, scatter_dimension=0, tiled=True)


def ring_plan(tokens, expert_ids, route_weights, w_up, w_down):
    rows, width = tokens.shape
    experts = lax.axis_size(BOTH)
    n = lax.axis_size("local")
    half = n // 2
    mine = lax.axis_index(BOTH)
    order = list(range(0, n, 2)) + list(range(n - 1, 0, -2))
    onward = [(order[i], order[(i + 1) % n]) for i in range(n)]
    pairs = onward + [(n + b, n + a) for a, b in onward]

    def hop(x):
        return lax.ppermute(x, BOTH, pairs)

    def swap(x):
        return lax.ppermute(x, "node", [(0, 1), (1, 0)])

    columns = -(-experts // LANES) * LANES
    named = expert_ids[:, :, None] == jnp.arange(columns, dtype=jnp.int32)[None, None, :]
    table = jnp.sum(jnp.where(named, route_weights.astype(jnp.float32)[:, :, None], 0.0), axis=1)
    own = jnp.concatenate([tokens, table.astype(jnp.bfloat16)], axis=1)

    def expert(blocks):
        x = jnp.concatenate(blocks, axis=0)
        here = jnp.arange(columns, dtype=jnp.int32)[None, :] == mine
        scale = jnp.sum(jnp.where(here, x[:, width:].astype(jnp.float32), 0.0), axis=1)
        up = jnp.dot(x[:, :width], w_up[0], preferred_element_type=jnp.float32)
        hidden = jax.nn.silu(up).astype(jnp.bfloat16)
        answer = jnp.dot(hidden, w_down[0], preferred_element_type=jnp.float32)
        answer = answer.astype(jnp.bfloat16).astype(jnp.float32)
        out = answer * scale[:, None]
        return [out[i * rows:(i + 1) * rows] for i in range(len(blocks))]

    a, b = [own], [swap(own)]
    for h in range(1, half):
        a.append(hop(a[-1]))
        b.append(hop(b[-1]))
    a.append(hop(a[-1]))
    ahead_b = [None] + [swap(a[h]) for h in range(1, half + 1)]
    ahead_a = [None] + [swap(b[h]) for h in range(1, half)]

    p_own = expert([a[0], b[0]])
    behind, ahead = {}, {}
    for h in range(1, half):
        r = expert([a[h], b[h], ahead_a[h], ahead_b[h]])
        behind[h] = r[:2]
        ahead[h] = r[2:]
    far = expert([a[half], ahead_b[half]])

    def bf(x):
        return x.astype(jnp.bfloat16)

    got_far = swap(bf(far[1]))
    sums = {half: [far[0] + got_far.astype(jnp.float32)]}
    for h in range(half - 1, 0, -1):
        ga = swap(bf(behind[h][1]))
        gb = swap(bf(behind[h][0]))
        sums[h] = [ahead[h][0] + ga.astype(jnp.float32), ahead[h][1] + gb.astype(jnp.float32)]

    run_b = hop(bf(sums[half - 1][1]))
    run_a = hop(bf(sums[half][0]))
    for h in range(half - 1, 0, -1):
        if h < half - 1:
            run_b = hop(bf(sums[h][1] + run_b.astype(jnp.float32)))
        run_a = hop(bf(sums[h][0] + run_a.astype(jnp.float32)))
    last = swap(bf(p_own[1] + run_b.astype(jnp.float32)))
    return bf(p_own[0] + run_a.astype(jnp.float32) + last.astype(jnp.float32))


def solution(mesh):
    placed = (
        P(("rep", "node", "local"), None),
        P(("rep", "node", "local"), None),
        P(("rep", "node", "local"), None),
        P(("node", "local"), None, None),
        P(("node", "local"), None, None),
    )
    n = mesh.shape["local"]
    ringed = mesh.shape["node"] == 2 and n % 2 == 0 and 4 <= n <= 16
    return jax.shard_map(
        ring_plan if ringed else gather_plan,
        mesh=mesh,
        in_specs=placed,
        out_specs=P(("rep", "node", "local"), None),
        check_vma=False,
    )
```

time: 162 us -> 113 us (0.70)
  blocking collectives: 64.1 us -> 0 us
  waiting for transfers between devices: 69 us -> 31.1 us
  starting transfers between devices: 0.04 us -> 28.9 us
  matrix products: 15 us -> 40.7 us
  between operations: 13.4 us -> 0.27 us
  other arithmetic: 0.03 us -> 6.84 us
  local copies, waits for them, and re-layouts: 0.08 us -> 5.21 us
    reduce_scatter x1 -> x0, waiting for transfers between devices: 68.2 us -> none  [per_device(): return lax.psum_scatter(part, axes, scatter_dimension=0, tiled=True)]
    all_gather x2 -> x0, blocking collectives: 64.1 us -> none  [the longest x1 34.7 us: per_device(): weights = lax.all_gather(route_weights, axes, tiled=True)]
    ppermute x0 -> x30, waiting for transfers between devices: none -> 31.1 us  [the longest x14 29.9 us: hop(): return lax.ppermute(x, BOTH, pairs)]
    ppermute x0 -> x30, starting transfers between devices: none -> 28.9 us  [the longest x14 26.3 us: hop(): return lax.ppermute(x, BOTH, pairs)]
    dot_general x1 -> x5, matrix products: 15 us -> 40.7 us  [expert(): answer = jnp.dot(hidden, w_down[0], preferred_element_type=jnp.float32)]
    convert_element_type x0 -> x6, other arithmetic: none -> 5.47 us  [bf(): return x.astype(jnp.bfloat16)]
    slice x0 -> x4, local copies, waits for them, and re-layouts: none -> 2.42 us  [expert(): return [out[i * rows:(i + 1) * rows] for i in range(len(blocks))]]
  transfers between devices with their start and end apart: 2 -> 30, of which waited for: 1 -> 12; matrix products, arithmetic and copies ran while one was open for 0% -> 44% of each run, Pallas kernels for 0% -> 0%
where the time goes in v2:
time: 113 us
  matrix products  40.7 us (36%)
  waiting for transfers between devices  31.1 us (28%)
  starting transfers between devices  28.9 us (26%)
  other arithmetic  6.84 us (6%)
  local copies, waits for them, and re-layouts  5.21 us (5%)
    dot_general x5, matrix products, expert(): answer = jnp.dot(hidden, w_down[0], preferred_element_type=jnp.float32)  40.7 us
    ppermute x14, waiting for transfers between devices, hop(): return lax.ppermute(x, BOTH, pairs)  29.9 us
    ppermute x14, starting transfers between devices, hop(): return lax.ppermute(x, BOTH, pairs)  26.3 us
    convert_element_type x6, other arithmetic, bf(): return x.astype(jnp.bfloat16)  5.47 us
    ppermute x16, starting transfers between devices, swap(): return lax.ppermute(x, 'node', [(0, 1), (1, 0)])  2.57 us
    slice x4, local copies, waits for them, and re-layouts, expert(): return [out[i * rows:(i + 1) * rows] for i in range(len(blocks))]  2.42 us
  transfers between devices with their start and end apart: 30, of which 12 were waited for; matrix products, arithmetic and copies ran while one was open for 44% of the time, Pallas kernels for 0%

profile of v2, /device:TPU:0, one launch (start us, length us, event | category | flops | bytes accessed | tf_op | source)
XLA Modules:
  0.0 113.0 jit_solution(15249949551490216449)
XLA Ops:
  0.0 0.8 copy.8
  0.8 0.8 copy.9
  1.5 0.1 select_reduce_fusion
  1.7 1.0 pad_maximum_fusion.1
  2.6 3.1 %collective-permute-start.1 = (bf16[32,3712]{1,0:T(8,128)(2,1)S(1)}, bf16[32,3712]{1,0:T(8,128)(2,1)S(1)}, u32[]{:S(2)}, u32[]{:S(2)}) collective-permute-start(bf16[32,3712]{1,0:T(8,128)(2,1)S(1)} %pad_maximum_fusion.1), channel_id=1, source_target_pairs={{0,2},{2,4},{4,6},{6,7},{7,5},{5,3},{3,1},{1,0},{10,8},{12,10},{14... | collective-permute-start | bytes 712712 | tf_op jit(solution)/shard_map/ppermute | solution.py:33
  5.7 0.0 collective-permute-start
  5.7 4.0 %collective-permute-done.1 = bf16[32,3712]{1,0:T(8,128)(2,1)S(1)} collective-permute-done((bf16[32,3712]{1,0:T(8,128)(2,1)S(1)}, bf16[32,3712]{1,0:T(8,128)(2,1)S(1)}, u32[]{:S(2)}, u32[]{:S(2)}) %collective-permute-start.1) | collective-permute-done | bytes 237600 | tf_op jit(solution)/shard_map/ppermute | solution.py:33
  9.7 2.1 %collective-permute-start.6 = (bf16[32,3712]{1,0:T(8,128)(2,1)S(1)}, bf16[32,3712]{1,0:T(8,128)(2,1)S(1)}, u32[]{:S(2)}, u32[]{:S(2)}) collective-permute-start(bf16[32,3712]{1,0:T(8,128)(2,1)S(1)} %collective-permute-done.1), channel_id=1, source_target_pairs={{0,2},{2,4},{4,6},{6,7},{7,5},{5,3},{3,1},{1,0},{10,8},{12,10},{14... | collective-permute-start | bytes 712712 | tf_op jit(solution)/shard_map/ppermute | solution.py:33
  11.8 1.6 %collective-permute-start.2 = (bf16[32,3712]{1,0:T(8,128)(2,1)S(1)}, bf16[32,3712]{1,0:T(8,128)(2,1)S(1)}, u32[]{:S(2)}, u32[]{:S(2)}) collective-permute-start(bf16[32,3712]{1,0:T(8,128)(2,1)S(1)} %collective-permute-done), channel_id=1, source_target_pairs={{0,2},{2,4},{4,6},{6,7},{7,5},{5,3},{3,1},{1,0},{10,8},{12,10},{14... | collective-permute-start | bytes 712712 | tf_op jit(solution)/shard_map/ppermute | solution.py:33
  13.4 2.4 %collective-permute-done.6 = bf16[32,3712]{1,0:T(8,128)(2,1)S(1)} collective-permute-done((bf16[32,3712]{1,0:T(8,128)(2,1)S(1)}, bf16[32,3712]{1,0:T(8,128)(2,1)S(1)}, u32[]{:S(2)}, u32[]{:S(2)}) %collective-permute-start.6) | collective-permute-done | bytes 237600 | tf_op jit(solution)/shard_map/ppermute | solution.py:33
  15.8 2.1 %collective-permute-start.11 = (bf16[32,3712]{1,0:T(8,128)(2,1)S(1)}, bf16[32,3712]{1,0:T(8,128)(2,1)S(1)}, u32[]{:S(2)}, u32[]{:S(2)}) collective-permute-start(bf16[32,3712]{1,0:T(8,128)(2,1)S(1)} %collective-permute-done.6), channel_id=1, source_target_pairs={{0,2},{2,4},{4,6},{6,7},{7,5},{5,3},{3,1},{1,0},{10,8},{12,10},{14... | collective-permute-start | bytes 712712 | tf_op jit(solution)/shard_map/ppermute | solution.py:33
  18.0 0.4 collective-permute-done.2
  18.4 2.1 %collective-permute-start.7 = (bf16[32,3712]{1,0:T(8,128)(2,1)S(1)}, bf16[32,3712]{1,0:T(8,128)(2,1)S(1)}, u32[]{:S(2)}, u32[]{:S(2)}) collective-permute-start(bf16[32,3712]{1,0:T(8,128)(2,1)S(1)} %collective-permute-done.2), channel_id=1, source_target_pairs={{0,2},{2,4},{4,6},{6,7},{7,5},{5,3},{3,1},{1,0},{10,8},{12,10},{14... | collective-permute-start | bytes 712712 | tf_op jit(solution)/shard_map/ppermute | solution.py:33
  20.5 1.5 %collective-permute-done.11 = bf16[32,3712]{1,0:T(8,128)(2,1)S(1)} collective-permute-done((bf16[32,3712]{1,0:T(8,128)(2,1)S(1)}, bf16[32,3712]{1,0:T(8,128)(2,1)S(1)}, u32[]{:S(2)}, u32[]{:S(2)}) %collective-permute-start.11) | collective-permute-done | bytes 237600 | tf_op jit(solution)/shard_map/ppermute | solution.py:33
  22.0 2.5 %collective-permute-done.7 = bf16[32,3712]{1,0:T(8,128)(2,1)S(1)} collective-permute-done((bf16[32,3712]{1,0:T(8,128)(2,1)S(1)}, bf16[32,3712]{1,0:T(8,128)(2,1)S(1)}, u32[]{:S(2)}, u32[]{:S(2)}) %collective-permute-start.7) | collective-permute-done | bytes 237600 | tf_op jit(solution)/shard_map/ppermute | solution.py:33
  24.5 2.1 %collective-permute-start.12 = (bf16[32,3712]{1,0:T(8,128)(2,1)S(1)}, bf16[32,3712]{1,0:T(8,128)(2,1)S(1)}, u32[]{:S(2)}, u32[]{:S(2)}) collective-permute-start(bf16[32,3712]{1,0:T(8,128)(2,1)S(1)} %collective-permute-done.7), channel_id=1, source_target_pairs={{0,2},{2,4},{4,6},{6,7},{7,5},{5,3},{3,1},{1,0},{10,8},{12,10},{14... | collective-permute-start | bytes 712712 | tf_op jit(solution)/shard_map/ppermute | solution.py:33
  26.6 0.1 collective-permute-start.8
  26.7 0.0 collective-permute-done.4
  26.7 1.6 %collective-permute-start.16 = (bf16[32,3712]{1,0:T(8,128)(2,1)S(1)}, bf16[32,3712]{1,0:T(8,128)(2,1)S(1)}, u32[]{:S(2)}, u32[]{:S(2)}) collective-permute-start(bf16[32,3712]{1,0:T(8,128)(2,1)S(1)} %collective-permute-done.11), channel_id=1, source_target_pairs={{0,2},{2,4},{4,6},{6,7},{7,5},{5,3},{3,1},{1,0},{10,8},{12,10},{14... | collective-permute-start | bytes 712712 | tf_op jit(solution)/shard_map/ppermute | solution.py:33
  28.4 4.8 %collective-permute-done.16 = bf16[32,3712]{1,0:T(8,128)(2,1)S(1)} collective-permute-done((bf16[32,3712]{1,0:T(8,128)(2,1)S(1)}, bf16[32,3712]{1,0:T(8,128)(2,1)S(1)}, u32[]{:S(2)}, u32[]{:S(2)}) %collective-permute-start.16) | collective-permute-done | bytes 237600 | tf_op jit(solution)/shard_map/ppermute | solution.py:33
  33.2 0.0 collective-permute-done.12
  33.2 0.6 collective-permute-start.13
  33.8 0.0 collective-permute-done.8
  33.9 1.1 collective-permute-done.13
  35.1 0.1 select_reduce_fusion.1
  35.2 0.0 copy-start
  35.2 8.7 %fusion.148 = (bf16[128,3584]{1,0:T(8,128)(2,1)S(1)}, f32[128,3584]{1,0:T(8,128)}) fusion(f32[128]{0:T(128)S(1)} %get-tuple-element.7, bf16[1,1024,3584]{2,1,0:T(8,128)(2,1)} %param.9, bf16[1,3584,1024]{2,1,0:T(8,128)(2,1)} %param.8, bf16[128,3712]{1,0:T(8,128)(2,1)S(1)} %constant_dynamic-update-slice_fusion.8), kind=kOutput, calls=%fused_computation.109 | convolution fusion | flops 1881538560 | bytes 18350592 | tf_op jit(solution)/shard_map/dot_general | solution.py:49
  43.9 0.8 fusion.137
  44.7 0.3 collective-permute-start.15
  45.0 0.2 collective-permute-start.25
  45.2 1.0 constant_dynamic-update-slice_fusion.12
  46.2 0.1 select_reduce_fusion.4
  46.3 7.9 %fusion.62 = f32[64,3584]{1,0:T(8,128)S(1)} fusion(bf16[1,1024,3584]{2,1,0:T(8,128)(2,1)} %param.9, f32[64]{0:T(128)S(1)} %get-tuple-element.5, bf16[1,3584,1024]{2,1,0:T(8,128)(2,1)} %param.8, bf16[64,3712]{1,0:T(8,128)(2,1)S(1)} %constant_dynamic-update-slice_fusion.12), kind=kOutput, calls=%fused_computation.34 | convolution fusion | flops 940539904 | bytes 16056832 | tf_op jit(solution)/shard_map/dot_general | solution.py:49
  54.3 0.7 slice.210
  55.0 0.3 collective-permute-start.18
  55.3 8.6 %fusion.143 = (bf16[128,3584]{1,0:T(8,128)(2,1)S(1)}, f32[128,3584]{1,0:T(8,128)}) fusion(f32[128]{0:T(128)S(1)} %get-tuple-element.8, bf16[1,1024,3584]{2,1,0:T(8,128)(2,1)} %param.9, bf16[1,3584,1024]{2,1,0:T(8,128)(2,1)} %param.8, bf16[128,3712]{1,0:T(8,128)(2,1)S(1)} %copy-done.2), kind=kOutput, calls=%fused_computation.108 | convolution fusion | flops 1881538560 | bytes 18350592 | tf_op jit(solution)/shard_map/dot_general | solution.py:49
  63.8 0.8 fusion.136
  64.7 0.2 collective-permute-start.10
  64.9 0.3 collective-permute-start.24
  65.2 1.7 %fusion.98 = bf16[32,3584]{1,0:T(8,128)(2,1)} fusion(f32[64,3584]{1,0:T(8,128)S(1)} %fusion.62, bf16[32,3584]{1,0:T(8,128)(2,1)} %collective-permute-done.18), kind=kLoop, calls=%fused_computation.54 | loop fusion | flops 344064 | bytes 917504 | tf_op jit(solution)/shard_map/convert_element_type | solution.py:71
  66.9 2.1 %collective-permute-start.19 = (bf16[32,3584]{1,0:T(8,128)(2,1)}, bf16[32,3584]{1,0:T(8,128)(2,1)}, u32[]{:S(2)}, u32[]{:S(2)}) collective-permute-start(bf16[32,3584]{1,0:T(8,128)(2,1)} %fusion.98), channel_id=1, source_target_pairs={{0,2},{2,4},{4,6},{6,7},{7,5},{5,3},{3,1},{1,0},{10,8},{12,10},{14... | collective-permute-start | bytes 688136 | tf_op jit(solution)/shard_map/ppermute | solution.py:33
  68.9 7.6 %fusion.138 = (bf16[128,3584]{1,0:T(8,128)(2,1)S(1)}, f32[128,3584]{1,0:T(8,128)S(1)}) fusion(f32[128]{0:T(128)S(1)} %get-tuple-element.9, bf16[1,1024,3584]{2,1,0:T(8,128)(2,1)} %param.9, bf16[1,3584,1024]{2,1,0:T(8,128)(2,1)} %param.8, bf16[128,3712]{1,0:T(8,128)(2,1)} %copy-done.3), kind=kOutput, calls=%fused_computation.107 | convolution fusion | flops 1881538560 | bytes 18350592 | tf_op jit(solution)/shard_map/dot_general | solution.py:49
  76.6 0.0 collective-permute-done.25
  76.6 0.0 collective-permute-done.19
  76.6 1.5 %fusion.101 = (bf16[32,3584]{1,0:T(8,128)(2,1)S(1)}, bf16[32,3584]{1,0:T(8,128)(2,1)S(1)}) fusion(f32[128,3584]{1,0:T(8,128)} %get-tuple-element.27, bf16[32,3584]{1,0:T(8,128)(2,1)} %collective-permute-done.19, bf16[32,3584]{1,0:T(8,128)(2,1)} %collective-permute-done.15, bf16[32,3584]{1,0:T(8,128)(2,1)} %collective-permute-done.25), kind=kLoop, calls=%fused_computation.58 | loop fusion | flops 917504 | bytes 2064384 | tf_op jit(solution)/shard_map/convert_element_type | solution.py:71
  78.1 1.6 %collective-permute-start.20 = (bf16[32,3584]{1,0:T(8,128)(2,1)S(1)}, bf16[32,3584]{1,0:T(8,128)(2,1)S(1)}, u32[]{:S(2)}, u32[]{:S(2)}) collective-permute-start(bf16[32,3584]{1,0:T(8,128)(2,1)S(1)} %get-tuple-element.14), channel_id=1, source_target_pairs={{0,2},{2,4},{4,6},{6,7},{7,5},{5,3},{3,1},{1,0},{10,8},{12,10},{14... | collective-permute-start | bytes 688136 | tf_op jit(solution)/shard_map/ppermute | solution.py:33
  79.7 1.6 %collective-permute-start.26 = (bf16[32,3584]{1,0:T(8,128)(2,1)S(1)}, bf16[32,3584]{1,0:T(8,128)(2,1)S(1)}, u32[]{:S(2)}, u32[]{:S(2)}) collective-permute-start(bf16[32,3584]{1,0:T(8,128)(2,1)S(1)} %get-tuple-element.15), channel_id=1, source_target_pairs={{0,2},{2,4},{4,6},{6,7},{7,5},{5,3},{3,1},{1,0},{10,8},{12,10},{14... | collective-permute-start | bytes 688136 | tf_op jit(solution)/shard_map/ppermute | solution.py:33
  81.3 0.1 collective-permute-start.23
  81.4 0.0 collective-permute-done.10
  81.4 0.5 collective-permute-start.5
  81.9 2.3 %collective-permute-done.20 = bf16[32,3584]{1,0:T(8,128)(2,1)S(1)} collective-permute-done((bf16[32,3584]{1,0:T(8,128)(2,1)S(1)}, bf16[32,3584]{1,0:T(8,128)(2,1)S(1)}, u32[]{:S(2)}, u32[]{:S(2)}) %collective-permute-start.20) | collective-permute-done | bytes 229408 | tf_op jit(solution)/shard_map/ppermute | solution.py:33
  84.2 2.5 %collective-permute-done.26 = bf16[32,3584]{1,0:T(8,128)(2,1)S(1)} collective-permute-done((bf16[32,3584]{1,0:T(8,128)(2,1)S(1)}, bf16[32,3584]{1,0:T(8,128)(2,1)S(1)}, u32[]{:S(2)}, u32[]{:S(2)}) %collective-permute-start.26) | collective-permute-done | bytes 229408 | tf_op jit(solution)/shard_map/ppermute | solution.py:33
  86.6 1.4 %fusion.103 = (bf16[32,3584]{1,0:T(8,128)(2,1)S(1)}, bf16[32,3584]{1,0:T(8,128)(2,1)S(1)}) fusion(f32[128,3584]{1,0:T(8,128)} %get-tuple-element.25, bf16[32,3584]{1,0:T(8,128)(2,1)S(1)} %collective-permute-done.20, bf16[32,3584]{1,0:T(8,128)(2,1)S(1)} %collective-permute-done.10, bf16[32,3584]{1,0:T(8,128)(2,1)S(1)} %collective-permute-done.26, ...), kind=kLoop, calls=%fused_computation.61 | loop fusion | flops 1146880 | bytes 2293760 | tf_op jit(solution)/shard_map/convert_element_type | solution.py:71
  88.0 1.6 %collective-permute-start.21 = (bf16[32,3584]{1,0:T(8,128)(2,1)S(1)}, bf16[32,3584]{1,0:T(8,128)(2,1)S(1)}, u32[]{:S(2)}, u32[]{:S(2)}) collective-permute-start(bf16[32,3584]{1,0:T(8,128)(2,1)S(1)} %get-tuple-element.12), channel_id=1, source_target_pairs={{0,2},{2,4},{4,6},{6,7},{7,5},{5,3},{3,1},{1,0},{10,8},{12,10},{14... | collective-permute-start | bytes 688136 | tf_op jit(solution)/shard_map/ppermute | solution.py:33
  89.6 1.6 %collective-permute-start.27 = (bf16[32,3584]{1,0:T(8,128)(2,1)S(1)}, bf16[32,3584]{1,0:T(8,128)(2,1)S(1)}, u32[]{:S(2)}, u32[]{:S(2)}) collective-permute-start(bf16[32,3584]{1,0:T(8,128)(2,1)S(1)} %get-tuple-element.13), channel_id=1, source_target_pairs={{0,2},{2,4},{4,6},{6,7},{7,5},{5,3},{3,1},{1,0},{10,8},{12,10},{14... | collective-permute-start | bytes 688136 | tf_op jit(solution)/shard_map/ppermute | solution.py:33
  91.3 2.8 %collective-permute-done.21 = bf16[32,3584]{1,0:T(8,128)(2,1)S(1)} collective-permute-done((bf16[32,3584]{1,0:T(8,128)(2,1)S(1)}, bf16[32,3584]{1,0:T(8,128)(2,1)S(1)}, u32[]{:S(2)}, u32[]{:S(2)}) %collective-permute-start.21) | collective-permute-done | bytes 229408 | tf_op jit(solution)/shard_map/ppermute | solution.py:33
  94.1 2.5 %collective-permute-done.27 = bf16[32,3584]{1,0:T(8,128)(2,1)S(1)} collective-permute-done((bf16[32,3584]{1,0:T(8,128)(2,1)S(1)}, bf16[32,3584]{1,0:T(8,128)(2,1)S(1)}, u32[]{:S(2)}, u32[]{:S(2)}) %collective-permute-start.27) | collective-permute-done | bytes 229408 | tf_op jit(solution)/shard_map/ppermute | solution.py:33
  96.5 0.1 fusion.105
  96.7 1.6 %collective-permute-start.28 = (bf16[32,3584]{1,0:T(8,128)(2,1)S(1)}, bf16[32,3584]{1,0:T(8,128)(2,1)S(1)}, u32[]{:S(2)}, u32[]{:S(2)}) collective-permute-start(bf16[32,3584]{1,0:T(8,128)(2,1)S(1)} %get-tuple-element.11), channel_id=1, source_target_pairs={{0,2},{2,4},{4,6},{6,7},{7,5},{5,3},{3,1},{1,0},{10,8},{12,10},{14... | collective-permute-start | bytes 688136 | tf_op jit(solution)/shard_map/ppermute | solution.py:33
  98.3 7.9 %fusion.53 = f32[64,3584]{1,0:T(8,128)S(1)} fusion(bf16[1,1024,3584]{2,1,0:T(8,128)(2,1)} %param.9, f32[64]{0:T(128)S(1)} %get-tuple-element.6, bf16[1,3584,1024]{2,1,0:T(8,128)(2,1)} %param.8, bf16[64,3712]{1,0:T(8,128)(2,1)S(1)} %pad_maximum_fusion), kind=kOutput, calls=%fused_computation.31 | convolution fusion | flops 940539904 | bytes 16056832 | tf_op jit(solution)/shard_map/dot_general | solution.py:49
  106.2 1.6 %collective-permute-start.22 = (bf16[32,3584]{1,0:T(8,128)(2,1)S(1)}, bf16[32,3584]{1,0:T(8,128)(2,1)S(1)}, u32[]{:S(2)}, u32[]{:S(2)}) collective-permute-start(bf16[32,3584]{1,0:T(8,128)(2,1)S(1)} %get-tuple-element.10), channel_id=1, source_target_pairs={{0,2},{2,4},{4,6},{6,7},{7,5},{5,3},{3,1},{1,0},{10,8},{12,10},{14... | collective-permute-start | bytes 688136 | tf_op jit(solution)/shard_map/ppermute | solution.py:33
  107.8 0.1 collective-permute-start.29
  107.9 4.3 %collective-permute-done.22 = bf16[32,3584]{1,0:T(8,128)(2,1)S(1)} collective-permute-done((bf16[32,3584]{1,0:T(8,128)(2,1)S(1)}, bf16[32,3584]{1,0:T(8,128)(2,1)S(1)}, u32[]{:S(2)}, u32[]{:S(2)}) %collective-permute-start.22) | collective-permute-done | bytes 229408 | tf_op jit(solution)/shard_map/ppermute | solution.py:33
  112.2 0.8 fusion.107
  (41 shorter events, 0.5 us)
Async XLA Ops:
  2.6 7.1 %collective-permute-start.1 = (bf16[32,3712]{1,0:T(8,128)(2,1)S(1)}, bf16[32,3712]{1,0:T(8,128)(2,1)S(1)}, u32[]{:S(2)}, u32[]{:S(2)}) collective-permute-start(bf16[32,3712]{1,0:T(8,128)(2,1)S(1)} %pad_maximum_fusion.1), channel_id=1, source_target_pairs={{0,2},{2,4},{4,6},{6,7},{7,5},{5,3},{3,1},{1,0},{10,8},{12,10},{14... | collective-permute-start | bytes 712712 | tf_op jit(solution)/shard_map/ppermute | solution.py:33
  5.7 6.1 %collective-permute-start = (bf16[32,3712]{1,0:T(8,128)(2,1)S(1)}, bf16[32,3712]{1,0:T(8,128)(2,1)S(1)}, u32[]{:S(2)}, u32[]{:S(2)}) collective-permute-start(bf16[32,3712]{1,0:T(8,128)(2,1)S(1)} %pad_maximum_fusion.1), channel_id=1, source_target_pairs={{0,8},{8,0},{1,9},{9,1},{2,10},{10,2},{3,11},{11,3},{4,12},{12,4},... | collective-permute-start | bytes 712712 | tf_op jit(solution)/shard_map/ppermute | solution.py:36
  9.7 6.1 %collective-permute-start.6 = (bf16[32,3712]{1,0:T(8,128)(2,1)S(1)}, bf16[32,3712]{1,0:T(8,128)(2,1)S(1)}, u32[]{:S(2)}, u32[]{:S(2)}) collective-permute-start(bf16[32,3712]{1,0:T(8,128)(2,1)S(1)} %collective-permute-done.1), channel_id=1, source_target_pairs={{0,2},{2,4},{4,6},{6,7},{7,5},{5,3},{3,1},{1,0},{10,8},{12,10},{14... | collective-permute-start | bytes 712712 | tf_op jit(solution)/shard_map/ppermute | solution.py:33
  11.8 14.9 %collective-permute-start.4 = (bf16[32,3712]{1,0:T(8,128)(2,1)S(1)}, bf16[32,3712]{1,0:T(8,128)(2,1)S(1)}, u32[]{:S(2)}, u32[]{:S(2)}) collective-permute-start(bf16[32,3712]{1,0:T(8,128)(2,1)S(1)} %collective-permute-done.1), channel_id=1, source_target_pairs={{0,8},{8,0},{1,9},{9,1},{2,10},{10,2},{3,11},{11,3},{4,12},{12,4},... | collective-permute-start | bytes 712712 | tf_op jit(solution)/shard_map/ppermute | solution.py:36
  11.8 6.6 %collective-permute-start.2 = (bf16[32,3712]{1,0:T(8,128)(2,1)S(1)}, bf16[32,3712]{1,0:T(8,128)(2,1)S(1)}, u32[]{:S(2)}, u32[]{:S(2)}) collective-permute-start(bf16[32,3712]{1,0:T(8,128)(2,1)S(1)} %collective-permute-done), channel_id=1, source_target_pairs={{0,2},{2,4},{4,6},{6,7},{7,5},{5,3},{3,1},{1,0},{10,8},{12,10},{14... | collective-permute-start | bytes 712712 | tf_op jit(solution)/shard_map/ppermute | solution.py:33
  15.8 6.1 %collective-permute-start.11 = (bf16[32,3712]{1,0:T(8,128)(2,1)S(1)}, bf16[32,3712]{1,0:T(8,128)(2,1)S(1)}, u32[]{:S(2)}, u32[]{:S(2)}) collective-permute-start(bf16[32,3712]{1,0:T(8,128)(2,1)S(1)} %collective-permute-done.6), channel_id=1, source_target_pairs={{0,2},{2,4},{4,6},{6,7},{7,5},{5,3},{3,1},{1,0},{10,8},{12,10},{14... | collective-permute-start | bytes 712712 | tf_op jit(solution)/shard_map/ppermute | solution.py:33
  17.9 15.9 %collective-permute-start.9 = (bf16[32,3712]{1,0:T(8,128)(2,1)S(1)}, bf16[32,3712]{1,0:T(8,128)(2,1)S(1)}, u32[]{:S(2)}, u32[]{:S(2)}) collective-permute-start(bf16[32,3712]{1,0:T(8,128)(2,1)S(1)} %collective-permute-done.6), channel_id=1, source_target_pairs={{0,8},{8,0},{1,9},{9,1},{2,10},{10,2},{3,11},{11,3},{4,12},{12,4},... | collective-permute-start | bytes 712712 | tf_op jit(solution)/shard_map/ppermute | solution.py:36
  18.4 6.1 %collective-permute-start.7 = (bf16[32,3712]{1,0:T(8,128)(2,1)S(1)}, bf16[32,3712]{1,0:T(8,128)(2,1)S(1)}, u32[]{:S(2)}, u32[]{:S(2)}) collective-permute-start(bf16[32,3712]{1,0:T(8,128)(2,1)S(1)} %collective-permute-done.2), channel_id=1, source_target_pairs={{0,2},{2,4},{4,6},{6,7},{7,5},{5,3},{3,1},{1,0},{10,8},{12,10},{14... | collective-permute-start | bytes 712712 | tf_op jit(solution)/shard_map/ppermute | solution.py:33
  20.5 6.1 %collective-permute-start.3 = (bf16[32,3712]{1,0:T(8,128)(2,1)S(1)}, bf16[32,3712]{1,0:T(8,128)(2,1)S(1)}, u32[]{:S(2)}, u32[]{:S(2)}) collective-permute-start(bf16[32,3712]{1,0:T(8,128)(2,1)S(1)} %collective-permute-done.2), channel_id=1, source_target_pairs={{0,8},{8,0},{1,9},{9,1},{2,10},{10,2},{3,11},{11,3},{4,12},{12,4},... | collective-permute-start | bytes 712712 | tf_op jit(solution)/shard_map/ppermute | solution.py:36
  22.0 13.1 %collective-permute-start.14 = (bf16[32,3712]{1,0:T(8,128)(2,1)S(1)}, bf16[32,3712]{1,0:T(8,128)(2,1)S(1)}, u32[]{:S(2)}, u32[]{:S(2)}) collective-permute-start(bf16[32,3712]{1,0:T(8,128)(2,1)S(1)} %collective-permute-done.11), channel_id=1, source_target_pairs={{0,8},{8,0},{1,9},{9,1},{2,10},{10,2},{3,11},{11,3},{4,12},{12,4},... | collective-permute-start | bytes 712712 | tf_op jit(solution)/shard_map/ppermute | solution.py:36
  24.5 8.7 %collective-permute-start.12 = (bf16[32,3712]{1,0:T(8,128)(2,1)S(1)}, bf16[32,3712]{1,0:T(8,128)(2,1)S(1)}, u32[]{:S(2)}, u32[]{:S(2)}) collective-permute-start(bf16[32,3712]{1,0:T(8,128)(2,1)S(1)} %collective-permute-done.7), channel_id=1, source_target_pairs={{0,2},{2,4},{4,6},{6,7},{7,5},{5,3},{3,1},{1,0},{10,8},{12,10},{14... | collective-permute-start | bytes 712712 | tf_op jit(solution)/shard_map/ppermute | solution.py:33
  26.6 7.2 %collective-permute-start.8 = (bf16[32,3712]{1,0:T(8,128)(2,1)S(1)}, bf16[32,3712]{1,0:T(8,128)(2,1)S(1)}, u32[]{:S(2)}, u32[]{:S(2)}) collective-permute-start(bf16[32,3712]{1,0:T(8,128)(2,1)S(1)} %collective-permute-done.7), channel_id=1, source_target_pairs={{0,8},{8,0},{1,9},{9,1},{2,10},{10,2},{3,11},{11,3},{4,12},{12,4},... | collective-permute-start | bytes 712712 | tf_op jit(solution)/shard_map/ppermute | solution.py:36
  26.7 6.4 %collective-permute-start.16 = (bf16[32,3712]{1,0:T(8,128)(2,1)S(1)}, bf16[32,3712]{1,0:T(8,128)(2,1)S(1)}, u32[]{:S(2)}, u32[]{:S(2)}) collective-permute-start(bf16[32,3712]{1,0:T(8,128)(2,1)S(1)} %collective-permute-done.11), channel_id=1, source_target_pairs={{0,2},{2,4},{4,6},{6,7},{7,5},{5,3},{3,1},{1,0},{10,8},{12,10},{14... | collective-permute-start | bytes 712712 | tf_op jit(solution)/shard_map/ppermute | solution.py:33
  28.4 6.8 %copy-start.3 = (bf16[128,3712]{1,0:T(8,128)(2,1)}, bf16[128,3712]{1,0:T(8,128)(2,1)S(1)}, u32[]{:S(2)}) copy-start(bf16[128,3712]{1,0:T(8,128)(2,1)S(1)} %constant_dynamic-update-slice_fusion) | copy-start | bytes 2850820
  33.2 12.1 %collective-permute-start.17 = (bf16[32,3712]{1,0:T(8,128)(2,1)S(1)}, bf16[32,3712]{1,0:T(8,128)(2,1)}, u32[]{:S(2)}, u32[]{:S(2)}) collective-permute-start(bf16[32,3712]{1,0:T(8,128)(2,1)S(1)} %collective-permute-done.16), channel_id=1, source_target_pairs={{0,8},{8,0},{1,9},{9,1},{2,10},{10,2},{3,11},{11,3},{4,12},{12,4},... | collective-permute-start | bytes 712712 | tf_op jit(solution)/shard_map/ppermute | solution.py:36
  33.2 1.8 %collective-permute-start.13 = (bf16[32,3712]{1,0:T(8,128)(2,1)S(1)}, bf16[32,3712]{1,0:T(8,128)(2,1)S(1)}, u32[]{:S(2)}, u32[]{:S(2)}) collective-permute-start(bf16[32,3712]{1,0:T(8,128)(2,1)S(1)} %collective-permute-done.12), channel_id=1, source_target_pairs={{0,8},{8,0},{1,9},{9,1},{2,10},{10,2},{3,11},{11,3},{4,12},{12,4},... | collective-permute-start | bytes 712712 | tf_op jit(solution)/shard_map/ppermute | solution.py:36
  33.9 1.3 %copy-start.1 = (bf16[128,3712]{1,0:T(8,128)(2,1)}, bf16[128,3712]{1,0:T(8,128)(2,1)S(1)}, u32[]{:S(2)}) copy-start(bf16[128,3712]{1,0:T(8,128)(2,1)S(1)} %constant_dynamic-update-slice_fusion.4) | copy-start | bytes 2850820
  35.2 11.0 %copy-start = (bf16[32,3584]{1,0:T(8,128)(2,1)S(1)}, bf16[32,3584]{1,0:T(8,128)(2,1)}, u32[]{:S(2)}) copy-start(bf16[32,3584]{1,0:T(8,128)(2,1)} %param.5) | copy-start | bytes 688132
  44.7 31.8 %collective-permute-start.15 = (bf16[32,3584]{1,0:T(8,128)(2,1)}, bf16[32,3584]{1,0:T(8,128)(2,1)}, u32[]{:S(2)}, u32[]{:S(2)}) collective-permute-start(bf16[32,3584]{1,0:T(8,128)(2,1)} %get-tuple-element.20), channel_id=1, source_target_pairs={{0,8},{8,0},{1,9},{9,1},{2,10},{10,2},{3,11},{11,3},{4,12},{12,4},... | collective-permute-start | bytes 688136 | tf_op jit(solution)/shard_map/ppermute | solution.py:36
  45.0 31.6 %collective-permute-start.25 = (bf16[32,3584]{1,0:T(8,128)(2,1)}, bf16[32,3584]{1,0:T(8,128)(2,1)}, u32[]{:S(2)}, u32[]{:S(2)}) collective-permute-start(bf16[32,3584]{1,0:T(8,128)(2,1)} %get-tuple-element.21), channel_id=1, source_target_pairs={{0,8},{8,0},{1,9},{9,1},{2,10},{10,2},{3,11},{11,3},{4,12},{12,4},... | collective-permute-start | bytes 688136 | tf_op jit(solution)/shard_map/ppermute | solution.py:36
  46.3 8.9 %copy-start.2 = (bf16[128,3712]{1,0:T(8,128)(2,1)S(1)}, bf16[128,3712]{1,0:T(8,128)(2,1)}, u32[]{:S(2)}) copy-start(bf16[128,3712]{1,0:T(8,128)(2,1)} %copy-done.1) | copy-start | bytes 2850820
  55.0 10.2 %collective-permute-start.18 = (bf16[32,3584]{1,0:T(8,128)(2,1)}, bf16[32,3584]{1,0:T(8,128)(2,1)}, u32[]{:S(2)}, u32[]{:S(2)}) collective-permute-start(bf16[32,3584]{1,0:T(8,128)(2,1)} %slice.210), channel_id=1, source_target_pairs={{0,8},{8,0},{1,9},{9,1},{2,10},{10,2},{3,11},{11,3},{4,12},{12,4},... | collective-permute-start | bytes 688136 | tf_op jit(solution)/shard_map/ppermute | solution.py:36
  64.7 16.7 %collective-permute-start.10 = (bf16[32,3584]{1,0:T(8,128)(2,1)}, bf16[32,3584]{1,0:T(8,128)(2,1)S(1)}, u32[]{:S(2)}, u32[]{:S(2)}) collective-permute-start(bf16[32,3584]{1,0:T(8,128)(2,1)} %get-tuple-element.18), channel_id=1, source_target_pairs={{0,8},{8,0},{1,9},{9,1},{2,10},{10,2},{3,11},{11,3},{4,12},{12,4},... | collective-permute-start | bytes 688136 | tf_op jit(solution)/shard_map/ppermute | solution.py:36
  64.9 17.0 %collective-permute-start.24 = (bf16[32,3584]{1,0:T(8,128)(2,1)}, bf16[32,3584]{1,0:T(8,128)(2,1)}, u32[]{:S(2)}, u32[]{:S(2)}) collective-permute-start(bf16[32,3584]{1,0:T(8,128)(2,1)} %get-tuple-element.19), channel_id=1, source_target_pairs={{0,8},{8,0},{1,9},{9,1},{2,10},{10,2},{3,11},{11,3},{4,12},{12,4},... | collective-permute-start | bytes 688136 | tf_op jit(solution)/shard_map/ppermute | solution.py:36
  66.9 9.7 %collective-permute-start.19 = (bf16[32,3584]{1,0:T(8,128)(2,1)}, bf16[32,3584]{1,0:T(8,128)(2,1)}, u32[]{:S(2)}, u32[]{:S(2)}) collective-permute-start(bf16[32,3584]{1,0:T(8,128)(2,1)} %fusion.98), channel_id=1, source_target_pairs={{0,2},{2,4},{4,6},{6,7},{7,5},{5,3},{3,1},{1,0},{10,8},{12,10},{14... | collective-permute-start | bytes 688136 | tf_op jit(solution)/shard_map/ppermute | solution.py:33
  78.1 6.1 %collective-permute-start.20 = (bf16[32,3584]{1,0:T(8,128)(2,1)S(1)}, bf16[32,3584]{1,0:T(8,128)(2,1)S(1)}, u32[]{:S(2)}, u32[]{:S(2)}) collective-permute-start(bf16[32,3584]{1,0:T(8,128)(2,1)S(1)} %get-tuple-element.14), channel_id=1, source_target_pairs={{0,2},{2,4},{4,6},{6,7},{7,5},{5,3},{3,1},{1,0},{10,8},{12,10},{14... | collective-permute-start | bytes 688136 | tf_op jit(solution)/shard_map/ppermute | solution.py:33
  79.7 6.9 %collective-permute-start.26 = (bf16[32,3584]{1,0:T(8,128)(2,1)S(1)}, bf16[32,3584]{1,0:T(8,128)(2,1)S(1)}, u32[]{:S(2)}, u32[]{:S(2)}) collective-permute-start(bf16[32,3584]{1,0:T(8,128)(2,1)S(1)} %get-tuple-element.15), channel_id=1, source_target_pairs={{0,2},{2,4},{4,6},{6,7},{7,5},{5,3},{3,1},{1,0},{10,8},{12,10},{14... | collective-permute-start | bytes 688136 | tf_op jit(solution)/shard_map/ppermute | solution.py:33
  81.3 9.9 %collective-permute-start.23 = (bf16[32,3584]{1,0:T(8,128)(2,1)S(1)}, bf16[32,3584]{1,0:T(8,128)(2,1)S(1)}, u32[]{:S(2)}, u32[]{:S(2)}) collective-permute-start(bf16[32,3584]{1,0:T(8,128)(2,1)S(1)} %get-tuple-element.17), channel_id=1, source_target_pairs={{0,8},{8,0},{1,9},{9,1},{2,10},{10,2},{3,11},{11,3},{4,12},{12,4},... | collective-permute-start | bytes 688136 | tf_op jit(solution)/shard_map/ppermute | solution.py:36
  81.4 9.8 %collective-permute-start.5 = (bf16[32,3584]{1,0:T(8,128)(2,1)S(1)}, bf16[32,3584]{1,0:T(8,128)(2,1)S(1)}, u32[]{:S(2)}, u32[]{:S(2)}) collective-permute-start(bf16[32,3584]{1,0:T(8,128)(2,1)S(1)} %get-tuple-element.16), channel_id=1, source_target_pairs={{0,8},{8,0},{1,9},{9,1},{2,10},{10,2},{3,11},{11,3},{4,12},{12,4},... | collective-permute-start | bytes 688136 | tf_op jit(solution)/shard_map/ppermute | solution.py:36
  88.0 6.1 %collective-permute-start.21 = (bf16[32,3584]{1,0:T(8,128)(2,1)S(1)}, bf16[32,3584]{1,0:T(8,128)(2,1)S(1)}, u32[]{:S(2)}, u32[]{:S(2)}) collective-permute-start(bf16[32,3584]{1,0:T(8,128)(2,1)S(1)} %get-tuple-element.12), channel_id=1, source_target_pairs={{0,2},{2,4},{4,6},{6,7},{7,5},{5,3},{3,1},{1,0},{10,8},{12,10},{14... | collective-permute-start | bytes 688136 | tf_op jit(solution)/shard_map/ppermute | solution.py:33
  89.6 6.9 %collective-permute-start.27 = (bf16[32,3584]{1,0:T(8,128)(2,1)S(1)}, bf16[32,3584]{1,0:T(8,128)(2,1)S(1)}, u32[]{:S(2)}, u32[]{:S(2)}) collective-permute-start(bf16[32,3584]{1,0:T(8,128)(2,1)S(1)} %get-tuple-element.13), channel_id=1, source_target_pairs={{0,2},{2,4},{4,6},{6,7},{7,5},{5,3},{3,1},{1,0},{10,8},{12,10},{14... | collective-permute-start | bytes 688136 | tf_op jit(solution)/shard_map/ppermute | solution.py:33
  96.7 11.1 %collective-permute-start.28 = (bf16[32,3584]{1,0:T(8,128)(2,1)S(1)}, bf16[32,3584]{1,0:T(8,128)(2,1)S(1)}, u32[]{:S(2)}, u32[]{:S(2)}) collective-permute-start(bf16[32,3584]{1,0:T(8,128)(2,1)S(1)} %get-tuple-element.11), channel_id=1, source_target_pairs={{0,2},{2,4},{4,6},{6,7},{7,5},{5,3},{3,1},{1,0},{10,8},{12,10},{14... | collective-permute-start | bytes 688136 | tf_op jit(solution)/shard_map/ppermute | solution.py:33
  106.2 6.1 %collective-permute-start.22 = (bf16[32,3584]{1,0:T(8,128)(2,1)S(1)}, bf16[32,3584]{1,0:T(8,128)(2,1)S(1)}, u32[]{:S(2)}, u32[]{:S(2)}) collective-permute-start(bf16[32,3584]{1,0:T(8,128)(2,1)S(1)} %get-tuple-element.10), channel_id=1, source_target_pairs={{0,2},{2,4},{4,6},{6,7},{7,5},{5,3},{3,1},{1,0},{10,8},{12,10},{14... | collective-permute-start | bytes 688136 | tf_op jit(solution)/shard_map/ppermute | solution.py:33
  107.8 4.4 %collective-permute-start.29 = (bf16[32,3584]{1,0:T(8,128)(2,1)S(1)}, bf16[32,3584]{1,0:T(8,128)(2,1)S(1)}, u32[]{:S(2)}, u32[]{:S(2)}) collective-permute-start(bf16[32,3584]{1,0:T(8,128)(2,1)S(1)} %fusion.97), channel_id=1, source_target_pairs={{0,8},{8,0},{1,9},{9,1},{2,10},{10,2},{3,11},{11,3},{4,12},{12,4},... | collective-permute-start | bytes 688136 | tf_op jit(solution)/shard_map/ppermute | solution.py:36

commit v3 on v2

v3 whole, which is shorter than its diff:
```python
import functools
import jax
import jax.numpy as jnp
from jax import lax
from jax.experimental import pallas as pl
from jax.experimental.pallas import tpu as pltpu
from jax.sharding import PartitionSpec as P

BOTH = ("node", "local")
LANES = 128


def gather_plan(tokens, expert_ids, route_weights, w_up, w_down):
    mine = lax.axis_index(BOTH)
    everyone = lax.all_gather(tokens, BOTH, tiled=True)
    ids = lax.all_gather(expert_ids, BOTH, tiled=True)
    weights = lax.all_gather(route_weights, BOTH, tiled=True)
    scale = jnp.sum(jnp.where(ids == mine, weights.astype(jnp.float32), 0.0), axis=1)
    hidden = jax.nn.silu(jnp.dot(everyone, w_up[0], preferred_element_type=jnp.float32)).astype(jnp.bfloat16)
    answer = jnp.dot(hidden, w_down[0], preferred_element_type=jnp.float32)
    part = (answer * scale[:, None]).astype(jnp.bfloat16)
    return lax.psum_scatter(part, BOTH, scatter_dimension=0, tiled=True)


def step_of(size, wanted):
    step = wanted
    while step > LANES and size % step:
        step //= 2
    return step if size % step == 0 else size


def expert_body(blocks, kept, mine_ref, *refs):
    tokens = refs[:blocks]
    up_ref, down_ref = refs[blocks:blocks + 2]
    outs = refs[blocks + 2:2 * blocks + 2]
    hidden_ref = refs[2 * blocks + 2]
    width, middle = up_ref.shape
    rows = tokens[0].shape[0]
    x = jnp.concatenate([t[:, :width] for t in tokens], axis=0)
    table = jnp.concatenate([t[:, width:] for t in tokens], axis=0).astype(jnp.float32)
    here = lax.broadcasted_iota(jnp.int32, table.shape, 1) == mine_ref[0]
    scale = jnp.sum(jnp.where(here, table, 0.0), axis=1, keepdims=True)
    step = step_of(middle, 256)
    for j in range(0, middle, step):
        up = jnp.dot(x, up_ref[:, j:j + step], preferred_element_type=jnp.float32)
        hidden_ref[:, j:j + step] = (up / (1.0 + jnp.exp(-up))).astype(jnp.bfloat16)
    hidden = hidden_ref[...]
    step = step_of(width, 512)
    for j in range(0, width, step):
        answer = jnp.dot(hidden, down_ref[:, j:j + step], preferred_element_type=jnp.float32)
        answer = answer.astype(jnp.bfloat16).astype(jnp.float32) * scale
        for i in range(blocks):
            outs[i][:, j:j + step] = answer[i * rows:(i + 1) * rows].astype(outs[i].dtype)


def expert(mine, blocks, kept, up, down):
    rows = blocks[0].shape[0]
    width, middle = up.shape
    total = rows * len(blocks)
    vmem = pl.BlockSpec(memory_space=pltpu.VMEM)
    return pl.pallas_call(
        functools.partial(expert_body, len(blocks), kept),
        out_shape=[
            jax.ShapeDtypeStruct((rows, width), jnp.float32 if k else jnp.bfloat16) for k in kept
        ],
        in_specs=[pl.BlockSpec(memory_space=pltpu.SMEM)] + [vmem] * (len(blocks) + 2),
        out_specs=[vmem] * len(blocks),
        scratch_shapes=[pltpu.VMEM((total, middle), jnp.bfloat16)],
        compiler_params=pltpu.CompilerParams(vmem_limit_bytes=24 * 2**20),
        cost_estimate=pl.CostEstimate(
            flops=4 * total * width * middle, bytes_accessed=4 * width * middle, transcendentals=total * middle
        ),
    )(mine, *blocks, up, down)


def first_body(mine_ref, own_ref, other_ref, up_hbm, down_hbm, out_own, out_other, up_ref, down_ref, hidden_ref, sems):
    width, middle = up_ref.shape
    up_step, down_step = step_of(middle, 256), step_of(width, 512)
    copies = []
    for j in range(0, middle, up_step):
        s = pl.ds(j, up_step)
        copies.append(pltpu.make_async_copy(up_hbm.at[:, s], up_ref.at[:, s], sems.at[len(copies)]))
    for j in range(0, width, down_step):
        s = pl.ds(j, down_step)
        copies.append(pltpu.make_async_copy(down_hbm.at[:, s], down_ref.at[:, s], sems.at[len(copies)]))
    for c in copies:
        c.start()
    rows = own_ref.shape[0]
    x = jnp.concatenate([own_ref[:, :width], other_ref[:, :width]], axis=0)
    table = jnp.concatenate([own_ref[:, width:], other_ref[:, width:]], axis=0).astype(jnp.float32)
    here = lax.broadcasted_iota(jnp.int32, table.shape, 1) == mine_ref[0]
    scale = jnp.sum(jnp.where(here, table, 0.0), axis=1, keepdims=True)
    for j in range(0, middle, up_step):
        copies[j // up_step].wait()
        up = jnp.dot(x, up_ref[:, j:j + up_step], preferred_element_type=jnp.float32)
        hidden_ref[:, j:j + up_step] = (up / (1.0 + jnp.exp(-up))).astype(jnp.bfloat16)
    hidden = hidden_ref[...]
    for j in range(0, width, down_step):
        copies[middle // up_step + j // down_step].wait()
        answer = jnp.dot(hidden, down_ref[:, j:j + down_step], preferred_element_type=jnp.float32)
        answer = answer.astype(jnp.bfloat16).astype(jnp.float32) * scale
        out_own[:, j:j + down_step] = answer[:rows]
        out_other[:, j:j + down_step] = answer[rows:]


def first_expert(mine, own, other, w_up, w_down):
    rows = own.shape[0]
    width, middle = w_up.shape
    chunks = middle // step_of(middle, 256) + width // step_of(width, 512)
    vmem, anywhere = pl.BlockSpec(memory_space=pltpu.VMEM), pl.BlockSpec(memory_space=pl.ANY)
    return pl.pallas_call(
        first_body,
        out_shape=[jax.ShapeDtypeStruct((rows, width), jnp.float32)] * 2
        + [pltpu.VMEM(w_up.shape, w_up.dtype), pltpu.VMEM(w_down.shape, w_down.dtype)],
        in_specs=[pl.BlockSpec(memory_space=pltpu.SMEM), vmem, vmem, anywhere, anywhere],
        out_specs=[vmem] * 4,
        scratch_shapes=[pltpu.VMEM((2 * rows, middle), jnp.bfloat16), pltpu.SemaphoreType.DMA((chunks,))],
        compiler_params=pltpu.CompilerParams(vmem_limit_bytes=32 * 2**20),
        cost_estimate=pl.CostEstimate(
            flops=8 * rows * width * middle, bytes_accessed=4 * width * middle, transcendentals=2 * rows * middle
        ),
    )(mine, own, other, w_up, w_down)


def label_body(tokens_ref, ids_ref, weights_ref, out_ref):
    rows, width = tokens_ref.shape
    out_ref[:, :width] = tokens_ref[...]
    columns = out_ref.shape[1] - width
    column = lax.broadcasted_iota(jnp.int32, (rows, columns), 1)
    weights = weights_ref[...].astype(jnp.float32)
    table = jnp.zeros((rows, columns), jnp.float32)
    for k in range(ids_ref.shape[1]):
        table = jnp.where(ids_ref[:, k:k + 1] == column, weights[:, k:k + 1], table)
    out_ref[:, width:] = table.astype(jnp.bfloat16)


def label(tokens, expert_ids, route_weights, columns):
    rows, width = tokens.shape
    vmem = pl.BlockSpec(memory_space=pltpu.VMEM)
    return pl.pallas_call(
        label_body,
        out_shape=jax.ShapeDtypeStruct((rows, width + columns), jnp.bfloat16),
        in_specs=[vmem] * 3,
        out_specs=vmem,
    )(tokens, expert_ids, route_weights)


def ring_plan(tokens, expert_ids, route_weights, w_up, w_down):
    rows, width = tokens.shape
    experts = lax.axis_size(BOTH)
    n = lax.axis_size("local")
    half = n // 2
    mine = lax.axis_index(BOTH).astype(jnp.int32)[None]
    order = list(range(0, n, 2)) + list(range(n - 1, 0, -2))
    onward = [(order[i], order[(i + 1) % n]) for i in range(n)]
    pairs = onward + [(n + b, n + a) for a, b in onward]
    def hop(x):
        return lax.ppermute(x, BOTH, pairs)

    def swap(x):
        return lax.ppermute(x, "node", [(0, 1), (1, 0)])

    def bf(x):
        return x.astype(jnp.bfloat16)

    columns = -(-experts // LANES) * LANES
    own = label(tokens, expert_ids, route_weights, columns)

    a, b = [own], [swap(own)]
    own_a, own_b, up, down = first_expert(mine, own, b[0], w_up[0], w_down[0])
    ahead_a, ahead_b = [None], [None]
    behind, ahead = {}, {}
    for h in range(1, half):
        a.append(hop(a[-1]))
        b.append(hop(b[-1]))
        if h == 1:
            up, down, b[1] = lax.optimization_barrier((up, down, b[1]))
            up = pltpu.with_memory_space_constraint(up, pltpu.VMEM)
            down = pltpu.with_memory_space_constraint(down, pltpu.VMEM)
        ahead_b.append(swap(a[h]))
        ahead_a.append(swap(b[h]))
        if h >= 2:
            done = (a[h - 1], b[h - 1], ahead_a[h - 1], ahead_b[h - 1])
            r = expert(mine, done, (False, False, True, True), up, down)
            behind[h - 1], ahead[h - 1] = r[:2], r[2:]
            a[h], behind[h - 1], ahead[h - 1] = lax.optimization_barrier((a[h], behind[h - 1], ahead[h - 1]))
    a.append(hop(a[-1]))
    ahead_b.append(swap(a[half]))
    h = half - 1
    r = expert(mine, (a[h], b[h], ahead_a[h], ahead_b[h]), (False, False, True, True), up, down)
    behind[h], ahead[h] = r[:2], r[2:]
    far = expert(mine, (a[half], ahead_b[half]), (True, False), up, down)

    sums = {half: [far[0] + swap(far[1]).astype(jnp.float32)]}
    for h in range(half - 1, 0, -1):
        sums[h] = [
            ahead[h][0] + swap(behind[h][1]).astype(jnp.float32),
            ahead[h][1] + swap(behind[h][0]).astype(jnp.float32),
        ]
    run_b = hop(bf(sums[half - 1][1]))
    run_a = hop(bf(sums[half][0]))
    for h in range(half - 1, 0, -1):
        if h < half - 1:
            run_b = hop(bf(sums[h][1] + run_b.astype(jnp.float32)))
        run_a = hop(bf(sums[h][0] + run_a.astype(jnp.float32)))
    last = swap(bf(own_b + run_b.astype(jnp.float32)))
    return bf(own_a + run_a.astype(jnp.float32) + last.astype(jnp.float32))


def solution(mesh):
    placed = (
        P(("rep", "node", "local"), None),
        P(("rep", "node", "local"), None),
        P(("rep", "node", "local"), None),
        P(("node", "local"), None, None),
        P(("node", "local"), None, None),
    )
    n = mesh.shape["local"]
    ringed = mesh.shape["node"] == 2 and n % 2 == 0 and 4 <= n <= 16
    return jax.shard_map(
        ring_plan if ringed else gather_plan,
        mesh=mesh,
        in_specs=placed,
        out_specs=P(("rep", "node", "local"), None),
        check_vma=False,
    )
```

time: 113 us -> 81.5 us (0.72)
  matrix products: 40.7 us -> 0 us
  Pallas kernels: 0 us -> 17.6 us
  other arithmetic: 6.84 us -> 1.35 us
  local copies, waits for them, and re-layouts: 5.21 us -> 3.66 us
  starting transfers between devices: 28.9 us -> 27.4 us
    dot_general x5 -> x0, matrix products: 40.7 us -> none  [expert(): answer = jnp.dot(hidden, w_down[0], preferred_element_type=jnp.float32)]
    pallas_call x0 -> x6, Pallas kernels: none -> 17.6 us  [the longest x4 9.42 us: expert(): pl.pallas_call(functools.partial(expert_body, len(blocks), kept), out_sha...]
    convert_element_type x6 -> x9, other arithmetic: 5.47 us -> 1.35 us  [bf(): return x.astype(jnp.bfloat16)]
    unnamed x19 -> x4, local copies, waits for them, and re-layouts: 0.99 us -> 3.66 us
    slice x4 -> x0, local copies, waits for them, and re-layouts: 2.42 us -> none  [expert(): return [out[i * rows:(i + 1) * rows] for i in range(len(blocks))]]
    ppermute x14, starting transfers between devices: 26.3 us -> 24 us  [hop(): return lax.ppermute(x, BOTH, pairs)]
  transfers between devices with their start and end apart: 30 -> 30, of which waited for: 12 -> 13; matrix products, arithmetic and copies ran while one was open for 44% -> 1% of each run, Pallas kernels for 0% -> 19%
where the time goes in v3:
time: 81.5 us; the launch traced here: 81.3 us
  waiting for transfers between devices  31.2 us (38%)
  starting transfers between devices  27.4 us (34%)
  Pallas kernels  17.6 us (22%)
  local copies, waits for them, and re-layouts  3.66 us (4%)
  other arithmetic  1.35 us (2%)
    ppermute x14, waiting for transfers between devices, hop(): return lax.ppermute(x, BOTH, pairs)  29.8 us
    ppermute x14, starting transfers between devices, hop(): return lax.ppermute(x, BOTH, pairs)  24 us
    pallas_call x4, Pallas kernels, expert(): pl.pallas_call(functools.partial(expert_body, len(blocks), kept), out_sha...  9.42 us
    pallas_call x1, Pallas kernels, first_expert(): pl.pallas_call(first_body, out_shape=[jax.ShapeDtypeStruct((rows, width),...  6.4 us
    unnamed x4, local copies, waits for them, and re-layouts  3.66 us
    ppermute x16, starting transfers between devices, swap(): return lax.ppermute(x, 'node', [(0, 1), (1, 0)])  3.36 us
    pallas_call x1, Pallas kernels, label(): pl.pallas_call(label_body, out_shape=jax.ShapeDtypeStruct((rows, width +...  1.77 us
  transfers between devices with their start and end apart: 30, of which 13 were waited for; matrix products, arithmetic and copies ran while one was open for 1% of the time, Pallas kernels for 19%

profile of v3, /device:TPU:0, one launch (start us, length us, event | category | flops | bytes accessed | tf_op | source)
XLA Modules:
  0.0 81.3 jit_solution(13281526776676666668)
XLA Ops:
  0.0 1.4 %copy.6.ids_ref = s32[32,8]{1,0:T(8,128)} copy(s32[32,8]{0,1:T(8,128)} %param.6) | data formatting | bytes 2048 | tf_op args[1]
  1.4 1.3 %copy.7.weights_ref = bf16[32,8]{1,0:T(8,128)(2,1)} copy(bf16[32,8]{0,1:T(8,128)(2,1)} %param.7) | data formatting | bytes 1024 | tf_op args[2]
  2.7 1.8 %shard_map.55.own_ref = bf16[32,3712]{1,0:T(8,128)(2,1)} custom-call(bf16[32,3584]{1,0:T(8,128)(2,1)} %tokens_ref.1, s32[32,8]{1,0:T(8,128)} %copy.6.ids_ref, bf16[32,8]{1,0:T(8,128)(2,1)} %copy.7.weights_ref), custom_call_target="tpu_custom_call" | custom-call | tf_op jit(solution)/shard_map/pallas_call | solution.py:140
  4.5 0.5 collective-permute-start
  4.9 2.6 %collective-permute-start.1 = (bf16[32,3712]{1,0:T(8,128)(2,1)}, bf16[32,3712]{1,0:T(8,128)(2,1)S(1)}, u32[]{:S(2)}, u32[]{:S(2)}) collective-permute-start(bf16[32,3712]{1,0:T(8,128)(2,1)} %shard_map.55.own_ref), channel_id=1, source_target_pairs={{0,2},{2,4},{4,6},{6,7},{7,5},{5,3},{3,1},{1,0},{10,8},{12,10},{14... | collective-permute-start | bytes 712712 | tf_op jit(solution)/shard_map/ppermute | solution.py:158
  7.5 1.7 %collective-permute-start.3 = (bf16[32,3712]{1,0:T(8,128)(2,1)S(1)}, bf16[32,3712]{1,0:T(8,128)(2,1)S(1)}, u32[]{:S(2)}, u32[]{:S(2)}) collective-permute-start(bf16[32,3712]{1,0:T(8,128)(2,1)S(1)} %collective-permute-done.other_ref), channel_id=1, source_target_pairs={{0,2},{2,4},{4,6},{6,7},{7,5},{5,3},{3,1},{1,0},{10,8},{12,10},{14... | collective-permute-start | bytes 712712 | tf_op jit(solution)/shard_map/ppermute | solution.py:158
  9.2 2.5 %collective-permute-done.1.refs_0_ = bf16[32,3712]{1,0:T(8,128)(2,1)S(1)} collective-permute-done((bf16[32,3712]{1,0:T(8,128)(2,1)}, bf16[32,3712]{1,0:T(8,128)(2,1)S(1)}, u32[]{:S(2)}, u32[]{:S(2)}) %collective-permute-start.1) | collective-permute-done | bytes 237600 | tf_op jit(solution)/shard_map/ppermute | solution.py:158
  11.8 2.1 %collective-permute-start.2 = (bf16[32,3712]{1,0:T(8,128)(2,1)S(1)}, bf16[32,3712]{1,0:T(8,128)(2,1)S(1)}, u32[]{:S(2)}, u32[]{:S(2)}) collective-permute-start(bf16[32,3712]{1,0:T(8,128)(2,1)S(1)} %collective-permute-done.1.refs_0_), channel_id=1, source_target_pairs={{0,2},{2,4},{4,6},{6,7},{7,5},{5,3},{3,1},{1,0},{10,8},{12,10},{14... | collective-permute-start | bytes 712712 | tf_op jit(solution)/shard_map/ppermute | solution.py:158
  13.8 0.9 %copy-done = bf16[32,3712]{1,0:T(8,128)(2,1)S(1)} copy-done((bf16[32,3712]{1,0:T(8,128)(2,1)S(1)}, bf16[32,3712]{1,0:T(8,128)(2,1)}, u32[]{:S(2)}) %copy-start) | copy-done | bytes 237592
  14.8 6.4 %shard_map.56 = (f32[32,3584]{1,0:T(8,128)S(1)}, f32[32,3584]{1,0:T(8,128)S(1)}, bf16[3584,1024]{1,0:T(8,128)(2,1)S(1)}, bf16[1024,3584]{1,0:T(8,128)(2,1)S(1)}) custom-call(s32[1]{0:T(128)} %bitcast.mine_ref, bf16[32,3712]{1,0:T(8,128)(2,1)S(1)} %copy-done, bf16[32,3712]{1,0:T(8,128)(2,1)S(1)} %collective-permute-done.other_ref, ...), custom_call_target="tpu_custom_call" | custom-call | flops 939524096 | bytes 14680064 | tf_op jit(solution)/shard_map/pallas_call | solution.py:111
  21.2 0.0 collective-permute-done.3.refs_1_
  21.2 1.6 %collective-permute-start.8 = (bf16[32,3712]{1,0:T(8,128)(2,1)S(1)}, bf16[32,3712]{1,0:T(8,128)(2,1)S(1)}, u32[]{:S(2)}, u32[]{:S(2)}) collective-permute-start(bf16[32,3712]{1,0:T(8,128)(2,1)S(1)} %collective-permute-done.3.refs_1_), channel_id=1, source_target_pairs={{0,2},{2,4},{4,6},{6,7},{7,5},{5,3},{3,1},{1,0},{10,8},{12,10},{14... | collective-permute-start | bytes 712712 | tf_op jit(solution)/shard_map/ppermute | solution.py:158
  22.8 0.5 collective-permute-start.4
  23.3 0.0 collective-permute-done.2.refs_0_
  23.3 0.0 collective-permute-start.10
  23.4 4.0 %collective-permute-done.8.refs_1_ = bf16[32,3712]{1,0:T(8,128)(2,1)S(1)} collective-permute-done((bf16[32,3712]{1,0:T(8,128)(2,1)S(1)}, bf16[32,3712]{1,0:T(8,128)(2,1)S(1)}, u32[]{:S(2)}, u32[]{:S(2)}) %collective-permute-start.8) | collective-permute-done | bytes 237600 | tf_op jit(solution)/shard_map/ppermute | solution.py:158
  27.4 0.0 collective-permute-done.4.refs_2_
  27.4 2.3 %shard_map.57 = (bf16[32,3584]{1,0:T(8,128)(2,1)S(1)}, bf16[32,3584]{1,0:T(8,128)(2,1)S(1)}, f32[32,3584]{1,0:T(8,128)S(1)}, f32[32,3584]{1,0:T(8,128)S(1)}) custom-call(s32[1]{0:T(128)} %bitcast.mine_ref, bf16[32,3712]{1,0:T(8,128)(2,1)S(1)} %collective-permute-done.1.refs_0_, bf16[32,3712]{1,0:T(8,128)(2,1)S(1)} %collective-permute-done.3.refs_1_, ...), custom_call_target="tpu_custom_call" | custom-call | flops 1879048192 | bytes 14680064 | tf_op jit(solution)/shard_map/pallas_call | solution.py:61
  29.6 1.6 %collective-permute-start.7 = (bf16[32,3712]{1,0:T(8,128)(2,1)S(1)}, bf16[32,3712]{1,0:T(8,128)(2,1)S(1)}, u32[]{:S(2)}, u32[]{:S(2)}) collective-permute-start(bf16[32,3712]{1,0:T(8,128)(2,1)S(1)} %collective-permute-done.2.refs_0_), channel_id=1, source_target_pairs={{0,2},{2,4},{4,6},{6,7},{7,5},{5,3},{3,1},{1,0},{10,8},{12,10},{14... | collective-permute-start | bytes 712712 | tf_op jit(solution)/shard_map/ppermute | solution.py:158
  31.3 1.6 %collective-permute-start.12 = (bf16[32,3712]{1,0:T(8,128)(2,1)S(1)}, bf16[32,3712]{1,0:T(8,128)(2,1)S(1)}, u32[]{:S(2)}, u32[]{:S(2)}) collective-permute-start(bf16[32,3712]{1,0:T(8,128)(2,1)S(1)} %collective-permute-done.8.refs_1_), channel_id=1, source_target_pairs={{0,2},{2,4},{4,6},{6,7},{7,5},{5,3},{3,1},{1,0},{10,8},{12,10},{14... | collective-permute-start | bytes 712712 | tf_op jit(solution)/shard_map/ppermute | solution.py:158
  32.8 2.2 %shard_map.58 = (bf16[32,3584]{1,0:T(8,128)(2,1)S(1)}, bf16[32,3584]{1,0:T(8,128)(2,1)S(1)}, f32[32,3584]{1,0:T(8,128)S(1)}, f32[32,3584]{1,0:T(8,128)S(1)}) custom-call(s32[1]{0:T(128)} %bitcast.mine_ref, bf16[32,3712]{1,0:T(8,128)(2,1)S(1)} %collective-permute-done.2.refs_0_, bf16[32,3712]{1,0:T(8,128)(2,1)S(1)} %collective-permute-done.8.refs_1_, ...), custom_call_target="tpu_custom_call" | custom-call | flops 1879048192 | bytes 14680064 | tf_op jit(solution)/shard_map/pallas_call | solution.py:61
  35.1 0.7 collective-permute-done.7.refs_0_
  35.8 1.6 %collective-permute-start.16 = (bf16[32,3712]{1,0:T(8,128)(2,1)S(1)}, bf16[32,3712]{1,0:T(8,128)(2,1)S(1)}, u32[]{:S(2)}, u32[]{:S(2)}) collective-permute-start(bf16[32,3712]{1,0:T(8,128)(2,1)S(1)} %collective-permute-done.7.refs_0_), channel_id=1, source_target_pairs={{0,2},{2,4},{4,6},{6,7},{7,5},{5,3},{3,1},{1,0},{10,8},{12,10},{14... | collective-permute-start | bytes 712712 | tf_op jit(solution)/shard_map/ppermute | solution.py:158
  37.4 1.0 %collective-permute-done.12.refs_1_ = bf16[32,3712]{1,0:T(8,128)(2,1)S(1)} collective-permute-done((bf16[32,3712]{1,0:T(8,128)(2,1)S(1)}, bf16[32,3712]{1,0:T(8,128)(2,1)S(1)}, u32[]{:S(2)}, u32[]{:S(2)}) %collective-permute-start.12) | collective-permute-done | bytes 237600 | tf_op jit(solution)/shard_map/ppermute | solution.py:158
  38.3 0.0 collective-permute-start.13
  38.3 0.5 collective-permute-start.14
  38.9 3.1 %collective-permute-done.16.refs_0_ = bf16[32,3712]{1,0:T(8,128)(2,1)S(1)} collective-permute-done((bf16[32,3712]{1,0:T(8,128)(2,1)S(1)}, bf16[32,3712]{1,0:T(8,128)(2,1)S(1)}, u32[]{:S(2)}, u32[]{:S(2)}) %collective-permute-start.16) | collective-permute-done | bytes 237600 | tf_op jit(solution)/shard_map/ppermute | solution.py:158
  41.9 0.0 collective-permute-start.17
  41.9 0.0 collective-permute-done.13.refs_2_
  41.9 2.2 %shard_map.59 = (bf16[32,3584]{1,0:T(8,128)(2,1)S(1)}, bf16[32,3584]{1,0:T(8,128)(2,1)S(1)}, f32[32,3584]{1,0:T(8,128)S(1)}, f32[32,3584]{1,0:T(8,128)S(1)}) custom-call(s32[1]{0:T(128)} %bitcast.mine_ref, bf16[32,3712]{1,0:T(8,128)(2,1)S(1)} %collective-permute-done.7.refs_0_, bf16[32,3712]{1,0:T(8,128)(2,1)S(1)} %collective-permute-done.12.refs_1_, ...), custom_call_target="tpu_custom_call" | custom-call | flops 1879048192 | bytes 14680064 | tf_op jit(solution)/shard_map/pallas_call | solution.py:61
  44.2 0.6 collective-permute-start.25
  44.7 0.1 collective-permute-start.23
  44.8 0.4 collective-permute-start.6
  45.2 0.1 collective-permute-start.24
  45.3 0.4 collective-permute-start.11
  45.8 2.7 %shard_map.60 = (f32[32,3584]{1,0:T(8,128)S(1)}, bf16[32,3584]{1,0:T(8,128)(2,1)S(1)}) custom-call(s32[1]{0:T(128)} %bitcast.mine_ref, bf16[32,3712]{1,0:T(8,128)(2,1)S(1)} %collective-permute-done.16.refs_0_, bf16[32,3712]{1,0:T(8,128)(2,1)S(1)} %collective-permute-done.17.refs_1_, bf16[3584,1024]{1,0:T(8,128)(2,1)S(1)} %get-tuple-element.40.refs_4_.refs_2_, ...), custom_call_target="tpu_custom_call" | custom-call | flops 939524096 | bytes 14680064 | tf_op jit(solution)/shard_map/pallas_call | solution.py:61
  48.5 0.0 collective-permute-done.25
  48.5 0.1 collective-permute-start.18
  48.6 0.1 add_convert_fusion.4
  48.7 1.4 %collective-permute-done.18 = bf16[32,3584]{1,0:T(8,128)(2,1)S(1)} collective-permute-done((bf16[32,3584]{1,0:T(8,128)(2,1)S(1)}, bf16[32,3584]{1,0:T(8,128)(2,1)S(1)}, u32[]{:S(2)}, u32[]{:S(2)}) %collective-permute-start.18) | collective-permute-done | bytes 229408 | tf_op jit(solution)/shard_map/ppermute | solution.py:161
  50.0 1.6 %collective-permute-start.26 = (bf16[32,3584]{1,0:T(8,128)(2,1)S(1)}, bf16[32,3584]{1,0:T(8,128)(2,1)S(1)}, u32[]{:S(2)}, u32[]{:S(2)}) collective-permute-start(bf16[32,3584]{1,0:T(8,128)(2,1)S(1)} %add_convert_fusion.4), channel_id=1, source_target_pairs={{0,2},{2,4},{4,6},{6,7},{7,5},{5,3},{3,1},{1,0},{10,8},{12,10},{14... | collective-permute-start | bytes 688136 | tf_op jit(solution)/shard_map/ppermute | solution.py:158
  51.6 0.1 add_convert_fusion.8
  51.7 0.1 collective-permute-start.15
  51.8 4.3 %collective-permute-done.26 = bf16[32,3584]{1,0:T(8,128)(2,1)S(1)} collective-permute-done((bf16[32,3584]{1,0:T(8,128)(2,1)S(1)}, bf16[32,3584]{1,0:T(8,128)(2,1)S(1)}, u32[]{:S(2)}, u32[]{:S(2)}) %collective-permute-start.26) | collective-permute-done | bytes 229408 | tf_op jit(solution)/shard_map/ppermute | solution.py:158
  56.0 1.6 %collective-permute-start.19 = (bf16[32,3584]{1,0:T(8,128)(2,1)S(1)}, bf16[32,3584]{1,0:T(8,128)(2,1)S(1)}, u32[]{:S(2)}, u32[]{:S(2)}) collective-permute-start(bf16[32,3584]{1,0:T(8,128)(2,1)S(1)} %add_convert_fusion.8), channel_id=1, source_target_pairs={{0,2},{2,4},{4,6},{6,7},{7,5},{5,3},{3,1},{1,0},{10,8},{12,10},{14... | collective-permute-start | bytes 688136 | tf_op jit(solution)/shard_map/ppermute | solution.py:158
  57.6 0.1 add_convert_fusion.3
  57.7 1.6 %collective-permute-start.27 = (bf16[32,3584]{1,0:T(8,128)(2,1)S(1)}, bf16[32,3584]{1,0:T(8,128)(2,1)S(1)}, u32[]{:S(2)}, u32[]{:S(2)}) collective-permute-start(bf16[32,3584]{1,0:T(8,128)(2,1)S(1)} %add_convert_fusion.3), channel_id=1, source_target_pairs={{0,2},{2,4},{4,6},{6,7},{7,5},{5,3},{3,1},{1,0},{10,8},{12,10},{14... | collective-permute-start | bytes 688136 | tf_op jit(solution)/shard_map/ppermute | solution.py:158
  59.3 2.7 %collective-permute-done.19 = bf16[32,3584]{1,0:T(8,128)(2,1)S(1)} collective-permute-done((bf16[32,3584]{1,0:T(8,128)(2,1)S(1)}, bf16[32,3584]{1,0:T(8,128)(2,1)S(1)}, u32[]{:S(2)}, u32[]{:S(2)}) %collective-permute-start.19) | collective-permute-done | bytes 229408 | tf_op jit(solution)/shard_map/ppermute | solution.py:158
  62.1 0.1 add_convert_fusion.7
  62.2 1.6 %collective-permute-start.20 = (bf16[32,3584]{1,0:T(8,128)(2,1)S(1)}, bf16[32,3584]{1,0:T(8,128)(2,1)S(1)}, u32[]{:S(2)}, u32[]{:S(2)}) collective-permute-start(bf16[32,3584]{1,0:T(8,128)(2,1)S(1)} %add_convert_fusion.7), channel_id=1, source_target_pairs={{0,2},{2,4},{4,6},{6,7},{7,5},{5,3},{3,1},{1,0},{10,8},{12,10},{14... | collective-permute-start | bytes 688136 | tf_op jit(solution)/shard_map/ppermute | solution.py:158
  63.8 0.7 collective-permute-done.27
  64.5 0.1 add_convert_fusion.2
  64.6 1.6 %collective-permute-start.28 = (bf16[32,3584]{1,0:T(8,128)(2,1)S(1)}, bf16[32,3584]{1,0:T(8,128)(2,1)S(1)}, u32[]{:S(2)}, u32[]{:S(2)}) collective-permute-start(bf16[32,3584]{1,0:T(8,128)(2,1)S(1)} %add_convert_fusion.2), channel_id=1, source_target_pairs={{0,2},{2,4},{4,6},{6,7},{7,5},{5,3},{3,1},{1,0},{10,8},{12,10},{14... | collective-permute-start | bytes 688136 | tf_op jit(solution)/shard_map/ppermute | solution.py:158
  66.3 2.0 %collective-permute-done.20 = bf16[32,3584]{1,0:T(8,128)(2,1)S(1)} collective-permute-done((bf16[32,3584]{1,0:T(8,128)(2,1)S(1)}, bf16[32,3584]{1,0:T(8,128)(2,1)S(1)}, u32[]{:S(2)}, u32[]{:S(2)}) %collective-permute-start.20) | collective-permute-done | bytes 229408 | tf_op jit(solution)/shard_map/ppermute | solution.py:158
  68.2 0.1 add_convert_fusion.6
  68.3 1.6 %collective-permute-start.21 = (bf16[32,3584]{1,0:T(8,128)(2,1)S(1)}, bf16[32,3584]{1,0:T(8,128)(2,1)S(1)}, u32[]{:S(2)}, u32[]{:S(2)}) collective-permute-start(bf16[32,3584]{1,0:T(8,128)(2,1)S(1)} %add_convert_fusion.6), channel_id=1, source_target_pairs={{0,2},{2,4},{4,6},{6,7},{7,5},{5,3},{3,1},{1,0},{10,8},{12,10},{14... | collective-permute-start | bytes 688136 | tf_op jit(solution)/shard_map/ppermute | solution.py:158
  69.9 0.7 collective-permute-done.28
  70.7 0.1 add_convert_fusion.1
  70.7 0.1 collective-permute-start.29
  70.8 3.6 %collective-permute-done.21 = bf16[32,3584]{1,0:T(8,128)(2,1)S(1)} collective-permute-done((bf16[32,3584]{1,0:T(8,128)(2,1)S(1)}, bf16[32,3584]{1,0:T(8,128)(2,1)S(1)}, u32[]{:S(2)}, u32[]{:S(2)}) %collective-permute-start.21) | collective-permute-done | bytes 229408 | tf_op jit(solution)/shard_map/ppermute | solution.py:158
  74.4 0.1 add_convert_fusion.5
  74.5 1.6 %collective-permute-start.22 = (bf16[32,3584]{1,0:T(8,128)(2,1)S(1)}, bf16[32,3584]{1,0:T(8,128)(2,1)S(1)}, u32[]{:S(2)}, u32[]{:S(2)}) collective-permute-start(bf16[32,3584]{1,0:T(8,128)(2,1)S(1)} %add_convert_fusion.5), channel_id=1, source_target_pairs={{0,2},{2,4},{4,6},{6,7},{7,5},{5,3},{3,1},{1,0},{10,8},{12,10},{14... | collective-permute-start | bytes 688136 | tf_op jit(solution)/shard_map/ppermute | solution.py:158
  76.1 4.4 %collective-permute-done.22 = bf16[32,3584]{1,0:T(8,128)(2,1)S(1)} collective-permute-done((bf16[32,3584]{1,0:T(8,128)(2,1)S(1)}, bf16[32,3584]{1,0:T(8,128)(2,1)S(1)}, u32[]{:S(2)}, u32[]{:S(2)}) %collective-permute-start.22) | collective-permute-done | bytes 229408 | tf_op jit(solution)/shard_map/ppermute | solution.py:158
  80.6 0.8 add_convert_fusion
  (15 shorter events, 0.0 us)
Async XLA Ops:
  4.5 3.0 %collective-permute-start = (bf16[32,3712]{1,0:T(8,128)(2,1)}, bf16[32,3712]{1,0:T(8,128)(2,1)S(1)}, u32[]{:S(2)}, u32[]{:S(2)}) collective-permute-start(bf16[32,3712]{1,0:T(8,128)(2,1)} %shard_map.55.own_ref), channel_id=1, source_target_pairs={{0,8},{8,0},{1,9},{9,1},{2,10},{10,2},{3,11},{11,3},{4,12},{12,4},... | collective-permute-start | bytes 712712 | tf_op jit(solution)/shard_map/ppermute | solution.py:161
  4.9 6.8 %collective-permute-start.1 = (bf16[32,3712]{1,0:T(8,128)(2,1)}, bf16[32,3712]{1,0:T(8,128)(2,1)S(1)}, u32[]{:S(2)}, u32[]{:S(2)}) collective-permute-start(bf16[32,3712]{1,0:T(8,128)(2,1)} %shard_map.55.own_ref), channel_id=1, source_target_pairs={{0,2},{2,4},{4,6},{6,7},{7,5},{5,3},{3,1},{1,0},{10,8},{12,10},{14... | collective-permute-start | bytes 712712 | tf_op jit(solution)/shard_map/ppermute | solution.py:158
  7.5 13.7 %collective-permute-start.3 = (bf16[32,3712]{1,0:T(8,128)(2,1)S(1)}, bf16[32,3712]{1,0:T(8,128)(2,1)S(1)}, u32[]{:S(2)}, u32[]{:S(2)}) collective-permute-start(bf16[32,3712]{1,0:T(8,128)(2,1)S(1)} %collective-permute-done.other_ref), channel_id=1, source_target_pairs={{0,2},{2,4},{4,6},{6,7},{7,5},{5,3},{3,1},{1,0},{10,8},{12,10},{14... | collective-permute-start | bytes 712712 | tf_op jit(solution)/shard_map/ppermute | solution.py:158
  11.8 11.6 %collective-permute-start.2 = (bf16[32,3712]{1,0:T(8,128)(2,1)S(1)}, bf16[32,3712]{1,0:T(8,128)(2,1)S(1)}, u32[]{:S(2)}, u32[]{:S(2)}) collective-permute-start(bf16[32,3712]{1,0:T(8,128)(2,1)S(1)} %collective-permute-done.1.refs_0_), channel_id=1, source_target_pairs={{0,2},{2,4},{4,6},{6,7},{7,5},{5,3},{3,1},{1,0},{10,8},{12,10},{14... | collective-permute-start | bytes 712712 | tf_op jit(solution)/shard_map/ppermute | solution.py:158
  13.8 0.9 %copy-start = (bf16[32,3712]{1,0:T(8,128)(2,1)S(1)}, bf16[32,3712]{1,0:T(8,128)(2,1)}, u32[]{:S(2)}) copy-start(bf16[32,3712]{1,0:T(8,128)(2,1)} %shard_map.55.own_ref) | copy-start | bytes 712708
  21.2 6.2 %collective-permute-start.8 = (bf16[32,3712]{1,0:T(8,128)(2,1)S(1)}, bf16[32,3712]{1,0:T(8,128)(2,1)S(1)}, u32[]{:S(2)}, u32[]{:S(2)}) collective-permute-start(bf16[32,3712]{1,0:T(8,128)(2,1)S(1)} %collective-permute-done.3.refs_1_), channel_id=1, source_target_pairs={{0,2},{2,4},{4,6},{6,7},{7,5},{5,3},{3,1},{1,0},{10,8},{12,10},{14... | collective-permute-start | bytes 712712 | tf_op jit(solution)/shard_map/ppermute | solution.py:158
  22.8 4.5 %collective-permute-start.5 = (bf16[32,3712]{1,0:T(8,128)(2,1)S(1)}, bf16[32,3712]{1,0:T(8,128)(2,1)S(1)}, u32[]{:S(2)}, u32[]{:S(2)}) collective-permute-start(bf16[32,3712]{1,0:T(8,128)(2,1)S(1)} %collective-permute-done.1.refs_0_), channel_id=1, source_target_pairs={{0,8},{8,0},{1,9},{9,1},{2,10},{10,2},{3,11},{11,3},{4,12},{12,4},... | collective-permute-start | bytes 712712 | tf_op jit(solution)/shard_map/ppermute | solution.py:161
  22.8 4.5 %collective-permute-start.4 = (bf16[32,3712]{1,0:T(8,128)(2,1)S(1)}, bf16[32,3712]{1,0:T(8,128)(2,1)S(1)}, u32[]{:S(2)}, u32[]{:S(2)}) collective-permute-start(bf16[32,3712]{1,0:T(8,128)(2,1)S(1)} %collective-permute-done.3.refs_1_), channel_id=1, source_target_pairs={{0,8},{8,0},{1,9},{9,1},{2,10},{10,2},{3,11},{11,3},{4,12},{12,4},... | collective-permute-start | bytes 712712 | tf_op jit(solution)/shard_map/ppermute | solution.py:161
  23.3 9.5 %collective-permute-start.10 = (bf16[32,3712]{1,0:T(8,128)(2,1)S(1)}, bf16[32,3712]{1,0:T(8,128)(2,1)S(1)}, u32[]{:S(2)}, u32[]{:S(2)}) collective-permute-start(bf16[32,3712]{1,0:T(8,128)(2,1)S(1)} %collective-permute-done.2.refs_0_), channel_id=1, source_target_pairs={{0,8},{8,0},{1,9},{9,1},{2,10},{10,2},{3,11},{11,3},{4,12},{12,4},... | collective-permute-start | bytes 712712 | tf_op jit(solution)/shard_map/ppermute | solution.py:161
  27.4 5.5 %collective-permute-start.9 = (bf16[32,3712]{1,0:T(8,128)(2,1)S(1)}, bf16[32,3712]{1,0:T(8,128)(2,1)S(1)}, u32[]{:S(2)}, u32[]{:S(2)}) collective-permute-start(bf16[32,3712]{1,0:T(8,128)(2,1)S(1)} %collective-permute-done.8.refs_1_), channel_id=1, source_target_pairs={{0,8},{8,0},{1,9},{9,1},{2,10},{10,2},{3,11},{11,3},{4,12},{12,4},... | collective-permute-start | bytes 712712 | tf_op jit(solution)/shard_map/ppermute | solution.py:161
  29.6 6.2 %collective-permute-start.7 = (bf16[32,3712]{1,0:T(8,128)(2,1)S(1)}, bf16[32,3712]{1,0:T(8,128)(2,1)S(1)}, u32[]{:S(2)}, u32[]{:S(2)}) collective-permute-start(bf16[32,3712]{1,0:T(8,128)(2,1)S(1)} %collective-permute-done.2.refs_0_), channel_id=1, source_target_pairs={{0,2},{2,4},{4,6},{6,7},{7,5},{5,3},{3,1},{1,0},{10,8},{12,10},{14... | collective-permute-start | bytes 712712 | tf_op jit(solution)/shard_map/ppermute | solution.py:158
  31.3 7.1 %collective-permute-start.12 = (bf16[32,3712]{1,0:T(8,128)(2,1)S(1)}, bf16[32,3712]{1,0:T(8,128)(2,1)S(1)}, u32[]{:S(2)}, u32[]{:S(2)}) collective-permute-start(bf16[32,3712]{1,0:T(8,128)(2,1)S(1)} %collective-permute-done.8.refs_1_), channel_id=1, source_target_pairs={{0,2},{2,4},{4,6},{6,7},{7,5},{5,3},{3,1},{1,0},{10,8},{12,10},{14... | collective-permute-start | bytes 712712 | tf_op jit(solution)/shard_map/ppermute | solution.py:158
  35.8 6.1 %collective-permute-start.16 = (bf16[32,3712]{1,0:T(8,128)(2,1)S(1)}, bf16[32,3712]{1,0:T(8,128)(2,1)S(1)}, u32[]{:S(2)}, u32[]{:S(2)}) collective-permute-start(bf16[32,3712]{1,0:T(8,128)(2,1)S(1)} %collective-permute-done.7.refs_0_), channel_id=1, source_target_pairs={{0,2},{2,4},{4,6},{6,7},{7,5},{5,3},{3,1},{1,0},{10,8},{12,10},{14... | collective-permute-start | bytes 712712 | tf_op jit(solution)/shard_map/ppermute | solution.py:158
  38.3 3.6 %collective-permute-start.13 = (bf16[32,3712]{1,0:T(8,128)(2,1)S(1)}, bf16[32,3712]{1,0:T(8,128)(2,1)S(1)}, u32[]{:S(2)}, u32[]{:S(2)}) collective-permute-start(bf16[32,3712]{1,0:T(8,128)(2,1)S(1)} %collective-permute-done.12.refs_1_), channel_id=1, source_target_pairs={{0,8},{8,0},{1,9},{9,1},{2,10},{10,2},{3,11},{11,3},{4,12},{12,4},... | collective-permute-start | bytes 712712 | tf_op jit(solution)/shard_map/ppermute | solution.py:161
  38.3 3.6 %collective-permute-start.14 = (bf16[32,3712]{1,0:T(8,128)(2,1)S(1)}, bf16[32,3712]{1,0:T(8,128)(2,1)S(1)}, u32[]{:S(2)}, u32[]{:S(2)}) collective-permute-start(bf16[32,3712]{1,0:T(8,128)(2,1)S(1)} %collective-permute-done.7.refs_0_), channel_id=1, source_target_pairs={{0,8},{8,0},{1,9},{9,1},{2,10},{10,2},{3,11},{11,3},{4,12},{12,4},... | collective-permute-start | bytes 712712 | tf_op jit(solution)/shard_map/ppermute | solution.py:161
  41.9 3.4 %collective-permute-start.17 = (bf16[32,3712]{1,0:T(8,128)(2,1)S(1)}, bf16[32,3712]{1,0:T(8,128)(2,1)S(1)}, u32[]{:S(2)}, u32[]{:S(2)}) collective-permute-start(bf16[32,3712]{1,0:T(8,128)(2,1)S(1)} %collective-permute-done.16.refs_0_), channel_id=1, source_target_pairs={{0,8},{8,0},{1,9},{9,1},{2,10},{10,2},{3,11},{11,3},{4,12},{12,4},... | collective-permute-start | bytes 712712 | tf_op jit(solution)/shard_map/ppermute | solution.py:161
  44.2 4.3 %collective-permute-start.25 = (bf16[32,3584]{1,0:T(8,128)(2,1)S(1)}, bf16[32,3584]{1,0:T(8,128)(2,1)S(1)}, u32[]{:S(2)}, u32[]{:S(2)}) collective-permute-start(bf16[32,3584]{1,0:T(8,128)(2,1)S(1)} %get-tuple-element.66), channel_id=1, source_target_pairs={{0,8},{8,0},{1,9},{9,1},{2,10},{10,2},{3,11},{11,3},{4,12},{12,4},... | collective-permute-start | bytes 688136 | tf_op jit(solution)/shard_map/ppermute | solution.py:161
  44.7 19.1 %collective-permute-start.23 = (bf16[32,3584]{1,0:T(8,128)(2,1)S(1)}, bf16[32,3584]{1,0:T(8,128)(2,1)S(1)}, u32[]{:S(2)}, u32[]{:S(2)}) collective-permute-start(bf16[32,3584]{1,0:T(8,128)(2,1)S(1)} %get-tuple-element.62), channel_id=1, source_target_pairs={{0,8},{8,0},{1,9},{9,1},{2,10},{10,2},{3,11},{11,3},{4,12},{12,4},... | collective-permute-start | bytes 688136 | tf_op jit(solution)/shard_map/ppermute | solution.py:161
  44.8 26.0 %collective-permute-start.6 = (bf16[32,3584]{1,0:T(8,128)(2,1)S(1)}, bf16[32,3584]{1,0:T(8,128)(2,1)S(1)}, u32[]{:S(2)}, u32[]{:S(2)}) collective-permute-start(bf16[32,3584]{1,0:T(8,128)(2,1)S(1)} %get-tuple-element.47), channel_id=1, source_target_pairs={{0,8},{8,0},{1,9},{9,1},{2,10},{10,2},{3,11},{11,3},{4,12},{12,4},... | collective-permute-start | bytes 688136 | tf_op jit(solution)/shard_map/ppermute | solution.py:161
  45.2 6.4 %collective-permute-start.24 = (bf16[32,3584]{1,0:T(8,128)(2,1)S(1)}, bf16[32,3584]{1,0:T(8,128)(2,1)S(1)}, u32[]{:S(2)}, u32[]{:S(2)}) collective-permute-start(bf16[32,3584]{1,0:T(8,128)(2,1)S(1)} %get-tuple-element.64), channel_id=1, source_target_pairs={{0,8},{8,0},{1,9},{9,1},{2,10},{10,2},{3,11},{11,3},{4,12},{12,4},... | collective-permute-start | bytes 688136 | tf_op jit(solution)/shard_map/ppermute | solution.py:161
  45.3 20.9 %collective-permute-start.11 = (bf16[32,3584]{1,0:T(8,128)(2,1)S(1)}, bf16[32,3584]{1,0:T(8,128)(2,1)S(1)}, u32[]{:S(2)}, u32[]{:S(2)}) collective-permute-start(bf16[32,3584]{1,0:T(8,128)(2,1)S(1)} %get-tuple-element.54), channel_id=1, source_target_pairs={{0,8},{8,0},{1,9},{9,1},{2,10},{10,2},{3,11},{11,3},{4,12},{12,4},... | collective-permute-start | bytes 688136 | tf_op jit(solution)/shard_map/ppermute | solution.py:161
  48.5 1.6 %collective-permute-start.18 = (bf16[32,3584]{1,0:T(8,128)(2,1)S(1)}, bf16[32,3584]{1,0:T(8,128)(2,1)S(1)}, u32[]{:S(2)}, u32[]{:S(2)}) collective-permute-start(bf16[32,3584]{1,0:T(8,128)(2,1)S(1)} %get-tuple-element.59), channel_id=1, source_target_pairs={{0,8},{8,0},{1,9},{9,1},{2,10},{10,2},{3,11},{11,3},{4,12},{12,4},... | collective-permute-start | bytes 688136 | tf_op jit(solution)/shard_map/ppermute | solution.py:161
  50.0 6.0 %collective-permute-start.26 = (bf16[32,3584]{1,0:T(8,128)(2,1)S(1)}, bf16[32,3584]{1,0:T(8,128)(2,1)S(1)}, u32[]{:S(2)}, u32[]{:S(2)}) collective-permute-start(bf16[32,3584]{1,0:T(8,128)(2,1)S(1)} %add_convert_fusion.4), channel_id=1, source_target_pairs={{0,2},{2,4},{4,6},{6,7},{7,5},{5,3},{3,1},{1,0},{10,8},{12,10},{14... | collective-permute-start | bytes 688136 | tf_op jit(solution)/shard_map/ppermute | solution.py:158
  51.7 6.0 %collective-permute-start.15 = (bf16[32,3584]{1,0:T(8,128)(2,1)S(1)}, bf16[32,3584]{1,0:T(8,128)(2,1)S(1)}, u32[]{:S(2)}, u32[]{:S(2)}) collective-permute-start(bf16[32,3584]{1,0:T(8,128)(2,1)S(1)} %get-tuple-element.57), channel_id=1, source_target_pairs={{0,8},{8,0},{1,9},{9,1},{2,10},{10,2},{3,11},{11,3},{4,12},{12,4},... | collective-permute-start | bytes 688136 | tf_op jit(solution)/shard_map/ppermute | solution.py:161
  56.0 6.0 %collective-permute-start.19 = (bf16[32,3584]{1,0:T(8,128)(2,1)S(1)}, bf16[32,3584]{1,0:T(8,128)(2,1)S(1)}, u32[]{:S(2)}, u32[]{:S(2)}) collective-permute-start(bf16[32,3584]{1,0:T(8,128)(2,1)S(1)} %add_convert_fusion.8), channel_id=1, source_target_pairs={{0,2},{2,4},{4,6},{6,7},{7,5},{5,3},{3,1},{1,0},{10,8},{12,10},{14... | collective-permute-start | bytes 688136 | tf_op jit(solution)/shard_map/ppermute | solution.py:158
  57.7 6.8 %collective-permute-start.27 = (bf16[32,3584]{1,0:T(8,128)(2,1)S(1)}, bf16[32,3584]{1,0:T(8,128)(2,1)S(1)}, u32[]{:S(2)}, u32[]{:S(2)}) collective-permute-start(bf16[32,3584]{1,0:T(8,128)(2,1)S(1)} %add_convert_fusion.3), channel_id=1, source_target_pairs={{0,2},{2,4},{4,6},{6,7},{7,5},{5,3},{3,1},{1,0},{10,8},{12,10},{14... | collective-permute-start | bytes 688136 | tf_op jit(solution)/shard_map/ppermute | solution.py:158
  62.2 6.1 %collective-permute-start.20 = (bf16[32,3584]{1,0:T(8,128)(2,1)S(1)}, bf16[32,3584]{1,0:T(8,128)(2,1)S(1)}, u32[]{:S(2)}, u32[]{:S(2)}) collective-permute-start(bf16[32,3584]{1,0:T(8,128)(2,1)S(1)} %add_convert_fusion.7), channel_id=1, source_target_pairs={{0,2},{2,4},{4,6},{6,7},{7,5},{5,3},{3,1},{1,0},{10,8},{12,10},{14... | collective-permute-start | bytes 688136 | tf_op jit(solution)/shard_map/ppermute | solution.py:158
  64.6 6.1 %collective-permute-start.28 = (bf16[32,3584]{1,0:T(8,128)(2,1)S(1)}, bf16[32,3584]{1,0:T(8,128)(2,1)S(1)}, u32[]{:S(2)}, u32[]{:S(2)}) collective-permute-start(bf16[32,3584]{1,0:T(8,128)(2,1)S(1)} %add_convert_fusion.2), channel_id=1, source_target_pairs={{0,2},{2,4},{4,6},{6,7},{7,5},{5,3},{3,1},{1,0},{10,8},{12,10},{14... | collective-permute-start | bytes 688136 | tf_op jit(solution)/shard_map/ppermute | solution.py:158
  68.3 6.1 %collective-permute-start.21 = (bf16[32,3584]{1,0:T(8,128)(2,1)S(1)}, bf16[32,3584]{1,0:T(8,128)(2,1)S(1)}, u32[]{:S(2)}, u32[]{:S(2)}) collective-permute-start(bf16[32,3584]{1,0:T(8,128)(2,1)S(1)} %add_convert_fusion.6), channel_id=1, source_target_pairs={{0,2},{2,4},{4,6},{6,7},{7,5},{5,3},{3,1},{1,0},{10,8},{12,10},{14... | collective-permute-start | bytes 688136 | tf_op jit(solution)/shard_map/ppermute | solution.py:158
  70.7 5.4 %collective-permute-start.29 = (bf16[32,3584]{1,0:T(8,128)(2,1)S(1)}, bf16[32,3584]{1,0:T(8,128)(2,1)S(1)}, u32[]{:S(2)}, u32[]{:S(2)}) collective-permute-start(bf16[32,3584]{1,0:T(8,128)(2,1)S(1)} %add_convert_fusion.1), channel_id=1, source_target_pairs={{0,8},{8,0},{1,9},{9,1},{2,10},{10,2},{3,11},{11,3},{4,12},{12,4},... | collective-permute-start | bytes 688136 | tf_op jit(solution)/shard_map/ppermute | solution.py:161
  74.5 6.1 %collective-permute-start.22 = (bf16[32,3584]{1,0:T(8,128)(2,1)S(1)}, bf16[32,3584]{1,0:T(8,128)(2,1)S(1)}, u32[]{:S(2)}, u32[]{:S(2)}) collective-permute-start(bf16[32,3584]{1,0:T(8,128)(2,1)S(1)} %add_convert_fusion.5), channel_id=1, source_target_pairs={{0,2},{2,4},{4,6},{6,7},{7,5},{5,3},{3,1},{1,0},{10,8},{12,10},{14... | collective-permute-start | bytes 688136 | tf_op jit(solution)/shard_map/ppermute | solution.py:158

commit v4 on v3

v4 whole, which is shorter than its diff:
```python
import functools
import jax
import jax.numpy as jnp
from jax import lax
from jax.experimental import pallas as pl
from jax.experimental.pallas import tpu as pltpu
from jax.sharding import PartitionSpec as P

BOTH = ("node", "local")
LANES = 128


def gather_plan(tokens, expert_ids, route_weights, w_up, w_down):
    mine = lax.axis_index(BOTH)
    everyone = lax.all_gather(tokens, BOTH, tiled=True)
    ids = lax.all_gather(expert_ids, BOTH, tiled=True)
    weights = lax.all_gather(route_weights, BOTH, tiled=True)
    scale = jnp.sum(jnp.where(ids == mine, weights.astype(jnp.float32), 0.0), axis=1)
    hidden = jax.nn.silu(jnp.dot(everyone, w_up[0], preferred_element_type=jnp.float32)).astype(jnp.bfloat16)
    answer = jnp.dot(hidden, w_down[0], preferred_element_type=jnp.float32)
    part = (answer * scale[:, None]).astype(jnp.bfloat16)
    return lax.psum_scatter(part, BOTH, scatter_dimension=0, tiled=True)


def step_of(size, wanted):
    step = wanted
    while step > LANES and size % step:
        step //= 2
    return step if size % step == 0 else size


def expert_body(blocks, kept, mine_ref, *refs):
    tokens = refs[:blocks]
    up_ref, down_ref = refs[blocks:blocks + 2]
    outs = refs[blocks + 2:2 * blocks + 2]
    hidden_ref = refs[2 * blocks + 2]
    width, middle = up_ref.shape
    rows = tokens[0].shape[0]
    x = jnp.concatenate([t[:, :width] for t in tokens], axis=0)
    table = jnp.concatenate([t[:, width:] for t in tokens], axis=0).astype(jnp.float32)
    here = lax.broadcasted_iota(jnp.int32, table.shape, 1) == mine_ref[0]
    scale = jnp.sum(jnp.where(here, table, 0.0), axis=1, keepdims=True)
    step = step_of(middle, 256)
    for j in range(0, middle, step):
        up = jnp.dot(x, up_ref[:, j:j + step], preferred_element_type=jnp.float32)
        hidden_ref[:, j:j + step] = (up / (1.0 + jnp.exp(-up))).astype(jnp.bfloat16)
    hidden = hidden_ref[...]
    step = step_of(width, 512)
    for j in range(0, width, step):
        answer = jnp.dot(hidden, down_ref[:, j:j + step], preferred_element_type=jnp.float32)
        answer = answer.astype(jnp.bfloat16).astype(jnp.float32) * scale
        for i in range(blocks):
            outs[i][:, j:j + step] = answer[i * rows:(i + 1) * rows].astype(outs[i].dtype)


def expert(mine, blocks, kept, up, down):
    rows = blocks[0].shape[0]
    width, middle = up.shape
    total = rows * len(blocks)
    vmem = pl.BlockSpec(memory_space=pltpu.VMEM)
    return pl.pallas_call(
        functools.partial(expert_body, len(blocks), kept),
        out_shape=[
            jax.ShapeDtypeStruct((rows, width), jnp.float32 if k else jnp.bfloat16) for k in kept
        ],
        in_specs=[pl.BlockSpec(memory_space=pltpu.SMEM)] + [vmem] * (len(blocks) + 2),
        out_specs=[vmem] * len(blocks),
        scratch_shapes=[pltpu.VMEM((total, middle), jnp.bfloat16)],
        compiler_params=pltpu.CompilerParams(vmem_limit_bytes=16 * 2**20),
        cost_estimate=pl.CostEstimate(
            flops=4 * total * width * middle, bytes_accessed=4 * width * middle, transcendentals=total * middle
        ),
    )(mine, *blocks, up, down)


def first_up_body(mine_ref, own_ref, other_ref, up_hbm, hidden_ref, scale_ref, up_ref, sems):
    width, middle = up_ref.shape
    step = step_of(middle, 256)
    copies = []
    for j in range(0, middle, step):
        s = pl.ds(j, step)
        copies.append(pltpu.make_async_copy(up_hbm.at[:, s], up_ref.at[:, s], sems.at[len(copies)]))
        copies[-1].start()
    x = jnp.concatenate([own_ref[:, :width], other_ref[:, :width]], axis=0)
    table = jnp.concatenate([own_ref[:, width:], other_ref[:, width:]], axis=0).astype(jnp.float32)
    here = lax.broadcasted_iota(jnp.int32, table.shape, 1) == mine_ref[0]
    scale_ref[...] = jnp.broadcast_to(jnp.sum(jnp.where(here, table, 0.0), axis=1, keepdims=True), scale_ref.shape)
    for j in range(0, middle, step):
        copies[j // step].wait()
        up = jnp.dot(x, up_ref[:, j:j + step], preferred_element_type=jnp.float32)
        hidden_ref[:, j:j + step] = (up / (1.0 + jnp.exp(-up))).astype(jnp.bfloat16)


def first_up(mine, own, other, w_up):
    rows = own.shape[0]
    width, middle = w_up.shape
    vmem, hbm = pl.BlockSpec(memory_space=pltpu.VMEM), pl.BlockSpec(memory_space=pltpu.HBM)
    return pl.pallas_call(
        first_up_body,
        out_shape=[
            pltpu.VMEM((2 * rows, middle), jnp.bfloat16),
            pltpu.VMEM((2 * rows, LANES), jnp.float32),
            pltpu.VMEM(w_up.shape, w_up.dtype),
        ],
        in_specs=[pl.BlockSpec(memory_space=pltpu.SMEM), vmem, vmem, hbm],
        out_specs=[vmem] * 3,
        scratch_shapes=[pltpu.SemaphoreType.DMA((middle // step_of(middle, 256),))],
        compiler_params=pltpu.CompilerParams(vmem_limit_bytes=16 * 2**20),
        cost_estimate=pl.CostEstimate(
            flops=4 * rows * width * middle, bytes_accessed=2 * width * middle, transcendentals=2 * rows * middle
        ),
    )(mine, own, other, pltpu.with_memory_space_constraint(w_up, pltpu.HBM))


def first_down_body(hidden_ref, scale_ref, down_hbm, out_own, out_other, down_ref, sems):
    middle, width = down_ref.shape
    step = step_of(width, 512)
    copies = []
    for j in range(0, width, step):
        s = pl.ds(j, step)
        copies.append(pltpu.make_async_copy(down_hbm.at[:, s], down_ref.at[:, s], sems.at[len(copies)]))
        copies[-1].start()
    rows = out_own.shape[0]
    scale = scale_ref[:, :1]
    hidden = hidden_ref[...]
    for j in range(0, width, step):
        copies[j // step].wait()
        answer = jnp.dot(hidden, down_ref[:, j:j + step], preferred_element_type=jnp.float32)
        answer = answer.astype(jnp.bfloat16).astype(jnp.float32) * scale
        out_own[:, j:j + step] = answer[:rows]
        out_other[:, j:j + step] = answer[rows:]


def first_down(hidden, scale, w_down):
    rows = hidden.shape[0] // 2
    middle, width = w_down.shape
    vmem, hbm = pl.BlockSpec(memory_space=pltpu.VMEM), pl.BlockSpec(memory_space=pltpu.HBM)
    return pl.pallas_call(
        first_down_body,
        out_shape=[pltpu.VMEM((rows, width), jnp.float32)] * 2 + [pltpu.VMEM(w_down.shape, w_down.dtype)],
        in_specs=[vmem, vmem, hbm],
        out_specs=[vmem] * 3,
        scratch_shapes=[pltpu.SemaphoreType.DMA((width // step_of(width, 512),))],
        compiler_params=pltpu.CompilerParams(vmem_limit_bytes=16 * 2**20),
        cost_estimate=pl.CostEstimate(
            flops=4 * rows * width * middle, bytes_accessed=2 * width * middle, transcendentals=0
        ),
    )(hidden, scale, pltpu.with_memory_space_constraint(w_down, pltpu.HBM))


def label_body(tokens_ref, ids_ref, weights_ref, out_ref):
    rows, width = tokens_ref.shape
    columns = out_ref.shape[1] - width
    expert_of = lax.broadcasted_iota(jnp.int32, (columns, rows), 0)
    weights = weights_ref[...].astype(jnp.float32)
    table = jnp.zeros((columns, rows), jnp.float32)
    for k in range(ids_ref.shape[0]):
        table = jnp.where(ids_ref[k:k + 1, :] == expert_of, weights[k:k + 1, :], table)
    one = lax.broadcasted_iota(jnp.int32, (rows, rows), 0) == lax.broadcasted_iota(jnp.int32, (rows, rows), 1)
    turned = lax.dot_general(
        one.astype(jnp.bfloat16),
        table.astype(jnp.bfloat16),
        (((1,), (1,)), ((), ())),
        preferred_element_type=jnp.float32,
    )
    out_ref[:, :width] = tokens_ref[...]
    out_ref[:, width:] = turned.astype(jnp.bfloat16)


def label(tokens, expert_ids, route_weights, columns):
    rows, width = tokens.shape
    vmem = pl.BlockSpec(memory_space=pltpu.VMEM)
    return pl.pallas_call(
        label_body,
        out_shape=pltpu.VMEM((rows, width + columns), jnp.bfloat16),
        in_specs=[vmem] * 3,
        out_specs=vmem,
    )(tokens, expert_ids.T, route_weights.T)


def ring_plan(tokens, expert_ids, route_weights, w_up, w_down):
    rows, width = tokens.shape
    experts = lax.axis_size(BOTH)
    n = lax.axis_size("local")
    half = n // 2
    mine = lax.axis_index(BOTH).astype(jnp.int32)[None]
    order = list(range(0, n, 2)) + list(range(n - 1, 0, -2))
    onward = [(order[i], order[(i + 1) % n]) for i in range(n)]
    pairs = onward + [(n + b, n + a) for a, b in onward]
    def hop(x):
        return lax.ppermute(x, BOTH, pairs)

    def swap(x):
        return lax.ppermute(x, "node", [(0, 1), (1, 0)])

    def bf(x):
        return x.astype(jnp.bfloat16)

    columns = -(-experts // LANES) * LANES
    own = label(tokens, expert_ids, route_weights, columns)

    a, b = [own], [swap(own)]
    ahead_a, ahead_b = [None], [None]
    behind, ahead = {}, {}

    def compute(h, first=None):
        blocks = (a[h], b[h], ahead_a[h], ahead_b[h])
        if first is not None:
            blocks, _ = lax.optimization_barrier((blocks, first))
        r = expert(mine, blocks, (False, False, True, True), up, down)
        behind[h], ahead[h] = r[:2], r[2:]

    hidden, scale, up = first_up(mine, own, b[0], w_up[0])
    for h in range(1, half + 1):
        a.append(hop(a[-1]))
        if h < half:
            b.append(hop(b[-1]))
        if h == 1:
            a[1], hidden, up = lax.optimization_barrier((a[1], hidden, up))
            up = pltpu.with_memory_space_constraint(up, pltpu.VMEM)
        elif h == 2:
            own_a, own_b, down = first_down(hidden, scale, w_down[0])
            a[2], own_a, own_b, down = lax.optimization_barrier((a[2], own_a, own_b, down))
            down = pltpu.with_memory_space_constraint(down, pltpu.VMEM)
        elif h < half:
            compute(h - 2)
            a[h], behind[h - 2], ahead[h - 2] = lax.optimization_barrier((a[h], behind[h - 2], ahead[h - 2]))
        if h < half:
            ahead_b.append(swap(a[h]))
            ahead_a.append(swap(b[h]))
    compute(half - 1, (ahead_a[half - 2], ahead_b[half - 2]))
    a[half], behind[half - 1], ahead[half - 1] = lax.optimization_barrier((a[half], behind[half - 1], ahead[half - 1]))
    ahead_b.append(swap(a[half]))

    def join(x, y):
        return x.astype(jnp.float32) + y.astype(jnp.float32)

    def total(h):
        return [join(ahead[h][0], swap(behind[h][1])), join(ahead[h][1], swap(behind[h][0]))]

    sums = total(half - 1)
    send_b = bf(sums[1])
    run_b = hop(send_b)
    last_blocks, send_b = lax.optimization_barrier(((a[half], ahead_b[half]), send_b))
    far = expert(mine, last_blocks, (True, False), up, down)
    send_a = bf(join(far[0], swap(far[1])))
    run_a = hop(send_a)
    for h in range(half - 1, 0, -1):
        if h < half - 1:
            if h not in behind:
                compute(h, far)
            sums = total(h)
            run_b = hop(bf(join(sums[1], run_b)))
        run_a = hop(bf(join(sums[0], run_a)))
    last = swap(bf(join(own_b, run_b)))
    return bf(join(join(own_a, run_a), last))


def solution(mesh):
    placed = (
        P(("rep", "node", "local"), None),
        P(("rep", "node", "local"), None),
        P(("rep", "node", "local"), None),
        P(("node", "local"), None, None),
        P(("node", "local"), None, None),
    )
    n = mesh.shape["local"]
    ringed = mesh.shape["node"] == 2 and n % 2 == 0 and 4 <= n <= 16
    return jax.shard_map(
        ring_plan if ringed else gather_plan,
        mesh=mesh,
        in_specs=placed,
        out_specs=P(("rep", "node", "local"), None),
        check_vma=False,
    )
```

time: 81.5 us -> 69.1 us (0.85)
  waiting for transfers between devices: 31.2 us -> 23.5 us
  local copies, waits for them, and re-layouts: 3.66 us -> 0 us
  starting transfers between devices: 27.4 us -> 25.5 us
  Pallas kernels: 17.6 us -> 18.5 us
    ppermute x14, waiting for transfers between devices: 29.8 us -> 22.2 us  [hop(): return lax.ppermute(x, BOTH, pairs)]
    unnamed x4 -> x0, local copies, waits for them, and re-layouts: 3.66 us -> none
    ppermute x14, starting transfers between devices: 24 us -> 22.3 us  [hop(): return lax.ppermute(x, BOTH, pairs)]
    pallas_call x2 -> x3, Pallas kernels: 8.18 us -> 8.87 us  [the longest x1 4.23 us: first_up(): pl.pallas_call(first_up_body, out_shape=[pltpu.VMEM((2 * rows, middle), j...]
  transfers between devices with their start and end apart: 30 -> 30, of which waited for: 13 -> 12; matrix products, arithmetic and copies ran while one was open for 1% -> 1% of each run, Pallas kernels for 19% -> 21%
where the time goes in v4:
time: 69.1 us; the launch traced here: 68.9 us
  starting transfers between devices  25.5 us (37%)
  waiting for transfers between devices  23.5 us (34%)
  Pallas kernels  18.5 us (27%)
  other arithmetic  1.28 us (2%)
    ppermute x14, starting transfers between devices, hop(): return lax.ppermute(x, BOTH, pairs)  22.3 us
    ppermute x14, waiting for transfers between devices, hop(): return lax.ppermute(x, BOTH, pairs)  22.2 us
    pallas_call x4, Pallas kernels, expert(): pl.pallas_call(functools.partial(expert_body, len(blocks), kept), out_sha...  9.59 us
    pallas_call x1, Pallas kernels, first_up(): pl.pallas_call(first_up_body, out_shape=[pltpu.VMEM((2 * rows, middle), j...  4.23 us
    pallas_call x1, Pallas kernels, first_down(): pl.pallas_call(first_down_body, out_shape=[pltpu.VMEM((rows, width), jnp....  3.52 us
    ppermute x16, starting transfers between devices, swap(): return lax.ppermute(x, 'node', [(0, 1), (1, 0)])  3.22 us
  transfers between devices with their start and end apart: 30, of which 12 were waited for; matrix products, arithmetic and copies ran while one was open for 1% of the time, Pallas kernels for 21%

profile of v4, /device:TPU:0, one launch (start us, length us, event | category | flops | bytes accessed | tf_op | source)
XLA Modules:
  0.0 68.9 jit_solution(3253485031042010088)
XLA Ops:
  0.0 1.1 %shard_map.55.own_ref = bf16[32,3712]{1,0:T(8,128)(2,1)S(1)} custom-call(bf16[32,3584]{1,0:T(8,128)(2,1)} %tokens_ref.1, s32[8,32]{1,0:T(8,128)} %bitcast.7, bf16[8,32]{1,0:T(8,128)(2,1)} %bitcast.8), custom_call_target="tpu_custom_call" | custom-call | tf_op jit(solution)/shard_map/pallas_call | solution.py:173
  1.1 0.5 collective-permute-start.1
  1.6 2.6 %collective-permute-start = (bf16[32,3712]{1,0:T(8,128)(2,1)S(1)}, bf16[32,3712]{1,0:T(8,128)(2,1)S(1)}, u32[]{:S(2)}, u32[]{:S(2)}) collective-permute-start(bf16[32,3712]{1,0:T(8,128)(2,1)S(1)} %shard_map.55.own_ref), channel_id=1, source_target_pairs={{0,2},{2,4},{4,6},{6,7},{7,5},{5,3},{3,1},{1,0},{10,8},{12,10},{14... | collective-permute-start | bytes 712712 | tf_op jit(solution)/shard_map/ppermute | solution.py:191
  4.2 0.0 collective-permute-done.1.other_ref
  4.2 1.6 %collective-permute-start.4 = (bf16[32,3712]{1,0:T(8,128)(2,1)S(1)}, bf16[32,3712]{1,0:T(8,128)(2,1)S(1)}, u32[]{:S(2)}, u32[]{:S(2)}) collective-permute-start(bf16[32,3712]{1,0:T(8,128)(2,1)S(1)} %collective-permute-done.1.other_ref), channel_id=1, source_target_pairs={{0,2},{2,4},{4,6},{6,7},{7,5},{5,3},{3,1},{1,0},{10,8},{12,10},{14... | collective-permute-start | bytes 712712 | tf_op jit(solution)/shard_map/ppermute | solution.py:191
  5.8 4.2 %shard_map.56 = (bf16[64,1024]{1,0:T(8,128)(2,1)S(1)}, f32[64,128]{1,0:T(8,128)S(1)}, bf16[3584,1024]{1,0:T(8,128)(2,1)S(1)}) custom-call(s32[1]{0:T(128)} %bitcast.2.mine_ref, bf16[32,3712]{1,0:T(8,128)(2,1)S(1)} %shard_map.55.own_ref, bf16[32,3712]{1,0:T(8,128)(2,1)S(1)} %collective-permute-done.1.other_ref, bf16[3584,1024]{1,0:T(8,128)(2,1)} %bitcast.6), custom_call_target="tpu_custom_call" | custom-call | flops 469762048 | bytes 7340032 | tf_op jit(solution)/shard_map/pallas_call | solution.py:98
  10.0 0.0 collective-permute-done.refs_0_
  10.0 1.6 %collective-permute-start.2 = (bf16[32,3712]{1,0:T(8,128)(2,1)S(1)}, bf16[32,3712]{1,0:T(8,128)(2,1)S(1)}, u32[]{:S(2)}, u32[]{:S(2)}) collective-permute-start(bf16[32,3712]{1,0:T(8,128)(2,1)S(1)} %collective-permute-done.refs_0_), channel_id=1, source_target_pairs={{0,2},{2,4},{4,6},{6,7},{7,5},{5,3},{3,1},{1,0},{10,8},{12,10},{14... | collective-permute-start | bytes 712712 | tf_op jit(solution)/shard_map/ppermute | solution.py:191
  11.6 0.0 collective-permute-done.4.refs_1_
  11.6 1.5 %collective-permute-start.8 = (bf16[32,3712]{1,0:T(8,128)(2,1)S(1)}, bf16[32,3712]{1,0:T(8,128)(2,1)S(1)}, u32[]{:S(2)}, u32[]{:S(2)}) collective-permute-start(bf16[32,3712]{1,0:T(8,128)(2,1)S(1)} %collective-permute-done.4.refs_1_), channel_id=1, source_target_pairs={{0,2},{2,4},{4,6},{6,7},{7,5},{5,3},{3,1},{1,0},{10,8},{12,10},{14... | collective-permute-start | bytes 712712 | tf_op jit(solution)/shard_map/ppermute | solution.py:191
  13.2 0.0 collective-permute-start.6
  13.2 0.5 collective-permute-start.5
  13.7 3.5 %shard_map.57 = (f32[32,3584]{1,0:T(8,128)S(1)}, f32[32,3584]{1,0:T(8,128)S(1)}, bf16[1024,3584]{1,0:T(8,128)(2,1)S(1)}) custom-call(bf16[64,1024]{1,0:T(8,128)(2,1)S(1)} %get-tuple-element.55.hidden_ref, f32[64,128]{1,0:T(8,128)S(1)} %get-tuple-element.56.scale_ref, bf16[1024,3584]{1,0:T(8,128)(2,1)} %bitcast.5), custom_call_target="tpu_custom_call" | custom-call | flops 469762048 | bytes 7340032 | tf_op jit(solution)/shard_map/pallas_call | solution.py:138
  17.2 0.0 collective-permute-done.2.refs_0_
  17.2 1.5 %collective-permute-start.3 = (bf16[32,3712]{1,0:T(8,128)(2,1)S(1)}, bf16[32,3712]{1,0:T(8,128)(2,1)S(1)}, u32[]{:S(2)}, u32[]{:S(2)}) collective-permute-start(bf16[32,3712]{1,0:T(8,128)(2,1)S(1)} %collective-permute-done.2.refs_0_), channel_id=1, source_target_pairs={{0,2},{2,4},{4,6},{6,7},{7,5},{5,3},{3,1},{1,0},{10,8},{12,10},{14... | collective-permute-start | bytes 712712 | tf_op jit(solution)/shard_map/ppermute | solution.py:191
  18.7 0.0 collective-permute-done.8.refs_1_
  18.7 1.6 %collective-permute-start.12 = (bf16[32,3712]{1,0:T(8,128)(2,1)S(1)}, bf16[32,3712]{1,0:T(8,128)(2,1)S(1)}, u32[]{:S(2)}, u32[]{:S(2)}) collective-permute-start(bf16[32,3712]{1,0:T(8,128)(2,1)S(1)} %collective-permute-done.8.refs_1_), channel_id=1, source_target_pairs={{0,2},{2,4},{4,6},{6,7},{7,5},{5,3},{3,1},{1,0},{10,8},{12,10},{14... | collective-permute-start | bytes 712712 | tf_op jit(solution)/shard_map/ppermute | solution.py:191
  20.3 2.3 %shard_map.58 = (bf16[32,3584]{1,0:T(8,128)(2,1)S(1)}, bf16[32,3584]{1,0:T(8,128)(2,1)S(1)}, f32[32,3584]{1,0:T(8,128)S(1)}, f32[32,3584]{1,0:T(8,128)S(1)}) custom-call(s32[1]{0:T(128)} %bitcast.2.mine_ref, bf16[32,3712]{1,0:T(8,128)(2,1)S(1)} %collective-permute-done.refs_0_, bf16[32,3712]{1,0:T(8,128)(2,1)S(1)} %collective-permute-done.4.refs_1_, ...), custom_call_target="tpu_custom_call" | custom-call | flops 1879048192 | bytes 14680064 | tf_op jit(solution)/shard_map/pallas_call | solution.py:61
  22.6 0.8 %collective-permute-done.3.refs_0_ = bf16[32,3712]{1,0:T(8,128)(2,1)S(1)} collective-permute-done((bf16[32,3712]{1,0:T(8,128)(2,1)S(1)}, bf16[32,3712]{1,0:T(8,128)(2,1)S(1)}, u32[]{:S(2)}, u32[]{:S(2)}) %collective-permute-start.3) | collective-permute-done | bytes 237600 | tf_op jit(solution)/shard_map/ppermute | solution.py:191
  23.4 0.0 collective-permute-start.14
  23.4 0.5 collective-permute-start.9
  23.9 2.0 %collective-permute-done.12.refs_1_ = bf16[32,3712]{1,0:T(8,128)(2,1)S(1)} collective-permute-done((bf16[32,3712]{1,0:T(8,128)(2,1)S(1)}, bf16[32,3712]{1,0:T(8,128)(2,1)S(1)}, u32[]{:S(2)}, u32[]{:S(2)}) %collective-permute-start.12) | collective-permute-done | bytes 237600 | tf_op jit(solution)/shard_map/ppermute | solution.py:191
  25.9 0.0 collective-permute-start.13
  25.9 1.5 %collective-permute-start.11 = (bf16[32,3712]{1,0:T(8,128)(2,1)S(1)}, bf16[32,3712]{1,0:T(8,128)(2,1)S(1)}, u32[]{:S(2)}, u32[]{:S(2)}) collective-permute-start(bf16[32,3712]{1,0:T(8,128)(2,1)S(1)} %collective-permute-done.3.refs_0_), channel_id=1, source_target_pairs={{0,2},{2,4},{4,6},{6,7},{7,5},{5,3},{3,1},{1,0},{10,8},{12,10},{14... | collective-permute-start | bytes 712712 | tf_op jit(solution)/shard_map/ppermute | solution.py:191
  27.4 0.0 collective-permute-done.13.refs_2_
  27.4 2.3 %shard_map.59 = (bf16[32,3584]{1,0:T(8,128)(2,1)S(1)}, bf16[32,3584]{1,0:T(8,128)(2,1)S(1)}, f32[32,3584]{1,0:T(8,128)S(1)}, f32[32,3584]{1,0:T(8,128)S(1)}) custom-call(s32[1]{0:T(128)} %bitcast.2.mine_ref, bf16[32,3712]{1,0:T(8,128)(2,1)S(1)} %collective-permute-done.3.refs_0_, bf16[32,3712]{1,0:T(8,128)(2,1)S(1)} %collective-permute-done.12.refs_1_, ...), custom_call_target="tpu_custom_call" | custom-call | flops 1879048192 | bytes 14680064 | tf_op jit(solution)/shard_map/pallas_call | solution.py:61
  29.7 2.3 %collective-permute-done.11.refs_0_ = bf16[32,3712]{1,0:T(8,128)(2,1)S(1)} collective-permute-done((bf16[32,3712]{1,0:T(8,128)(2,1)S(1)}, bf16[32,3712]{1,0:T(8,128)(2,1)S(1)}, u32[]{:S(2)}, u32[]{:S(2)}) %collective-permute-start.11) | collective-permute-done | bytes 237600 | tf_op jit(solution)/shard_map/ppermute | solution.py:191
  32.0 0.0 collective-permute-start.16
  32.0 0.5 collective-permute-start.15
  32.5 1.0 %collective-permute-done.16 = bf16[32,3584]{1,0:T(8,128)(2,1)S(1)} collective-permute-done((bf16[32,3584]{1,0:T(8,128)(2,1)S(1)}, bf16[32,3584]{1,0:T(8,128)(2,1)S(1)}, u32[]{:S(2)}, u32[]{:S(2)}) %collective-permute-start.16) | collective-permute-done | bytes 229408 | tf_op jit(solution)/shard_map/ppermute | solution.py:194
  33.5 0.1 add_convert_fusion.8
  33.6 0.3 collective-permute-done.15.refs_1_
  33.9 2.7 %shard_map.60 = (f32[32,3584]{1,0:T(8,128)S(1)}, bf16[32,3584]{1,0:T(8,128)(2,1)S(1)}) custom-call(s32[1]{0:T(128)} %bitcast.2.mine_ref, bf16[32,3712]{1,0:T(8,128)(2,1)S(1)} %collective-permute-done.11.refs_0_, bf16[32,3712]{1,0:T(8,128)(2,1)S(1)} %collective-permute-done.15.refs_1_, bf16[3584,1024]{1,0:T(8,128)(2,1)S(1)} %get-tuple-element.62.refs_4_.refs_2_, ...), custom_call_target="tpu_custom_call" | custom-call | flops 939524096 | bytes 14680064 | tf_op jit(solution)/shard_map/pallas_call | solution.py:61
  36.6 0.2 collective-permute-start.19
  36.8 0.3 collective-permute-start.7
  37.1 0.2 collective-permute-start.24
  37.3 0.3 collective-permute-start.18
  37.7 1.5 %collective-permute-start.26 = (bf16[32,3584]{1,0:T(8,128)(2,1)S(1)}, bf16[32,3584]{1,0:T(8,128)(2,1)S(1)}, u32[]{:S(2)}, u32[]{:S(2)}) collective-permute-start(bf16[32,3584]{1,0:T(8,128)(2,1)S(1)} %add_convert_fusion.8), channel_id=1, source_target_pairs={{0,2},{2,4},{4,6},{6,7},{7,5},{5,3},{3,1},{1,0},{10,8},{12,10},{14... | collective-permute-start | bytes 688136 | tf_op jit(solution)/shard_map/ppermute | solution.py:191
  39.1 2.3 %shard_map.61 = (bf16[32,3584]{1,0:T(8,128)(2,1)S(1)}, bf16[32,3584]{1,0:T(8,128)(2,1)S(1)}, f32[32,3584]{1,0:T(8,128)S(1)}, f32[32,3584]{1,0:T(8,128)S(1)}) custom-call(s32[1]{0:T(128)} %bitcast.2.mine_ref, bf16[32,3712]{1,0:T(8,128)(2,1)S(1)} %collective-permute-done.2.refs_0_, bf16[32,3712]{1,0:T(8,128)(2,1)S(1)} %collective-permute-done.8.refs_1_, ...), custom_call_target="tpu_custom_call" | custom-call | flops 1879048192 | bytes 14680064 | tf_op jit(solution)/shard_map/pallas_call | solution.py:61
  41.4 0.0 collective-permute-done.19
  41.4 0.1 collective-permute-start.25
  41.6 2.1 %collective-permute-done.26 = bf16[32,3584]{1,0:T(8,128)(2,1)S(1)} collective-permute-done((bf16[32,3584]{1,0:T(8,128)(2,1)S(1)}, bf16[32,3584]{1,0:T(8,128)(2,1)S(1)}, u32[]{:S(2)}, u32[]{:S(2)}) %collective-permute-start.26) | collective-permute-done | bytes 229408 | tf_op jit(solution)/shard_map/ppermute | solution.py:191
  43.7 1.5 %collective-permute-start.20 = (bf16[32,3584]{1,0:T(8,128)(2,1)S(1)}, bf16[32,3584]{1,0:T(8,128)(2,1)S(1)}, u32[]{:S(2)}, u32[]{:S(2)}) collective-permute-start(bf16[32,3584]{1,0:T(8,128)(2,1)S(1)} %add_convert_fusion.7), channel_id=1, source_target_pairs={{0,2},{2,4},{4,6},{6,7},{7,5},{5,3},{3,1},{1,0},{10,8},{12,10},{14... | collective-permute-start | bytes 688136 | tf_op jit(solution)/shard_map/ppermute | solution.py:191
  45.2 0.1 add_convert_fusion.3
  45.2 0.0 collective-permute-done.18
  45.3 1.4 %collective-permute-start.27 = (bf16[32,3584]{1,0:T(8,128)(2,1)S(1)}, bf16[32,3584]{1,0:T(8,128)(2,1)S(1)}, u32[]{:S(2)}, u32[]{:S(2)}) collective-permute-start(bf16[32,3584]{1,0:T(8,128)(2,1)S(1)} %add_convert_fusion.3), channel_id=1, source_target_pairs={{0,2},{2,4},{4,6},{6,7},{7,5},{5,3},{3,1},{1,0},{10,8},{12,10},{14... | collective-permute-start | bytes 688136 | tf_op jit(solution)/shard_map/ppermute | solution.py:191
  46.7 3.0 %collective-permute-done.20 = bf16[32,3584]{1,0:T(8,128)(2,1)S(1)} collective-permute-done((bf16[32,3584]{1,0:T(8,128)(2,1)S(1)}, bf16[32,3584]{1,0:T(8,128)(2,1)S(1)}, u32[]{:S(2)}, u32[]{:S(2)}) %collective-permute-start.20) | collective-permute-done | bytes 229408 | tf_op jit(solution)/shard_map/ppermute | solution.py:191
  49.7 0.1 add_convert_fusion.6
  49.8 1.5 %collective-permute-start.21 = (bf16[32,3584]{1,0:T(8,128)(2,1)S(1)}, bf16[32,3584]{1,0:T(8,128)(2,1)S(1)}, u32[]{:S(2)}, u32[]{:S(2)}) collective-permute-start(bf16[32,3584]{1,0:T(8,128)(2,1)S(1)} %add_convert_fusion.6), channel_id=1, source_target_pairs={{0,2},{2,4},{4,6},{6,7},{7,5},{5,3},{3,1},{1,0},{10,8},{12,10},{14... | collective-permute-start | bytes 688136 | tf_op jit(solution)/shard_map/ppermute | solution.py:191
  51.3 0.0 collective-permute-done.24
  51.3 0.9 %collective-permute-done.27 = bf16[32,3584]{1,0:T(8,128)(2,1)S(1)} collective-permute-done((bf16[32,3584]{1,0:T(8,128)(2,1)S(1)}, bf16[32,3584]{1,0:T(8,128)(2,1)S(1)}, u32[]{:S(2)}, u32[]{:S(2)}) %collective-permute-start.27) | collective-permute-done | bytes 229408 | tf_op jit(solution)/shard_map/ppermute | solution.py:191
  52.2 0.1 add_convert_fusion.2
  52.2 1.5 %collective-permute-start.28 = (bf16[32,3584]{1,0:T(8,128)(2,1)S(1)}, bf16[32,3584]{1,0:T(8,128)(2,1)S(1)}, u32[]{:S(2)}, u32[]{:S(2)}) collective-permute-start(bf16[32,3584]{1,0:T(8,128)(2,1)S(1)} %add_convert_fusion.2), channel_id=1, source_target_pairs={{0,2},{2,4},{4,6},{6,7},{7,5},{5,3},{3,1},{1,0},{10,8},{12,10},{14... | collective-permute-start | bytes 688136 | tf_op jit(solution)/shard_map/ppermute | solution.py:191
  53.8 2.1 %collective-permute-done.21 = bf16[32,3584]{1,0:T(8,128)(2,1)S(1)} collective-permute-done((bf16[32,3584]{1,0:T(8,128)(2,1)S(1)}, bf16[32,3584]{1,0:T(8,128)(2,1)S(1)}, u32[]{:S(2)}, u32[]{:S(2)}) %collective-permute-start.21) | collective-permute-done | bytes 229408 | tf_op jit(solution)/shard_map/ppermute | solution.py:191
  55.9 0.1 add_convert_fusion.5
  56.0 1.5 %collective-permute-start.22 = (bf16[32,3584]{1,0:T(8,128)(2,1)S(1)}, bf16[32,3584]{1,0:T(8,128)(2,1)S(1)}, u32[]{:S(2)}, u32[]{:S(2)}) collective-permute-start(bf16[32,3584]{1,0:T(8,128)(2,1)S(1)} %add_convert_fusion.5), channel_id=1, source_target_pairs={{0,2},{2,4},{4,6},{6,7},{7,5},{5,3},{3,1},{1,0},{10,8},{12,10},{14... | collective-permute-start | bytes 688136 | tf_op jit(solution)/shard_map/ppermute | solution.py:191
  57.5 0.8 %collective-permute-done.28 = bf16[32,3584]{1,0:T(8,128)(2,1)S(1)} collective-permute-done((bf16[32,3584]{1,0:T(8,128)(2,1)S(1)}, bf16[32,3584]{1,0:T(8,128)(2,1)S(1)}, u32[]{:S(2)}, u32[]{:S(2)}) %collective-permute-start.28) | collective-permute-done | bytes 229408 | tf_op jit(solution)/shard_map/ppermute | solution.py:191
  58.4 0.1 collective-permute-start.29
  58.4 3.6 %collective-permute-done.22 = bf16[32,3584]{1,0:T(8,128)(2,1)S(1)} collective-permute-done((bf16[32,3584]{1,0:T(8,128)(2,1)S(1)}, bf16[32,3584]{1,0:T(8,128)(2,1)S(1)}, u32[]{:S(2)}, u32[]{:S(2)}) %collective-permute-start.22) | collective-permute-done | bytes 229408 | tf_op jit(solution)/shard_map/ppermute | solution.py:191
  62.0 0.1 add_convert_fusion.4
  62.1 1.5 %collective-permute-start.23 = (bf16[32,3584]{1,0:T(8,128)(2,1)S(1)}, bf16[32,3584]{1,0:T(8,128)(2,1)S(1)}, u32[]{:S(2)}, u32[]{:S(2)}) collective-permute-start(bf16[32,3584]{1,0:T(8,128)(2,1)S(1)} %add_convert_fusion.4), channel_id=1, source_target_pairs={{0,2},{2,4},{4,6},{6,7},{7,5},{5,3},{3,1},{1,0},{10,8},{12,10},{14... | collective-permute-start | bytes 688136 | tf_op jit(solution)/shard_map/ppermute | solution.py:191
  63.6 0.0 collective-permute-done.29
  63.6 4.5 %collective-permute-done.23 = bf16[32,3584]{1,0:T(8,128)(2,1)S(1)} collective-permute-done((bf16[32,3584]{1,0:T(8,128)(2,1)S(1)}, bf16[32,3584]{1,0:T(8,128)(2,1)S(1)}, u32[]{:S(2)}, u32[]{:S(2)}) %collective-permute-start.23) | collective-permute-done | bytes 229408 | tf_op jit(solution)/shard_map/ppermute | solution.py:191
  68.2 0.8 %add_convert_fusion = bf16[32,3584]{1,0:T(8,128)(2,1)} fusion(bf16[32,3584]{1,0:T(8,128)(2,1)S(1)} %collective-permute-done.29, f32[32,3584]{1,0:T(8,128)S(1)} %get-tuple-element.60, bf16[32,3584]{1,0:T(8,128)(2,1)S(1)} %collective-permute-done.23), kind=kLoop, calls=%fused_computation | loop fusion | flops 573440 | bytes 1146880 | tf_op jit(solution)/shard_map/convert_element_type | solution.py:197
  (12 shorter events, 0.1 us)
Async XLA Ops:
  1.1 3.1 %collective-permute-start.1 = (bf16[32,3712]{1,0:T(8,128)(2,1)S(1)}, bf16[32,3712]{1,0:T(8,128)(2,1)S(1)}, u32[]{:S(2)}, u32[]{:S(2)}) collective-permute-start(bf16[32,3712]{1,0:T(8,128)(2,1)S(1)} %shard_map.55.own_ref), channel_id=1, source_target_pairs={{0,8},{8,0},{1,9},{9,1},{2,10},{10,2},{3,11},{11,3},{4,12},{12,4},... | collective-permute-start | bytes 712712 | tf_op jit(solution)/shard_map/ppermute | solution.py:194
  1.6 8.4 %collective-permute-start = (bf16[32,3712]{1,0:T(8,128)(2,1)S(1)}, bf16[32,3712]{1,0:T(8,128)(2,1)S(1)}, u32[]{:S(2)}, u32[]{:S(2)}) collective-permute-start(bf16[32,3712]{1,0:T(8,128)(2,1)S(1)} %shard_map.55.own_ref), channel_id=1, source_target_pairs={{0,2},{2,4},{4,6},{6,7},{7,5},{5,3},{3,1},{1,0},{10,8},{12,10},{14... | collective-permute-start | bytes 712712 | tf_op jit(solution)/shard_map/ppermute | solution.py:191
  4.2 7.5 %collective-permute-start.4 = (bf16[32,3712]{1,0:T(8,128)(2,1)S(1)}, bf16[32,3712]{1,0:T(8,128)(2,1)S(1)}, u32[]{:S(2)}, u32[]{:S(2)}) collective-permute-start(bf16[32,3712]{1,0:T(8,128)(2,1)S(1)} %collective-permute-done.1.other_ref), channel_id=1, source_target_pairs={{0,2},{2,4},{4,6},{6,7},{7,5},{5,3},{3,1},{1,0},{10,8},{12,10},{14... | collective-permute-start | bytes 712712 | tf_op jit(solution)/shard_map/ppermute | solution.py:191
  10.0 7.2 %collective-permute-start.2 = (bf16[32,3712]{1,0:T(8,128)(2,1)S(1)}, bf16[32,3712]{1,0:T(8,128)(2,1)S(1)}, u32[]{:S(2)}, u32[]{:S(2)}) collective-permute-start(bf16[32,3712]{1,0:T(8,128)(2,1)S(1)} %collective-permute-done.refs_0_), channel_id=1, source_target_pairs={{0,2},{2,4},{4,6},{6,7},{7,5},{5,3},{3,1},{1,0},{10,8},{12,10},{14... | collective-permute-start | bytes 712712 | tf_op jit(solution)/shard_map/ppermute | solution.py:191
  11.6 7.1 %collective-permute-start.8 = (bf16[32,3712]{1,0:T(8,128)(2,1)S(1)}, bf16[32,3712]{1,0:T(8,128)(2,1)S(1)}, u32[]{:S(2)}, u32[]{:S(2)}) collective-permute-start(bf16[32,3712]{1,0:T(8,128)(2,1)S(1)} %collective-permute-done.4.refs_1_), channel_id=1, source_target_pairs={{0,2},{2,4},{4,6},{6,7},{7,5},{5,3},{3,1},{1,0},{10,8},{12,10},{14... | collective-permute-start | bytes 712712 | tf_op jit(solution)/shard_map/ppermute | solution.py:191
  13.2 7.1 %collective-permute-start.6 = (bf16[32,3712]{1,0:T(8,128)(2,1)S(1)}, bf16[32,3712]{1,0:T(8,128)(2,1)S(1)}, u32[]{:S(2)}, u32[]{:S(2)}) collective-permute-start(bf16[32,3712]{1,0:T(8,128)(2,1)S(1)} %collective-permute-done.refs_0_), channel_id=1, source_target_pairs={{0,8},{8,0},{1,9},{9,1},{2,10},{10,2},{3,11},{11,3},{4,12},{12,4},... | collective-permute-start | bytes 712712 | tf_op jit(solution)/shard_map/ppermute | solution.py:194
  13.2 7.1 %collective-permute-start.5 = (bf16[32,3712]{1,0:T(8,128)(2,1)S(1)}, bf16[32,3712]{1,0:T(8,128)(2,1)S(1)}, u32[]{:S(2)}, u32[]{:S(2)}) collective-permute-start(bf16[32,3712]{1,0:T(8,128)(2,1)S(1)} %collective-permute-done.4.refs_1_), channel_id=1, source_target_pairs={{0,8},{8,0},{1,9},{9,1},{2,10},{10,2},{3,11},{11,3},{4,12},{12,4},... | collective-permute-start | bytes 712712 | tf_op jit(solution)/shard_map/ppermute | solution.py:194
  17.2 6.2 %collective-permute-start.3 = (bf16[32,3712]{1,0:T(8,128)(2,1)S(1)}, bf16[32,3712]{1,0:T(8,128)(2,1)S(1)}, u32[]{:S(2)}, u32[]{:S(2)}) collective-permute-start(bf16[32,3712]{1,0:T(8,128)(2,1)S(1)} %collective-permute-done.2.refs_0_), channel_id=1, source_target_pairs={{0,2},{2,4},{4,6},{6,7},{7,5},{5,3},{3,1},{1,0},{10,8},{12,10},{14... | collective-permute-start | bytes 712712 | tf_op jit(solution)/shard_map/ppermute | solution.py:191
  18.7 7.2 %collective-permute-start.12 = (bf16[32,3712]{1,0:T(8,128)(2,1)S(1)}, bf16[32,3712]{1,0:T(8,128)(2,1)S(1)}, u32[]{:S(2)}, u32[]{:S(2)}) collective-permute-start(bf16[32,3712]{1,0:T(8,128)(2,1)S(1)} %collective-permute-done.8.refs_1_), channel_id=1, source_target_pairs={{0,2},{2,4},{4,6},{6,7},{7,5},{5,3},{3,1},{1,0},{10,8},{12,10},{14... | collective-permute-start | bytes 712712 | tf_op jit(solution)/shard_map/ppermute | solution.py:191
  20.3 7.1 %collective-permute-start.10 = (bf16[32,3712]{1,0:T(8,128)(2,1)S(1)}, bf16[32,3712]{1,0:T(8,128)(2,1)S(1)}, u32[]{:S(2)}, u32[]{:S(2)}) collective-permute-start(bf16[32,3712]{1,0:T(8,128)(2,1)S(1)} %collective-permute-done.2.refs_0_), channel_id=1, source_target_pairs={{0,8},{8,0},{1,9},{9,1},{2,10},{10,2},{3,11},{11,3},{4,12},{12,4},... | collective-permute-start | bytes 712712 | tf_op jit(solution)/shard_map/ppermute | solution.py:194
  23.4 4.0 %collective-permute-start.14 = (bf16[32,3712]{1,0:T(8,128)(2,1)S(1)}, bf16[32,3712]{1,0:T(8,128)(2,1)S(1)}, u32[]{:S(2)}, u32[]{:S(2)}) collective-permute-start(bf16[32,3712]{1,0:T(8,128)(2,1)S(1)} %collective-permute-done.3.refs_0_), channel_id=1, source_target_pairs={{0,8},{8,0},{1,9},{9,1},{2,10},{10,2},{3,11},{11,3},{4,12},{12,4},... | collective-permute-start | bytes 712712 | tf_op jit(solution)/shard_map/ppermute | solution.py:194
  23.4 4.0 %collective-permute-start.9 = (bf16[32,3712]{1,0:T(8,128)(2,1)S(1)}, bf16[32,3712]{1,0:T(8,128)(2,1)S(1)}, u32[]{:S(2)}, u32[]{:S(2)}) collective-permute-start(bf16[32,3712]{1,0:T(8,128)(2,1)S(1)} %collective-permute-done.8.refs_1_), channel_id=1, source_target_pairs={{0,8},{8,0},{1,9},{9,1},{2,10},{10,2},{3,11},{11,3},{4,12},{12,4},... | collective-permute-start | bytes 712712 | tf_op jit(solution)/shard_map/ppermute | solution.py:194
  25.9 1.5 %collective-permute-start.13 = (bf16[32,3712]{1,0:T(8,128)(2,1)S(1)}, bf16[32,3712]{1,0:T(8,128)(2,1)S(1)}, u32[]{:S(2)}, u32[]{:S(2)}) collective-permute-start(bf16[32,3712]{1,0:T(8,128)(2,1)S(1)} %collective-permute-done.12.refs_1_), channel_id=1, source_target_pairs={{0,8},{8,0},{1,9},{9,1},{2,10},{10,2},{3,11},{11,3},{4,12},{12,4},... | collective-permute-start | bytes 712712 | tf_op jit(solution)/shard_map/ppermute | solution.py:194
  25.9 6.1 %collective-permute-start.11 = (bf16[32,3712]{1,0:T(8,128)(2,1)S(1)}, bf16[32,3712]{1,0:T(8,128)(2,1)S(1)}, u32[]{:S(2)}, u32[]{:S(2)}) collective-permute-start(bf16[32,3712]{1,0:T(8,128)(2,1)S(1)} %collective-permute-done.3.refs_0_), channel_id=1, source_target_pairs={{0,2},{2,4},{4,6},{6,7},{7,5},{5,3},{3,1},{1,0},{10,8},{12,10},{14... | collective-permute-start | bytes 712712 | tf_op jit(solution)/shard_map/ppermute | solution.py:191
  32.0 1.5 %collective-permute-start.16 = (bf16[32,3584]{1,0:T(8,128)(2,1)S(1)}, bf16[32,3584]{1,0:T(8,128)(2,1)S(1)}, u32[]{:S(2)}, u32[]{:S(2)}) collective-permute-start(bf16[32,3584]{1,0:T(8,128)(2,1)S(1)} %get-tuple-element.81), channel_id=1, source_target_pairs={{0,8},{8,0},{1,9},{9,1},{2,10},{10,2},{3,11},{11,3},{4,12},{12,4},... | collective-permute-start | bytes 688136 | tf_op jit(solution)/shard_map/ppermute | solution.py:194
  32.0 1.8 %collective-permute-start.15 = (bf16[32,3712]{1,0:T(8,128)(2,1)S(1)}, bf16[32,3712]{1,0:T(8,128)(2,1)S(1)}, u32[]{:S(2)}, u32[]{:S(2)}) collective-permute-start(bf16[32,3712]{1,0:T(8,128)(2,1)S(1)} %collective-permute-done.11.refs_0_), channel_id=1, source_target_pairs={{0,8},{8,0},{1,9},{9,1},{2,10},{10,2},{3,11},{11,3},{4,12},{12,4},... | collective-permute-start | bytes 712712 | tf_op jit(solution)/shard_map/ppermute | solution.py:194
  36.6 4.9 %collective-permute-start.19 = (bf16[32,3584]{1,0:T(8,128)(2,1)S(1)}, bf16[32,3584]{1,0:T(8,128)(2,1)S(1)}, u32[]{:S(2)}, u32[]{:S(2)}) collective-permute-start(bf16[32,3584]{1,0:T(8,128)(2,1)S(1)} %get-tuple-element.85), channel_id=1, source_target_pairs={{0,8},{8,0},{1,9},{9,1},{2,10},{10,2},{3,11},{11,3},{4,12},{12,4},... | collective-permute-start | bytes 688136 | tf_op jit(solution)/shard_map/ppermute | solution.py:194
  36.8 21.6 %collective-permute-start.7 = (bf16[32,3584]{1,0:T(8,128)(2,1)S(1)}, bf16[32,3584]{1,0:T(8,128)(2,1)S(1)}, u32[]{:S(2)}, u32[]{:S(2)}) collective-permute-start(bf16[32,3584]{1,0:T(8,128)(2,1)S(1)} %get-tuple-element.69), channel_id=1, source_target_pairs={{0,8},{8,0},{1,9},{9,1},{2,10},{10,2},{3,11},{11,3},{4,12},{12,4},... | collective-permute-start | bytes 688136 | tf_op jit(solution)/shard_map/ppermute | solution.py:194
  37.1 14.2 %collective-permute-start.24 = (bf16[32,3584]{1,0:T(8,128)(2,1)S(1)}, bf16[32,3584]{1,0:T(8,128)(2,1)S(1)}, u32[]{:S(2)}, u32[]{:S(2)}) collective-permute-start(bf16[32,3584]{1,0:T(8,128)(2,1)S(1)} %get-tuple-element.96), channel_id=1, source_target_pairs={{0,8},{8,0},{1,9},{9,1},{2,10},{10,2},{3,11},{11,3},{4,12},{12,4},... | collective-permute-start | bytes 688136 | tf_op jit(solution)/shard_map/ppermute | solution.py:194
  37.3 7.9 %collective-permute-start.18 = (bf16[32,3584]{1,0:T(8,128)(2,1)S(1)}, bf16[32,3584]{1,0:T(8,128)(2,1)S(1)}, u32[]{:S(2)}, u32[]{:S(2)}) collective-permute-start(bf16[32,3584]{1,0:T(8,128)(2,1)S(1)} %get-tuple-element.93), channel_id=1, source_target_pairs={{0,8},{8,0},{1,9},{9,1},{2,10},{10,2},{3,11},{11,3},{4,12},{12,4},... | collective-permute-start | bytes 688136 | tf_op jit(solution)/shard_map/ppermute | solution.py:194
  37.7 6.0 %collective-permute-start.26 = (bf16[32,3584]{1,0:T(8,128)(2,1)S(1)}, bf16[32,3584]{1,0:T(8,128)(2,1)S(1)}, u32[]{:S(2)}, u32[]{:S(2)}) collective-permute-start(bf16[32,3584]{1,0:T(8,128)(2,1)S(1)} %add_convert_fusion.8), channel_id=1, source_target_pairs={{0,2},{2,4},{4,6},{6,7},{7,5},{5,3},{3,1},{1,0},{10,8},{12,10},{14... | collective-permute-start | bytes 688136 | tf_op jit(solution)/shard_map/ppermute | solution.py:191
  41.4 2.2 %collective-permute-start.25 = (bf16[32,3584]{1,0:T(8,128)(2,1)S(1)}, bf16[32,3584]{1,0:T(8,128)(2,1)S(1)}, u32[]{:S(2)}, u32[]{:S(2)}) collective-permute-start(bf16[32,3584]{1,0:T(8,128)(2,1)S(1)} %get-tuple-element.98), channel_id=1, source_target_pairs={{0,8},{8,0},{1,9},{9,1},{2,10},{10,2},{3,11},{11,3},{4,12},{12,4},... | collective-permute-start | bytes 688136 | tf_op jit(solution)/shard_map/ppermute | solution.py:194
  43.7 10.1 %collective-permute-start.17 = (bf16[32,3584]{1,0:T(8,128)(2,1)S(1)}, bf16[32,3584]{1,0:T(8,128)(2,1)S(1)}, u32[]{:S(2)}, u32[]{:S(2)}) collective-permute-start(bf16[32,3584]{1,0:T(8,128)(2,1)S(1)} %get-tuple-element.91), channel_id=1, source_target_pairs={{0,8},{8,0},{1,9},{9,1},{2,10},{10,2},{3,11},{11,3},{4,12},{12,4},... | collective-permute-start | bytes 688136 | tf_op jit(solution)/shard_map/ppermute | solution.py:194
  43.7 6.0 %collective-permute-start.20 = (bf16[32,3584]{1,0:T(8,128)(2,1)S(1)}, bf16[32,3584]{1,0:T(8,128)(2,1)S(1)}, u32[]{:S(2)}, u32[]{:S(2)}) collective-permute-start(bf16[32,3584]{1,0:T(8,128)(2,1)S(1)} %add_convert_fusion.7), channel_id=1, source_target_pairs={{0,2},{2,4},{4,6},{6,7},{7,5},{5,3},{3,1},{1,0},{10,8},{12,10},{14... | collective-permute-start | bytes 688136 | tf_op jit(solution)/shard_map/ppermute | solution.py:191
  45.3 6.9 %collective-permute-start.27 = (bf16[32,3584]{1,0:T(8,128)(2,1)S(1)}, bf16[32,3584]{1,0:T(8,128)(2,1)S(1)}, u32[]{:S(2)}, u32[]{:S(2)}) collective-permute-start(bf16[32,3584]{1,0:T(8,128)(2,1)S(1)} %add_convert_fusion.3), channel_id=1, source_target_pairs={{0,2},{2,4},{4,6},{6,7},{7,5},{5,3},{3,1},{1,0},{10,8},{12,10},{14... | collective-permute-start | bytes 688136 | tf_op jit(solution)/shard_map/ppermute | solution.py:191
  49.8 6.1 %collective-permute-start.21 = (bf16[32,3584]{1,0:T(8,128)(2,1)S(1)}, bf16[32,3584]{1,0:T(8,128)(2,1)S(1)}, u32[]{:S(2)}, u32[]{:S(2)}) collective-permute-start(bf16[32,3584]{1,0:T(8,128)(2,1)S(1)} %add_convert_fusion.6), channel_id=1, source_target_pairs={{0,2},{2,4},{4,6},{6,7},{7,5},{5,3},{3,1},{1,0},{10,8},{12,10},{14... | collective-permute-start | bytes 688136 | tf_op jit(solution)/shard_map/ppermute | solution.py:191
  52.2 6.1 %collective-permute-start.28 = (bf16[32,3584]{1,0:T(8,128)(2,1)S(1)}, bf16[32,3584]{1,0:T(8,128)(2,1)S(1)}, u32[]{:S(2)}, u32[]{:S(2)}) collective-permute-start(bf16[32,3584]{1,0:T(8,128)(2,1)S(1)} %add_convert_fusion.2), channel_id=1, source_target_pairs={{0,2},{2,4},{4,6},{6,7},{7,5},{5,3},{3,1},{1,0},{10,8},{12,10},{14... | collective-permute-start | bytes 688136 | tf_op jit(solution)/shard_map/ppermute | solution.py:191
  56.0 6.1 %collective-permute-start.22 = (bf16[32,3584]{1,0:T(8,128)(2,1)S(1)}, bf16[32,3584]{1,0:T(8,128)(2,1)S(1)}, u32[]{:S(2)}, u32[]{:S(2)}) collective-permute-start(bf16[32,3584]{1,0:T(8,128)(2,1)S(1)} %add_convert_fusion.5), channel_id=1, source_target_pairs={{0,2},{2,4},{4,6},{6,7},{7,5},{5,3},{3,1},{1,0},{10,8},{12,10},{14... | collective-permute-start | bytes 688136 | tf_op jit(solution)/shard_map/ppermute | solution.py:191
  58.4 5.3 %collective-permute-start.29 = (bf16[32,3584]{1,0:T(8,128)(2,1)S(1)}, bf16[32,3584]{1,0:T(8,128)(2,1)S(1)}, u32[]{:S(2)}, u32[]{:S(2)}) collective-permute-start(bf16[32,3584]{1,0:T(8,128)(2,1)S(1)} %add_convert_fusion.1), channel_id=1, source_target_pairs={{0,8},{8,0},{1,9},{9,1},{2,10},{10,2},{3,11},{11,3},{4,12},{12,4},... | collective-permute-start | bytes 688136 | tf_op jit(solution)/shard_map/ppermute | solution.py:194
  62.1 6.1 %collective-permute-start.23 = (bf16[32,3584]{1,0:T(8,128)(2,1)S(1)}, bf16[32,3584]{1,0:T(8,128)(2,1)S(1)}, u32[]{:S(2)}, u32[]{:S(2)}) collective-permute-start(bf16[32,3584]{1,0:T(8,128)(2,1)S(1)} %add_convert_fusion.4), channel_id=1, source_target_pairs={{0,2},{2,4},{4,6},{6,7},{7,5},{5,3},{3,1},{1,0},{10,8},{12,10},{14... | collective-permute-start | bytes 688136 | tf_op jit(solution)/shard_map/ppermute | solution.py:191

commit v5 on v4

--- a/solution.py
+++ b/solution.py
@@ -225,33 +225,39 @@
         elif h < half:
             compute(h - 2)
             a[h], behind[h - 2], ahead[h - 2] = lax.optimization_barrier((a[h], behind[h - 2], ahead[h - 2]))
+        if 1 < h < half:
+            a[h], ahead_a[h - 1], ahead_b[h - 1] = lax.optimization_barrier((a[h], ahead_a[h - 1], ahead_b[h - 1]))
         if h < half:
             ahead_b.append(swap(a[h]))
             ahead_a.append(swap(b[h]))
-    compute(half - 1, (ahead_a[half - 2], ahead_b[half - 2]))
+    compute(half - 2, b[half - 1])
+    compute(half - 1, behind[half - 2])
     a[half], behind[half - 1], ahead[half - 1] = lax.optimization_barrier((a[half], behind[half - 1], ahead[half - 1]))
     ahead_b.append(swap(a[half]))
 
     def join(x, y):
         return x.astype(jnp.float32) + y.astype(jnp.float32)
 
-    def total(h):
-        return [join(ahead[h][0], swap(behind[h][1])), join(ahead[h][1], swap(behind[h][0]))]
-
-    sums = total(half - 1)
-    send_b = bf(sums[1])
+    def total(h, after=None):
+        mine_a, mine_b = behind[h]
+        if after is not None:
+            mine_a, mine_b, _ = lax.optimization_barrier((mine_a, mine_b, after))
+        sum_b = join(ahead[h][1], swap(mine_a))
+        return [join(ahead[h][0], swap(mine_b)), sum_b]
+
+    sums = {half - 1: total(half - 1)}
+    send_b = bf(sums[half - 1][1])
     run_b = hop(send_b)
-    last_blocks, send_b = lax.optimization_barrier(((a[half], ahead_b[half]), send_b))
+    last_blocks, send_b, sums[half - 1] = lax.optimization_barrier(((a[half], ahead_b[half]), send_b, sums[half - 1]))
     far = expert(mine, last_blocks, (True, False), up, down)
-    send_a = bf(join(far[0], swap(far[1])))
-    run_a = hop(send_a)
+    sums[half - 2] = total(half - 2, far[0])
+    run_a = hop(bf(join(far[0], swap(far[1]))))
     for h in range(half - 1, 0, -1):
         if h < half - 1:
-            if h not in behind:
-                compute(h, far)
-            sums = total(h)
-            run_b = hop(bf(join(sums[1], run_b)))
-        run_a = hop(bf(join(sums[0], run_a)))
+            run_b = hop(bf(join(sums[h][1], run_b)))
+        if h - 1 > 0 and h - 1 not in sums:
+            sums[h - 1] = total(h - 1, run_a)
+        run_a = hop(bf(join(sums[h][0], run_a)))
     last = swap(bf(join(own_b, run_b)))
     return bf(join(join(own_a, run_a), last))
 
@@ -265,7 +271,7 @@
         P(("node", "local"), None, None),
     )
     n = mesh.shape["local"]
-    ringed = mesh.shape["node"] == 2 and n % 2 == 0 and 4 <= n <= 16
+    ringed = mesh.shape["node"] == 2 and n % 2 == 0 and 6 <= n <= 16
     return jax.shard_map(
         ring_plan if ringed else gather_plan,
         mesh=mesh,

time: 69.1 us -> 64 us (0.926)
  waiting for transfers between devices: 23.5 us -> 19.8 us
  starting transfers between devices: 25.5 us -> 24.1 us
    ppermute x14, waiting for transfers between devices: 22.2 us -> 17 us  [hop(): return lax.ppermute(x, BOTH, pairs)]
    ppermute x16, waiting for transfers between devices: 1.31 us -> 2.79 us  [swap(): return lax.ppermute(x, 'node', [(0, 1), (1, 0)])]
    ppermute x14, starting transfers between devices: 22.3 us -> 21.2 us  [hop(): return lax.ppermute(x, BOTH, pairs)]
  transfers between devices with their start and end apart: 30 -> 30, of which waited for: 12 -> 13; matrix products, arithmetic and copies ran while one was open for 1% -> 1% of each run, Pallas kernels for 21% -> 23%
where the time goes in v5:
time: 64 us; the launch traced here: 63.8 us
  starting transfers between devices  24.1 us (38%)
  waiting for transfers between devices  19.8 us (31%)
  Pallas kernels  18.5 us (29%)
  other arithmetic  1.3 us (2%)
    ppermute x14, starting transfers between devices, hop(): return lax.ppermute(x, BOTH, pairs)  21.2 us
    ppermute x14, waiting for transfers between devices, hop(): return lax.ppermute(x, BOTH, pairs)  17 us
    pallas_call x4, Pallas kernels, expert(): pl.pallas_call(functools.partial(expert_body, len(blocks), kept), out_sha...  9.59 us
    pallas_call x1, Pallas kernels, first_up(): pl.pallas_call(first_up_body, out_shape=[pltpu.VMEM((2 * rows, middle), j...  4.23 us
    pallas_call x1, Pallas kernels, first_down(): pl.pallas_call(first_down_body, out_shape=[pltpu.VMEM((rows, width), jnp....  3.52 us
    ppermute x16, starting transfers between devices, swap(): return lax.ppermute(x, 'node', [(0, 1), (1, 0)])  2.93 us
    ppermute x16, waiting for transfers between devices, swap(): return lax.ppermute(x, 'node', [(0, 1), (1, 0)])  2.79 us
  transfers between devices with their start and end apart: 30, of which 13 were waited for; matrix products, arithmetic and copies ran while one was open for 1% of the time, Pallas kernels for 23%

profile of v5, /device:TPU:0, one launch (start us, length us, event | category | flops | bytes accessed | tf_op | source)
XLA Modules:
  0.0 63.8 jit_solution(9055990536151778654)
XLA Ops:
  0.0 1.1 %shard_map.55.own_ref = bf16[32,3712]{1,0:T(8,128)(2,1)S(1)} custom-call(bf16[32,3584]{1,0:T(8,128)(2,1)} %tokens_ref.1, s32[8,32]{1,0:T(8,128)} %bitcast.7, bf16[8,32]{1,0:T(8,128)(2,1)} %bitcast.8), custom_call_target="tpu_custom_call" | custom-call | tf_op jit(solution)/shard_map/pallas_call | solution.py:173
  1.1 0.5 collective-permute-start.1
  1.6 2.6 %collective-permute-start = (bf16[32,3712]{1,0:T(8,128)(2,1)S(1)}, bf16[32,3712]{1,0:T(8,128)(2,1)S(1)}, u32[]{:S(2)}, u32[]{:S(2)}) collective-permute-start(bf16[32,3712]{1,0:T(8,128)(2,1)S(1)} %shard_map.55.own_ref), channel_id=1, source_target_pairs={{0,2},{2,4},{4,6},{6,7},{7,5},{5,3},{3,1},{1,0},{10,8},{12,10},{14... | collective-permute-start | bytes 712712 | tf_op jit(solution)/shard_map/ppermute | solution.py:191
  4.2 0.0 collective-permute-done.1.other_ref
  4.2 1.6 %collective-permute-start.3 = (bf16[32,3712]{1,0:T(8,128)(2,1)S(1)}, bf16[32,3712]{1,0:T(8,128)(2,1)S(1)}, u32[]{:S(2)}, u32[]{:S(2)}) collective-permute-start(bf16[32,3712]{1,0:T(8,128)(2,1)S(1)} %collective-permute-done.1.other_ref), channel_id=1, source_target_pairs={{0,2},{2,4},{4,6},{6,7},{7,5},{5,3},{3,1},{1,0},{10,8},{12,10},{14... | collective-permute-start | bytes 712712 | tf_op jit(solution)/shard_map/ppermute | solution.py:191
  5.8 4.2 %shard_map.56 = (bf16[64,1024]{1,0:T(8,128)(2,1)S(1)}, f32[64,128]{1,0:T(8,128)S(1)}, bf16[3584,1024]{1,0:T(8,128)(2,1)S(1)}) custom-call(s32[1]{0:T(128)} %bitcast.2.mine_ref, bf16[32,3712]{1,0:T(8,128)(2,1)S(1)} %shard_map.55.own_ref, bf16[32,3712]{1,0:T(8,128)(2,1)S(1)} %collective-permute-done.1.other_ref, bf16[3584,1024]{1,0:T(8,128)(2,1)} %bitcast.6), custom_call_target="tpu_custom_call" | custom-call | flops 469762048 | bytes 7340032 | tf_op jit(solution)/shard_map/pallas_call | solution.py:98
  10.0 0.0 collective-permute-done.refs_0_
  10.0 1.6 %collective-permute-start.2 = (bf16[32,3712]{1,0:T(8,128)(2,1)S(1)}, bf16[32,3712]{1,0:T(8,128)(2,1)S(1)}, u32[]{:S(2)}, u32[]{:S(2)}) collective-permute-start(bf16[32,3712]{1,0:T(8,128)(2,1)S(1)} %collective-permute-done.refs_0_), channel_id=1, source_target_pairs={{0,2},{2,4},{4,6},{6,7},{7,5},{5,3},{3,1},{1,0},{10,8},{12,10},{14... | collective-permute-start | bytes 712712 | tf_op jit(solution)/shard_map/ppermute | solution.py:191
  11.6 0.0 collective-permute-start.5
  11.6 0.0 collective-permute-done.3.refs_1_
  11.6 0.5 collective-permute-start.4
  12.2 1.5 %collective-permute-start.7 = (bf16[32,3712]{1,0:T(8,128)(2,1)S(1)}, bf16[32,3712]{1,0:T(8,128)(2,1)S(1)}, u32[]{:S(2)}, u32[]{:S(2)}) collective-permute-start(bf16[32,3712]{1,0:T(8,128)(2,1)S(1)} %collective-permute-done.3.refs_1_), channel_id=1, source_target_pairs={{0,2},{2,4},{4,6},{6,7},{7,5},{5,3},{3,1},{1,0},{10,8},{12,10},{14... | collective-permute-start | bytes 712712 | tf_op jit(solution)/shard_map/ppermute | solution.py:191
  13.7 3.5 %shard_map.57 = (f32[32,3584]{1,0:T(8,128)S(1)}, f32[32,3584]{1,0:T(8,128)S(1)}, bf16[1024,3584]{1,0:T(8,128)(2,1)S(1)}) custom-call(bf16[64,1024]{1,0:T(8,128)(2,1)S(1)} %get-tuple-element.66.hidden_ref, f32[64,128]{1,0:T(8,128)S(1)} %get-tuple-element.67.scale_ref, bf16[1024,3584]{1,0:T(8,128)(2,1)} %bitcast.5), custom_call_target="tpu_custom_call" | custom-call | flops 469762048 | bytes 7340032 | tf_op jit(solution)/shard_map/pallas_call | solution.py:138
  17.2 0.0 collective-permute-done.2.refs_0_
  17.2 0.0 collective-permute-done.4.refs_2_
  17.2 1.5 %collective-permute-start.6 = (bf16[32,3712]{1,0:T(8,128)(2,1)S(1)}, bf16[32,3712]{1,0:T(8,128)(2,1)S(1)}, u32[]{:S(2)}, u32[]{:S(2)}) collective-permute-start(bf16[32,3712]{1,0:T(8,128)(2,1)S(1)} %collective-permute-done.2.refs_0_), channel_id=1, source_target_pairs={{0,2},{2,4},{4,6},{6,7},{7,5},{5,3},{3,1},{1,0},{10,8},{12,10},{14... | collective-permute-start | bytes 712712 | tf_op jit(solution)/shard_map/ppermute | solution.py:191
  18.8 0.5 collective-permute-start.8
  19.3 1.0 %collective-permute-start.11 = (bf16[32,3712]{1,0:T(8,128)(2,1)S(1)}, bf16[32,3712]{1,0:T(8,128)(2,1)S(1)}, u32[]{:S(2)}, u32[]{:S(2)}) collective-permute-start(bf16[32,3712]{1,0:T(8,128)(2,1)S(1)} %collective-permute-done.7.refs_1_), channel_id=1, source_target_pairs={{0,2},{2,4},{4,6},{6,7},{7,5},{5,3},{3,1},{1,0},{10,8},{12,10},{14... | collective-permute-start | bytes 712712 | tf_op jit(solution)/shard_map/ppermute | solution.py:191
  20.3 2.3 %shard_map.58 = (bf16[32,3584]{1,0:T(8,128)(2,1)S(1)}, bf16[32,3584]{1,0:T(8,128)(2,1)S(1)}, f32[32,3584]{1,0:T(8,128)S(1)}, f32[32,3584]{1,0:T(8,128)S(1)}) custom-call(s32[1]{0:T(128)} %bitcast.2.mine_ref, bf16[32,3712]{1,0:T(8,128)(2,1)S(1)} %collective-permute-done.refs_0_, bf16[32,3712]{1,0:T(8,128)(2,1)S(1)} %collective-permute-done.3.refs_1_, ...), custom_call_target="tpu_custom_call" | custom-call | flops 1879048192 | bytes 14680064 | tf_op jit(solution)/shard_map/pallas_call | solution.py:61
  22.6 0.8 %collective-permute-done.6.refs_0_ = bf16[32,3712]{1,0:T(8,128)(2,1)S(1)} collective-permute-done((bf16[32,3712]{1,0:T(8,128)(2,1)S(1)}, bf16[32,3712]{1,0:T(8,128)(2,1)S(1)}, u32[]{:S(2)}, u32[]{:S(2)}) %collective-permute-start.6) | collective-permute-done | bytes 237600 | tf_op jit(solution)/shard_map/ppermute | solution.py:191
  23.4 0.0 collective-permute-done.9.refs_3_
  23.4 0.0 collective-permute-done.8.refs_2_
  23.4 0.0 collective-permute-start.13
  23.4 2.5 %collective-permute-done.11.refs_1_ = bf16[32,3712]{1,0:T(8,128)(2,1)S(1)} collective-permute-done((bf16[32,3712]{1,0:T(8,128)(2,1)S(1)}, bf16[32,3712]{1,0:T(8,128)(2,1)S(1)}, u32[]{:S(2)}, u32[]{:S(2)}) %collective-permute-start.11) | collective-permute-done | bytes 237600 | tf_op jit(solution)/shard_map/ppermute | solution.py:191
  25.9 0.0 collective-permute-start.12
  25.9 1.5 %collective-permute-start.10 = (bf16[32,3712]{1,0:T(8,128)(2,1)S(1)}, bf16[32,3712]{1,0:T(8,128)(2,1)S(1)}, u32[]{:S(2)}, u32[]{:S(2)}) collective-permute-start(bf16[32,3712]{1,0:T(8,128)(2,1)S(1)} %collective-permute-done.6.refs_0_), channel_id=1, source_target_pairs={{0,2},{2,4},{4,6},{6,7},{7,5},{5,3},{3,1},{1,0},{10,8},{12,10},{14... | collective-permute-start | bytes 712712 | tf_op jit(solution)/shard_map/ppermute | solution.py:191
  27.4 2.3 %shard_map.59 = (bf16[32,3584]{1,0:T(8,128)(2,1)S(1)}, bf16[32,3584]{1,0:T(8,128)(2,1)S(1)}, f32[32,3584]{1,0:T(8,128)S(1)}, f32[32,3584]{1,0:T(8,128)S(1)}) custom-call(s32[1]{0:T(128)} %bitcast.2.mine_ref, bf16[32,3712]{1,0:T(8,128)(2,1)S(1)} %collective-permute-done.2.refs_0_, bf16[32,3712]{1,0:T(8,128)(2,1)S(1)} %collective-permute-done.7.refs_1_, ...), custom_call_target="tpu_custom_call" | custom-call | flops 1879048192 | bytes 14680064 | tf_op jit(solution)/shard_map/pallas_call | solution.py:61
  29.7 0.0 collective-permute-done.12.refs_2_
  29.7 2.3 %shard_map.60 = (bf16[32,3584]{1,0:T(8,128)(2,1)S(1)}, bf16[32,3584]{1,0:T(8,128)(2,1)S(1)}, f32[32,3584]{1,0:T(8,128)S(1)}, f32[32,3584]{1,0:T(8,128)S(1)}) custom-call(s32[1]{0:T(128)} %bitcast.2.mine_ref, bf16[32,3712]{1,0:T(8,128)(2,1)S(1)} %collective-permute-done.6.refs_0_, bf16[32,3712]{1,0:T(8,128)(2,1)S(1)} %collective-permute-done.11.refs_1_, ...), custom_call_target="tpu_custom_call" | custom-call | flops 1879048192 | bytes 14680064 | tf_op jit(solution)/shard_map/pallas_call | solution.py:61
  32.0 0.0 collective-permute-done.10.refs_0_
  32.0 0.0 collective-permute-start.16
  32.1 0.5 collective-permute-start.15
  32.6 0.1 collective-permute-start.14
  32.7 0.9 %collective-permute-done.16 = bf16[32,3584]{1,0:T(8,128)(2,1)S(1)} collective-permute-done((bf16[32,3584]{1,0:T(8,128)(2,1)S(1)}, bf16[32,3584]{1,0:T(8,128)(2,1)S(1)}, u32[]{:S(2)}, u32[]{:S(2)}) %collective-permute-start.16) | collective-permute-done | bytes 229408 | tf_op jit(solution)/shard_map/ppermute | solution.py:194
  33.6 0.1 convert_add_fusion
  33.6 0.3 collective-permute-done.15
  33.9 0.1 convert_add_fusion.1
  34.0 0.3 collective-permute-done.14.refs_1_
  34.2 2.7 %shard_map.61 = (f32[32,3584]{1,0:T(8,128)S(1)}, bf16[32,3584]{1,0:T(8,128)(2,1)S(1)}) custom-call(s32[1]{0:T(128)} %bitcast.2.mine_ref, bf16[32,3712]{1,0:T(8,128)(2,1)S(1)} %collective-permute-done.10.refs_0_, bf16[32,3712]{1,0:T(8,128)(2,1)S(1)} %collective-permute-done.14.refs_1_, bf16[3584,1024]{1,0:T(8,128)(2,1)S(1)} %get-tuple-element.76.refs_4_.refs_2_, ...), custom_call_target="tpu_custom_call" | custom-call | flops 939524096 | bytes 14680064 | tf_op jit(solution)/shard_map/pallas_call | solution.py:61
  37.0 0.2 collective-permute-start.17
  37.2 1.3 %collective-permute-done.17 = bf16[32,3584]{1,0:T(8,128)(2,1)S(1)} collective-permute-done((bf16[32,3584]{1,0:T(8,128)(2,1)S(1)}, bf16[32,3584]{1,0:T(8,128)(2,1)S(1)}, u32[]{:S(2)}, u32[]{:S(2)}) %collective-permute-start.17) | collective-permute-done | bytes 229408 | tf_op jit(solution)/shard_map/ppermute | solution.py:194
  38.5 0.1 add_convert_fusion.7
  38.6 1.5 %collective-permute-start.18 = (bf16[32,3584]{1,0:T(8,128)(2,1)S(1)}, bf16[32,3584]{1,0:T(8,128)(2,1)S(1)}, u32[]{:S(2)}, u32[]{:S(2)}) collective-permute-start(bf16[32,3584]{1,0:T(8,128)(2,1)S(1)} %add_convert_fusion.7), channel_id=1, source_target_pairs={{0,2},{2,4},{4,6},{6,7},{7,5},{5,3},{3,1},{1,0},{10,8},{12,10},{14... | collective-permute-start | bytes 688136 | tf_op jit(solution)/shard_map/ppermute | solution.py:191
  40.1 1.0 %collective-permute-start.26 = (bf16[32,3584]{1,0:T(8,128)(2,1)S(1)}, bf16[32,3584]{1,0:T(8,128)(2,1)S(1)}, u32[]{:S(2)}, u32[]{:S(2)}) collective-permute-start(bf16[32,3584]{1,0:T(8,128)(2,1)S(1)} %convert_add_fusion.1), channel_id=1, source_target_pairs={{0,2},{2,4},{4,6},{6,7},{7,5},{5,3},{3,1},{1,0},{10,8},{12,10},{14... | collective-permute-start | bytes 688136 | tf_op jit(solution)/shard_map/ppermute | solution.py:191
  41.0 0.5 collective-permute-start.25
  41.5 3.1 %collective-permute-done.18 = bf16[32,3584]{1,0:T(8,128)(2,1)S(1)} collective-permute-done((bf16[32,3584]{1,0:T(8,128)(2,1)S(1)}, bf16[32,3584]{1,0:T(8,128)(2,1)S(1)}, u32[]{:S(2)}, u32[]{:S(2)}) %collective-permute-start.18) | collective-permute-done | bytes 229408 | tf_op jit(solution)/shard_map/ppermute | solution.py:191
  44.6 0.1 add_convert_fusion.6
  44.7 1.5 %collective-permute-start.19 = (bf16[32,3584]{1,0:T(8,128)(2,1)S(1)}, bf16[32,3584]{1,0:T(8,128)(2,1)S(1)}, u32[]{:S(2)}, u32[]{:S(2)}) collective-permute-start(bf16[32,3584]{1,0:T(8,128)(2,1)S(1)} %add_convert_fusion.6), channel_id=1, source_target_pairs={{0,2},{2,4},{4,6},{6,7},{7,5},{5,3},{3,1},{1,0},{10,8},{12,10},{14... | collective-permute-start | bytes 688136 | tf_op jit(solution)/shard_map/ppermute | solution.py:191
  46.2 0.9 %collective-permute-done.26 = bf16[32,3584]{1,0:T(8,128)(2,1)S(1)} collective-permute-done((bf16[32,3584]{1,0:T(8,128)(2,1)S(1)}, bf16[32,3584]{1,0:T(8,128)(2,1)S(1)}, u32[]{:S(2)}, u32[]{:S(2)}) %collective-permute-start.26) | collective-permute-done | bytes 229408 | tf_op jit(solution)/shard_map/ppermute | solution.py:191
  47.1 0.1 add_convert_fusion.3
  47.2 1.5 %collective-permute-start.27 = (bf16[32,3584]{1,0:T(8,128)(2,1)S(1)}, bf16[32,3584]{1,0:T(8,128)(2,1)S(1)}, u32[]{:S(2)}, u32[]{:S(2)}) collective-permute-start(bf16[32,3584]{1,0:T(8,128)(2,1)S(1)} %add_convert_fusion.3), channel_id=1, source_target_pairs={{0,2},{2,4},{4,6},{6,7},{7,5},{5,3},{3,1},{1,0},{10,8},{12,10},{14... | collective-permute-start | bytes 688136 | tf_op jit(solution)/shard_map/ppermute | solution.py:191
  48.7 2.1 %collective-permute-done.19 = bf16[32,3584]{1,0:T(8,128)(2,1)S(1)} collective-permute-done((bf16[32,3584]{1,0:T(8,128)(2,1)S(1)}, bf16[32,3584]{1,0:T(8,128)(2,1)S(1)}, u32[]{:S(2)}, u32[]{:S(2)}) %collective-permute-start.19) | collective-permute-done | bytes 229408 | tf_op jit(solution)/shard_map/ppermute | solution.py:191
  50.8 0.1 add_convert_fusion.5
  50.9 1.5 %collective-permute-start.22 = (bf16[32,3584]{1,0:T(8,128)(2,1)S(1)}, bf16[32,3584]{1,0:T(8,128)(2,1)S(1)}, u32[]{:S(2)}, u32[]{:S(2)}) collective-permute-start(bf16[32,3584]{1,0:T(8,128)(2,1)S(1)} %add_convert_fusion.5), channel_id=1, source_target_pairs={{0,2},{2,4},{4,6},{6,7},{7,5},{5,3},{3,1},{1,0},{10,8},{12,10},{14... | collective-permute-start | bytes 688136 | tf_op jit(solution)/shard_map/ppermute | solution.py:191
  52.3 0.9 %collective-permute-done.27 = bf16[32,3584]{1,0:T(8,128)(2,1)S(1)} collective-permute-done((bf16[32,3584]{1,0:T(8,128)(2,1)S(1)}, bf16[32,3584]{1,0:T(8,128)(2,1)S(1)}, u32[]{:S(2)}, u32[]{:S(2)}) %collective-permute-start.27) | collective-permute-done | bytes 229408 | tf_op jit(solution)/shard_map/ppermute | solution.py:191
  53.3 0.1 add_convert_fusion.2
  53.3 1.5 %collective-permute-start.28 = (bf16[32,3584]{1,0:T(8,128)(2,1)S(1)}, bf16[32,3584]{1,0:T(8,128)(2,1)S(1)}, u32[]{:S(2)}, u32[]{:S(2)}) collective-permute-start(bf16[32,3584]{1,0:T(8,128)(2,1)S(1)} %add_convert_fusion.2), channel_id=1, source_target_pairs={{0,2},{2,4},{4,6},{6,7},{7,5},{5,3},{3,1},{1,0},{10,8},{12,10},{14... | collective-permute-start | bytes 688136 | tf_op jit(solution)/shard_map/ppermute | solution.py:191
  54.8 2.1 %collective-permute-done.22 = bf16[32,3584]{1,0:T(8,128)(2,1)S(1)} collective-permute-done((bf16[32,3584]{1,0:T(8,128)(2,1)S(1)}, bf16[32,3584]{1,0:T(8,128)(2,1)S(1)}, u32[]{:S(2)}, u32[]{:S(2)}) %collective-permute-start.22) | collective-permute-done | bytes 229408 | tf_op jit(solution)/shard_map/ppermute | solution.py:191
  56.9 0.1 add_convert_fusion.4
  57.0 1.5 %collective-permute-start.23 = (bf16[32,3584]{1,0:T(8,128)(2,1)S(1)}, bf16[32,3584]{1,0:T(8,128)(2,1)S(1)}, u32[]{:S(2)}, u32[]{:S(2)}) collective-permute-start(bf16[32,3584]{1,0:T(8,128)(2,1)S(1)} %add_convert_fusion.4), channel_id=1, source_target_pairs={{0,2},{2,4},{4,6},{6,7},{7,5},{5,3},{3,1},{1,0},{10,8},{12,10},{14... | collective-permute-start | bytes 688136 | tf_op jit(solution)/shard_map/ppermute | solution.py:191
  58.5 0.9 %collective-permute-done.28 = bf16[32,3584]{1,0:T(8,128)(2,1)S(1)} collective-permute-done((bf16[32,3584]{1,0:T(8,128)(2,1)S(1)}, bf16[32,3584]{1,0:T(8,128)(2,1)S(1)}, u32[]{:S(2)}, u32[]{:S(2)}) %collective-permute-start.28) | collective-permute-done | bytes 229408 | tf_op jit(solution)/shard_map/ppermute | solution.py:191
  59.5 0.1 collective-permute-start.29
  59.5 3.5 %collective-permute-done.23 = bf16[32,3584]{1,0:T(8,128)(2,1)S(1)} collective-permute-done((bf16[32,3584]{1,0:T(8,128)(2,1)S(1)}, bf16[32,3584]{1,0:T(8,128)(2,1)S(1)}, u32[]{:S(2)}, u32[]{:S(2)}) %collective-permute-start.23) | collective-permute-done | bytes 229408 | tf_op jit(solution)/shard_map/ppermute | solution.py:191
  63.1 0.8 %add_convert_fusion = bf16[32,3584]{1,0:T(8,128)(2,1)} fusion(bf16[32,3584]{1,0:T(8,128)(2,1)S(1)} %collective-permute-done.29, f32[32,3584]{1,0:T(8,128)S(1)} %get-tuple-element.71, bf16[32,3584]{1,0:T(8,128)(2,1)S(1)} %collective-permute-done.23), kind=kLoop, calls=%fused_computation | loop fusion | flops 573440 | bytes 1146880 | tf_op jit(solution)/shard_map/convert_element_type | solution.py:197
  (13 shorter events, 0.1 us)
Async XLA Ops:
  1.1 3.1 %collective-permute-start.1 = (bf16[32,3712]{1,0:T(8,128)(2,1)S(1)}, bf16[32,3712]{1,0:T(8,128)(2,1)S(1)}, u32[]{:S(2)}, u32[]{:S(2)}) collective-permute-start(bf16[32,3712]{1,0:T(8,128)(2,1)S(1)} %shard_map.55.own_ref), channel_id=1, source_target_pairs={{0,8},{8,0},{1,9},{9,1},{2,10},{10,2},{3,11},{11,3},{4,12},{12,4},... | collective-permute-start | bytes 712712 | tf_op jit(solution)/shard_map/ppermute | solution.py:194
  1.6 8.4 %collective-permute-start = (bf16[32,3712]{1,0:T(8,128)(2,1)S(1)}, bf16[32,3712]{1,0:T(8,128)(2,1)S(1)}, u32[]{:S(2)}, u32[]{:S(2)}) collective-permute-start(bf16[32,3712]{1,0:T(8,128)(2,1)S(1)} %shard_map.55.own_ref), channel_id=1, source_target_pairs={{0,2},{2,4},{4,6},{6,7},{7,5},{5,3},{3,1},{1,0},{10,8},{12,10},{14... | collective-permute-start | bytes 712712 | tf_op jit(solution)/shard_map/ppermute | solution.py:191
  4.2 7.5 %collective-permute-start.3 = (bf16[32,3712]{1,0:T(8,128)(2,1)S(1)}, bf16[32,3712]{1,0:T(8,128)(2,1)S(1)}, u32[]{:S(2)}, u32[]{:S(2)}) collective-permute-start(bf16[32,3712]{1,0:T(8,128)(2,1)S(1)} %collective-permute-done.1.other_ref), channel_id=1, source_target_pairs={{0,2},{2,4},{4,6},{6,7},{7,5},{5,3},{3,1},{1,0},{10,8},{12,10},{14... | collective-permute-start | bytes 712712 | tf_op jit(solution)/shard_map/ppermute | solution.py:191
  10.0 7.2 %collective-permute-start.2 = (bf16[32,3712]{1,0:T(8,128)(2,1)S(1)}, bf16[32,3712]{1,0:T(8,128)(2,1)S(1)}, u32[]{:S(2)}, u32[]{:S(2)}) collective-permute-start(bf16[32,3712]{1,0:T(8,128)(2,1)S(1)} %collective-permute-done.refs_0_), channel_id=1, source_target_pairs={{0,2},{2,4},{4,6},{6,7},{7,5},{5,3},{3,1},{1,0},{10,8},{12,10},{14... | collective-permute-start | bytes 712712 | tf_op jit(solution)/shard_map/ppermute | solution.py:191
  11.6 5.6 %collective-permute-start.5 = (bf16[32,3712]{1,0:T(8,128)(2,1)S(1)}, bf16[32,3712]{1,0:T(8,128)(2,1)S(1)}, u32[]{:S(2)}, u32[]{:S(2)}) collective-permute-start(bf16[32,3712]{1,0:T(8,128)(2,1)S(1)} %collective-permute-done.refs_0_), channel_id=1, source_target_pairs={{0,8},{8,0},{1,9},{9,1},{2,10},{10,2},{3,11},{11,3},{4,12},{12,4},... | collective-permute-start | bytes 712712 | tf_op jit(solution)/shard_map/ppermute | solution.py:194
  11.6 5.6 %collective-permute-start.4 = (bf16[32,3712]{1,0:T(8,128)(2,1)S(1)}, bf16[32,3712]{1,0:T(8,128)(2,1)S(1)}, u32[]{:S(2)}, u32[]{:S(2)}) collective-permute-start(bf16[32,3712]{1,0:T(8,128)(2,1)S(1)} %collective-permute-done.3.refs_1_), channel_id=1, source_target_pairs={{0,8},{8,0},{1,9},{9,1},{2,10},{10,2},{3,11},{11,3},{4,12},{12,4},... | collective-permute-start | bytes 712712 | tf_op jit(solution)/shard_map/ppermute | solution.py:194
  12.2 6.6 %collective-permute-start.7 = (bf16[32,3712]{1,0:T(8,128)(2,1)S(1)}, bf16[32,3712]{1,0:T(8,128)(2,1)S(1)}, u32[]{:S(2)}, u32[]{:S(2)}) collective-permute-start(bf16[32,3712]{1,0:T(8,128)(2,1)S(1)} %collective-permute-done.3.refs_1_), channel_id=1, source_target_pairs={{0,2},{2,4},{4,6},{6,7},{7,5},{5,3},{3,1},{1,0},{10,8},{12,10},{14... | collective-permute-start | bytes 712712 | tf_op jit(solution)/shard_map/ppermute | solution.py:191
  17.2 6.2 %collective-permute-start.6 = (bf16[32,3712]{1,0:T(8,128)(2,1)S(1)}, bf16[32,3712]{1,0:T(8,128)(2,1)S(1)}, u32[]{:S(2)}, u32[]{:S(2)}) collective-permute-start(bf16[32,3712]{1,0:T(8,128)(2,1)S(1)} %collective-permute-done.2.refs_0_), channel_id=1, source_target_pairs={{0,2},{2,4},{4,6},{6,7},{7,5},{5,3},{3,1},{1,0},{10,8},{12,10},{14... | collective-permute-start | bytes 712712 | tf_op jit(solution)/shard_map/ppermute | solution.py:191
  18.8 4.6 %collective-permute-start.9 = (bf16[32,3712]{1,0:T(8,128)(2,1)S(1)}, bf16[32,3712]{1,0:T(8,128)(2,1)S(1)}, u32[]{:S(2)}, u32[]{:S(2)}) collective-permute-start(bf16[32,3712]{1,0:T(8,128)(2,1)S(1)} %collective-permute-done.2.refs_0_), channel_id=1, source_target_pairs={{0,8},{8,0},{1,9},{9,1},{2,10},{10,2},{3,11},{11,3},{4,12},{12,4},... | collective-permute-start | bytes 712712 | tf_op jit(solution)/shard_map/ppermute | solution.py:194
  18.8 4.6 %collective-permute-start.8 = (bf16[32,3712]{1,0:T(8,128)(2,1)S(1)}, bf16[32,3712]{1,0:T(8,128)(2,1)S(1)}, u32[]{:S(2)}, u32[]{:S(2)}) collective-permute-start(bf16[32,3712]{1,0:T(8,128)(2,1)S(1)} %collective-permute-done.7.refs_1_), channel_id=1, source_target_pairs={{0,8},{8,0},{1,9},{9,1},{2,10},{10,2},{3,11},{11,3},{4,12},{12,4},... | collective-permute-start | bytes 712712 | tf_op jit(solution)/shard_map/ppermute | solution.py:194
  19.3 6.7 %collective-permute-start.11 = (bf16[32,3712]{1,0:T(8,128)(2,1)S(1)}, bf16[32,3712]{1,0:T(8,128)(2,1)S(1)}, u32[]{:S(2)}, u32[]{:S(2)}) collective-permute-start(bf16[32,3712]{1,0:T(8,128)(2,1)S(1)} %collective-permute-done.7.refs_1_), channel_id=1, source_target_pairs={{0,2},{2,4},{4,6},{6,7},{7,5},{5,3},{3,1},{1,0},{10,8},{12,10},{14... | collective-permute-start | bytes 712712 | tf_op jit(solution)/shard_map/ppermute | solution.py:191
  23.4 6.3 %collective-permute-start.13 = (bf16[32,3712]{1,0:T(8,128)(2,1)S(1)}, bf16[32,3712]{1,0:T(8,128)(2,1)S(1)}, u32[]{:S(2)}, u32[]{:S(2)}) collective-permute-start(bf16[32,3712]{1,0:T(8,128)(2,1)S(1)} %collective-permute-done.6.refs_0_), channel_id=1, source_target_pairs={{0,8},{8,0},{1,9},{9,1},{2,10},{10,2},{3,11},{11,3},{4,12},{12,4},... | collective-permute-start | bytes 712712 | tf_op jit(solution)/shard_map/ppermute | solution.py:194
  25.9 3.8 %collective-permute-start.12 = (bf16[32,3712]{1,0:T(8,128)(2,1)S(1)}, bf16[32,3712]{1,0:T(8,128)(2,1)S(1)}, u32[]{:S(2)}, u32[]{:S(2)}) collective-permute-start(bf16[32,3712]{1,0:T(8,128)(2,1)S(1)} %collective-permute-done.11.refs_1_), channel_id=1, source_target_pairs={{0,8},{8,0},{1,9},{9,1},{2,10},{10,2},{3,11},{11,3},{4,12},{12,4},... | collective-permute-start | bytes 712712 | tf_op jit(solution)/shard_map/ppermute | solution.py:194
  25.9 6.1 %collective-permute-start.10 = (bf16[32,3712]{1,0:T(8,128)(2,1)S(1)}, bf16[32,3712]{1,0:T(8,128)(2,1)S(1)}, u32[]{:S(2)}, u32[]{:S(2)}) collective-permute-start(bf16[32,3712]{1,0:T(8,128)(2,1)S(1)} %collective-permute-done.6.refs_0_), channel_id=1, source_target_pairs={{0,2},{2,4},{4,6},{6,7},{7,5},{5,3},{3,1},{1,0},{10,8},{12,10},{14... | collective-permute-start | bytes 712712 | tf_op jit(solution)/shard_map/ppermute | solution.py:191
  32.0 1.5 %collective-permute-start.16 = (bf16[32,3584]{1,0:T(8,128)(2,1)S(1)}, bf16[32,3584]{1,0:T(8,128)(2,1)S(1)}, u32[]{:S(2)}, u32[]{:S(2)}) collective-permute-start(bf16[32,3584]{1,0:T(8,128)(2,1)S(1)} %get-tuple-element.107), channel_id=1, source_target_pairs={{0,8},{8,0},{1,9},{9,1},{2,10},{10,2},{3,11},{11,3},{4,12},{12,4},... | collective-permute-start | bytes 688136 | tf_op jit(solution)/shard_map/ppermute | solution.py:194
  32.1 1.8 %collective-permute-start.15 = (bf16[32,3584]{1,0:T(8,128)(2,1)S(1)}, bf16[32,3584]{1,0:T(8,128)(2,1)S(1)}, u32[]{:S(2)}, u32[]{:S(2)}) collective-permute-start(bf16[32,3584]{1,0:T(8,128)(2,1)S(1)} %get-tuple-element.105), channel_id=1, source_target_pairs={{0,8},{8,0},{1,9},{9,1},{2,10},{10,2},{3,11},{11,3},{4,12},{12,4},... | collective-permute-start | bytes 688136 | tf_op jit(solution)/shard_map/ppermute | solution.py:194
  32.6 1.6 %collective-permute-start.14 = (bf16[32,3712]{1,0:T(8,128)(2,1)S(1)}, bf16[32,3712]{1,0:T(8,128)(2,1)S(1)}, u32[]{:S(2)}, u32[]{:S(2)}) collective-permute-start(bf16[32,3712]{1,0:T(8,128)(2,1)S(1)} %collective-permute-done.10.refs_0_), channel_id=1, source_target_pairs={{0,8},{8,0},{1,9},{9,1},{2,10},{10,2},{3,11},{11,3},{4,12},{12,4},... | collective-permute-start | bytes 712712 | tf_op jit(solution)/shard_map/ppermute | solution.py:194
  37.0 1.6 %collective-permute-start.17 = (bf16[32,3584]{1,0:T(8,128)(2,1)S(1)}, bf16[32,3584]{1,0:T(8,128)(2,1)S(1)}, u32[]{:S(2)}, u32[]{:S(2)}) collective-permute-start(bf16[32,3584]{1,0:T(8,128)(2,1)S(1)} %get-tuple-element.112), channel_id=1, source_target_pairs={{0,8},{8,0},{1,9},{9,1},{2,10},{10,2},{3,11},{11,3},{4,12},{12,4},... | collective-permute-start | bytes 688136 | tf_op jit(solution)/shard_map/ppermute | solution.py:194
  38.6 6.1 %collective-permute-start.18 = (bf16[32,3584]{1,0:T(8,128)(2,1)S(1)}, bf16[32,3584]{1,0:T(8,128)(2,1)S(1)}, u32[]{:S(2)}, u32[]{:S(2)}) collective-permute-start(bf16[32,3584]{1,0:T(8,128)(2,1)S(1)} %add_convert_fusion.7), channel_id=1, source_target_pairs={{0,2},{2,4},{4,6},{6,7},{7,5},{5,3},{3,1},{1,0},{10,8},{12,10},{14... | collective-permute-start | bytes 688136 | tf_op jit(solution)/shard_map/ppermute | solution.py:191
  40.1 7.0 %collective-permute-start.26 = (bf16[32,3584]{1,0:T(8,128)(2,1)S(1)}, bf16[32,3584]{1,0:T(8,128)(2,1)S(1)}, u32[]{:S(2)}, u32[]{:S(2)}) collective-permute-start(bf16[32,3584]{1,0:T(8,128)(2,1)S(1)} %convert_add_fusion.1), channel_id=1, source_target_pairs={{0,2},{2,4},{4,6},{6,7},{7,5},{5,3},{3,1},{1,0},{10,8},{12,10},{14... | collective-permute-start | bytes 688136 | tf_op jit(solution)/shard_map/ppermute | solution.py:191
  41.0 9.8 %collective-permute-start.21 = (bf16[32,3584]{1,0:T(8,128)(2,1)S(1)}, bf16[32,3584]{1,0:T(8,128)(2,1)S(1)}, u32[]{:S(2)}, u32[]{:S(2)}) collective-permute-start(bf16[32,3584]{1,0:T(8,128)(2,1)S(1)} %get-tuple-element.115), channel_id=1, source_target_pairs={{0,8},{8,0},{1,9},{9,1},{2,10},{10,2},{3,11},{11,3},{4,12},{12,4},... | collective-permute-start | bytes 688136 | tf_op jit(solution)/shard_map/ppermute | solution.py:194
  41.0 6.1 %collective-permute-start.25 = (bf16[32,3584]{1,0:T(8,128)(2,1)S(1)}, bf16[32,3584]{1,0:T(8,128)(2,1)S(1)}, u32[]{:S(2)}, u32[]{:S(2)}) collective-permute-start(bf16[32,3584]{1,0:T(8,128)(2,1)S(1)} %get-tuple-element.120), channel_id=1, source_target_pairs={{0,8},{8,0},{1,9},{9,1},{2,10},{10,2},{3,11},{11,3},{4,12},{12,4},... | collective-permute-start | bytes 688136 | tf_op jit(solution)/shard_map/ppermute | solution.py:194
  44.7 6.1 %collective-permute-start.19 = (bf16[32,3584]{1,0:T(8,128)(2,1)S(1)}, bf16[32,3584]{1,0:T(8,128)(2,1)S(1)}, u32[]{:S(2)}, u32[]{:S(2)}) collective-permute-start(bf16[32,3584]{1,0:T(8,128)(2,1)S(1)} %add_convert_fusion.6), channel_id=1, source_target_pairs={{0,2},{2,4},{4,6},{6,7},{7,5},{5,3},{3,1},{1,0},{10,8},{12,10},{14... | collective-permute-start | bytes 688136 | tf_op jit(solution)/shard_map/ppermute | solution.py:191
  47.2 6.1 %collective-permute-start.27 = (bf16[32,3584]{1,0:T(8,128)(2,1)S(1)}, bf16[32,3584]{1,0:T(8,128)(2,1)S(1)}, u32[]{:S(2)}, u32[]{:S(2)}) collective-permute-start(bf16[32,3584]{1,0:T(8,128)(2,1)S(1)} %add_convert_fusion.3), channel_id=1, source_target_pairs={{0,2},{2,4},{4,6},{6,7},{7,5},{5,3},{3,1},{1,0},{10,8},{12,10},{14... | collective-permute-start | bytes 688136 | tf_op jit(solution)/shard_map/ppermute | solution.py:191
  50.8 2.5 %collective-permute-start.24 = (bf16[32,3584]{1,0:T(8,128)(2,1)S(1)}, bf16[32,3584]{1,0:T(8,128)(2,1)S(1)}, u32[]{:S(2)}, u32[]{:S(2)}) collective-permute-start(bf16[32,3584]{1,0:T(8,128)(2,1)S(1)} %get-tuple-element.118), channel_id=1, source_target_pairs={{0,8},{8,0},{1,9},{9,1},{2,10},{10,2},{3,11},{11,3},{4,12},{12,4},... | collective-permute-start | bytes 688136 | tf_op jit(solution)/shard_map/ppermute | solution.py:194
  50.9 6.1 %collective-permute-start.22 = (bf16[32,3584]{1,0:T(8,128)(2,1)S(1)}, bf16[32,3584]{1,0:T(8,128)(2,1)S(1)}, u32[]{:S(2)}, u32[]{:S(2)}) collective-permute-start(bf16[32,3584]{1,0:T(8,128)(2,1)S(1)} %add_convert_fusion.5), channel_id=1, source_target_pairs={{0,2},{2,4},{4,6},{6,7},{7,5},{5,3},{3,1},{1,0},{10,8},{12,10},{14... | collective-permute-start | bytes 688136 | tf_op jit(solution)/shard_map/ppermute | solution.py:191
  52.3 4.6 %collective-permute-start.20 = (bf16[32,3584]{1,0:T(8,128)(2,1)S(1)}, bf16[32,3584]{1,0:T(8,128)(2,1)S(1)}, u32[]{:S(2)}, u32[]{:S(2)}) collective-permute-start(bf16[32,3584]{1,0:T(8,128)(2,1)S(1)} %get-tuple-element.113), channel_id=1, source_target_pairs={{0,8},{8,0},{1,9},{9,1},{2,10},{10,2},{3,11},{11,3},{4,12},{12,4},... | collective-permute-start | bytes 688136 | tf_op jit(solution)/shard_map/ppermute | solution.py:194
  53.3 6.1 %collective-permute-start.28 = (bf16[32,3584]{1,0:T(8,128)(2,1)S(1)}, bf16[32,3584]{1,0:T(8,128)(2,1)S(1)}, u32[]{:S(2)}, u32[]{:S(2)}) collective-permute-start(bf16[32,3584]{1,0:T(8,128)(2,1)S(1)} %add_convert_fusion.2), channel_id=1, source_target_pairs={{0,2},{2,4},{4,6},{6,7},{7,5},{5,3},{3,1},{1,0},{10,8},{12,10},{14... | collective-permute-start | bytes 688136 | tf_op jit(solution)/shard_map/ppermute | solution.py:191
  57.0 6.1 %collective-permute-start.23 = (bf16[32,3584]{1,0:T(8,128)(2,1)S(1)}, bf16[32,3584]{1,0:T(8,128)(2,1)S(1)}, u32[]{:S(2)}, u32[]{:S(2)}) collective-permute-start(bf16[32,3584]{1,0:T(8,128)(2,1)S(1)} %add_convert_fusion.4), channel_id=1, source_target_pairs={{0,2},{2,4},{4,6},{6,7},{7,5},{5,3},{3,1},{1,0},{10,8},{12,10},{14... | collective-permute-start | bytes 688136 | tf_op jit(solution)/shard_map/ppermute | solution.py:191
  59.5 3.6 %collective-permute-start.29 = (bf16[32,3584]{1,0:T(8,128)(2,1)S(1)}, bf16[32,3584]{1,0:T(8,128)(2,1)S(1)}, u32[]{:S(2)}, u32[]{:S(2)}) collective-permute-start(bf16[32,3584]{1,0:T(8,128)(2,1)S(1)} %add_convert_fusion.1), channel_id=1, source_target_pairs={{0,8},{8,0},{1,9},{9,1},{2,10},{10,2},{3,11},{11,3},{4,12},{12,4},... | collective-permute-start | bytes 688136 | tf_op jit(solution)/shard_map/ppermute | solution.py:194

commit v6 on v5

v6 whole, which is shorter than its diff:
```python
import functools
import jax
import jax.numpy as jnp
from jax import lax
from jax.experimental import pallas as pl
from jax.experimental.pallas import tpu as pltpu
from jax.sharding import PartitionSpec as P

BOTH = ("node", "local")
LANES = 128
LATE = (3, 4)


def gather_plan(tokens, expert_ids, route_weights, w_up, w_down):
    mine = lax.axis_index(BOTH)
    everyone = lax.all_gather(tokens, BOTH, tiled=True)
    ids = lax.all_gather(expert_ids, BOTH, tiled=True)
    weights = lax.all_gather(route_weights, BOTH, tiled=True)
    scale = jnp.sum(jnp.where(ids == mine, weights.astype(jnp.float32), 0.0), axis=1)
    hidden = jax.nn.silu(jnp.dot(everyone, w_up[0], preferred_element_type=jnp.float32)).astype(jnp.bfloat16)
    answer = jnp.dot(hidden, w_down[0], preferred_element_type=jnp.float32)
    part = (answer * scale[:, None]).astype(jnp.bfloat16)
    return lax.psum_scatter(part, BOTH, scatter_dimension=0, tiled=True)


def step_of(size, wanted):
    step = wanted
    while step > LANES and size % step:
        step //= 2
    return step if size % step == 0 else size


def expert_body(blocks, parts, mine_ref, *refs):
    tokens = refs[:blocks]
    up_ref, downs = refs[blocks], refs[blocks + 1:blocks + 1 + parts]
    outs = refs[blocks + 1 + parts:2 * blocks + 1 + parts]
    hidden_ref = refs[2 * blocks + 1 + parts]
    width, middle = up_ref.shape
    rows = tokens[0].shape[0]
    x = jnp.concatenate([t[:, :width] for t in tokens], axis=0)
    table = jnp.concatenate([t[:, width:] for t in tokens], axis=0).astype(jnp.float32)
    here = lax.broadcasted_iota(jnp.int32, table.shape, 1) == mine_ref[0]
    scale = jnp.sum(jnp.where(here, table, 0.0), axis=1, keepdims=True)
    step = step_of(middle, 256)
    for j in range(0, middle, step):
        up = jnp.dot(x, up_ref[:, j:j + step], preferred_element_type=jnp.float32)
        hidden_ref[:, j:j + step] = (up / (1.0 + jnp.exp(-up))).astype(jnp.bfloat16)
    hidden = hidden_ref[...]
    at = 0
    for down_ref in downs:
        step = step_of(down_ref.shape[1], 512)
        for j in range(0, down_ref.shape[1], step):
            answer = jnp.dot(hidden, down_ref[:, j:j + step], preferred_element_type=jnp.float32)
            answer = answer.astype(jnp.bfloat16).astype(jnp.float32) * scale
            for i in range(blocks):
                outs[i][:, at:at + step] = answer[i * rows:(i + 1) * rows].astype(outs[i].dtype)
            at += step


def expert(mine, blocks, kept, up, down):
    rows = blocks[0].shape[0]
    width, middle = up.shape
    total = rows * len(blocks)
    vmem = pl.BlockSpec(memory_space=pltpu.VMEM)
    return pl.pallas_call(
        functools.partial(expert_body, len(blocks), len(down)),
        out_shape=[
            jax.ShapeDtypeStruct((rows, width), jnp.float32 if k else jnp.bfloat16) for k in kept
        ],
        in_specs=[pl.BlockSpec(memory_space=pltpu.SMEM)] + [vmem] * (len(blocks) + 1 + len(down)),
        out_specs=[vmem] * len(blocks),
        scratch_shapes=[pltpu.VMEM((total, middle), jnp.bfloat16)],
        compiler_params=pltpu.CompilerParams(vmem_limit_bytes=16 * 2**20),
        cost_estimate=pl.CostEstimate(
            flops=4 * total * width * middle, bytes_accessed=4 * width * middle, transcendentals=total * middle
        ),
    )(mine, *blocks, up, *down)


def load_body(first, pieces, source, out, sems):
    height, columns = out.shape[0] // pieces, out.shape[1]
    copies = []
    for i in range(pieces):
        s = pl.ds(i * height, height)
        copies.append(pltpu.make_async_copy(source.at[s, pl.ds(first, columns)], out.at[s], sems.at[i]))
        copies[-1].start()
    for c in copies:
        c.wait()


def load(matrix, first, last, after):
    matrix, _ = lax.optimization_barrier((matrix, after))
    height = matrix.shape[0]
    pieces = 8 if height % (8 * 16) == 0 else 1
    return pl.pallas_call(
        functools.partial(load_body, first, pieces),
        out_shape=pltpu.VMEM((height, last - first), matrix.dtype),
        in_specs=[pl.BlockSpec(memory_space=pltpu.HBM)],
        out_specs=pl.BlockSpec(memory_space=pltpu.VMEM),
        scratch_shapes=[pltpu.SemaphoreType.DMA((pieces,))],
        compiler_params=pltpu.CompilerParams(vmem_limit_bytes=16 * 2**20),
    )(pltpu.with_memory_space_constraint(matrix, pltpu.HBM))


def label_body(tokens_ref, ids_ref, weights_ref, out_ref):
    rows, width = tokens_ref.shape
    columns = out_ref.shape[1] - width
    expert_of = lax.broadcasted_iota(jnp.int32, (columns, rows), 0)
    weights = weights_ref[...].astype(jnp.float32)
    table = jnp.zeros((columns, rows), jnp.float32)
    for k in range(ids_ref.shape[0]):
        table = jnp.where(ids_ref[k:k + 1, :] == expert_of, weights[k:k + 1, :], table)
    one = lax.broadcasted_iota(jnp.int32, (rows, rows), 0) == lax.broadcasted_iota(jnp.int32, (rows, rows), 1)
    turned = lax.dot_general(
        one.astype(jnp.bfloat16),
        table.astype(jnp.bfloat16),
        (((1,), (1,)), ((), ())),
        preferred_element_type=jnp.float32,
    )
    out_ref[:, :width] = tokens_ref[...]
    out_ref[:, width:] = turned.astype(jnp.bfloat16)


def label(tokens, expert_ids, route_weights, columns):
    rows, width = tokens.shape
    vmem = pl.BlockSpec(memory_space=pltpu.VMEM)
    return pl.pallas_call(
        label_body,
        out_shape=pltpu.VMEM((rows, width + columns), jnp.bfloat16),
        in_specs=[vmem] * 3,
        out_specs=vmem,
    )(tokens, expert_ids.T, route_weights.T)


def ring_plan(tokens, expert_ids, route_weights, w_up, w_down):
    rows, width = tokens.shape
    experts = lax.axis_size(BOTH)
    n = lax.axis_size("local")
    half = n // 2
    mine = lax.axis_index(BOTH).astype(jnp.int32)[None]
    order = list(range(0, n, 2)) + list(range(n - 1, 0, -2))
    onward = [(order[i], order[(i + 1) % n]) for i in range(n)]
    pairs = onward + [(n + b, n + a) for a, b in onward]
    def hop(x):
        return lax.ppermute(x, BOTH, pairs)

    def swap(x):
        return lax.ppermute(x, "node", [(0, 1), (1, 0)])

    def bf(x):
        return x.astype(jnp.bfloat16)

    columns = -(-experts // LANES) * LANES
    own = label(tokens, expert_ids, route_weights, columns)

    a, b = [own], [swap(own)]
    ahead_a, ahead_b = [None], [None]
    behind, ahead = {}, {}

    def compute(h, first=None):
        blocks = (a[h], b[h], ahead_a[h], ahead_b[h])
        if first is not None:
            blocks, _ = lax.optimization_barrier((blocks, first))
        r = expert(mine, blocks, (False, False, True, True), up, down)
        behind[h], ahead[h] = r[:2], r[2:]

    step = step_of(width, 512)
    cut = (width // step * LATE[0] // LATE[1]) * step
    up, mine = lax.optimization_barrier((load(w_up[0], 0, w_up.shape[2], b[0]), mine))
    for h in range(1, half + 1):
        a.append(hop(a[-1]))
        if h < half:
            b.append(hop(b[-1]))
        if h == 1:
            a[1], up = lax.optimization_barrier((a[1], up))
            up = pltpu.with_memory_space_constraint(up, pltpu.VMEM)
        elif h == 2:
            down = load(w_down[0], 0, cut, a[1])
            a[2], down_first = lax.optimization_barrier((a[2], down))
        elif h == 3:
            down = load(w_down[0], cut, width, a[2])
            a[3], down_last = lax.optimization_barrier((a[3], down))
        if 1 < h < half:
            a[h], ahead_a[h - 1], ahead_b[h - 1] = lax.optimization_barrier((a[h], ahead_a[h - 1], ahead_b[h - 1]))
        if h < half:
            ahead_b.append(swap(a[h]))
            ahead_a.append(swap(b[h]))
    down = [pltpu.with_memory_space_constraint(d, pltpu.VMEM) for d in (down_first, down_last)]
    near = range(1, half - 2)
    blocks = [a[0], b[0]]
    for h in near:
        blocks += [a[h], b[h], ahead_a[h], ahead_b[h]]
    blocks, _ = lax.optimization_barrier((blocks, a[half - 1]))
    r = expert(mine, blocks, (True, True) + (False, False, True, True) * len(near), up, down)
    r, a[half] = lax.optimization_barrier((r, a[half]))
    own_a, own_b = r[:2]
    for i, h in enumerate(near):
        behind[h], ahead[h] = r[4 * i + 2:4 * i + 4], r[4 * i + 4:4 * i + 6]
    ahead_b.append(swap(a[half]))
    h = half - 1
    r = expert(
        mine,
        (a[h], b[h], ahead_a[h], ahead_b[h], a[half], ahead_b[half]),
        (False, False, True, True, True, False),
        up,
        down,
    )
    behind[h], ahead[h], far = r[:2], r[2:4], r[4:]

    def join(x, y):
        return x.astype(jnp.float32) + y.astype(jnp.float32)

    def total(h, after=None):
        mine_a, mine_b = behind[h]
        if after is not None:
            mine_a, mine_b, _ = lax.optimization_barrier((mine_a, mine_b, after))
        sum_b = join(ahead[h][1], swap(mine_a))
        return [join(ahead[h][0], swap(mine_b)), sum_b]

    send_a = bf(join(far[0], swap(far[1])))
    sums = {half - 1: total(half - 1)}
    send_b = bf(sums[half - 1][1])
    run_a = hop(send_a)
    run_b = hop(send_b)
    compute(half - 2, (send_a, send_b))
    sums[half - 2] = total(half - 2)
    for h in range(half - 1, 0, -1):
        if h < half - 1:
            run_b = hop(bf(join(sums[h][1], run_b)))
        if h - 1 > 0 and h - 1 not in sums:
            sums[h - 1] = total(h - 1, run_a)
        send_a = bf(join(sums[h][0], run_a))
        run_a = hop(send_a)
    last = swap(bf(join(own_b, run_b)))
    return bf(join(join(own_a, run_a), last))


def solution(mesh):
    placed = (
        P(("rep", "node", "local"), None),
        P(("rep", "node", "local"), None),
        P(("rep", "node", "local"), None),
        P(("node", "local"), None, None),
        P(("node", "local"), None, None),
    )
    n = mesh.shape["local"]
    ringed = mesh.shape["node"] == 2 and n % 2 == 0 and 6 <= n <= 16
    return jax.shard_map(
        ring_plan if ringed else gather_plan,
        mesh=mesh,
        in_specs=placed,
        out_specs=P(("rep", "node", "local"), None),
        check_vma=False,
    )
```

time: 64 us -> 60.1 us (0.939)
  waiting for transfers between devices: 19.8 us -> 14.4 us
  starting transfers between devices: 24.1 us -> 27.1 us
  Pallas kernels: 18.5 us -> 17 us
    ppermute x14, waiting for transfers between devices: 17 us -> 12.4 us  [hop(): return lax.ppermute(x, BOTH, pairs)]
    ppermute x14, starting transfers between devices: 21.2 us -> 23.5 us  [hop(): return lax.ppermute(x, BOTH, pairs)]
    pallas_call x6, Pallas kernels: 17.3 us -> 15.9 us  [the longest x3 8.57 us: expert(): pl.pallas_call(functools.partial(expert_body, len(blocks), len(down)), ou...]
    ppermute x16, waiting for transfers between devices: 2.79 us -> 1.98 us  [swap(): return lax.ppermute(x, 'node', [(0, 1), (1, 0)])]
    convert_element_type x8 -> x9, other arithmetic: 1.19 us -> 1.35 us  [bf(): return x.astype(jnp.bfloat16)]
  transfers between devices with their start and end apart: 30 -> 30, of which waited for: 13 -> 13; matrix products, arithmetic and copies ran while one was open for 1% -> 1% of each run, Pallas kernels for 23% -> 21%
where the time goes in v6:
time: 60.1 us; the launch traced here: 60 us
  starting transfers between devices  27.1 us (45%)
  Pallas kernels  17 us (28%)
  waiting for transfers between devices  14.4 us (24%)
  other arithmetic  1.35 us (2%)
    ppermute x14, starting transfers between devices, hop(): return lax.ppermute(x, BOTH, pairs)  23.5 us
    ppermute x14, waiting for transfers between devices, hop(): return lax.ppermute(x, BOTH, pairs)  12.4 us
    pallas_call x3, Pallas kernels, expert(): pl.pallas_call(functools.partial(expert_body, len(blocks), len(down)), ou...  8.57 us
    pallas_call x3, Pallas kernels, load(): pl.pallas_call(functools.partial(load_body, first, pieces), out_shape=plt...  7.28 us
    ppermute x16, starting transfers between devices, swap(): return lax.ppermute(x, 'node', [(0, 1), (1, 0)])  3.56 us
    ppermute x16, waiting for transfers between devices, swap(): return lax.ppermute(x, 'node', [(0, 1), (1, 0)])  1.98 us
    convert_element_type x9, other arithmetic, bf(): return x.astype(jnp.bfloat16)  1.35 us
  transfers between devices with their start and end apart: 30, of which 13 were waited for; matrix products, arithmetic and copies ran while one was open for 1% of the time, Pallas kernels for 21%

profile of v6, /device:TPU:0, one launch (start us, length us, event | category | flops | bytes accessed | tf_op | source)
XLA Modules:
  0.0 60.0 jit_solution(2435544990073457169)
XLA Ops:
  0.0 1.1 %shard_map.55.refs_0_ = bf16[32,3712]{1,0:T(8,128)(2,1)S(1)} custom-call(bf16[32,3584]{1,0:T(8,128)(2,1)} %tokens_ref.1, s32[8,32]{1,0:T(8,128)} %bitcast.8, bf16[8,32]{1,0:T(8,128)(2,1)} %bitcast.9), custom_call_target="tpu_custom_call" | custom-call | tf_op jit(solution)/shard_map/pallas_call | solution.py:127
  1.1 0.5 collective-permute-start
  1.6 2.6 %collective-permute-start.1 = (bf16[32,3712]{1,0:T(8,128)(2,1)S(1)}, bf16[32,3712]{1,0:T(8,128)(2,1)S(1)}, u32[]{:S(2)}, u32[]{:S(2)}) collective-permute-start(bf16[32,3712]{1,0:T(8,128)(2,1)S(1)} %shard_map.55.refs_0_), channel_id=1, source_target_pairs={{0,2},{2,4},{4,6},{6,7},{7,5},{5,3},{3,1},{1,0},{10,8},{12,10},{14... | collective-permute-start | bytes 712712 | tf_op jit(solution)/shard_map/ppermute | solution.py:145
  4.2 0.0 collective-permute-done.refs_1_
  4.2 1.6 %collective-permute-start.2 = (bf16[32,3712]{1,0:T(8,128)(2,1)S(1)}, bf16[32,3712]{1,0:T(8,128)(2,1)S(1)}, u32[]{:S(2)}, u32[]{:S(2)}) collective-permute-start(bf16[32,3712]{1,0:T(8,128)(2,1)S(1)} %collective-permute-done.refs_1_), channel_id=1, source_target_pairs={{0,2},{2,4},{4,6},{6,7},{7,5},{5,3},{3,1},{1,0},{10,8},{12,10},{14... | collective-permute-start | bytes 712712 | tf_op jit(solution)/shard_map/ppermute | solution.py:145
  5.8 3.2 %shard_map.56.refs_6_.refs_4_ = bf16[3584,1024]{1,0:T(8,128)(2,1)S(1)} custom-call(bf16[3584,1024]{1,0:T(8,128)(2,1)} %bitcast.7), custom_call_target="tpu_custom_call" | custom-call | tf_op jit(solution)/shard_map/pallas_call | solution.py:95
  8.9 0.0 collective-permute-done.1.refs_2_
  8.9 1.6 %collective-permute-start.3 = (bf16[32,3712]{1,0:T(8,128)(2,1)S(1)}, bf16[32,3712]{1,0:T(8,128)(2,1)S(1)}, u32[]{:S(2)}, u32[]{:S(2)}) collective-permute-start(bf16[32,3712]{1,0:T(8,128)(2,1)S(1)} %collective-permute-done.1.refs_2_), channel_id=1, source_target_pairs={{0,2},{2,4},{4,6},{6,7},{7,5},{5,3},{3,1},{1,0},{10,8},{12,10},{14... | collective-permute-start | bytes 712712 | tf_op jit(solution)/shard_map/ppermute | solution.py:145
  10.6 0.0 collective-permute-start.5
  10.6 0.2 collective-permute-done.2.refs_3_
  10.8 0.3 collective-permute-start.4
  11.1 1.7 %collective-permute-start.7 = (bf16[32,3712]{1,0:T(8,128)(2,1)S(1)}, bf16[32,3712]{1,0:T(8,128)(2,1)S(1)}, u32[]{:S(2)}, u32[]{:S(2)}) collective-permute-start(bf16[32,3712]{1,0:T(8,128)(2,1)S(1)} %collective-permute-done.2.refs_3_), channel_id=1, source_target_pairs={{0,2},{2,4},{4,6},{6,7},{7,5},{5,3},{3,1},{1,0},{10,8},{12,10},{14... | collective-permute-start | bytes 712712 | tf_op jit(solution)/shard_map/ppermute | solution.py:145
  12.8 2.5 %shard_map.57.refs_7_.refs_5_ = bf16[1024,2560]{1,0:T(8,128)(2,1)S(1)} custom-call(bf16[1024,3584]{1,0:T(8,128)(2,1)} %bitcast.5), custom_call_target="tpu_custom_call" | custom-call | tf_op jit(solution)/shard_map/pallas_call | solution.py:95
  15.4 0.0 collective-permute-done.3.refs_0_
  15.4 0.0 collective-permute-done.4.refs_4_
  15.4 1.6 %collective-permute-start.6 = (bf16[32,3712]{1,0:T(8,128)(2,1)S(1)}, bf16[32,3712]{1,0:T(8,128)(2,1)S(1)}, u32[]{:S(2)}, u32[]{:S(2)}) collective-permute-start(bf16[32,3712]{1,0:T(8,128)(2,1)S(1)} %collective-permute-done.3.refs_0_), channel_id=1, source_target_pairs={{0,2},{2,4},{4,6},{6,7},{7,5},{5,3},{3,1},{1,0},{10,8},{12,10},{14... | collective-permute-start | bytes 712712 | tf_op jit(solution)/shard_map/ppermute | solution.py:145
  17.0 0.6 %collective-permute-done.7.refs_1_ = bf16[32,3712]{1,0:T(8,128)(2,1)S(1)} collective-permute-done((bf16[32,3712]{1,0:T(8,128)(2,1)S(1)}, bf16[32,3712]{1,0:T(8,128)(2,1)S(1)}, u32[]{:S(2)}, u32[]{:S(2)}) %collective-permute-start.7) | collective-permute-done | bytes 237600 | tf_op jit(solution)/shard_map/ppermute | solution.py:145
  17.7 0.5 collective-permute-start.9
  18.2 1.6 %collective-permute-start.11 = (bf16[32,3712]{1,0:T(8,128)(2,1)S(1)}, bf16[32,3712]{1,0:T(8,128)(2,1)S(1)}, u32[]{:S(2)}, u32[]{:S(2)}) collective-permute-start(bf16[32,3712]{1,0:T(8,128)(2,1)S(1)} %collective-permute-done.7.refs_1_), channel_id=1, source_target_pairs={{0,2},{2,4},{4,6},{6,7},{7,5},{5,3},{3,1},{1,0},{10,8},{12,10},{14... | collective-permute-start | bytes 712712 | tf_op jit(solution)/shard_map/ppermute | solution.py:145
  19.7 1.6 %shard_map.58.refs_8_.refs_6_ = bf16[1024,1024]{1,0:T(8,128)(2,1)S(1)} custom-call(bf16[1024,3584]{1,0:T(8,128)(2,1)} %bitcast.6), custom_call_target="tpu_custom_call" | custom-call | tf_op jit(solution)/shard_map/pallas_call | solution.py:95
  21.3 0.3 collective-permute-done.6.refs_0_
  21.6 0.0 collective-permute-done.8.refs_2_
  21.6 0.0 collective-permute-done.9.refs_3_
  21.6 0.0 collective-permute-start.13
  21.6 1.6 %collective-permute-start.10 = (bf16[32,3712]{1,0:T(8,128)(2,1)S(1)}, bf16[32,3712]{1,0:T(8,128)(2,1)S(1)}, u32[]{:S(2)}, u32[]{:S(2)}) collective-permute-start(bf16[32,3712]{1,0:T(8,128)(2,1)S(1)} %collective-permute-done.6.refs_0_), channel_id=1, source_target_pairs={{0,2},{2,4},{4,6},{6,7},{7,5},{5,3},{3,1},{1,0},{10,8},{12,10},{14... | collective-permute-start | bytes 712712 | tf_op jit(solution)/shard_map/ppermute | solution.py:145
  23.2 1.1 %collective-permute-done.11.refs_1_ = bf16[32,3712]{1,0:T(8,128)(2,1)S(1)} collective-permute-done((bf16[32,3712]{1,0:T(8,128)(2,1)S(1)}, bf16[32,3712]{1,0:T(8,128)(2,1)S(1)}, u32[]{:S(2)}, u32[]{:S(2)}) %collective-permute-start.11) | collective-permute-done | bytes 237600 | tf_op jit(solution)/shard_map/ppermute | solution.py:145
  24.3 0.0 collective-permute-start.12
  24.3 3.2 %shard_map.59 = (f32[32,3584]{1,0:T(8,128)S(1)}, f32[32,3584]{1,0:T(8,128)S(1)}, bf16[32,3584]{1,0:T(8,128)(2,1)S(1)}, bf16[32,3584]{1,0:T(8,128)(2,1)S(1)}, f32...) custom-call(s32[1]{0:T(128)} %bitcast.3.mine_ref, bf16[32,3712]{1,0:T(8,128)(2,1)S(1)} %shard_map.55.refs_0_, ...), custom_call_target="tpu_custom_call" | custom-call | flops 2818572288 | bytes 14680064 | tf_op jit(solution)/shard_map/pallas_call | solution.py:65
  27.4 0.3 collective-permute-done.10.refs_4_
  27.8 0.3 collective-permute-start.14
  28.0 0.0 collective-permute-done.12.refs_2_
  28.0 0.0 collective-permute-done.13.refs_3_
  28.0 1.2 %collective-permute-done.14.refs_5_ = bf16[32,3712]{1,0:T(8,128)(2,1)S(1)} collective-permute-done((bf16[32,3712]{1,0:T(8,128)(2,1)S(1)}, bf16[32,3712]{1,0:T(8,128)(2,1)S(1)}, u32[]{:S(2)}, u32[]{:S(2)}) %collective-permute-start.14) | collective-permute-done | bytes 237600 | tf_op jit(solution)/shard_map/ppermute | solution.py:148
  29.3 3.1 %shard_map.60 = (bf16[32,3584]{1,0:T(8,128)(2,1)S(1)}, bf16[32,3584]{1,0:T(8,128)(2,1)S(1)}, f32[32,3584]{1,0:T(8,128)S(1)}, f32[32,3584]{1,0:T(8,128)S(1)}, f32...) custom-call(s32[1]{0:T(128)} %bitcast.3.mine_ref, bf16[32,3712]{1,0:T(8,128)(2,1)S(1)} %collective-permute-done.6.refs_0_, ...), custom_call_target="tpu_custom_call" | custom-call | flops 2818572288 | bytes 14680064 | tf_op jit(solution)/shard_map/pallas_call | solution.py:65
  32.4 0.3 collective-permute-start.16
  32.7 0.2 collective-permute-start.15
  33.0 0.3 collective-permute-start.20
  33.2 0.7 %collective-permute-done.16 = bf16[32,3584]{1,0:T(8,128)(2,1)S(1)} collective-permute-done((bf16[32,3584]{1,0:T(8,128)(2,1)S(1)}, bf16[32,3584]{1,0:T(8,128)(2,1)S(1)}, u32[]{:S(2)}, u32[]{:S(2)}) %collective-permute-start.16) | collective-permute-done | bytes 229408 | tf_op jit(solution)/shard_map/ppermute | solution.py:148
  34.0 1.6 %collective-permute-start.17 = (bf16[32,3584]{1,0:T(8,128)(2,1)S(1)}, bf16[32,3584]{1,0:T(8,128)(2,1)S(1)}, u32[]{:S(2)}, u32[]{:S(2)}) collective-permute-start(bf16[32,3584]{1,0:T(8,128)(2,1)S(1)} %add_convert_fusion.8), channel_id=1, source_target_pairs={{0,2},{2,4},{4,6},{6,7},{7,5},{5,3},{3,1},{1,0},{10,8},{12,10},{14... | collective-permute-start | bytes 688136 | tf_op jit(solution)/shard_map/ppermute | solution.py:145
  35.6 0.1 add_convert_fusion.6
  35.7 1.6 %collective-permute-start.26 = (bf16[32,3584]{1,0:T(8,128)(2,1)S(1)}, bf16[32,3584]{1,0:T(8,128)(2,1)S(1)}, u32[]{:S(2)}, u32[]{:S(2)}) collective-permute-start(bf16[32,3584]{1,0:T(8,128)(2,1)S(1)} %add_convert_fusion.6), channel_id=1, source_target_pairs={{0,2},{2,4},{4,6},{6,7},{7,5},{5,3},{3,1},{1,0},{10,8},{12,10},{14... | collective-permute-start | bytes 688136 | tf_op jit(solution)/shard_map/ppermute | solution.py:145
  37.3 2.3 %shard_map.61 = (bf16[32,3584]{1,0:T(8,128)(2,1)S(1)}, bf16[32,3584]{1,0:T(8,128)(2,1)S(1)}, f32[32,3584]{1,0:T(8,128)S(1)}, f32[32,3584]{1,0:T(8,128)S(1)}) custom-call(s32[1]{0:T(128)} %bitcast.3.mine_ref, bf16[32,3712]{1,0:T(8,128)(2,1)S(1)} %collective-permute-done.3.refs_0_, bf16[32,3712]{1,0:T(8,128)(2,1)S(1)} %collective-permute-done.7.refs_1_, ...), custom_call_target="tpu_custom_call" | custom-call | flops 1879048192 | bytes 14680064 | tf_op jit(solution)/shard_map/pallas_call | solution.py:65
  39.6 0.1 collective-permute-start.21
  39.7 0.5 collective-permute-start.25
  40.2 0.1 add_convert_fusion.7
  40.3 1.6 %collective-permute-start.18 = (bf16[32,3584]{1,0:T(8,128)(2,1)S(1)}, bf16[32,3584]{1,0:T(8,128)(2,1)S(1)}, u32[]{:S(2)}, u32[]{:S(2)}) collective-permute-start(bf16[32,3584]{1,0:T(8,128)(2,1)S(1)} %add_convert_fusion.7), channel_id=1, source_target_pairs={{0,2},{2,4},{4,6},{6,7},{7,5},{5,3},{3,1},{1,0},{10,8},{12,10},{14... | collective-permute-start | bytes 688136 | tf_op jit(solution)/shard_map/ppermute | solution.py:145
  41.9 0.7 %collective-permute-done.26 = bf16[32,3584]{1,0:T(8,128)(2,1)S(1)} collective-permute-done((bf16[32,3584]{1,0:T(8,128)(2,1)S(1)}, bf16[32,3584]{1,0:T(8,128)(2,1)S(1)}, u32[]{:S(2)}, u32[]{:S(2)}) %collective-permute-start.26) | collective-permute-done | bytes 229408 | tf_op jit(solution)/shard_map/ppermute | solution.py:145
  42.5 0.1 add_convert_fusion.3
  42.6 1.6 %collective-permute-start.27 = (bf16[32,3584]{1,0:T(8,128)(2,1)S(1)}, bf16[32,3584]{1,0:T(8,128)(2,1)S(1)}, u32[]{:S(2)}, u32[]{:S(2)}) collective-permute-start(bf16[32,3584]{1,0:T(8,128)(2,1)S(1)} %add_convert_fusion.3), channel_id=1, source_target_pairs={{0,2},{2,4},{4,6},{6,7},{7,5},{5,3},{3,1},{1,0},{10,8},{12,10},{14... | collective-permute-start | bytes 688136 | tf_op jit(solution)/shard_map/ppermute | solution.py:145
  44.2 2.1 %collective-permute-done.18 = bf16[32,3584]{1,0:T(8,128)(2,1)S(1)} collective-permute-done((bf16[32,3584]{1,0:T(8,128)(2,1)S(1)}, bf16[32,3584]{1,0:T(8,128)(2,1)S(1)}, u32[]{:S(2)}, u32[]{:S(2)}) %collective-permute-start.18) | collective-permute-done | bytes 229408 | tf_op jit(solution)/shard_map/ppermute | solution.py:145
  46.4 0.5 collective-permute-start.24
  46.9 0.1 add_convert_fusion.5
  47.0 1.6 %collective-permute-start.22 = (bf16[32,3584]{1,0:T(8,128)(2,1)S(1)}, bf16[32,3584]{1,0:T(8,128)(2,1)S(1)}, u32[]{:S(2)}, u32[]{:S(2)}) collective-permute-start(bf16[32,3584]{1,0:T(8,128)(2,1)S(1)} %add_convert_fusion.5), channel_id=1, source_target_pairs={{0,2},{2,4},{4,6},{6,7},{7,5},{5,3},{3,1},{1,0},{10,8},{12,10},{14... | collective-permute-start | bytes 688136 | tf_op jit(solution)/shard_map/ppermute | solution.py:145
  48.5 0.3 collective-permute-done.27
  48.8 0.1 add_convert_fusion.2
  48.9 1.6 %collective-permute-start.28 = (bf16[32,3584]{1,0:T(8,128)(2,1)S(1)}, bf16[32,3584]{1,0:T(8,128)(2,1)S(1)}, u32[]{:S(2)}, u32[]{:S(2)}) collective-permute-start(bf16[32,3584]{1,0:T(8,128)(2,1)S(1)} %add_convert_fusion.2), channel_id=1, source_target_pairs={{0,2},{2,4},{4,6},{6,7},{7,5},{5,3},{3,1},{1,0},{10,8},{12,10},{14... | collective-permute-start | bytes 688136 | tf_op jit(solution)/shard_map/ppermute | solution.py:145
  50.5 2.6 %collective-permute-done.22 = bf16[32,3584]{1,0:T(8,128)(2,1)S(1)} collective-permute-done((bf16[32,3584]{1,0:T(8,128)(2,1)S(1)}, bf16[32,3584]{1,0:T(8,128)(2,1)S(1)}, u32[]{:S(2)}, u32[]{:S(2)}) %collective-permute-start.22) | collective-permute-done | bytes 229408 | tf_op jit(solution)/shard_map/ppermute | solution.py:145
  53.0 0.1 add_convert_fusion.4
  53.1 1.6 %collective-permute-start.23 = (bf16[32,3584]{1,0:T(8,128)(2,1)S(1)}, bf16[32,3584]{1,0:T(8,128)(2,1)S(1)}, u32[]{:S(2)}, u32[]{:S(2)}) collective-permute-start(bf16[32,3584]{1,0:T(8,128)(2,1)S(1)} %add_convert_fusion.4), channel_id=1, source_target_pairs={{0,2},{2,4},{4,6},{6,7},{7,5},{5,3},{3,1},{1,0},{10,8},{12,10},{14... | collective-permute-start | bytes 688136 | tf_op jit(solution)/shard_map/ppermute | solution.py:145
  54.7 0.8 %collective-permute-done.28 = bf16[32,3584]{1,0:T(8,128)(2,1)S(1)} collective-permute-done((bf16[32,3584]{1,0:T(8,128)(2,1)S(1)}, bf16[32,3584]{1,0:T(8,128)(2,1)S(1)}, u32[]{:S(2)}, u32[]{:S(2)}) %collective-permute-start.28) | collective-permute-done | bytes 229408 | tf_op jit(solution)/shard_map/ppermute | solution.py:145
  55.5 0.1 add_convert_fusion.1
  55.5 0.1 collective-permute-start.29
  55.6 3.6 %collective-permute-done.23 = bf16[32,3584]{1,0:T(8,128)(2,1)S(1)} collective-permute-done((bf16[32,3584]{1,0:T(8,128)(2,1)S(1)}, bf16[32,3584]{1,0:T(8,128)(2,1)S(1)}, u32[]{:S(2)}, u32[]{:S(2)}) %collective-permute-start.23) | collective-permute-done | bytes 229408 | tf_op jit(solution)/shard_map/ppermute | solution.py:145
  59.2 0.8 %add_convert_fusion = bf16[32,3584]{1,0:T(8,128)(2,1)} fusion(bf16[32,3584]{1,0:T(8,128)(2,1)S(1)} %collective-permute-done.29, f32[32,3584]{1,0:T(8,128)S(1)} %get-tuple-element.84, bf16[32,3584]{1,0:T(8,128)(2,1)S(1)} %collective-permute-done.23), kind=kLoop, calls=%fused_computation | loop fusion | flops 573440 | bytes 1146880 | tf_op jit(solution)/shard_map/convert_element_type | solution.py:151
  (12 shorter events, 0.1 us)
Async XLA Ops:
  1.1 3.1 %collective-permute-start = (bf16[32,3712]{1,0:T(8,128)(2,1)S(1)}, bf16[32,3712]{1,0:T(8,128)(2,1)S(1)}, u32[]{:S(2)}, u32[]{:S(2)}) collective-permute-start(bf16[32,3712]{1,0:T(8,128)(2,1)S(1)} %shard_map.55.refs_0_), channel_id=1, source_target_pairs={{0,8},{8,0},{1,9},{9,1},{2,10},{10,2},{3,11},{11,3},{4,12},{12,4},... | collective-permute-start | bytes 712712 | tf_op jit(solution)/shard_map/ppermute | solution.py:148
  1.6 7.4 %collective-permute-start.1 = (bf16[32,3712]{1,0:T(8,128)(2,1)S(1)}, bf16[32,3712]{1,0:T(8,128)(2,1)S(1)}, u32[]{:S(2)}, u32[]{:S(2)}) collective-permute-start(bf16[32,3712]{1,0:T(8,128)(2,1)S(1)} %shard_map.55.refs_0_), channel_id=1, source_target_pairs={{0,2},{2,4},{4,6},{6,7},{7,5},{5,3},{3,1},{1,0},{10,8},{12,10},{14... | collective-permute-start | bytes 712712 | tf_op jit(solution)/shard_map/ppermute | solution.py:145
  4.2 6.6 %collective-permute-start.2 = (bf16[32,3712]{1,0:T(8,128)(2,1)S(1)}, bf16[32,3712]{1,0:T(8,128)(2,1)S(1)}, u32[]{:S(2)}, u32[]{:S(2)}) collective-permute-start(bf16[32,3712]{1,0:T(8,128)(2,1)S(1)} %collective-permute-done.refs_1_), channel_id=1, source_target_pairs={{0,2},{2,4},{4,6},{6,7},{7,5},{5,3},{3,1},{1,0},{10,8},{12,10},{14... | collective-permute-start | bytes 712712 | tf_op jit(solution)/shard_map/ppermute | solution.py:145
  8.9 6.4 %collective-permute-start.3 = (bf16[32,3712]{1,0:T(8,128)(2,1)S(1)}, bf16[32,3712]{1,0:T(8,128)(2,1)S(1)}, u32[]{:S(2)}, u32[]{:S(2)}) collective-permute-start(bf16[32,3712]{1,0:T(8,128)(2,1)S(1)} %collective-permute-done.1.refs_2_), channel_id=1, source_target_pairs={{0,2},{2,4},{4,6},{6,7},{7,5},{5,3},{3,1},{1,0},{10,8},{12,10},{14... | collective-permute-start | bytes 712712 | tf_op jit(solution)/shard_map/ppermute | solution.py:145
  10.6 4.8 %collective-permute-start.5 = (bf16[32,3712]{1,0:T(8,128)(2,1)S(1)}, bf16[32,3712]{1,0:T(8,128)(2,1)S(1)}, u32[]{:S(2)}, u32[]{:S(2)}) collective-permute-start(bf16[32,3712]{1,0:T(8,128)(2,1)S(1)} %collective-permute-done.1.refs_2_), channel_id=1, source_target_pairs={{0,8},{8,0},{1,9},{9,1},{2,10},{10,2},{3,11},{11,3},{4,12},{12,4},... | collective-permute-start | bytes 712712 | tf_op jit(solution)/shard_map/ppermute | solution.py:148
  10.8 4.6 %collective-permute-start.4 = (bf16[32,3712]{1,0:T(8,128)(2,1)S(1)}, bf16[32,3712]{1,0:T(8,128)(2,1)S(1)}, u32[]{:S(2)}, u32[]{:S(2)}) collective-permute-start(bf16[32,3712]{1,0:T(8,128)(2,1)S(1)} %collective-permute-done.2.refs_3_), channel_id=1, source_target_pairs={{0,8},{8,0},{1,9},{9,1},{2,10},{10,2},{3,11},{11,3},{4,12},{12,4},... | collective-permute-start | bytes 712712 | tf_op jit(solution)/shard_map/ppermute | solution.py:148
  11.1 6.6 %collective-permute-start.7 = (bf16[32,3712]{1,0:T(8,128)(2,1)S(1)}, bf16[32,3712]{1,0:T(8,128)(2,1)S(1)}, u32[]{:S(2)}, u32[]{:S(2)}) collective-permute-start(bf16[32,3712]{1,0:T(8,128)(2,1)S(1)} %collective-permute-done.2.refs_3_), channel_id=1, source_target_pairs={{0,2},{2,4},{4,6},{6,7},{7,5},{5,3},{3,1},{1,0},{10,8},{12,10},{14... | collective-permute-start | bytes 712712 | tf_op jit(solution)/shard_map/ppermute | solution.py:145
  15.4 6.2 %collective-permute-start.6 = (bf16[32,3712]{1,0:T(8,128)(2,1)S(1)}, bf16[32,3712]{1,0:T(8,128)(2,1)S(1)}, u32[]{:S(2)}, u32[]{:S(2)}) collective-permute-start(bf16[32,3712]{1,0:T(8,128)(2,1)S(1)} %collective-permute-done.3.refs_0_), channel_id=1, source_target_pairs={{0,2},{2,4},{4,6},{6,7},{7,5},{5,3},{3,1},{1,0},{10,8},{12,10},{14... | collective-permute-start | bytes 712712 | tf_op jit(solution)/shard_map/ppermute | solution.py:145
  17.7 3.9 %collective-permute-start.8 = (bf16[32,3712]{1,0:T(8,128)(2,1)S(1)}, bf16[32,3712]{1,0:T(8,128)(2,1)S(1)}, u32[]{:S(2)}, u32[]{:S(2)}) collective-permute-start(bf16[32,3712]{1,0:T(8,128)(2,1)S(1)} %collective-permute-done.7.refs_1_), channel_id=1, source_target_pairs={{0,8},{8,0},{1,9},{9,1},{2,10},{10,2},{3,11},{11,3},{4,12},{12,4},... | collective-permute-start | bytes 712712 | tf_op jit(solution)/shard_map/ppermute | solution.py:148
  17.7 3.9 %collective-permute-start.9 = (bf16[32,3712]{1,0:T(8,128)(2,1)S(1)}, bf16[32,3712]{1,0:T(8,128)(2,1)S(1)}, u32[]{:S(2)}, u32[]{:S(2)}) collective-permute-start(bf16[32,3712]{1,0:T(8,128)(2,1)S(1)} %collective-permute-done.3.refs_0_), channel_id=1, source_target_pairs={{0,8},{8,0},{1,9},{9,1},{2,10},{10,2},{3,11},{11,3},{4,12},{12,4},... | collective-permute-start | bytes 712712 | tf_op jit(solution)/shard_map/ppermute | solution.py:148
  18.2 6.1 %collective-permute-start.11 = (bf16[32,3712]{1,0:T(8,128)(2,1)S(1)}, bf16[32,3712]{1,0:T(8,128)(2,1)S(1)}, u32[]{:S(2)}, u32[]{:S(2)}) collective-permute-start(bf16[32,3712]{1,0:T(8,128)(2,1)S(1)} %collective-permute-done.7.refs_1_), channel_id=1, source_target_pairs={{0,2},{2,4},{4,6},{6,7},{7,5},{5,3},{3,1},{1,0},{10,8},{12,10},{14... | collective-permute-start | bytes 712712 | tf_op jit(solution)/shard_map/ppermute | solution.py:145
  21.6 6.4 %collective-permute-start.13 = (bf16[32,3712]{1,0:T(8,128)(2,1)S(1)}, bf16[32,3712]{1,0:T(8,128)(2,1)S(1)}, u32[]{:S(2)}, u32[]{:S(2)}) collective-permute-start(bf16[32,3712]{1,0:T(8,128)(2,1)S(1)} %collective-permute-done.6.refs_0_), channel_id=1, source_target_pairs={{0,8},{8,0},{1,9},{9,1},{2,10},{10,2},{3,11},{11,3},{4,12},{12,4},... | collective-permute-start | bytes 712712 | tf_op jit(solution)/shard_map/ppermute | solution.py:148
  21.6 6.2 %collective-permute-start.10 = (bf16[32,3712]{1,0:T(8,128)(2,1)S(1)}, bf16[32,3712]{1,0:T(8,128)(2,1)S(1)}, u32[]{:S(2)}, u32[]{:S(2)}) collective-permute-start(bf16[32,3712]{1,0:T(8,128)(2,1)S(1)} %collective-permute-done.6.refs_0_), channel_id=1, source_target_pairs={{0,2},{2,4},{4,6},{6,7},{7,5},{5,3},{3,1},{1,0},{10,8},{12,10},{14... | collective-permute-start | bytes 712712 | tf_op jit(solution)/shard_map/ppermute | solution.py:145
  24.3 3.8 %collective-permute-start.12 = (bf16[32,3712]{1,0:T(8,128)(2,1)S(1)}, bf16[32,3712]{1,0:T(8,128)(2,1)S(1)}, u32[]{:S(2)}, u32[]{:S(2)}) collective-permute-start(bf16[32,3712]{1,0:T(8,128)(2,1)S(1)} %collective-permute-done.11.refs_1_), channel_id=1, source_target_pairs={{0,8},{8,0},{1,9},{9,1},{2,10},{10,2},{3,11},{11,3},{4,12},{12,4},... | collective-permute-start | bytes 712712 | tf_op jit(solution)/shard_map/ppermute | solution.py:148
  27.8 1.5 %collective-permute-start.14 = (bf16[32,3712]{1,0:T(8,128)(2,1)S(1)}, bf16[32,3712]{1,0:T(8,128)(2,1)S(1)}, u32[]{:S(2)}, u32[]{:S(2)}) collective-permute-start(bf16[32,3712]{1,0:T(8,128)(2,1)S(1)} %collective-permute-done.10.refs_4_), channel_id=1, source_target_pairs={{0,8},{8,0},{1,9},{9,1},{2,10},{10,2},{3,11},{11,3},{4,12},{12,4},... | collective-permute-start | bytes 712712 | tf_op jit(solution)/shard_map/ppermute | solution.py:148
  32.4 1.6 %collective-permute-start.16 = (bf16[32,3584]{1,0:T(8,128)(2,1)S(1)}, bf16[32,3584]{1,0:T(8,128)(2,1)S(1)}, u32[]{:S(2)}, u32[]{:S(2)}) collective-permute-start(bf16[32,3584]{1,0:T(8,128)(2,1)S(1)} %get-tuple-element.92), channel_id=1, source_target_pairs={{0,8},{8,0},{1,9},{9,1},{2,10},{10,2},{3,11},{11,3},{4,12},{12,4},... | collective-permute-start | bytes 688136 | tf_op jit(solution)/shard_map/ppermute | solution.py:148
  32.7 7.5 %collective-permute-start.15 = (bf16[32,3584]{1,0:T(8,128)(2,1)S(1)}, bf16[32,3584]{1,0:T(8,128)(2,1)S(1)}, u32[]{:S(2)}, u32[]{:S(2)}) collective-permute-start(bf16[32,3584]{1,0:T(8,128)(2,1)S(1)} %get-tuple-element.90), channel_id=1, source_target_pairs={{0,8},{8,0},{1,9},{9,1},{2,10},{10,2},{3,11},{11,3},{4,12},{12,4},... | collective-permute-start | bytes 688136 | tf_op jit(solution)/shard_map/ppermute | solution.py:148
  33.0 2.7 %collective-permute-start.20 = (bf16[32,3584]{1,0:T(8,128)(2,1)S(1)}, bf16[32,3584]{1,0:T(8,128)(2,1)S(1)}, u32[]{:S(2)}, u32[]{:S(2)}) collective-permute-start(bf16[32,3584]{1,0:T(8,128)(2,1)S(1)} %get-tuple-element.97), channel_id=1, source_target_pairs={{0,8},{8,0},{1,9},{9,1},{2,10},{10,2},{3,11},{11,3},{4,12},{12,4},... | collective-permute-start | bytes 688136 | tf_op jit(solution)/shard_map/ppermute | solution.py:148
  34.0 6.2 %collective-permute-start.17 = (bf16[32,3584]{1,0:T(8,128)(2,1)S(1)}, bf16[32,3584]{1,0:T(8,128)(2,1)S(1)}, u32[]{:S(2)}, u32[]{:S(2)}) collective-permute-start(bf16[32,3584]{1,0:T(8,128)(2,1)S(1)} %add_convert_fusion.8), channel_id=1, source_target_pairs={{0,2},{2,4},{4,6},{6,7},{7,5},{5,3},{3,1},{1,0},{10,8},{12,10},{14... | collective-permute-start | bytes 688136 | tf_op jit(solution)/shard_map/ppermute | solution.py:145
  35.7 6.8 %collective-permute-start.26 = (bf16[32,3584]{1,0:T(8,128)(2,1)S(1)}, bf16[32,3584]{1,0:T(8,128)(2,1)S(1)}, u32[]{:S(2)}, u32[]{:S(2)}) collective-permute-start(bf16[32,3584]{1,0:T(8,128)(2,1)S(1)} %add_convert_fusion.6), channel_id=1, source_target_pairs={{0,2},{2,4},{4,6},{6,7},{7,5},{5,3},{3,1},{1,0},{10,8},{12,10},{14... | collective-permute-start | bytes 688136 | tf_op jit(solution)/shard_map/ppermute | solution.py:145
  39.6 7.3 %collective-permute-start.21 = (bf16[32,3584]{1,0:T(8,128)(2,1)S(1)}, bf16[32,3584]{1,0:T(8,128)(2,1)S(1)}, u32[]{:S(2)}, u32[]{:S(2)}) collective-permute-start(bf16[32,3584]{1,0:T(8,128)(2,1)S(1)} %get-tuple-element.103), channel_id=1, source_target_pairs={{0,8},{8,0},{1,9},{9,1},{2,10},{10,2},{3,11},{11,3},{4,12},{12,4},... | collective-permute-start | bytes 688136 | tf_op jit(solution)/shard_map/ppermute | solution.py:148
  39.7 2.2 %collective-permute-start.25 = (bf16[32,3584]{1,0:T(8,128)(2,1)S(1)}, bf16[32,3584]{1,0:T(8,128)(2,1)S(1)}, u32[]{:S(2)}, u32[]{:S(2)}) collective-permute-start(bf16[32,3584]{1,0:T(8,128)(2,1)S(1)} %get-tuple-element.108), channel_id=1, source_target_pairs={{0,8},{8,0},{1,9},{9,1},{2,10},{10,2},{3,11},{11,3},{4,12},{12,4},... | collective-permute-start | bytes 688136 | tf_op jit(solution)/shard_map/ppermute | solution.py:148
  40.3 6.1 %collective-permute-start.18 = (bf16[32,3584]{1,0:T(8,128)(2,1)S(1)}, bf16[32,3584]{1,0:T(8,128)(2,1)S(1)}, u32[]{:S(2)}, u32[]{:S(2)}) collective-permute-start(bf16[32,3584]{1,0:T(8,128)(2,1)S(1)} %add_convert_fusion.7), channel_id=1, source_target_pairs={{0,2},{2,4},{4,6},{6,7},{7,5},{5,3},{3,1},{1,0},{10,8},{12,10},{14... | collective-permute-start | bytes 688136 | tf_op jit(solution)/shard_map/ppermute | solution.py:145
  42.6 6.2 %collective-permute-start.27 = (bf16[32,3584]{1,0:T(8,128)(2,1)S(1)}, bf16[32,3584]{1,0:T(8,128)(2,1)S(1)}, u32[]{:S(2)}, u32[]{:S(2)}) collective-permute-start(bf16[32,3584]{1,0:T(8,128)(2,1)S(1)} %add_convert_fusion.3), channel_id=1, source_target_pairs={{0,2},{2,4},{4,6},{6,7},{7,5},{5,3},{3,1},{1,0},{10,8},{12,10},{14... | collective-permute-start | bytes 688136 | tf_op jit(solution)/shard_map/ppermute | solution.py:145
  46.4 4.1 %collective-permute-start.19 = (bf16[32,3584]{1,0:T(8,128)(2,1)S(1)}, bf16[32,3584]{1,0:T(8,128)(2,1)S(1)}, u32[]{:S(2)}, u32[]{:S(2)}) collective-permute-start(bf16[32,3584]{1,0:T(8,128)(2,1)S(1)} %get-tuple-element.93), channel_id=1, source_target_pairs={{0,8},{8,0},{1,9},{9,1},{2,10},{10,2},{3,11},{11,3},{4,12},{12,4},... | collective-permute-start | bytes 688136 | tf_op jit(solution)/shard_map/ppermute | solution.py:148
  46.4 2.5 %collective-permute-start.24 = (bf16[32,3584]{1,0:T(8,128)(2,1)S(1)}, bf16[32,3584]{1,0:T(8,128)(2,1)S(1)}, u32[]{:S(2)}, u32[]{:S(2)}) collective-permute-start(bf16[32,3584]{1,0:T(8,128)(2,1)S(1)} %get-tuple-element.106), channel_id=1, source_target_pairs={{0,8},{8,0},{1,9},{9,1},{2,10},{10,2},{3,11},{11,3},{4,12},{12,4},... | collective-permute-start | bytes 688136 | tf_op jit(solution)/shard_map/ppermute | solution.py:148
  47.0 6.1 %collective-permute-start.22 = (bf16[32,3584]{1,0:T(8,128)(2,1)S(1)}, bf16[32,3584]{1,0:T(8,128)(2,1)S(1)}, u32[]{:S(2)}, u32[]{:S(2)}) collective-permute-start(bf16[32,3584]{1,0:T(8,128)(2,1)S(1)} %add_convert_fusion.5), channel_id=1, source_target_pairs={{0,2},{2,4},{4,6},{6,7},{7,5},{5,3},{3,1},{1,0},{10,8},{12,10},{14... | collective-permute-start | bytes 688136 | tf_op jit(solution)/shard_map/ppermute | solution.py:145
  48.9 6.6 %collective-permute-start.28 = (bf16[32,3584]{1,0:T(8,128)(2,1)S(1)}, bf16[32,3584]{1,0:T(8,128)(2,1)S(1)}, u32[]{:S(2)}, u32[]{:S(2)}) collective-permute-start(bf16[32,3584]{1,0:T(8,128)(2,1)S(1)} %add_convert_fusion.2), channel_id=1, source_target_pairs={{0,2},{2,4},{4,6},{6,7},{7,5},{5,3},{3,1},{1,0},{10,8},{12,10},{14... | collective-permute-start | bytes 688136 | tf_op jit(solution)/shard_map/ppermute | solution.py:145
  53.1 6.1 %collective-permute-start.23 = (bf16[32,3584]{1,0:T(8,128)(2,1)S(1)}, bf16[32,3584]{1,0:T(8,128)(2,1)S(1)}, u32[]{:S(2)}, u32[]{:S(2)}) collective-permute-start(bf16[32,3584]{1,0:T(8,128)(2,1)S(1)} %add_convert_fusion.4), channel_id=1, source_target_pairs={{0,2},{2,4},{4,6},{6,7},{7,5},{5,3},{3,1},{1,0},{10,8},{12,10},{14... | collective-permute-start | bytes 688136 | tf_op jit(solution)/shard_map/ppermute | solution.py:145
  55.5 3.7 %collective-permute-start.29 = (bf16[32,3584]{1,0:T(8,128)(2,1)S(1)}, bf16[32,3584]{1,0:T(8,128)(2,1)S(1)}, u32[]{:S(2)}, u32[]{:S(2)}) collective-permute-start(bf16[32,3584]{1,0:T(8,128)(2,1)S(1)} %add_convert_fusion.1), channel_id=1, source_target_pairs={{0,8},{8,0},{1,9},{9,1},{2,10},{10,2},{3,11},{11,3},{4,12},{12,4},... | collective-permute-start | bytes 688136 | tf_op jit(solution)/shard_map/ppermute | solution.py:148

commit v7 on v6

--- a/solution.py
+++ b/solution.py
@@ -227,9 +227,9 @@
     for h in range(half - 1, 0, -1):
         if h < half - 1:
             run_b = hop(bf(join(sums[h][1], run_b)))
+        send_a = bf(join(sums[h][0], run_a))
         if h - 1 > 0 and h - 1 not in sums:
-            sums[h - 1] = total(h - 1, run_a)
-        send_a = bf(join(sums[h][0], run_a))
+            sums[h - 1] = total(h - 1, send_a)
         run_a = hop(send_a)
     last = swap(bf(join(own_b, run_b)))
     return bf(join(join(own_a, run_a), last))

time: 60.1 us -> 59.7 us (level)
  no operation moved by 1% of the time
where the time goes in v7:
time: 59.7 us; the launch traced here: 59.5 us
  starting transfers between devices  26.6 us (45%)
  Pallas kernels  17 us (28%)
  waiting for transfers between devices  14.4 us (24%)
  other arithmetic  1.34 us (2%)
    ppermute x14, starting transfers between devices, hop(): return lax.ppermute(x, BOTH, pairs)  23.5 us
    ppermute x14, waiting for transfers between devices, hop(): return lax.ppermute(x, BOTH, pairs)  12.4 us
    pallas_call x3, Pallas kernels, expert(): pl.pallas_call(functools.partial(expert_body, len(blocks), len(down)), ou...  8.57 us
    pallas_call x3, Pallas kernels, load(): pl.pallas_call(functools.partial(load_body, first, pieces), out_shape=plt...  7.28 us
    ppermute x16, starting transfers between devices, swap(): return lax.ppermute(x, 'node', [(0, 1), (1, 0)])  3.12 us
    ppermute x16, waiting for transfers between devices, swap(): return lax.ppermute(x, 'node', [(0, 1), (1, 0)])  1.98 us
    convert_element_type x9, other arithmetic, bf(): return x.astype(jnp.bfloat16)  1.34 us
  transfers between devices with their start and end apart: 30, of which 13 were waited for; matrix products, arithmetic and copies ran while one was open for 1% of the time, Pallas kernels for 21%

profile of v7, /device:TPU:0, one launch (start us, length us, event | category | flops | bytes accessed | tf_op | source)
XLA Modules:
  0.0 59.5 jit_solution(15517405590415140488)
XLA Ops:
  0.0 1.1 %shard_map.55.refs_0_ = bf16[32,3712]{1,0:T(8,128)(2,1)S(1)} custom-call(bf16[32,3584]{1,0:T(8,128)(2,1)} %tokens_ref.1, s32[8,32]{1,0:T(8,128)} %bitcast.8, bf16[8,32]{1,0:T(8,128)(2,1)} %bitcast.9), custom_call_target="tpu_custom_call" | custom-call | tf_op jit(solution)/shard_map/pallas_call | solution.py:127
  1.1 0.5 collective-permute-start
  1.6 2.6 %collective-permute-start.1 = (bf16[32,3712]{1,0:T(8,128)(2,1)S(1)}, bf16[32,3712]{1,0:T(8,128)(2,1)S(1)}, u32[]{:S(2)}, u32[]{:S(2)}) collective-permute-start(bf16[32,3712]{1,0:T(8,128)(2,1)S(1)} %shard_map.55.refs_0_), channel_id=1, source_target_pairs={{0,2},{2,4},{4,6},{6,7},{7,5},{5,3},{3,1},{1,0},{10,8},{12,10},{14... | collective-permute-start | bytes 712712 | tf_op jit(solution)/shard_map/ppermute | solution.py:145
  4.2 0.0 collective-permute-done.refs_1_
  4.2 1.6 %collective-permute-start.2 = (bf16[32,3712]{1,0:T(8,128)(2,1)S(1)}, bf16[32,3712]{1,0:T(8,128)(2,1)S(1)}, u32[]{:S(2)}, u32[]{:S(2)}) collective-permute-start(bf16[32,3712]{1,0:T(8,128)(2,1)S(1)} %collective-permute-done.refs_1_), channel_id=1, source_target_pairs={{0,2},{2,4},{4,6},{6,7},{7,5},{5,3},{3,1},{1,0},{10,8},{12,10},{14... | collective-permute-start | bytes 712712 | tf_op jit(solution)/shard_map/ppermute | solution.py:145
  5.8 3.2 %shard_map.56.refs_6_.refs_4_ = bf16[3584,1024]{1,0:T(8,128)(2,1)S(1)} custom-call(bf16[3584,1024]{1,0:T(8,128)(2,1)} %bitcast.7), custom_call_target="tpu_custom_call" | custom-call | tf_op jit(solution)/shard_map/pallas_call | solution.py:95
  8.9 0.0 collective-permute-done.1.refs_2_
  8.9 1.6 %collective-permute-start.3 = (bf16[32,3712]{1,0:T(8,128)(2,1)S(1)}, bf16[32,3712]{1,0:T(8,128)(2,1)S(1)}, u32[]{:S(2)}, u32[]{:S(2)}) collective-permute-start(bf16[32,3712]{1,0:T(8,128)(2,1)S(1)} %collective-permute-done.1.refs_2_), channel_id=1, source_target_pairs={{0,2},{2,4},{4,6},{6,7},{7,5},{5,3},{3,1},{1,0},{10,8},{12,10},{14... | collective-permute-start | bytes 712712 | tf_op jit(solution)/shard_map/ppermute | solution.py:145
  10.6 0.0 collective-permute-start.5
  10.6 0.2 collective-permute-done.2.refs_3_
  10.8 0.3 collective-permute-start.4
  11.1 1.7 %collective-permute-start.7 = (bf16[32,3712]{1,0:T(8,128)(2,1)S(1)}, bf16[32,3712]{1,0:T(8,128)(2,1)S(1)}, u32[]{:S(2)}, u32[]{:S(2)}) collective-permute-start(bf16[32,3712]{1,0:T(8,128)(2,1)S(1)} %collective-permute-done.2.refs_3_), channel_id=1, source_target_pairs={{0,2},{2,4},{4,6},{6,7},{7,5},{5,3},{3,1},{1,0},{10,8},{12,10},{14... | collective-permute-start | bytes 712712 | tf_op jit(solution)/shard_map/ppermute | solution.py:145
  12.8 2.5 %shard_map.57.refs_7_.refs_5_ = bf16[1024,2560]{1,0:T(8,128)(2,1)S(1)} custom-call(bf16[1024,3584]{1,0:T(8,128)(2,1)} %bitcast.5), custom_call_target="tpu_custom_call" | custom-call | tf_op jit(solution)/shard_map/pallas_call | solution.py:95
  15.4 0.0 collective-permute-done.3.refs_0_
  15.4 0.0 collective-permute-done.4.refs_4_
  15.4 1.6 %collective-permute-start.6 = (bf16[32,3712]{1,0:T(8,128)(2,1)S(1)}, bf16[32,3712]{1,0:T(8,128)(2,1)S(1)}, u32[]{:S(2)}, u32[]{:S(2)}) collective-permute-start(bf16[32,3712]{1,0:T(8,128)(2,1)S(1)} %collective-permute-done.3.refs_0_), channel_id=1, source_target_pairs={{0,2},{2,4},{4,6},{6,7},{7,5},{5,3},{3,1},{1,0},{10,8},{12,10},{14... | collective-permute-start | bytes 712712 | tf_op jit(solution)/shard_map/ppermute | solution.py:145
  17.0 0.6 %collective-permute-done.7.refs_1_ = bf16[32,3712]{1,0:T(8,128)(2,1)S(1)} collective-permute-done((bf16[32,3712]{1,0:T(8,128)(2,1)S(1)}, bf16[32,3712]{1,0:T(8,128)(2,1)S(1)}, u32[]{:S(2)}, u32[]{:S(2)}) %collective-permute-start.7) | collective-permute-done | bytes 237600 | tf_op jit(solution)/shard_map/ppermute | solution.py:145
  17.7 0.5 collective-permute-start.9
  18.2 1.6 %collective-permute-start.11 = (bf16[32,3712]{1,0:T(8,128)(2,1)S(1)}, bf16[32,3712]{1,0:T(8,128)(2,1)S(1)}, u32[]{:S(2)}, u32[]{:S(2)}) collective-permute-start(bf16[32,3712]{1,0:T(8,128)(2,1)S(1)} %collective-permute-done.7.refs_1_), channel_id=1, source_target_pairs={{0,2},{2,4},{4,6},{6,7},{7,5},{5,3},{3,1},{1,0},{10,8},{12,10},{14... | collective-permute-start | bytes 712712 | tf_op jit(solution)/shard_map/ppermute | solution.py:145
  19.7 1.6 %shard_map.58.refs_8_.refs_6_ = bf16[1024,1024]{1,0:T(8,128)(2,1)S(1)} custom-call(bf16[1024,3584]{1,0:T(8,128)(2,1)} %bitcast.6), custom_call_target="tpu_custom_call" | custom-call | tf_op jit(solution)/shard_map/pallas_call | solution.py:95
  21.3 0.3 collective-permute-done.6.refs_0_
  21.6 0.0 collective-permute-done.8.refs_2_
  21.6 0.0 collective-permute-done.9.refs_3_
  21.6 0.0 collective-permute-start.13
  21.6 1.6 %collective-permute-start.10 = (bf16[32,3712]{1,0:T(8,128)(2,1)S(1)}, bf16[32,3712]{1,0:T(8,128)(2,1)S(1)}, u32[]{:S(2)}, u32[]{:S(2)}) collective-permute-start(bf16[32,3712]{1,0:T(8,128)(2,1)S(1)} %collective-permute-done.6.refs_0_), channel_id=1, source_target_pairs={{0,2},{2,4},{4,6},{6,7},{7,5},{5,3},{3,1},{1,0},{10,8},{12,10},{14... | collective-permute-start | bytes 712712 | tf_op jit(solution)/shard_map/ppermute | solution.py:145
  23.2 1.1 %collective-permute-done.11.refs_1_ = bf16[32,3712]{1,0:T(8,128)(2,1)S(1)} collective-permute-done((bf16[32,3712]{1,0:T(8,128)(2,1)S(1)}, bf16[32,3712]{1,0:T(8,128)(2,1)S(1)}, u32[]{:S(2)}, u32[]{:S(2)}) %collective-permute-start.11) | collective-permute-done | bytes 237600 | tf_op jit(solution)/shard_map/ppermute | solution.py:145
  24.3 0.0 collective-permute-start.12
  24.3 3.2 %shard_map.59 = (f32[32,3584]{1,0:T(8,128)S(1)}, f32[32,3584]{1,0:T(8,128)S(1)}, bf16[32,3584]{1,0:T(8,128)(2,1)S(1)}, bf16[32,3584]{1,0:T(8,128)(2,1)S(1)}, f32...) custom-call(s32[1]{0:T(128)} %bitcast.3.mine_ref, bf16[32,3712]{1,0:T(8,128)(2,1)S(1)} %shard_map.55.refs_0_, ...), custom_call_target="tpu_custom_call" | custom-call | flops 2818572288 | bytes 14680064 | tf_op jit(solution)/shard_map/pallas_call | solution.py:65
  27.4 0.3 collective-permute-done.10.refs_4_
  27.8 0.3 collective-permute-start.14
  28.0 0.0 collective-permute-done.12.refs_2_
  28.0 0.0 collective-permute-done.13.refs_3_
  28.0 1.2 %collective-permute-done.14.refs_5_ = bf16[32,3712]{1,0:T(8,128)(2,1)S(1)} collective-permute-done((bf16[32,3712]{1,0:T(8,128)(2,1)S(1)}, bf16[32,3712]{1,0:T(8,128)(2,1)S(1)}, u32[]{:S(2)}, u32[]{:S(2)}) %collective-permute-start.14) | collective-permute-done | bytes 237600 | tf_op jit(solution)/shard_map/ppermute | solution.py:148
  29.3 3.1 %shard_map.60 = (bf16[32,3584]{1,0:T(8,128)(2,1)S(1)}, bf16[32,3584]{1,0:T(8,128)(2,1)S(1)}, f32[32,3584]{1,0:T(8,128)S(1)}, f32[32,3584]{1,0:T(8,128)S(1)}, f32...) custom-call(s32[1]{0:T(128)} %bitcast.3.mine_ref, bf16[32,3712]{1,0:T(8,128)(2,1)S(1)} %collective-permute-done.6.refs_0_, ...), custom_call_target="tpu_custom_call" | custom-call | flops 2818572288 | bytes 14680064 | tf_op jit(solution)/shard_map/pallas_call | solution.py:65
  32.4 0.3 collective-permute-start.15
  32.7 0.2 collective-permute-start.16
  33.0 0.3 collective-permute-start.18
  33.2 0.7 %collective-permute-done.15 = bf16[32,3584]{1,0:T(8,128)(2,1)S(1)} collective-permute-done((bf16[32,3584]{1,0:T(8,128)(2,1)S(1)}, bf16[32,3584]{1,0:T(8,128)(2,1)S(1)}, u32[]{:S(2)}, u32[]{:S(2)}) %collective-permute-start.15) | collective-permute-done | bytes 229408 | tf_op jit(solution)/shard_map/ppermute | solution.py:148
  34.0 1.6 %collective-permute-start.19 = (bf16[32,3584]{1,0:T(8,128)(2,1)S(1)}, bf16[32,3584]{1,0:T(8,128)(2,1)S(1)}, u32[]{:S(2)}, u32[]{:S(2)}) collective-permute-start(bf16[32,3584]{1,0:T(8,128)(2,1)S(1)} %add_convert_fusion.8), channel_id=1, source_target_pairs={{0,2},{2,4},{4,6},{6,7},{7,5},{5,3},{3,1},{1,0},{10,8},{12,10},{14... | collective-permute-start | bytes 688136 | tf_op jit(solution)/shard_map/ppermute | solution.py:145
  35.6 0.1 add_convert_fusion.7
  35.7 1.6 %collective-permute-start.26 = (bf16[32,3584]{1,0:T(8,128)(2,1)S(1)}, bf16[32,3584]{1,0:T(8,128)(2,1)S(1)}, u32[]{:S(2)}, u32[]{:S(2)}) collective-permute-start(bf16[32,3584]{1,0:T(8,128)(2,1)S(1)} %add_convert_fusion.7), channel_id=1, source_target_pairs={{0,2},{2,4},{4,6},{6,7},{7,5},{5,3},{3,1},{1,0},{10,8},{12,10},{14... | collective-permute-start | bytes 688136 | tf_op jit(solution)/shard_map/ppermute | solution.py:145
  37.3 2.3 %shard_map.61 = (bf16[32,3584]{1,0:T(8,128)(2,1)S(1)}, bf16[32,3584]{1,0:T(8,128)(2,1)S(1)}, f32[32,3584]{1,0:T(8,128)S(1)}, f32[32,3584]{1,0:T(8,128)S(1)}) custom-call(s32[1]{0:T(128)} %bitcast.3.mine_ref, bf16[32,3712]{1,0:T(8,128)(2,1)S(1)} %collective-permute-done.3.refs_0_, bf16[32,3712]{1,0:T(8,128)(2,1)S(1)} %collective-permute-done.7.refs_1_, ...), custom_call_target="tpu_custom_call" | custom-call | flops 1879048192 | bytes 14680064 | tf_op jit(solution)/shard_map/pallas_call | solution.py:65
  39.6 0.1 collective-permute-start.17
  39.7 0.5 collective-permute-start.25
  40.2 0.1 add_convert_fusion.6
  40.3 1.6 %collective-permute-start.20 = (bf16[32,3584]{1,0:T(8,128)(2,1)S(1)}, bf16[32,3584]{1,0:T(8,128)(2,1)S(1)}, u32[]{:S(2)}, u32[]{:S(2)}) collective-permute-start(bf16[32,3584]{1,0:T(8,128)(2,1)S(1)} %add_convert_fusion.6), channel_id=1, source_target_pairs={{0,2},{2,4},{4,6},{6,7},{7,5},{5,3},{3,1},{1,0},{10,8},{12,10},{14... | collective-permute-start | bytes 688136 | tf_op jit(solution)/shard_map/ppermute | solution.py:145
  41.9 0.7 %collective-permute-done.26 = bf16[32,3584]{1,0:T(8,128)(2,1)S(1)} collective-permute-done((bf16[32,3584]{1,0:T(8,128)(2,1)S(1)}, bf16[32,3584]{1,0:T(8,128)(2,1)S(1)}, u32[]{:S(2)}, u32[]{:S(2)}) %collective-permute-start.26) | collective-permute-done | bytes 229408 | tf_op jit(solution)/shard_map/ppermute | solution.py:145
  42.5 0.1 add_convert_fusion.3
  42.6 1.6 %collective-permute-start.27 = (bf16[32,3584]{1,0:T(8,128)(2,1)S(1)}, bf16[32,3584]{1,0:T(8,128)(2,1)S(1)}, u32[]{:S(2)}, u32[]{:S(2)}) collective-permute-start(bf16[32,3584]{1,0:T(8,128)(2,1)S(1)} %add_convert_fusion.3), channel_id=1, source_target_pairs={{0,2},{2,4},{4,6},{6,7},{7,5},{5,3},{3,1},{1,0},{10,8},{12,10},{14... | collective-permute-start | bytes 688136 | tf_op jit(solution)/shard_map/ppermute | solution.py:145
  44.2 2.1 %collective-permute-done.20 = bf16[32,3584]{1,0:T(8,128)(2,1)S(1)} collective-permute-done((bf16[32,3584]{1,0:T(8,128)(2,1)S(1)}, bf16[32,3584]{1,0:T(8,128)(2,1)S(1)}, u32[]{:S(2)}, u32[]{:S(2)}) %collective-permute-start.20) | collective-permute-done | bytes 229408 | tf_op jit(solution)/shard_map/ppermute | solution.py:145
  46.4 0.1 add_convert_fusion.5
  46.4 0.1 collective-permute-start.24
  46.5 1.6 %collective-permute-start.22 = (bf16[32,3584]{1,0:T(8,128)(2,1)S(1)}, bf16[32,3584]{1,0:T(8,128)(2,1)S(1)}, u32[]{:S(2)}, u32[]{:S(2)}) collective-permute-start(bf16[32,3584]{1,0:T(8,128)(2,1)S(1)} %add_convert_fusion.5), channel_id=1, source_target_pairs={{0,2},{2,4},{4,6},{6,7},{7,5},{5,3},{3,1},{1,0},{10,8},{12,10},{14... | collective-permute-start | bytes 688136 | tf_op jit(solution)/shard_map/ppermute | solution.py:145
  48.1 0.7 %collective-permute-done.27 = bf16[32,3584]{1,0:T(8,128)(2,1)S(1)} collective-permute-done((bf16[32,3584]{1,0:T(8,128)(2,1)S(1)}, bf16[32,3584]{1,0:T(8,128)(2,1)S(1)}, u32[]{:S(2)}, u32[]{:S(2)}) %collective-permute-start.27) | collective-permute-done | bytes 229408 | tf_op jit(solution)/shard_map/ppermute | solution.py:145
  48.8 0.1 add_convert_fusion.2
  48.9 1.6 %collective-permute-start.28 = (bf16[32,3584]{1,0:T(8,128)(2,1)S(1)}, bf16[32,3584]{1,0:T(8,128)(2,1)S(1)}, u32[]{:S(2)}, u32[]{:S(2)}) collective-permute-start(bf16[32,3584]{1,0:T(8,128)(2,1)S(1)} %add_convert_fusion.2), channel_id=1, source_target_pairs={{0,2},{2,4},{4,6},{6,7},{7,5},{5,3},{3,1},{1,0},{10,8},{12,10},{14... | collective-permute-start | bytes 688136 | tf_op jit(solution)/shard_map/ppermute | solution.py:145
  50.5 2.1 %collective-permute-done.22 = bf16[32,3584]{1,0:T(8,128)(2,1)S(1)} collective-permute-done((bf16[32,3584]{1,0:T(8,128)(2,1)S(1)}, bf16[32,3584]{1,0:T(8,128)(2,1)S(1)}, u32[]{:S(2)}, u32[]{:S(2)}) %collective-permute-start.22) | collective-permute-done | bytes 229408 | tf_op jit(solution)/shard_map/ppermute | solution.py:145
  52.6 0.1 add_convert_fusion.4
  52.7 1.6 %collective-permute-start.23 = (bf16[32,3584]{1,0:T(8,128)(2,1)S(1)}, bf16[32,3584]{1,0:T(8,128)(2,1)S(1)}, u32[]{:S(2)}, u32[]{:S(2)}) collective-permute-start(bf16[32,3584]{1,0:T(8,128)(2,1)S(1)} %add_convert_fusion.4), channel_id=1, source_target_pairs={{0,2},{2,4},{4,6},{6,7},{7,5},{5,3},{3,1},{1,0},{10,8},{12,10},{14... | collective-permute-start | bytes 688136 | tf_op jit(solution)/shard_map/ppermute | solution.py:145
  54.3 0.8 %collective-permute-done.28 = bf16[32,3584]{1,0:T(8,128)(2,1)S(1)} collective-permute-done((bf16[32,3584]{1,0:T(8,128)(2,1)S(1)}, bf16[32,3584]{1,0:T(8,128)(2,1)S(1)}, u32[]{:S(2)}, u32[]{:S(2)}) %collective-permute-start.28) | collective-permute-done | bytes 229408 | tf_op jit(solution)/shard_map/ppermute | solution.py:145
  55.1 0.1 add_convert_fusion.1
  55.1 0.1 collective-permute-start.29
  55.2 3.6 %collective-permute-done.23 = bf16[32,3584]{1,0:T(8,128)(2,1)S(1)} collective-permute-done((bf16[32,3584]{1,0:T(8,128)(2,1)S(1)}, bf16[32,3584]{1,0:T(8,128)(2,1)S(1)}, u32[]{:S(2)}, u32[]{:S(2)}) %collective-permute-start.23) | collective-permute-done | bytes 229408 | tf_op jit(solution)/shard_map/ppermute | solution.py:145
  58.8 0.8 %add_convert_fusion = bf16[32,3584]{1,0:T(8,128)(2,1)} fusion(bf16[32,3584]{1,0:T(8,128)(2,1)S(1)} %collective-permute-done.29, f32[32,3584]{1,0:T(8,128)S(1)} %get-tuple-element.84, bf16[32,3584]{1,0:T(8,128)(2,1)S(1)} %collective-permute-done.23), kind=kLoop, calls=%fused_computation | loop fusion | flops 573440 | bytes 1146880 | tf_op jit(solution)/shard_map/convert_element_type | solution.py:151
  (12 shorter events, 0.1 us)
Async XLA Ops:
  1.1 3.1 %collective-permute-start = (bf16[32,3712]{1,0:T(8,128)(2,1)S(1)}, bf16[32,3712]{1,0:T(8,128)(2,1)S(1)}, u32[]{:S(2)}, u32[]{:S(2)}) collective-permute-start(bf16[32,3712]{1,0:T(8,128)(2,1)S(1)} %shard_map.55.refs_0_), channel_id=1, source_target_pairs={{0,8},{8,0},{1,9},{9,1},{2,10},{10,2},{3,11},{11,3},{4,12},{12,4},... | collective-permute-start | bytes 712712 | tf_op jit(solution)/shard_map/ppermute | solution.py:148
  1.6 7.4 %collective-permute-start.1 = (bf16[32,3712]{1,0:T(8,128)(2,1)S(1)}, bf16[32,3712]{1,0:T(8,128)(2,1)S(1)}, u32[]{:S(2)}, u32[]{:S(2)}) collective-permute-start(bf16[32,3712]{1,0:T(8,128)(2,1)S(1)} %shard_map.55.refs_0_), channel_id=1, source_target_pairs={{0,2},{2,4},{4,6},{6,7},{7,5},{5,3},{3,1},{1,0},{10,8},{12,10},{14... | collective-permute-start | bytes 712712 | tf_op jit(solution)/shard_map/ppermute | solution.py:145
  4.2 6.6 %collective-permute-start.2 = (bf16[32,3712]{1,0:T(8,128)(2,1)S(1)}, bf16[32,3712]{1,0:T(8,128)(2,1)S(1)}, u32[]{:S(2)}, u32[]{:S(2)}) collective-permute-start(bf16[32,3712]{1,0:T(8,128)(2,1)S(1)} %collective-permute-done.refs_1_), channel_id=1, source_target_pairs={{0,2},{2,4},{4,6},{6,7},{7,5},{5,3},{3,1},{1,0},{10,8},{12,10},{14... | collective-permute-start | bytes 712712 | tf_op jit(solution)/shard_map/ppermute | solution.py:145
  8.9 6.4 %collective-permute-start.3 = (bf16[32,3712]{1,0:T(8,128)(2,1)S(1)}, bf16[32,3712]{1,0:T(8,128)(2,1)S(1)}, u32[]{:S(2)}, u32[]{:S(2)}) collective-permute-start(bf16[32,3712]{1,0:T(8,128)(2,1)S(1)} %collective-permute-done.1.refs_2_), channel_id=1, source_target_pairs={{0,2},{2,4},{4,6},{6,7},{7,5},{5,3},{3,1},{1,0},{10,8},{12,10},{14... | collective-permute-start | bytes 712712 | tf_op jit(solution)/shard_map/ppermute | solution.py:145
  10.6 4.8 %collective-permute-start.5 = (bf16[32,3712]{1,0:T(8,128)(2,1)S(1)}, bf16[32,3712]{1,0:T(8,128)(2,1)S(1)}, u32[]{:S(2)}, u32[]{:S(2)}) collective-permute-start(bf16[32,3712]{1,0:T(8,128)(2,1)S(1)} %collective-permute-done.1.refs_2_), channel_id=1, source_target_pairs={{0,8},{8,0},{1,9},{9,1},{2,10},{10,2},{3,11},{11,3},{4,12},{12,4},... | collective-permute-start | bytes 712712 | tf_op jit(solution)/shard_map/ppermute | solution.py:148
  10.8 4.6 %collective-permute-start.4 = (bf16[32,3712]{1,0:T(8,128)(2,1)S(1)}, bf16[32,3712]{1,0:T(8,128)(2,1)S(1)}, u32[]{:S(2)}, u32[]{:S(2)}) collective-permute-start(bf16[32,3712]{1,0:T(8,128)(2,1)S(1)} %collective-permute-done.2.refs_3_), channel_id=1, source_target_pairs={{0,8},{8,0},{1,9},{9,1},{2,10},{10,2},{3,11},{11,3},{4,12},{12,4},... | collective-permute-start | bytes 712712 | tf_op jit(solution)/shard_map/ppermute | solution.py:148
  11.1 6.6 %collective-permute-start.7 = (bf16[32,3712]{1,0:T(8,128)(2,1)S(1)}, bf16[32,3712]{1,0:T(8,128)(2,1)S(1)}, u32[]{:S(2)}, u32[]{:S(2)}) collective-permute-start(bf16[32,3712]{1,0:T(8,128)(2,1)S(1)} %collective-permute-done.2.refs_3_), channel_id=1, source_target_pairs={{0,2},{2,4},{4,6},{6,7},{7,5},{5,3},{3,1},{1,0},{10,8},{12,10},{14... | collective-permute-start | bytes 712712 | tf_op jit(solution)/shard_map/ppermute | solution.py:145
  15.4 6.2 %collective-permute-start.6 = (bf16[32,3712]{1,0:T(8,128)(2,1)S(1)}, bf16[32,3712]{1,0:T(8,128)(2,1)S(1)}, u32[]{:S(2)}, u32[]{:S(2)}) collective-permute-start(bf16[32,3712]{1,0:T(8,128)(2,1)S(1)} %collective-permute-done.3.refs_0_), channel_id=1, source_target_pairs={{0,2},{2,4},{4,6},{6,7},{7,5},{5,3},{3,1},{1,0},{10,8},{12,10},{14... | collective-permute-start | bytes 712712 | tf_op jit(solution)/shard_map/ppermute | solution.py:145
  17.7 3.9 %collective-permute-start.8 = (bf16[32,3712]{1,0:T(8,128)(2,1)S(1)}, bf16[32,3712]{1,0:T(8,128)(2,1)S(1)}, u32[]{:S(2)}, u32[]{:S(2)}) collective-permute-start(bf16[32,3712]{1,0:T(8,128)(2,1)S(1)} %collective-permute-done.7.refs_1_), channel_id=1, source_target_pairs={{0,8},{8,0},{1,9},{9,1},{2,10},{10,2},{3,11},{11,3},{4,12},{12,4},... | collective-permute-start | bytes 712712 | tf_op jit(solution)/shard_map/ppermute | solution.py:148
  17.7 3.9 %collective-permute-start.9 = (bf16[32,3712]{1,0:T(8,128)(2,1)S(1)}, bf16[32,3712]{1,0:T(8,128)(2,1)S(1)}, u32[]{:S(2)}, u32[]{:S(2)}) collective-permute-start(bf16[32,3712]{1,0:T(8,128)(2,1)S(1)} %collective-permute-done.3.refs_0_), channel_id=1, source_target_pairs={{0,8},{8,0},{1,9},{9,1},{2,10},{10,2},{3,11},{11,3},{4,12},{12,4},... | collective-permute-start | bytes 712712 | tf_op jit(solution)/shard_map/ppermute | solution.py:148
  18.2 6.1 %collective-permute-start.11 = (bf16[32,3712]{1,0:T(8,128)(2,1)S(1)}, bf16[32,3712]{1,0:T(8,128)(2,1)S(1)}, u32[]{:S(2)}, u32[]{:S(2)}) collective-permute-start(bf16[32,3712]{1,0:T(8,128)(2,1)S(1)} %collective-permute-done.7.refs_1_), channel_id=1, source_target_pairs={{0,2},{2,4},{4,6},{6,7},{7,5},{5,3},{3,1},{1,0},{10,8},{12,10},{14... | collective-permute-start | bytes 712712 | tf_op jit(solution)/shard_map/ppermute | solution.py:145
  21.6 6.4 %collective-permute-start.13 = (bf16[32,3712]{1,0:T(8,128)(2,1)S(1)}, bf16[32,3712]{1,0:T(8,128)(2,1)S(1)}, u32[]{:S(2)}, u32[]{:S(2)}) collective-permute-start(bf16[32,3712]{1,0:T(8,128)(2,1)S(1)} %collective-permute-done.6.refs_0_), channel_id=1, source_target_pairs={{0,8},{8,0},{1,9},{9,1},{2,10},{10,2},{3,11},{11,3},{4,12},{12,4},... | collective-permute-start | bytes 712712 | tf_op jit(solution)/shard_map/ppermute | solution.py:148
  21.6 6.2 %collective-permute-start.10 = (bf16[32,3712]{1,0:T(8,128)(2,1)S(1)}, bf16[32,3712]{1,0:T(8,128)(2,1)S(1)}, u32[]{:S(2)}, u32[]{:S(2)}) collective-permute-start(bf16[32,3712]{1,0:T(8,128)(2,1)S(1)} %collective-permute-done.6.refs_0_), channel_id=1, source_target_pairs={{0,2},{2,4},{4,6},{6,7},{7,5},{5,3},{3,1},{1,0},{10,8},{12,10},{14... | collective-permute-start | bytes 712712 | tf_op jit(solution)/shard_map/ppermute | solution.py:145
  24.3 3.8 %collective-permute-start.12 = (bf16[32,3712]{1,0:T(8,128)(2,1)S(1)}, bf16[32,3712]{1,0:T(8,128)(2,1)S(1)}, u32[]{:S(2)}, u32[]{:S(2)}) collective-permute-start(bf16[32,3712]{1,0:T(8,128)(2,1)S(1)} %collective-permute-done.11.refs_1_), channel_id=1, source_target_pairs={{0,8},{8,0},{1,9},{9,1},{2,10},{10,2},{3,11},{11,3},{4,12},{12,4},... | collective-permute-start | bytes 712712 | tf_op jit(solution)/shard_map/ppermute | solution.py:148
  27.8 1.5 %collective-permute-start.14 = (bf16[32,3712]{1,0:T(8,128)(2,1)S(1)}, bf16[32,3712]{1,0:T(8,128)(2,1)S(1)}, u32[]{:S(2)}, u32[]{:S(2)}) collective-permute-start(bf16[32,3712]{1,0:T(8,128)(2,1)S(1)} %collective-permute-done.10.refs_4_), channel_id=1, source_target_pairs={{0,8},{8,0},{1,9},{9,1},{2,10},{10,2},{3,11},{11,3},{4,12},{12,4},... | collective-permute-start | bytes 712712 | tf_op jit(solution)/shard_map/ppermute | solution.py:148
  32.4 1.6 %collective-permute-start.15 = (bf16[32,3584]{1,0:T(8,128)(2,1)S(1)}, bf16[32,3584]{1,0:T(8,128)(2,1)S(1)}, u32[]{:S(2)}, u32[]{:S(2)}) collective-permute-start(bf16[32,3584]{1,0:T(8,128)(2,1)S(1)} %get-tuple-element.92), channel_id=1, source_target_pairs={{0,8},{8,0},{1,9},{9,1},{2,10},{10,2},{3,11},{11,3},{4,12},{12,4},... | collective-permute-start | bytes 688136 | tf_op jit(solution)/shard_map/ppermute | solution.py:148
  32.7 2.9 %collective-permute-start.16 = (bf16[32,3584]{1,0:T(8,128)(2,1)S(1)}, bf16[32,3584]{1,0:T(8,128)(2,1)S(1)}, u32[]{:S(2)}, u32[]{:S(2)}) collective-permute-start(bf16[32,3584]{1,0:T(8,128)(2,1)S(1)} %get-tuple-element.94), channel_id=1, source_target_pairs={{0,8},{8,0},{1,9},{9,1},{2,10},{10,2},{3,11},{11,3},{4,12},{12,4},... | collective-permute-start | bytes 688136 | tf_op jit(solution)/shard_map/ppermute | solution.py:148
  33.0 7.2 %collective-permute-start.18 = (bf16[32,3584]{1,0:T(8,128)(2,1)S(1)}, bf16[32,3584]{1,0:T(8,128)(2,1)S(1)}, u32[]{:S(2)}, u32[]{:S(2)}) collective-permute-start(bf16[32,3584]{1,0:T(8,128)(2,1)S(1)} %get-tuple-element.102), channel_id=1, source_target_pairs={{0,8},{8,0},{1,9},{9,1},{2,10},{10,2},{3,11},{11,3},{4,12},{12,4},... | collective-permute-start | bytes 688136 | tf_op jit(solution)/shard_map/ppermute | solution.py:148
  34.0 6.2 %collective-permute-start.19 = (bf16[32,3584]{1,0:T(8,128)(2,1)S(1)}, bf16[32,3584]{1,0:T(8,128)(2,1)S(1)}, u32[]{:S(2)}, u32[]{:S(2)}) collective-permute-start(bf16[32,3584]{1,0:T(8,128)(2,1)S(1)} %add_convert_fusion.8), channel_id=1, source_target_pairs={{0,2},{2,4},{4,6},{6,7},{7,5},{5,3},{3,1},{1,0},{10,8},{12,10},{14... | collective-permute-start | bytes 688136 | tf_op jit(solution)/shard_map/ppermute | solution.py:145
  35.7 6.8 %collective-permute-start.26 = (bf16[32,3584]{1,0:T(8,128)(2,1)S(1)}, bf16[32,3584]{1,0:T(8,128)(2,1)S(1)}, u32[]{:S(2)}, u32[]{:S(2)}) collective-permute-start(bf16[32,3584]{1,0:T(8,128)(2,1)S(1)} %add_convert_fusion.7), channel_id=1, source_target_pairs={{0,2},{2,4},{4,6},{6,7},{7,5},{5,3},{3,1},{1,0},{10,8},{12,10},{14... | collective-permute-start | bytes 688136 | tf_op jit(solution)/shard_map/ppermute | solution.py:145
  39.6 4.6 %collective-permute-start.17 = (bf16[32,3584]{1,0:T(8,128)(2,1)S(1)}, bf16[32,3584]{1,0:T(8,128)(2,1)S(1)}, u32[]{:S(2)}, u32[]{:S(2)}) collective-permute-start(bf16[32,3584]{1,0:T(8,128)(2,1)S(1)} %get-tuple-element.100), channel_id=1, source_target_pairs={{0,8},{8,0},{1,9},{9,1},{2,10},{10,2},{3,11},{11,3},{4,12},{12,4},... | collective-permute-start | bytes 688136 | tf_op jit(solution)/shard_map/ppermute | solution.py:148
  39.7 2.2 %collective-permute-start.25 = (bf16[32,3584]{1,0:T(8,128)(2,1)S(1)}, bf16[32,3584]{1,0:T(8,128)(2,1)S(1)}, u32[]{:S(2)}, u32[]{:S(2)}) collective-permute-start(bf16[32,3584]{1,0:T(8,128)(2,1)S(1)} %get-tuple-element.108), channel_id=1, source_target_pairs={{0,8},{8,0},{1,9},{9,1},{2,10},{10,2},{3,11},{11,3},{4,12},{12,4},... | collective-permute-start | bytes 688136 | tf_op jit(solution)/shard_map/ppermute | solution.py:148
  40.3 6.1 %collective-permute-start.20 = (bf16[32,3584]{1,0:T(8,128)(2,1)S(1)}, bf16[32,3584]{1,0:T(8,128)(2,1)S(1)}, u32[]{:S(2)}, u32[]{:S(2)}) collective-permute-start(bf16[32,3584]{1,0:T(8,128)(2,1)S(1)} %add_convert_fusion.6), channel_id=1, source_target_pairs={{0,2},{2,4},{4,6},{6,7},{7,5},{5,3},{3,1},{1,0},{10,8},{12,10},{14... | collective-permute-start | bytes 688136 | tf_op jit(solution)/shard_map/ppermute | solution.py:145
  42.6 6.2 %collective-permute-start.27 = (bf16[32,3584]{1,0:T(8,128)(2,1)S(1)}, bf16[32,3584]{1,0:T(8,128)(2,1)S(1)}, u32[]{:S(2)}, u32[]{:S(2)}) collective-permute-start(bf16[32,3584]{1,0:T(8,128)(2,1)S(1)} %add_convert_fusion.3), channel_id=1, source_target_pairs={{0,2},{2,4},{4,6},{6,7},{7,5},{5,3},{3,1},{1,0},{10,8},{12,10},{14... | collective-permute-start | bytes 688136 | tf_op jit(solution)/shard_map/ppermute | solution.py:145
  46.4 2.4 %collective-permute-start.24 = (bf16[32,3584]{1,0:T(8,128)(2,1)S(1)}, bf16[32,3584]{1,0:T(8,128)(2,1)S(1)}, u32[]{:S(2)}, u32[]{:S(2)}) collective-permute-start(bf16[32,3584]{1,0:T(8,128)(2,1)S(1)} %get-tuple-element.106), channel_id=1, source_target_pairs={{0,8},{8,0},{1,9},{9,1},{2,10},{10,2},{3,11},{11,3},{4,12},{12,4},... | collective-permute-start | bytes 688136 | tf_op jit(solution)/shard_map/ppermute | solution.py:148
  46.5 6.1 %collective-permute-start.22 = (bf16[32,3584]{1,0:T(8,128)(2,1)S(1)}, bf16[32,3584]{1,0:T(8,128)(2,1)S(1)}, u32[]{:S(2)}, u32[]{:S(2)}) collective-permute-start(bf16[32,3584]{1,0:T(8,128)(2,1)S(1)} %add_convert_fusion.5), channel_id=1, source_target_pairs={{0,2},{2,4},{4,6},{6,7},{7,5},{5,3},{3,1},{1,0},{10,8},{12,10},{14... | collective-permute-start | bytes 688136 | tf_op jit(solution)/shard_map/ppermute | solution.py:145
  48.1 2.4 %collective-permute-start.21 = (bf16[32,3584]{1,0:T(8,128)(2,1)S(1)}, bf16[32,3584]{1,0:T(8,128)(2,1)S(1)}, u32[]{:S(2)}, u32[]{:S(2)}) collective-permute-start(bf16[32,3584]{1,0:T(8,128)(2,1)S(1)} %get-tuple-element.103), channel_id=1, source_target_pairs={{0,8},{8,0},{1,9},{9,1},{2,10},{10,2},{3,11},{11,3},{4,12},{12,4},... | collective-permute-start | bytes 688136 | tf_op jit(solution)/shard_map/ppermute | solution.py:148
  48.9 6.1 %collective-permute-start.28 = (bf16[32,3584]{1,0:T(8,128)(2,1)S(1)}, bf16[32,3584]{1,0:T(8,128)(2,1)S(1)}, u32[]{:S(2)}, u32[]{:S(2)}) collective-permute-start(bf16[32,3584]{1,0:T(8,128)(2,1)S(1)} %add_convert_fusion.2), channel_id=1, source_target_pairs={{0,2},{2,4},{4,6},{6,7},{7,5},{5,3},{3,1},{1,0},{10,8},{12,10},{14... | collective-permute-start | bytes 688136 | tf_op jit(solution)/shard_map/ppermute | solution.py:145
  52.7 6.1 %collective-permute-start.23 = (bf16[32,3584]{1,0:T(8,128)(2,1)S(1)}, bf16[32,3584]{1,0:T(8,128)(2,1)S(1)}, u32[]{:S(2)}, u32[]{:S(2)}) collective-permute-start(bf16[32,3584]{1,0:T(8,128)(2,1)S(1)} %add_convert_fusion.4), channel_id=1, source_target_pairs={{0,2},{2,4},{4,6},{6,7},{7,5},{5,3},{3,1},{1,0},{10,8},{12,10},{14... | collective-permute-start | bytes 688136 | tf_op jit(solution)/shard_map/ppermute | solution.py:145
  55.1 3.7 %collective-permute-start.29 = (bf16[32,3584]{1,0:T(8,128)(2,1)S(1)}, bf16[32,3584]{1,0:T(8,128)(2,1)S(1)}, u32[]{:S(2)}, u32[]{:S(2)}) collective-permute-start(bf16[32,3584]{1,0:T(8,128)(2,1)S(1)} %add_convert_fusion.1), channel_id=1, source_target_pairs={{0,8},{8,0},{1,9},{9,1},{2,10},{10,2},{3,11},{11,3},{4,12},{12,4},... | collective-permute-start | bytes 688136 | tf_op jit(solution)/shard_map/ppermute | solution.py:148

commit v8 on v7

--- a/solution.py
+++ b/solution.py
@@ -178,7 +178,7 @@
             down = load(w_down[0], 0, cut, a[1])
             a[2], down_first = lax.optimization_barrier((a[2], down))
         elif h == 3:
-            down = load(w_down[0], cut, width, a[2])
+            down = load(w_down[0], cut, width, (a[2], ahead_b[2]))
             a[3], down_last = lax.optimization_barrier((a[3], down))
         if 1 < h < half:
             a[h], ahead_a[h - 1], ahead_b[h - 1] = lax.optimization_barrier((a[h], ahead_a[h - 1], ahead_b[h - 1]))
@@ -186,26 +186,17 @@
             ahead_b.append(swap(a[h]))
             ahead_a.append(swap(b[h]))
     down = [pltpu.with_memory_space_constraint(d, pltpu.VMEM) for d in (down_first, down_last)]
-    near = range(1, half - 2)
-    blocks = [a[0], b[0]]
-    for h in near:
-        blocks += [a[h], b[h], ahead_a[h], ahead_b[h]]
-    blocks, _ = lax.optimization_barrier((blocks, a[half - 1]))
-    r = expert(mine, blocks, (True, True) + (False, False, True, True) * len(near), up, down)
+    near, h = range(1, half - 2), half - 1
+    blocks = [a[h], ahead_b[h]]
+    for i in near:
+        blocks += [a[i], b[i], ahead_a[i], ahead_b[i]]
+    r = expert(mine, blocks, (False, True) + (False, False, True, True) * len(near), up, down)
     r, a[half] = lax.optimization_barrier((r, a[half]))
-    own_a, own_b = r[:2]
-    for i, h in enumerate(near):
-        behind[h], ahead[h] = r[4 * i + 2:4 * i + 4], r[4 * i + 4:4 * i + 6]
+    for i in near:
+        behind[i], ahead[i] = r[4 * i - 2:4 * i], r[4 * i:4 * i + 2]
     ahead_b.append(swap(a[half]))
-    h = half - 1
-    r = expert(
-        mine,
-        (a[h], b[h], ahead_a[h], ahead_b[h], a[half], ahead_b[half]),
-        (False, False, True, True, True, False),
-        up,
-        down,
-    )
-    behind[h], ahead[h], far = r[:2], r[2:4], r[4:]
+    last = expert(mine, (b[h], ahead_a[h], a[half], ahead_b[half]), (False, True, True, False), up, down)
+    behind[h], ahead[h], far = (r[0], last[0]), (last[1], r[1]), last[2:]
 
     def join(x, y):
         return x.astype(jnp.float32) + y.astype(jnp.float32)
@@ -231,6 +222,8 @@
         if h - 1 > 0 and h - 1 not in sums:
             sums[h - 1] = total(h - 1, send_a)
         run_a = hop(send_a)
+    blocks, _ = lax.optimization_barrier(((a[0], b[0]), send_a))
+    own_a, own_b = expert(mine, blocks, (True, True), up, down)
     last = swap(bf(join(own_b, run_b)))
     return bf(join(join(own_a, run_a), last))
 

time: 59.7 us -> 58.8 us (0.985)
  waiting for transfers between devices: 14.4 us -> 12.5 us
  Pallas kernels: 17 us -> 18.8 us
  starting transfers between devices: 26.6 us -> 25.9 us
    ppermute x14, waiting for transfers between devices: 12.4 us -> 10.3 us  [hop(): return lax.ppermute(x, BOTH, pairs)]
    pallas_call x3 -> x4, Pallas kernels: 8.57 us -> 10.4 us  [expert(): pl.pallas_call(functools.partial(expert_body, len(blocks), len(down)), ou...]
  transfers between devices with their start and end apart: 30 -> 30, of which waited for: 13 -> 12; matrix products, arithmetic and copies ran while one was open for 1% -> 1% of each run, Pallas kernels for 21% -> 26%
where the time goes in v8:
time: 58.8 us; the launch traced here: 58.7 us
  starting transfers between devices  25.9 us (44%)
  Pallas kernels  18.8 us (32%)
  waiting for transfers between devices  12.5 us (21%)
  other arithmetic  1.36 us (2%)
    ppermute x14, starting transfers between devices, hop(): return lax.ppermute(x, BOTH, pairs)  23 us
    pallas_call x4, Pallas kernels, expert(): pl.pallas_call(functools.partial(expert_body, len(blocks), len(down)), ou...  10.4 us
    ppermute x14, waiting for transfers between devices, hop(): return lax.ppermute(x, BOTH, pairs)  10.3 us
    pallas_call x3, Pallas kernels, load(): pl.pallas_call(functools.partial(load_body, first, pieces), out_shape=plt...  7.28 us
    ppermute x16, starting transfers between devices, swap(): return lax.ppermute(x, 'node', [(0, 1), (1, 0)])  2.84 us
    ppermute x16, waiting for transfers between devices, swap(): return lax.ppermute(x, 'node', [(0, 1), (1, 0)])  2.19 us
    convert_element_type x9, other arithmetic, bf(): return x.astype(jnp.bfloat16)  1.36 us
  transfers between devices with their start and end apart: 30, of which 12 were waited for; matrix products, arithmetic and copies ran while one was open for 1% of the time, Pallas kernels for 26%

profile of v8, /device:TPU:0, one launch (start us, length us, event | category | flops | bytes accessed | tf_op | source)
XLA Modules:
  0.0 58.7 jit_solution(13026489219636020579)
XLA Ops:
  0.0 1.1 %shard_map.55.refs_0_ = bf16[32,3712]{1,0:T(8,128)(2,1)S(1)} custom-call(bf16[32,3584]{1,0:T(8,128)(2,1)} %tokens_ref.1, s32[8,32]{1,0:T(8,128)} %bitcast.8, bf16[8,32]{1,0:T(8,128)(2,1)} %bitcast.9), custom_call_target="tpu_custom_call" | custom-call | tf_op jit(solution)/shard_map/pallas_call | solution.py:127
  1.1 0.5 collective-permute-start
  1.6 2.6 %collective-permute-start.1 = (bf16[32,3712]{1,0:T(8,128)(2,1)S(1)}, bf16[32,3712]{1,0:T(8,128)(2,1)S(1)}, u32[]{:S(2)}, u32[]{:S(2)}) collective-permute-start(bf16[32,3712]{1,0:T(8,128)(2,1)S(1)} %shard_map.55.refs_0_), channel_id=1, source_target_pairs={{0,2},{2,4},{4,6},{6,7},{7,5},{5,3},{3,1},{1,0},{10,8},{12,10},{14... | collective-permute-start | bytes 712712 | tf_op jit(solution)/shard_map/ppermute | solution.py:145
  4.2 1.6 %collective-permute-start.3 = (bf16[32,3712]{1,0:T(8,128)(2,1)S(1)}, bf16[32,3712]{1,0:T(8,128)(2,1)S(1)}, u32[]{:S(2)}, u32[]{:S(2)}) collective-permute-start(bf16[32,3712]{1,0:T(8,128)(2,1)S(1)} %collective-permute-done.refs_1_), channel_id=1, source_target_pairs={{0,2},{2,4},{4,6},{6,7},{7,5},{5,3},{3,1},{1,0},{10,8},{12,10},{14... | collective-permute-start | bytes 712712 | tf_op jit(solution)/shard_map/ppermute | solution.py:145
  5.8 3.2 %shard_map.56.refs_6_.refs_4_.refs_2_ = bf16[3584,1024]{1,0:T(8,128)(2,1)S(1)} custom-call(bf16[3584,1024]{1,0:T(8,128)(2,1)} %bitcast.7), custom_call_target="tpu_custom_call" | custom-call | tf_op jit(solution)/shard_map/pallas_call | solution.py:95
  8.9 1.6 %collective-permute-start.2 = (bf16[32,3712]{1,0:T(8,128)(2,1)S(1)}, bf16[32,3712]{1,0:T(8,128)(2,1)S(1)}, u32[]{:S(2)}, u32[]{:S(2)}) collective-permute-start(bf16[32,3712]{1,0:T(8,128)(2,1)S(1)} %collective-permute-done.1.refs_2_), channel_id=1, source_target_pairs={{0,2},{2,4},{4,6},{6,7},{7,5},{5,3},{3,1},{1,0},{10,8},{12,10},{14... | collective-permute-start | bytes 712712 | tf_op jit(solution)/shard_map/ppermute | solution.py:145
  10.6 0.0 collective-permute-start.5
  10.6 0.2 collective-permute-done.3.refs_3_
  10.8 0.3 collective-permute-start.4
  11.1 1.7 %collective-permute-start.8 = (bf16[32,3712]{1,0:T(8,128)(2,1)S(1)}, bf16[32,3712]{1,0:T(8,128)(2,1)S(1)}, u32[]{:S(2)}, u32[]{:S(2)}) collective-permute-start(bf16[32,3712]{1,0:T(8,128)(2,1)S(1)} %collective-permute-done.3.refs_3_), channel_id=1, source_target_pairs={{0,2},{2,4},{4,6},{6,7},{7,5},{5,3},{3,1},{1,0},{10,8},{12,10},{14... | collective-permute-start | bytes 712712 | tf_op jit(solution)/shard_map/ppermute | solution.py:145
  12.8 2.5 %shard_map.57.refs_7_.refs_5_.refs_3_ = bf16[1024,2560]{1,0:T(8,128)(2,1)S(1)} custom-call(bf16[1024,3584]{1,0:T(8,128)(2,1)} %bitcast.5), custom_call_target="tpu_custom_call" | custom-call | tf_op jit(solution)/shard_map/pallas_call | solution.py:95
  15.4 0.0 collective-permute-done.4.refs_4_
  15.4 0.2 collective-permute-start.7
  15.7 1.5 %collective-permute-start.6 = (bf16[32,3712]{1,0:T(8,128)(2,1)S(1)}, bf16[32,3712]{1,0:T(8,128)(2,1)S(1)}, u32[]{:S(2)}, u32[]{:S(2)}) collective-permute-start(bf16[32,3712]{1,0:T(8,128)(2,1)S(1)} %collective-permute-done.2.refs_0_), channel_id=1, source_target_pairs={{0,2},{2,4},{4,6},{6,7},{7,5},{5,3},{3,1},{1,0},{10,8},{12,10},{14... | collective-permute-start | bytes 712712 | tf_op jit(solution)/shard_map/ppermute | solution.py:145
  17.1 0.5 collective-permute-done.8.refs_1_
  17.7 0.0 collective-permute-start.9
  17.7 1.6 %collective-permute-start.12 = (bf16[32,3712]{1,0:T(8,128)(2,1)S(1)}, bf16[32,3712]{1,0:T(8,128)(2,1)S(1)}, u32[]{:S(2)}, u32[]{:S(2)}) collective-permute-start(bf16[32,3712]{1,0:T(8,128)(2,1)S(1)} %collective-permute-done.8.refs_1_), channel_id=1, source_target_pairs={{0,2},{2,4},{4,6},{6,7},{7,5},{5,3},{3,1},{1,0},{10,8},{12,10},{14... | collective-permute-start | bytes 712712 | tf_op jit(solution)/shard_map/ppermute | solution.py:145
  19.2 0.0 collective-permute-done.7.refs_3_
  19.2 1.6 %shard_map.58.refs_8_.refs_6_.refs_4_ = bf16[1024,1024]{1,0:T(8,128)(2,1)S(1)} custom-call(bf16[1024,3584]{1,0:T(8,128)(2,1)} %bitcast.6), custom_call_target="tpu_custom_call" | custom-call | tf_op jit(solution)/shard_map/pallas_call | solution.py:95
  20.8 0.9 %collective-permute-done.6.refs_0_ = bf16[32,3712]{1,0:T(8,128)(2,1)S(1)} collective-permute-done((bf16[32,3712]{1,0:T(8,128)(2,1)S(1)}, bf16[32,3712]{1,0:T(8,128)(2,1)S(1)}, u32[]{:S(2)}, u32[]{:S(2)}) %collective-permute-start.6) | collective-permute-done | bytes 237600 | tf_op jit(solution)/shard_map/ppermute | solution.py:145
  21.8 1.5 %collective-permute-start.11 = (bf16[32,3712]{1,0:T(8,128)(2,1)S(1)}, bf16[32,3712]{1,0:T(8,128)(2,1)S(1)}, u32[]{:S(2)}, u32[]{:S(2)}) collective-permute-start(bf16[32,3712]{1,0:T(8,128)(2,1)S(1)} %collective-permute-done.6.refs_0_), channel_id=1, source_target_pairs={{0,2},{2,4},{4,6},{6,7},{7,5},{5,3},{3,1},{1,0},{10,8},{12,10},{14... | collective-permute-start | bytes 712712 | tf_op jit(solution)/shard_map/ppermute | solution.py:145
  23.2 1.1 %collective-permute-done.12.refs_0_ = bf16[32,3712]{1,0:T(8,128)(2,1)S(1)} collective-permute-done((bf16[32,3712]{1,0:T(8,128)(2,1)S(1)}, bf16[32,3712]{1,0:T(8,128)(2,1)S(1)}, u32[]{:S(2)}, u32[]{:S(2)}) %collective-permute-start.12) | collective-permute-done | bytes 237600 | tf_op jit(solution)/shard_map/ppermute | solution.py:145
  24.3 3.1 %shard_map.59 = (bf16[32,3584]{1,0:T(8,128)(2,1)S(1)}, f32[32,3584]{1,0:T(8,128)S(1)}, bf16[32,3584]{1,0:T(8,128)(2,1)S(1)}, bf16[32,3584]{1,0:T(8,128)(2,1)S(1)...) custom-call(s32[1]{0:T(128)} %bitcast.3.mine_ref, bf16[32,3712]{1,0:T(8,128)(2,1)S(1)} %collective-permute-done.6.refs_0_, ...), custom_call_target="tpu_custom_call" | custom-call | flops 2818572288 | bytes 14680064 | tf_op jit(solution)/shard_map/pallas_call | solution.py:65
  27.5 0.4 collective-permute-done.11.refs_2_
  27.9 0.2 collective-permute-start.14
  28.0 0.0 collective-permute-done.13.refs_1_
  28.0 1.3 %collective-permute-done.14.refs_3_ = bf16[32,3712]{1,0:T(8,128)(2,1)S(1)} collective-permute-done((bf16[32,3712]{1,0:T(8,128)(2,1)S(1)}, bf16[32,3712]{1,0:T(8,128)(2,1)S(1)}, u32[]{:S(2)}, u32[]{:S(2)}) %collective-permute-start.14) | collective-permute-done | bytes 237600 | tf_op jit(solution)/shard_map/ppermute | solution.py:148
  29.4 2.2 %shard_map.60 = (bf16[32,3584]{1,0:T(8,128)(2,1)S(1)}, f32[32,3584]{1,0:T(8,128)S(1)}, f32[32,3584]{1,0:T(8,128)S(1)}, bf16[32,3584]{1,0:T(8,128)(2,1)S(1)}) custom-call(s32[1]{0:T(128)} %bitcast.3.mine_ref, bf16[32,3712]{1,0:T(8,128)(2,1)S(1)} %collective-permute-done.12.refs_0_, bf16[32,3712]{1,0:T(8,128)(2,1)S(1)} %collective-permute-done.13.refs_1_, ...), custom_call_target="tpu_custom_call" | custom-call | flops 1879048192 | bytes 14680064 | tf_op jit(solution)/shard_map/pallas_call | solution.py:65
  31.6 0.2 collective-permute-start.15
  31.9 0.3 collective-permute-start.16
  32.2 0.2 collective-permute-start.18
  32.4 0.8 %collective-permute-done.15 = bf16[32,3584]{1,0:T(8,128)(2,1)S(1)} collective-permute-done((bf16[32,3584]{1,0:T(8,128)(2,1)S(1)}, bf16[32,3584]{1,0:T(8,128)(2,1)S(1)}, u32[]{:S(2)}, u32[]{:S(2)}) %collective-permute-start.15) | collective-permute-done | bytes 229408 | tf_op jit(solution)/shard_map/ppermute | solution.py:148
  33.2 1.5 %collective-permute-start.19 = (bf16[32,3584]{1,0:T(8,128)(2,1)S(1)}, bf16[32,3584]{1,0:T(8,128)(2,1)S(1)}, u32[]{:S(2)}, u32[]{:S(2)}) collective-permute-start(bf16[32,3584]{1,0:T(8,128)(2,1)S(1)} %add_convert_fusion.8), channel_id=1, source_target_pairs={{0,2},{2,4},{4,6},{6,7},{7,5},{5,3},{3,1},{1,0},{10,8},{12,10},{14... | collective-permute-start | bytes 688136 | tf_op jit(solution)/shard_map/ppermute | solution.py:145
  34.7 0.0 collective-permute-done.16
  34.8 0.1 add_convert_fusion.7
  34.8 1.6 %collective-permute-start.26 = (bf16[32,3584]{1,0:T(8,128)(2,1)S(1)}, bf16[32,3584]{1,0:T(8,128)(2,1)S(1)}, u32[]{:S(2)}, u32[]{:S(2)}) collective-permute-start(bf16[32,3584]{1,0:T(8,128)(2,1)S(1)} %add_convert_fusion.7), channel_id=1, source_target_pairs={{0,2},{2,4},{4,6},{6,7},{7,5},{5,3},{3,1},{1,0},{10,8},{12,10},{14... | collective-permute-start | bytes 688136 | tf_op jit(solution)/shard_map/ppermute | solution.py:145
  36.4 2.3 %shard_map.61 = (bf16[32,3584]{1,0:T(8,128)(2,1)S(1)}, bf16[32,3584]{1,0:T(8,128)(2,1)S(1)}, f32[32,3584]{1,0:T(8,128)S(1)}, f32[32,3584]{1,0:T(8,128)S(1)}) custom-call(s32[1]{0:T(128)} %bitcast.3.mine_ref, bf16[32,3712]{1,0:T(8,128)(2,1)S(1)} %collective-permute-done.2.refs_0_, bf16[32,3712]{1,0:T(8,128)(2,1)S(1)} %collective-permute-done.8.refs_1_, ...), custom_call_target="tpu_custom_call" | custom-call | flops 1879048192 | bytes 14680064 | tf_op jit(solution)/shard_map/pallas_call | solution.py:65
  38.7 0.1 collective-permute-start.25
  38.8 0.5 collective-permute-start.17
  39.3 0.1 add_convert_fusion.6
  39.4 1.6 %collective-permute-start.20 = (bf16[32,3584]{1,0:T(8,128)(2,1)S(1)}, bf16[32,3584]{1,0:T(8,128)(2,1)S(1)}, u32[]{:S(2)}, u32[]{:S(2)}) collective-permute-start(bf16[32,3584]{1,0:T(8,128)(2,1)S(1)} %add_convert_fusion.6), channel_id=1, source_target_pairs={{0,2},{2,4},{4,6},{6,7},{7,5},{5,3},{3,1},{1,0},{10,8},{12,10},{14... | collective-permute-start | bytes 688136 | tf_op jit(solution)/shard_map/ppermute | solution.py:145
  41.0 0.8 %collective-permute-done.26 = bf16[32,3584]{1,0:T(8,128)(2,1)S(1)} collective-permute-done((bf16[32,3584]{1,0:T(8,128)(2,1)S(1)}, bf16[32,3584]{1,0:T(8,128)(2,1)S(1)}, u32[]{:S(2)}, u32[]{:S(2)}) %collective-permute-start.26) | collective-permute-done | bytes 229408 | tf_op jit(solution)/shard_map/ppermute | solution.py:145
  41.8 0.0 collective-permute-done.25
  41.8 0.1 add_convert_fusion.3
  41.9 1.5 %collective-permute-start.27 = (bf16[32,3584]{1,0:T(8,128)(2,1)S(1)}, bf16[32,3584]{1,0:T(8,128)(2,1)S(1)}, u32[]{:S(2)}, u32[]{:S(2)}) collective-permute-start(bf16[32,3584]{1,0:T(8,128)(2,1)S(1)} %add_convert_fusion.3), channel_id=1, source_target_pairs={{0,2},{2,4},{4,6},{6,7},{7,5},{5,3},{3,1},{1,0},{10,8},{12,10},{14... | collective-permute-start | bytes 688136 | tf_op jit(solution)/shard_map/ppermute | solution.py:145
  43.4 2.1 %collective-permute-done.20 = bf16[32,3584]{1,0:T(8,128)(2,1)S(1)} collective-permute-done((bf16[32,3584]{1,0:T(8,128)(2,1)S(1)}, bf16[32,3584]{1,0:T(8,128)(2,1)S(1)}, u32[]{:S(2)}, u32[]{:S(2)}) %collective-permute-start.20) | collective-permute-done | bytes 229408 | tf_op jit(solution)/shard_map/ppermute | solution.py:145
  45.5 0.1 add_convert_fusion.5
  45.6 0.1 collective-permute-start.24
  45.7 1.6 %collective-permute-start.22 = (bf16[32,3584]{1,0:T(8,128)(2,1)S(1)}, bf16[32,3584]{1,0:T(8,128)(2,1)S(1)}, u32[]{:S(2)}, u32[]{:S(2)}) collective-permute-start(bf16[32,3584]{1,0:T(8,128)(2,1)S(1)} %add_convert_fusion.5), channel_id=1, source_target_pairs={{0,2},{2,4},{4,6},{6,7},{7,5},{5,3},{3,1},{1,0},{10,8},{12,10},{14... | collective-permute-start | bytes 688136 | tf_op jit(solution)/shard_map/ppermute | solution.py:145
  47.2 0.2 collective-permute-start.21
  47.4 0.5 collective-permute-done.27
  48.0 0.0 collective-permute-done.24
  48.0 0.1 add_convert_fusion.2
  48.0 1.6 %collective-permute-start.28 = (bf16[32,3584]{1,0:T(8,128)(2,1)S(1)}, bf16[32,3584]{1,0:T(8,128)(2,1)S(1)}, u32[]{:S(2)}, u32[]{:S(2)}) collective-permute-start(bf16[32,3584]{1,0:T(8,128)(2,1)S(1)} %add_convert_fusion.2), channel_id=1, source_target_pairs={{0,2},{2,4},{4,6},{6,7},{7,5},{5,3},{3,1},{1,0},{10,8},{12,10},{14... | collective-permute-start | bytes 688136 | tf_op jit(solution)/shard_map/ppermute | solution.py:145
  49.6 0.0 collective-permute-done.21
  49.6 2.1 %collective-permute-done.22 = bf16[32,3584]{1,0:T(8,128)(2,1)S(1)} collective-permute-done((bf16[32,3584]{1,0:T(8,128)(2,1)S(1)}, bf16[32,3584]{1,0:T(8,128)(2,1)S(1)}, u32[]{:S(2)}, u32[]{:S(2)}) %collective-permute-start.22) | collective-permute-done | bytes 229408 | tf_op jit(solution)/shard_map/ppermute | solution.py:145
  51.7 0.1 add_convert_fusion.4
  51.8 1.6 %collective-permute-start.23 = (bf16[32,3584]{1,0:T(8,128)(2,1)S(1)}, bf16[32,3584]{1,0:T(8,128)(2,1)S(1)}, u32[]{:S(2)}, u32[]{:S(2)}) collective-permute-start(bf16[32,3584]{1,0:T(8,128)(2,1)S(1)} %add_convert_fusion.4), channel_id=1, source_target_pairs={{0,2},{2,4},{4,6},{6,7},{7,5},{5,3},{3,1},{1,0},{10,8},{12,10},{14... | collective-permute-start | bytes 688136 | tf_op jit(solution)/shard_map/ppermute | solution.py:145
  53.4 2.7 %shard_map.62 = (f32[32,3584]{1,0:T(8,128)S(1)}, f32[32,3584]{1,0:T(8,128)S(1)}) custom-call(s32[1]{0:T(128)} %bitcast.3.mine_ref, bf16[32,3712]{1,0:T(8,128)(2,1)S(1)} %shard_map.55.refs_0_, bf16[32,3712]{1,0:T(8,128)(2,1)S(1)} %collective-permute-done.refs_1_, bf16[3584,1024]{1,0:T(8,128)(2,1)S(1)} %shard_map.56.refs_6_.refs_4_.refs_2_, ...), custom_call_target="tpu_custom_call" | custom-call | flops 939524096 | bytes 14680064 | tf_op jit(solution)/shard_map/pallas_call | solution.py:65
  56.1 0.1 add_convert_fusion.1
  56.2 0.1 collective-permute-start.29
  56.3 1.6 %collective-permute-done.23 = bf16[32,3584]{1,0:T(8,128)(2,1)S(1)} collective-permute-done((bf16[32,3584]{1,0:T(8,128)(2,1)S(1)}, bf16[32,3584]{1,0:T(8,128)(2,1)S(1)}, u32[]{:S(2)}, u32[]{:S(2)}) %collective-permute-start.23) | collective-permute-done | bytes 229408 | tf_op jit(solution)/shard_map/ppermute | solution.py:145
  57.9 0.0 collective-permute-done.29
  57.9 0.8 %add_convert_fusion = bf16[32,3584]{1,0:T(8,128)(2,1)} fusion(bf16[32,3584]{1,0:T(8,128)(2,1)S(1)} %collective-permute-done.29, f32[32,3584]{1,0:T(8,128)S(1)} %get-tuple-element.95, bf16[32,3584]{1,0:T(8,128)(2,1)S(1)} %collective-permute-done.23), kind=kLoop, calls=%fused_computation | loop fusion | flops 573440 | bytes 1146880 | tf_op jit(solution)/shard_map/convert_element_type | solution.py:151
  (13 shorter events, 0.1 us)
Async XLA Ops:
  1.1 3.1 %collective-permute-start = (bf16[32,3712]{1,0:T(8,128)(2,1)S(1)}, bf16[32,3712]{1,0:T(8,128)(2,1)S(1)}, u32[]{:S(2)}, u32[]{:S(2)}) collective-permute-start(bf16[32,3712]{1,0:T(8,128)(2,1)S(1)} %shard_map.55.refs_0_), channel_id=1, source_target_pairs={{0,8},{8,0},{1,9},{9,1},{2,10},{10,2},{3,11},{11,3},{4,12},{12,4},... | collective-permute-start | bytes 712712 | tf_op jit(solution)/shard_map/ppermute | solution.py:148
  1.6 7.4 %collective-permute-start.1 = (bf16[32,3712]{1,0:T(8,128)(2,1)S(1)}, bf16[32,3712]{1,0:T(8,128)(2,1)S(1)}, u32[]{:S(2)}, u32[]{:S(2)}) collective-permute-start(bf16[32,3712]{1,0:T(8,128)(2,1)S(1)} %shard_map.55.refs_0_), channel_id=1, source_target_pairs={{0,2},{2,4},{4,6},{6,7},{7,5},{5,3},{3,1},{1,0},{10,8},{12,10},{14... | collective-permute-start | bytes 712712 | tf_op jit(solution)/shard_map/ppermute | solution.py:145
  4.2 6.6 %collective-permute-start.3 = (bf16[32,3712]{1,0:T(8,128)(2,1)S(1)}, bf16[32,3712]{1,0:T(8,128)(2,1)S(1)}, u32[]{:S(2)}, u32[]{:S(2)}) collective-permute-start(bf16[32,3712]{1,0:T(8,128)(2,1)S(1)} %collective-permute-done.refs_1_), channel_id=1, source_target_pairs={{0,2},{2,4},{4,6},{6,7},{7,5},{5,3},{3,1},{1,0},{10,8},{12,10},{14... | collective-permute-start | bytes 712712 | tf_op jit(solution)/shard_map/ppermute | solution.py:145
  8.9 6.4 %collective-permute-start.2 = (bf16[32,3712]{1,0:T(8,128)(2,1)S(1)}, bf16[32,3712]{1,0:T(8,128)(2,1)S(1)}, u32[]{:S(2)}, u32[]{:S(2)}) collective-permute-start(bf16[32,3712]{1,0:T(8,128)(2,1)S(1)} %collective-permute-done.1.refs_2_), channel_id=1, source_target_pairs={{0,2},{2,4},{4,6},{6,7},{7,5},{5,3},{3,1},{1,0},{10,8},{12,10},{14... | collective-permute-start | bytes 712712 | tf_op jit(solution)/shard_map/ppermute | solution.py:145
  10.6 4.8 %collective-permute-start.5 = (bf16[32,3712]{1,0:T(8,128)(2,1)S(1)}, bf16[32,3712]{1,0:T(8,128)(2,1)S(1)}, u32[]{:S(2)}, u32[]{:S(2)}) collective-permute-start(bf16[32,3712]{1,0:T(8,128)(2,1)S(1)} %collective-permute-done.1.refs_2_), channel_id=1, source_target_pairs={{0,8},{8,0},{1,9},{9,1},{2,10},{10,2},{3,11},{11,3},{4,12},{12,4},... | collective-permute-start | bytes 712712 | tf_op jit(solution)/shard_map/ppermute | solution.py:148
  10.8 4.6 %collective-permute-start.4 = (bf16[32,3712]{1,0:T(8,128)(2,1)S(1)}, bf16[32,3712]{1,0:T(8,128)(2,1)S(1)}, u32[]{:S(2)}, u32[]{:S(2)}) collective-permute-start(bf16[32,3712]{1,0:T(8,128)(2,1)S(1)} %collective-permute-done.3.refs_3_), channel_id=1, source_target_pairs={{0,8},{8,0},{1,9},{9,1},{2,10},{10,2},{3,11},{11,3},{4,12},{12,4},... | collective-permute-start | bytes 712712 | tf_op jit(solution)/shard_map/ppermute | solution.py:148
  11.1 6.6 %collective-permute-start.8 = (bf16[32,3712]{1,0:T(8,128)(2,1)S(1)}, bf16[32,3712]{1,0:T(8,128)(2,1)S(1)}, u32[]{:S(2)}, u32[]{:S(2)}) collective-permute-start(bf16[32,3712]{1,0:T(8,128)(2,1)S(1)} %collective-permute-done.3.refs_3_), channel_id=1, source_target_pairs={{0,2},{2,4},{4,6},{6,7},{7,5},{5,3},{3,1},{1,0},{10,8},{12,10},{14... | collective-permute-start | bytes 712712 | tf_op jit(solution)/shard_map/ppermute | solution.py:145
  15.4 3.8 %collective-permute-start.7 = (bf16[32,3712]{1,0:T(8,128)(2,1)S(1)}, bf16[32,3712]{1,0:T(8,128)(2,1)S(1)}, u32[]{:S(2)}, u32[]{:S(2)}) collective-permute-start(bf16[32,3712]{1,0:T(8,128)(2,1)S(1)} %collective-permute-done.2.refs_0_), channel_id=1, source_target_pairs={{0,8},{8,0},{1,9},{9,1},{2,10},{10,2},{3,11},{11,3},{4,12},{12,4},... | collective-permute-start | bytes 712712 | tf_op jit(solution)/shard_map/ppermute | solution.py:148
  15.7 6.1 %collective-permute-start.6 = (bf16[32,3712]{1,0:T(8,128)(2,1)S(1)}, bf16[32,3712]{1,0:T(8,128)(2,1)S(1)}, u32[]{:S(2)}, u32[]{:S(2)}) collective-permute-start(bf16[32,3712]{1,0:T(8,128)(2,1)S(1)} %collective-permute-done.2.refs_0_), channel_id=1, source_target_pairs={{0,2},{2,4},{4,6},{6,7},{7,5},{5,3},{3,1},{1,0},{10,8},{12,10},{14... | collective-permute-start | bytes 712712 | tf_op jit(solution)/shard_map/ppermute | solution.py:145
  17.7 4.1 %collective-permute-start.9 = (bf16[32,3712]{1,0:T(8,128)(2,1)S(1)}, bf16[32,3712]{1,0:T(8,128)(2,1)S(1)}, u32[]{:S(2)}, u32[]{:S(2)}) collective-permute-start(bf16[32,3712]{1,0:T(8,128)(2,1)S(1)} %collective-permute-done.8.refs_1_), channel_id=1, source_target_pairs={{0,8},{8,0},{1,9},{9,1},{2,10},{10,2},{3,11},{11,3},{4,12},{12,4},... | collective-permute-start | bytes 712712 | tf_op jit(solution)/shard_map/ppermute | solution.py:148
  17.7 6.6 %collective-permute-start.12 = (bf16[32,3712]{1,0:T(8,128)(2,1)S(1)}, bf16[32,3712]{1,0:T(8,128)(2,1)S(1)}, u32[]{:S(2)}, u32[]{:S(2)}) collective-permute-start(bf16[32,3712]{1,0:T(8,128)(2,1)S(1)} %collective-permute-done.8.refs_1_), channel_id=1, source_target_pairs={{0,2},{2,4},{4,6},{6,7},{7,5},{5,3},{3,1},{1,0},{10,8},{12,10},{14... | collective-permute-start | bytes 712712 | tf_op jit(solution)/shard_map/ppermute | solution.py:145
  21.8 2.5 %collective-permute-start.10 = (bf16[32,3712]{1,0:T(8,128)(2,1)S(1)}, bf16[32,3712]{1,0:T(8,128)(2,1)S(1)}, u32[]{:S(2)}, u32[]{:S(2)}) collective-permute-start(bf16[32,3712]{1,0:T(8,128)(2,1)S(1)} %collective-permute-done.6.refs_0_), channel_id=1, source_target_pairs={{0,8},{8,0},{1,9},{9,1},{2,10},{10,2},{3,11},{11,3},{4,12},{12,4},... | collective-permute-start | bytes 712712 | tf_op jit(solution)/shard_map/ppermute | solution.py:148
  21.8 6.1 %collective-permute-start.11 = (bf16[32,3712]{1,0:T(8,128)(2,1)S(1)}, bf16[32,3712]{1,0:T(8,128)(2,1)S(1)}, u32[]{:S(2)}, u32[]{:S(2)}) collective-permute-start(bf16[32,3712]{1,0:T(8,128)(2,1)S(1)} %collective-permute-done.6.refs_0_), channel_id=1, source_target_pairs={{0,2},{2,4},{4,6},{6,7},{7,5},{5,3},{3,1},{1,0},{10,8},{12,10},{14... | collective-permute-start | bytes 712712 | tf_op jit(solution)/shard_map/ppermute | solution.py:145
  24.3 3.7 %collective-permute-start.13 = (bf16[32,3712]{1,0:T(8,128)(2,1)S(1)}, bf16[32,3712]{1,0:T(8,128)(2,1)S(1)}, u32[]{:S(2)}, u32[]{:S(2)}) collective-permute-start(bf16[32,3712]{1,0:T(8,128)(2,1)S(1)} %collective-permute-done.12.refs_0_), channel_id=1, source_target_pairs={{0,8},{8,0},{1,9},{9,1},{2,10},{10,2},{3,11},{11,3},{4,12},{12,4},... | collective-permute-start | bytes 712712 | tf_op jit(solution)/shard_map/ppermute | solution.py:148
  27.9 1.5 %collective-permute-start.14 = (bf16[32,3712]{1,0:T(8,128)(2,1)S(1)}, bf16[32,3712]{1,0:T(8,128)(2,1)S(1)}, u32[]{:S(2)}, u32[]{:S(2)}) collective-permute-start(bf16[32,3712]{1,0:T(8,128)(2,1)S(1)} %collective-permute-done.11.refs_2_), channel_id=1, source_target_pairs={{0,8},{8,0},{1,9},{9,1},{2,10},{10,2},{3,11},{11,3},{4,12},{12,4},... | collective-permute-start | bytes 712712 | tf_op jit(solution)/shard_map/ppermute | solution.py:148
  31.6 1.6 %collective-permute-start.15 = (bf16[32,3584]{1,0:T(8,128)(2,1)S(1)}, bf16[32,3584]{1,0:T(8,128)(2,1)S(1)}, u32[]{:S(2)}, u32[]{:S(2)}) collective-permute-start(bf16[32,3584]{1,0:T(8,128)(2,1)S(1)} %get-tuple-element.81), channel_id=1, source_target_pairs={{0,8},{8,0},{1,9},{9,1},{2,10},{10,2},{3,11},{11,3},{4,12},{12,4},... | collective-permute-start | bytes 688136 | tf_op jit(solution)/shard_map/ppermute | solution.py:148
  31.9 2.9 %collective-permute-start.16 = (bf16[32,3584]{1,0:T(8,128)(2,1)S(1)}, bf16[32,3584]{1,0:T(8,128)(2,1)S(1)}, u32[]{:S(2)}, u32[]{:S(2)}) collective-permute-start(bf16[32,3584]{1,0:T(8,128)(2,1)S(1)} %get-tuple-element.83), channel_id=1, source_target_pairs={{0,8},{8,0},{1,9},{9,1},{2,10},{10,2},{3,11},{11,3},{4,12},{12,4},... | collective-permute-start | bytes 688136 | tf_op jit(solution)/shard_map/ppermute | solution.py:148
  32.2 7.1 %collective-permute-start.18 = (bf16[32,3584]{1,0:T(8,128)(2,1)S(1)}, bf16[32,3584]{1,0:T(8,128)(2,1)S(1)}, u32[]{:S(2)}, u32[]{:S(2)}) collective-permute-start(bf16[32,3584]{1,0:T(8,128)(2,1)S(1)} %get-tuple-element.91), channel_id=1, source_target_pairs={{0,8},{8,0},{1,9},{9,1},{2,10},{10,2},{3,11},{11,3},{4,12},{12,4},... | collective-permute-start | bytes 688136 | tf_op jit(solution)/shard_map/ppermute | solution.py:148
  33.2 6.1 %collective-permute-start.19 = (bf16[32,3584]{1,0:T(8,128)(2,1)S(1)}, bf16[32,3584]{1,0:T(8,128)(2,1)S(1)}, u32[]{:S(2)}, u32[]{:S(2)}) collective-permute-start(bf16[32,3584]{1,0:T(8,128)(2,1)S(1)} %add_convert_fusion.8), channel_id=1, source_target_pairs={{0,2},{2,4},{4,6},{6,7},{7,5},{5,3},{3,1},{1,0},{10,8},{12,10},{14... | collective-permute-start | bytes 688136 | tf_op jit(solution)/shard_map/ppermute | solution.py:145
  34.8 6.9 %collective-permute-start.26 = (bf16[32,3584]{1,0:T(8,128)(2,1)S(1)}, bf16[32,3584]{1,0:T(8,128)(2,1)S(1)}, u32[]{:S(2)}, u32[]{:S(2)}) collective-permute-start(bf16[32,3584]{1,0:T(8,128)(2,1)S(1)} %add_convert_fusion.7), channel_id=1, source_target_pairs={{0,2},{2,4},{4,6},{6,7},{7,5},{5,3},{3,1},{1,0},{10,8},{12,10},{14... | collective-permute-start | bytes 688136 | tf_op jit(solution)/shard_map/ppermute | solution.py:145
  38.7 3.0 %collective-permute-start.25 = (bf16[32,3584]{1,0:T(8,128)(2,1)S(1)}, bf16[32,3584]{1,0:T(8,128)(2,1)S(1)}, u32[]{:S(2)}, u32[]{:S(2)}) collective-permute-start(bf16[32,3584]{1,0:T(8,128)(2,1)S(1)} %get-tuple-element.100), channel_id=1, source_target_pairs={{0,8},{8,0},{1,9},{9,1},{2,10},{10,2},{3,11},{11,3},{4,12},{12,4},... | collective-permute-start | bytes 688136 | tf_op jit(solution)/shard_map/ppermute | solution.py:148
  38.8 4.6 %collective-permute-start.17 = (bf16[32,3584]{1,0:T(8,128)(2,1)S(1)}, bf16[32,3584]{1,0:T(8,128)(2,1)S(1)}, u32[]{:S(2)}, u32[]{:S(2)}) collective-permute-start(bf16[32,3584]{1,0:T(8,128)(2,1)S(1)} %get-tuple-element.89), channel_id=1, source_target_pairs={{0,8},{8,0},{1,9},{9,1},{2,10},{10,2},{3,11},{11,3},{4,12},{12,4},... | collective-permute-start | bytes 688136 | tf_op jit(solution)/shard_map/ppermute | solution.py:148
  39.4 6.1 %collective-permute-start.20 = (bf16[32,3584]{1,0:T(8,128)(2,1)S(1)}, bf16[32,3584]{1,0:T(8,128)(2,1)S(1)}, u32[]{:S(2)}, u32[]{:S(2)}) collective-permute-start(bf16[32,3584]{1,0:T(8,128)(2,1)S(1)} %add_convert_fusion.6), channel_id=1, source_target_pairs={{0,2},{2,4},{4,6},{6,7},{7,5},{5,3},{3,1},{1,0},{10,8},{12,10},{14... | collective-permute-start | bytes 688136 | tf_op jit(solution)/shard_map/ppermute | solution.py:145
  41.9 6.1 %collective-permute-start.27 = (bf16[32,3584]{1,0:T(8,128)(2,1)S(1)}, bf16[32,3584]{1,0:T(8,128)(2,1)S(1)}, u32[]{:S(2)}, u32[]{:S(2)}) collective-permute-start(bf16[32,3584]{1,0:T(8,128)(2,1)S(1)} %add_convert_fusion.3), channel_id=1, source_target_pairs={{0,2},{2,4},{4,6},{6,7},{7,5},{5,3},{3,1},{1,0},{10,8},{12,10},{14... | collective-permute-start | bytes 688136 | tf_op jit(solution)/shard_map/ppermute | solution.py:145
  45.6 2.4 %collective-permute-start.24 = (bf16[32,3584]{1,0:T(8,128)(2,1)S(1)}, bf16[32,3584]{1,0:T(8,128)(2,1)S(1)}, u32[]{:S(2)}, u32[]{:S(2)}) collective-permute-start(bf16[32,3584]{1,0:T(8,128)(2,1)S(1)} %get-tuple-element.98), channel_id=1, source_target_pairs={{0,8},{8,0},{1,9},{9,1},{2,10},{10,2},{3,11},{11,3},{4,12},{12,4},... | collective-permute-start | bytes 688136 | tf_op jit(solution)/shard_map/ppermute | solution.py:148
  45.7 6.1 %collective-permute-start.22 = (bf16[32,3584]{1,0:T(8,128)(2,1)S(1)}, bf16[32,3584]{1,0:T(8,128)(2,1)S(1)}, u32[]{:S(2)}, u32[]{:S(2)}) collective-permute-start(bf16[32,3584]{1,0:T(8,128)(2,1)S(1)} %add_convert_fusion.5), channel_id=1, source_target_pairs={{0,2},{2,4},{4,6},{6,7},{7,5},{5,3},{3,1},{1,0},{10,8},{12,10},{14... | collective-permute-start | bytes 688136 | tf_op jit(solution)/shard_map/ppermute | solution.py:145
  47.2 2.4 %collective-permute-start.21 = (bf16[32,3584]{1,0:T(8,128)(2,1)S(1)}, bf16[32,3584]{1,0:T(8,128)(2,1)S(1)}, u32[]{:S(2)}, u32[]{:S(2)}) collective-permute-start(bf16[32,3584]{1,0:T(8,128)(2,1)S(1)} %get-tuple-element.92), channel_id=1, source_target_pairs={{0,8},{8,0},{1,9},{9,1},{2,10},{10,2},{3,11},{11,3},{4,12},{12,4},... | collective-permute-start | bytes 688136 | tf_op jit(solution)/shard_map/ppermute | solution.py:148
  48.0 8.1 %collective-permute-start.28 = (bf16[32,3584]{1,0:T(8,128)(2,1)S(1)}, bf16[32,3584]{1,0:T(8,128)(2,1)S(1)}, u32[]{:S(2)}, u32[]{:S(2)}) collective-permute-start(bf16[32,3584]{1,0:T(8,128)(2,1)S(1)} %add_convert_fusion.2), channel_id=1, source_target_pairs={{0,2},{2,4},{4,6},{6,7},{7,5},{5,3},{3,1},{1,0},{10,8},{12,10},{14... | collective-permute-start | bytes 688136 | tf_op jit(solution)/shard_map/ppermute | solution.py:145
  51.8 6.1 %collective-permute-start.23 = (bf16[32,3584]{1,0:T(8,128)(2,1)S(1)}, bf16[32,3584]{1,0:T(8,128)(2,1)S(1)}, u32[]{:S(2)}, u32[]{:S(2)}) collective-permute-start(bf16[32,3584]{1,0:T(8,128)(2,1)S(1)} %add_convert_fusion.4), channel_id=1, source_target_pairs={{0,2},{2,4},{4,6},{6,7},{7,5},{5,3},{3,1},{1,0},{10,8},{12,10},{14... | collective-permute-start | bytes 688136 | tf_op jit(solution)/shard_map/ppermute | solution.py:145
  56.2 1.7 %collective-permute-start.29 = (bf16[32,3584]{1,0:T(8,128)(2,1)S(1)}, bf16[32,3584]{1,0:T(8,128)(2,1)S(1)}, u32[]{:S(2)}, u32[]{:S(2)}) collective-permute-start(bf16[32,3584]{1,0:T(8,128)(2,1)S(1)} %add_convert_fusion.1), channel_id=1, source_target_pairs={{0,8},{8,0},{1,9},{9,1},{2,10},{10,2},{3,11},{11,3},{4,12},{12,4},... | collective-permute-start | bytes 688136 | tf_op jit(solution)/shard_map/ppermute | solution.py:148

commit v9 on v8

--- a/solution.py
+++ b/solution.py
@@ -8,7 +8,7 @@
 
 BOTH = ("node", "local")
 LANES = 128
-LATE = (3, 4)
+LATE = (2, 3)
 
 
 def gather_plan(tokens, expert_ids, route_weights, w_up, w_down):

time: 58.8 us -> 58.5 us (level)
  no operation moved by 1% of the time
where the time goes in v9:
time: 58.5 us; the launch traced here: 58.3 us
  starting transfers between devices  26 us (44%)
  Pallas kernels  18.8 us (32%)
  waiting for transfers between devices  12.1 us (21%)
  other arithmetic  1.31 us (2%)
    ppermute x14, starting transfers between devices, hop(): return lax.ppermute(x, BOTH, pairs)  23.1 us
    pallas_call x4, Pallas kernels, expert(): pl.pallas_call(functools.partial(expert_body, len(blocks), len(down)), ou...  10.4 us
    ppermute x14, waiting for transfers between devices, hop(): return lax.ppermute(x, BOTH, pairs)  9.9 us
    pallas_call x3, Pallas kernels, load(): pl.pallas_call(functools.partial(load_body, first, pieces), out_shape=plt...  7.29 us
    ppermute x16, starting transfers between devices, swap(): return lax.ppermute(x, 'node', [(0, 1), (1, 0)])  2.84 us
    ppermute x16, waiting for transfers between devices, swap(): return lax.ppermute(x, 'node', [(0, 1), (1, 0)])  2.18 us
    convert_element_type x9, other arithmetic, bf(): return x.astype(jnp.bfloat16)  1.31 us
  transfers between devices with their start and end apart: 30, of which 12 were waited for; matrix products, arithmetic and copies ran while one was open for 1% of the time, Pallas kernels for 26%

profile of v9, /device:TPU:0, one launch (start us, length us, event | category | flops | bytes accessed | tf_op | source)
XLA Modules:
  0.0 58.3 jit_solution(14217653679280119897)
XLA Ops:
  0.0 1.1 %shard_map.55.refs_0_ = bf16[32,3712]{1,0:T(8,128)(2,1)S(1)} custom-call(bf16[32,3584]{1,0:T(8,128)(2,1)} %tokens_ref.1, s32[8,32]{1,0:T(8,128)} %bitcast.8, bf16[8,32]{1,0:T(8,128)(2,1)} %bitcast.9), custom_call_target="tpu_custom_call" | custom-call | tf_op jit(solution)/shard_map/pallas_call | solution.py:127
  1.1 0.5 collective-permute-start
  1.6 2.6 %collective-permute-start.1 = (bf16[32,3712]{1,0:T(8,128)(2,1)S(1)}, bf16[32,3712]{1,0:T(8,128)(2,1)S(1)}, u32[]{:S(2)}, u32[]{:S(2)}) collective-permute-start(bf16[32,3712]{1,0:T(8,128)(2,1)S(1)} %shard_map.55.refs_0_), channel_id=1, source_target_pairs={{0,2},{2,4},{4,6},{6,7},{7,5},{5,3},{3,1},{1,0},{10,8},{12,10},{14... | collective-permute-start | bytes 712712 | tf_op jit(solution)/shard_map/ppermute | solution.py:145
  4.2 0.0 collective-permute-done.refs_1_
  4.2 1.6 %collective-permute-start.3 = (bf16[32,3712]{1,0:T(8,128)(2,1)S(1)}, bf16[32,3712]{1,0:T(8,128)(2,1)S(1)}, u32[]{:S(2)}, u32[]{:S(2)}) collective-permute-start(bf16[32,3712]{1,0:T(8,128)(2,1)S(1)} %collective-permute-done.refs_1_), channel_id=1, source_target_pairs={{0,2},{2,4},{4,6},{6,7},{7,5},{5,3},{3,1},{1,0},{10,8},{12,10},{14... | collective-permute-start | bytes 712712 | tf_op jit(solution)/shard_map/ppermute | solution.py:145
  5.8 3.2 %shard_map.56.refs_6_.refs_4_.refs_2_ = bf16[3584,1024]{1,0:T(8,128)(2,1)S(1)} custom-call(bf16[3584,1024]{1,0:T(8,128)(2,1)} %bitcast.7), custom_call_target="tpu_custom_call" | custom-call | tf_op jit(solution)/shard_map/pallas_call | solution.py:95
  8.9 0.0 collective-permute-done.1.refs_2_
  8.9 1.6 %collective-permute-start.2 = (bf16[32,3712]{1,0:T(8,128)(2,1)S(1)}, bf16[32,3712]{1,0:T(8,128)(2,1)S(1)}, u32[]{:S(2)}, u32[]{:S(2)}) collective-permute-start(bf16[32,3712]{1,0:T(8,128)(2,1)S(1)} %collective-permute-done.1.refs_2_), channel_id=1, source_target_pairs={{0,2},{2,4},{4,6},{6,7},{7,5},{5,3},{3,1},{1,0},{10,8},{12,10},{14... | collective-permute-start | bytes 712712 | tf_op jit(solution)/shard_map/ppermute | solution.py:145
  10.6 0.2 collective-permute-done.3.refs_3_
  10.8 0.3 collective-permute-start.4
  11.1 1.7 %collective-permute-start.8 = (bf16[32,3712]{1,0:T(8,128)(2,1)S(1)}, bf16[32,3712]{1,0:T(8,128)(2,1)S(1)}, u32[]{:S(2)}, u32[]{:S(2)}) collective-permute-start(bf16[32,3712]{1,0:T(8,128)(2,1)S(1)} %collective-permute-done.3.refs_3_), channel_id=1, source_target_pairs={{0,2},{2,4},{4,6},{6,7},{7,5},{5,3},{3,1},{1,0},{10,8},{12,10},{14... | collective-permute-start | bytes 712712 | tf_op jit(solution)/shard_map/ppermute | solution.py:145
  12.8 2.2 %shard_map.57.refs_7_.refs_5_.refs_3_ = bf16[1024,2048]{1,0:T(8,128)(2,1)S(1)} custom-call(bf16[1024,3584]{1,0:T(8,128)(2,1)} %bitcast.5), custom_call_target="tpu_custom_call" | custom-call | tf_op jit(solution)/shard_map/pallas_call | solution.py:95
  15.1 0.0 collective-permute-done.2.refs_0_
  15.1 0.0 collective-permute-done.5.refs_5_
  15.1 0.0 collective-permute-done.4.refs_4_
  15.1 0.2 collective-permute-start.7
  15.3 1.5 %collective-permute-start.6 = (bf16[32,3712]{1,0:T(8,128)(2,1)S(1)}, bf16[32,3712]{1,0:T(8,128)(2,1)S(1)}, u32[]{:S(2)}, u32[]{:S(2)}) collective-permute-start(bf16[32,3712]{1,0:T(8,128)(2,1)S(1)} %collective-permute-done.2.refs_0_), channel_id=1, source_target_pairs={{0,2},{2,4},{4,6},{6,7},{7,5},{5,3},{3,1},{1,0},{10,8},{12,10},{14... | collective-permute-start | bytes 712712 | tf_op jit(solution)/shard_map/ppermute | solution.py:145
  16.8 0.8 %collective-permute-done.8.refs_1_ = bf16[32,3712]{1,0:T(8,128)(2,1)S(1)} collective-permute-done((bf16[32,3712]{1,0:T(8,128)(2,1)S(1)}, bf16[32,3712]{1,0:T(8,128)(2,1)S(1)}, u32[]{:S(2)}, u32[]{:S(2)}) %collective-permute-start.8) | collective-permute-done | bytes 237600 | tf_op jit(solution)/shard_map/ppermute | solution.py:145
  17.7 0.0 collective-permute-start.9
  17.7 1.6 %collective-permute-start.12 = (bf16[32,3712]{1,0:T(8,128)(2,1)S(1)}, bf16[32,3712]{1,0:T(8,128)(2,1)S(1)}, u32[]{:S(2)}, u32[]{:S(2)}) collective-permute-start(bf16[32,3712]{1,0:T(8,128)(2,1)S(1)} %collective-permute-done.8.refs_1_), channel_id=1, source_target_pairs={{0,2},{2,4},{4,6},{6,7},{7,5},{5,3},{3,1},{1,0},{10,8},{12,10},{14... | collective-permute-start | bytes 712712 | tf_op jit(solution)/shard_map/ppermute | solution.py:145
  19.2 1.9 %shard_map.58.refs_8_.refs_6_.refs_4_ = bf16[1024,1536]{1,0:T(8,128)(2,1)S(1)} custom-call(bf16[1024,3584]{1,0:T(8,128)(2,1)} %bitcast.6), custom_call_target="tpu_custom_call" | custom-call | tf_op jit(solution)/shard_map/pallas_call | solution.py:95
  21.1 0.3 collective-permute-done.6.refs_0_
  21.4 0.0 collective-permute-done.9.refs_2_
  21.4 0.0 collective-permute-start.10
  21.5 1.5 %collective-permute-start.11 = (bf16[32,3712]{1,0:T(8,128)(2,1)S(1)}, bf16[32,3712]{1,0:T(8,128)(2,1)S(1)}, u32[]{:S(2)}, u32[]{:S(2)}) collective-permute-start(bf16[32,3712]{1,0:T(8,128)(2,1)S(1)} %collective-permute-done.6.refs_0_), channel_id=1, source_target_pairs={{0,2},{2,4},{4,6},{6,7},{7,5},{5,3},{3,1},{1,0},{10,8},{12,10},{14... | collective-permute-start | bytes 712712 | tf_op jit(solution)/shard_map/ppermute | solution.py:145
  22.9 1.1 %collective-permute-done.12.refs_0_ = bf16[32,3712]{1,0:T(8,128)(2,1)S(1)} collective-permute-done((bf16[32,3712]{1,0:T(8,128)(2,1)S(1)}, bf16[32,3712]{1,0:T(8,128)(2,1)S(1)}, u32[]{:S(2)}, u32[]{:S(2)}) %collective-permute-start.12) | collective-permute-done | bytes 237600 | tf_op jit(solution)/shard_map/ppermute | solution.py:145
  24.0 0.0 collective-permute-done.10.refs_1_
  24.0 3.1 %shard_map.59 = (bf16[32,3584]{1,0:T(8,128)(2,1)S(1)}, f32[32,3584]{1,0:T(8,128)S(1)}, bf16[32,3584]{1,0:T(8,128)(2,1)S(1)}, bf16[32,3584]{1,0:T(8,128)(2,1)S(1)...) custom-call(s32[1]{0:T(128)} %bitcast.3.mine_ref, bf16[32,3712]{1,0:T(8,128)(2,1)S(1)} %collective-permute-done.6.refs_0_, ...), custom_call_target="tpu_custom_call" | custom-call | flops 2818572288 | bytes 14680064 | tf_op jit(solution)/shard_map/pallas_call | solution.py:65
  27.1 0.4 collective-permute-done.11.refs_2_
  27.6 0.2 collective-permute-start.14
  27.7 1.3 %collective-permute-done.14.refs_3_ = bf16[32,3712]{1,0:T(8,128)(2,1)S(1)} collective-permute-done((bf16[32,3712]{1,0:T(8,128)(2,1)S(1)}, bf16[32,3712]{1,0:T(8,128)(2,1)S(1)}, u32[]{:S(2)}, u32[]{:S(2)}) %collective-permute-start.14) | collective-permute-done | bytes 237600 | tf_op jit(solution)/shard_map/ppermute | solution.py:148
  29.1 2.2 %shard_map.60 = (bf16[32,3584]{1,0:T(8,128)(2,1)S(1)}, f32[32,3584]{1,0:T(8,128)S(1)}, f32[32,3584]{1,0:T(8,128)S(1)}, bf16[32,3584]{1,0:T(8,128)(2,1)S(1)}) custom-call(s32[1]{0:T(128)} %bitcast.3.mine_ref, bf16[32,3712]{1,0:T(8,128)(2,1)S(1)} %collective-permute-done.12.refs_0_, bf16[32,3712]{1,0:T(8,128)(2,1)S(1)} %collective-permute-done.13.refs_1_, ...), custom_call_target="tpu_custom_call" | custom-call | flops 1879048192 | bytes 14680064 | tf_op jit(solution)/shard_map/pallas_call | solution.py:65
  31.3 0.2 collective-permute-start.15
  31.5 0.3 collective-permute-start.16
  31.9 0.2 collective-permute-start.18
  32.0 0.8 %collective-permute-done.15 = bf16[32,3584]{1,0:T(8,128)(2,1)S(1)} collective-permute-done((bf16[32,3584]{1,0:T(8,128)(2,1)S(1)}, bf16[32,3584]{1,0:T(8,128)(2,1)S(1)}, u32[]{:S(2)}, u32[]{:S(2)}) %collective-permute-start.15) | collective-permute-done | bytes 229408 | tf_op jit(solution)/shard_map/ppermute | solution.py:148
  32.9 1.5 %collective-permute-start.19 = (bf16[32,3584]{1,0:T(8,128)(2,1)S(1)}, bf16[32,3584]{1,0:T(8,128)(2,1)S(1)}, u32[]{:S(2)}, u32[]{:S(2)}) collective-permute-start(bf16[32,3584]{1,0:T(8,128)(2,1)S(1)} %add_convert_fusion.8), channel_id=1, source_target_pairs={{0,2},{2,4},{4,6},{6,7},{7,5},{5,3},{3,1},{1,0},{10,8},{12,10},{14... | collective-permute-start | bytes 688136 | tf_op jit(solution)/shard_map/ppermute | solution.py:145
  34.4 0.0 collective-permute-done.16
  34.5 1.6 %collective-permute-start.26 = (bf16[32,3584]{1,0:T(8,128)(2,1)S(1)}, bf16[32,3584]{1,0:T(8,128)(2,1)S(1)}, u32[]{:S(2)}, u32[]{:S(2)}) collective-permute-start(bf16[32,3584]{1,0:T(8,128)(2,1)S(1)} %add_convert_fusion.7), channel_id=1, source_target_pairs={{0,2},{2,4},{4,6},{6,7},{7,5},{5,3},{3,1},{1,0},{10,8},{12,10},{14... | collective-permute-start | bytes 688136 | tf_op jit(solution)/shard_map/ppermute | solution.py:145
  36.1 2.3 %shard_map.61 = (bf16[32,3584]{1,0:T(8,128)(2,1)S(1)}, bf16[32,3584]{1,0:T(8,128)(2,1)S(1)}, f32[32,3584]{1,0:T(8,128)S(1)}, f32[32,3584]{1,0:T(8,128)S(1)}) custom-call(s32[1]{0:T(128)} %bitcast.3.mine_ref, bf16[32,3712]{1,0:T(8,128)(2,1)S(1)} %collective-permute-done.2.refs_0_, bf16[32,3712]{1,0:T(8,128)(2,1)S(1)} %collective-permute-done.8.refs_1_, ...), custom_call_target="tpu_custom_call" | custom-call | flops 1879048192 | bytes 14680064 | tf_op jit(solution)/shard_map/pallas_call | solution.py:65
  38.4 0.1 collective-permute-start.25
  38.5 0.5 collective-permute-start.17
  39.0 0.0 collective-permute-done.18
  39.0 0.1 add_convert_fusion.6
  39.1 1.6 %collective-permute-start.20 = (bf16[32,3584]{1,0:T(8,128)(2,1)S(1)}, bf16[32,3584]{1,0:T(8,128)(2,1)S(1)}, u32[]{:S(2)}, u32[]{:S(2)}) collective-permute-start(bf16[32,3584]{1,0:T(8,128)(2,1)S(1)} %add_convert_fusion.6), channel_id=1, source_target_pairs={{0,2},{2,4},{4,6},{6,7},{7,5},{5,3},{3,1},{1,0},{10,8},{12,10},{14... | collective-permute-start | bytes 688136 | tf_op jit(solution)/shard_map/ppermute | solution.py:145
  40.7 0.8 %collective-permute-done.26 = bf16[32,3584]{1,0:T(8,128)(2,1)S(1)} collective-permute-done((bf16[32,3584]{1,0:T(8,128)(2,1)S(1)}, bf16[32,3584]{1,0:T(8,128)(2,1)S(1)}, u32[]{:S(2)}, u32[]{:S(2)}) %collective-permute-start.26) | collective-permute-done | bytes 229408 | tf_op jit(solution)/shard_map/ppermute | solution.py:145
  41.4 0.0 collective-permute-done.25
  41.4 0.1 add_convert_fusion.3
  41.5 1.5 %collective-permute-start.27 = (bf16[32,3584]{1,0:T(8,128)(2,1)S(1)}, bf16[32,3584]{1,0:T(8,128)(2,1)S(1)}, u32[]{:S(2)}, u32[]{:S(2)}) collective-permute-start(bf16[32,3584]{1,0:T(8,128)(2,1)S(1)} %add_convert_fusion.3), channel_id=1, source_target_pairs={{0,2},{2,4},{4,6},{6,7},{7,5},{5,3},{3,1},{1,0},{10,8},{12,10},{14... | collective-permute-start | bytes 688136 | tf_op jit(solution)/shard_map/ppermute | solution.py:145
  43.1 2.1 %collective-permute-done.20 = bf16[32,3584]{1,0:T(8,128)(2,1)S(1)} collective-permute-done((bf16[32,3584]{1,0:T(8,128)(2,1)S(1)}, bf16[32,3584]{1,0:T(8,128)(2,1)S(1)}, u32[]{:S(2)}, u32[]{:S(2)}) %collective-permute-start.20) | collective-permute-done | bytes 229408 | tf_op jit(solution)/shard_map/ppermute | solution.py:145
  45.1 0.1 add_convert_fusion.5
  45.2 0.1 collective-permute-start.24
  45.3 1.6 %collective-permute-start.22 = (bf16[32,3584]{1,0:T(8,128)(2,1)S(1)}, bf16[32,3584]{1,0:T(8,128)(2,1)S(1)}, u32[]{:S(2)}, u32[]{:S(2)}) collective-permute-start(bf16[32,3584]{1,0:T(8,128)(2,1)S(1)} %add_convert_fusion.5), channel_id=1, source_target_pairs={{0,2},{2,4},{4,6},{6,7},{7,5},{5,3},{3,1},{1,0},{10,8},{12,10},{14... | collective-permute-start | bytes 688136 | tf_op jit(solution)/shard_map/ppermute | solution.py:145
  46.9 0.2 collective-permute-start.21
  47.1 0.5 collective-permute-done.27
  47.6 0.1 add_convert_fusion.2
  47.7 1.6 %collective-permute-start.28 = (bf16[32,3584]{1,0:T(8,128)(2,1)S(1)}, bf16[32,3584]{1,0:T(8,128)(2,1)S(1)}, u32[]{:S(2)}, u32[]{:S(2)}) collective-permute-start(bf16[32,3584]{1,0:T(8,128)(2,1)S(1)} %add_convert_fusion.2), channel_id=1, source_target_pairs={{0,2},{2,4},{4,6},{6,7},{7,5},{5,3},{3,1},{1,0},{10,8},{12,10},{14... | collective-permute-start | bytes 688136 | tf_op jit(solution)/shard_map/ppermute | solution.py:145
  49.3 2.1 %collective-permute-done.22 = bf16[32,3584]{1,0:T(8,128)(2,1)S(1)} collective-permute-done((bf16[32,3584]{1,0:T(8,128)(2,1)S(1)}, bf16[32,3584]{1,0:T(8,128)(2,1)S(1)}, u32[]{:S(2)}, u32[]{:S(2)}) %collective-permute-start.22) | collective-permute-done | bytes 229408 | tf_op jit(solution)/shard_map/ppermute | solution.py:145
  51.4 0.1 add_convert_fusion.4
  51.5 1.6 %collective-permute-start.23 = (bf16[32,3584]{1,0:T(8,128)(2,1)S(1)}, bf16[32,3584]{1,0:T(8,128)(2,1)S(1)}, u32[]{:S(2)}, u32[]{:S(2)}) collective-permute-start(bf16[32,3584]{1,0:T(8,128)(2,1)S(1)} %add_convert_fusion.4), channel_id=1, source_target_pairs={{0,2},{2,4},{4,6},{6,7},{7,5},{5,3},{3,1},{1,0},{10,8},{12,10},{14... | collective-permute-start | bytes 688136 | tf_op jit(solution)/shard_map/ppermute | solution.py:145
  53.1 2.7 %shard_map.62 = (f32[32,3584]{1,0:T(8,128)S(1)}, f32[32,3584]{1,0:T(8,128)S(1)}) custom-call(s32[1]{0:T(128)} %bitcast.3.mine_ref, bf16[32,3712]{1,0:T(8,128)(2,1)S(1)} %shard_map.55.refs_0_, bf16[32,3712]{1,0:T(8,128)(2,1)S(1)} %collective-permute-done.refs_1_, bf16[3584,1024]{1,0:T(8,128)(2,1)S(1)} %shard_map.56.refs_6_.refs_4_.refs_2_, ...), custom_call_target="tpu_custom_call" | custom-call | flops 939524096 | bytes 14680064 | tf_op jit(solution)/shard_map/pallas_call | solution.py:65
  55.9 0.1 collective-permute-start.29
  55.9 1.6 %collective-permute-done.23 = bf16[32,3584]{1,0:T(8,128)(2,1)S(1)} collective-permute-done((bf16[32,3584]{1,0:T(8,128)(2,1)S(1)}, bf16[32,3584]{1,0:T(8,128)(2,1)S(1)}, u32[]{:S(2)}, u32[]{:S(2)}) %collective-permute-start.23) | collective-permute-done | bytes 229408 | tf_op jit(solution)/shard_map/ppermute | solution.py:145
  57.6 0.8 %add_convert_fusion = bf16[32,3584]{1,0:T(8,128)(2,1)} fusion(bf16[32,3584]{1,0:T(8,128)(2,1)S(1)} %collective-permute-done.29, f32[32,3584]{1,0:T(8,128)S(1)} %get-tuple-element.95, bf16[32,3584]{1,0:T(8,128)(2,1)S(1)} %collective-permute-done.23), kind=kLoop, calls=%fused_computation | loop fusion | flops 573440 | bytes 1146880 | tf_op jit(solution)/shard_map/convert_element_type | solution.py:151
  (13 shorter events, 0.1 us)
Async XLA Ops:
  1.1 3.1 %collective-permute-start = (bf16[32,3712]{1,0:T(8,128)(2,1)S(1)}, bf16[32,3712]{1,0:T(8,128)(2,1)S(1)}, u32[]{:S(2)}, u32[]{:S(2)}) collective-permute-start(bf16[32,3712]{1,0:T(8,128)(2,1)S(1)} %shard_map.55.refs_0_), channel_id=1, source_target_pairs={{0,8},{8,0},{1,9},{9,1},{2,10},{10,2},{3,11},{11,3},{4,12},{12,4},... | collective-permute-start | bytes 712712 | tf_op jit(solution)/shard_map/ppermute | solution.py:148
  1.6 7.4 %collective-permute-start.1 = (bf16[32,3712]{1,0:T(8,128)(2,1)S(1)}, bf16[32,3712]{1,0:T(8,128)(2,1)S(1)}, u32[]{:S(2)}, u32[]{:S(2)}) collective-permute-start(bf16[32,3712]{1,0:T(8,128)(2,1)S(1)} %shard_map.55.refs_0_), channel_id=1, source_target_pairs={{0,2},{2,4},{4,6},{6,7},{7,5},{5,3},{3,1},{1,0},{10,8},{12,10},{14... | collective-permute-start | bytes 712712 | tf_op jit(solution)/shard_map/ppermute | solution.py:145
  4.2 6.6 %collective-permute-start.3 = (bf16[32,3712]{1,0:T(8,128)(2,1)S(1)}, bf16[32,3712]{1,0:T(8,128)(2,1)S(1)}, u32[]{:S(2)}, u32[]{:S(2)}) collective-permute-start(bf16[32,3712]{1,0:T(8,128)(2,1)S(1)} %collective-permute-done.refs_1_), channel_id=1, source_target_pairs={{0,2},{2,4},{4,6},{6,7},{7,5},{5,3},{3,1},{1,0},{10,8},{12,10},{14... | collective-permute-start | bytes 712712 | tf_op jit(solution)/shard_map/ppermute | solution.py:145
  8.9 6.2 %collective-permute-start.2 = (bf16[32,3712]{1,0:T(8,128)(2,1)S(1)}, bf16[32,3712]{1,0:T(8,128)(2,1)S(1)}, u32[]{:S(2)}, u32[]{:S(2)}) collective-permute-start(bf16[32,3712]{1,0:T(8,128)(2,1)S(1)} %collective-permute-done.1.refs_2_), channel_id=1, source_target_pairs={{0,2},{2,4},{4,6},{6,7},{7,5},{5,3},{3,1},{1,0},{10,8},{12,10},{14... | collective-permute-start | bytes 712712 | tf_op jit(solution)/shard_map/ppermute | solution.py:145
  10.6 4.5 %collective-permute-start.5 = (bf16[32,3712]{1,0:T(8,128)(2,1)S(1)}, bf16[32,3712]{1,0:T(8,128)(2,1)S(1)}, u32[]{:S(2)}, u32[]{:S(2)}) collective-permute-start(bf16[32,3712]{1,0:T(8,128)(2,1)S(1)} %collective-permute-done.1.refs_2_), channel_id=1, source_target_pairs={{0,8},{8,0},{1,9},{9,1},{2,10},{10,2},{3,11},{11,3},{4,12},{12,4},... | collective-permute-start | bytes 712712 | tf_op jit(solution)/shard_map/ppermute | solution.py:148
  10.8 4.4 %collective-permute-start.4 = (bf16[32,3712]{1,0:T(8,128)(2,1)S(1)}, bf16[32,3712]{1,0:T(8,128)(2,1)S(1)}, u32[]{:S(2)}, u32[]{:S(2)}) collective-permute-start(bf16[32,3712]{1,0:T(8,128)(2,1)S(1)} %collective-permute-done.3.refs_3_), channel_id=1, source_target_pairs={{0,8},{8,0},{1,9},{9,1},{2,10},{10,2},{3,11},{11,3},{4,12},{12,4},... | collective-permute-start | bytes 712712 | tf_op jit(solution)/shard_map/ppermute | solution.py:148
  11.1 6.6 %collective-permute-start.8 = (bf16[32,3712]{1,0:T(8,128)(2,1)S(1)}, bf16[32,3712]{1,0:T(8,128)(2,1)S(1)}, u32[]{:S(2)}, u32[]{:S(2)}) collective-permute-start(bf16[32,3712]{1,0:T(8,128)(2,1)S(1)} %collective-permute-done.3.refs_3_), channel_id=1, source_target_pairs={{0,2},{2,4},{4,6},{6,7},{7,5},{5,3},{3,1},{1,0},{10,8},{12,10},{14... | collective-permute-start | bytes 712712 | tf_op jit(solution)/shard_map/ppermute | solution.py:145
  15.1 4.1 %collective-permute-start.7 = (bf16[32,3712]{1,0:T(8,128)(2,1)S(1)}, bf16[32,3712]{1,0:T(8,128)(2,1)S(1)}, u32[]{:S(2)}, u32[]{:S(2)}) collective-permute-start(bf16[32,3712]{1,0:T(8,128)(2,1)S(1)} %collective-permute-done.2.refs_0_), channel_id=1, source_target_pairs={{0,8},{8,0},{1,9},{9,1},{2,10},{10,2},{3,11},{11,3},{4,12},{12,4},... | collective-permute-start | bytes 712712 | tf_op jit(solution)/shard_map/ppermute | solution.py:148
  15.3 6.1 %collective-permute-start.6 = (bf16[32,3712]{1,0:T(8,128)(2,1)S(1)}, bf16[32,3712]{1,0:T(8,128)(2,1)S(1)}, u32[]{:S(2)}, u32[]{:S(2)}) collective-permute-start(bf16[32,3712]{1,0:T(8,128)(2,1)S(1)} %collective-permute-done.2.refs_0_), channel_id=1, source_target_pairs={{0,2},{2,4},{4,6},{6,7},{7,5},{5,3},{3,1},{1,0},{10,8},{12,10},{14... | collective-permute-start | bytes 712712 | tf_op jit(solution)/shard_map/ppermute | solution.py:145
  17.7 3.8 %collective-permute-start.9 = (bf16[32,3712]{1,0:T(8,128)(2,1)S(1)}, bf16[32,3712]{1,0:T(8,128)(2,1)S(1)}, u32[]{:S(2)}, u32[]{:S(2)}) collective-permute-start(bf16[32,3712]{1,0:T(8,128)(2,1)S(1)} %collective-permute-done.8.refs_1_), channel_id=1, source_target_pairs={{0,8},{8,0},{1,9},{9,1},{2,10},{10,2},{3,11},{11,3},{4,12},{12,4},... | collective-permute-start | bytes 712712 | tf_op jit(solution)/shard_map/ppermute | solution.py:148
  17.7 6.3 %collective-permute-start.12 = (bf16[32,3712]{1,0:T(8,128)(2,1)S(1)}, bf16[32,3712]{1,0:T(8,128)(2,1)S(1)}, u32[]{:S(2)}, u32[]{:S(2)}) collective-permute-start(bf16[32,3712]{1,0:T(8,128)(2,1)S(1)} %collective-permute-done.8.refs_1_), channel_id=1, source_target_pairs={{0,2},{2,4},{4,6},{6,7},{7,5},{5,3},{3,1},{1,0},{10,8},{12,10},{14... | collective-permute-start | bytes 712712 | tf_op jit(solution)/shard_map/ppermute | solution.py:145
  21.4 2.5 %collective-permute-start.10 = (bf16[32,3712]{1,0:T(8,128)(2,1)S(1)}, bf16[32,3712]{1,0:T(8,128)(2,1)S(1)}, u32[]{:S(2)}, u32[]{:S(2)}) collective-permute-start(bf16[32,3712]{1,0:T(8,128)(2,1)S(1)} %collective-permute-done.6.refs_0_), channel_id=1, source_target_pairs={{0,8},{8,0},{1,9},{9,1},{2,10},{10,2},{3,11},{11,3},{4,12},{12,4},... | collective-permute-start | bytes 712712 | tf_op jit(solution)/shard_map/ppermute | solution.py:148
  21.5 6.1 %collective-permute-start.11 = (bf16[32,3712]{1,0:T(8,128)(2,1)S(1)}, bf16[32,3712]{1,0:T(8,128)(2,1)S(1)}, u32[]{:S(2)}, u32[]{:S(2)}) collective-permute-start(bf16[32,3712]{1,0:T(8,128)(2,1)S(1)} %collective-permute-done.6.refs_0_), channel_id=1, source_target_pairs={{0,2},{2,4},{4,6},{6,7},{7,5},{5,3},{3,1},{1,0},{10,8},{12,10},{14... | collective-permute-start | bytes 712712 | tf_op jit(solution)/shard_map/ppermute | solution.py:145
  24.0 3.7 %collective-permute-start.13 = (bf16[32,3712]{1,0:T(8,128)(2,1)S(1)}, bf16[32,3712]{1,0:T(8,128)(2,1)S(1)}, u32[]{:S(2)}, u32[]{:S(2)}) collective-permute-start(bf16[32,3712]{1,0:T(8,128)(2,1)S(1)} %collective-permute-done.12.refs_0_), channel_id=1, source_target_pairs={{0,8},{8,0},{1,9},{9,1},{2,10},{10,2},{3,11},{11,3},{4,12},{12,4},... | collective-permute-start | bytes 712712 | tf_op jit(solution)/shard_map/ppermute | solution.py:148
  27.6 1.5 %collective-permute-start.14 = (bf16[32,3712]{1,0:T(8,128)(2,1)S(1)}, bf16[32,3712]{1,0:T(8,128)(2,1)S(1)}, u32[]{:S(2)}, u32[]{:S(2)}) collective-permute-start(bf16[32,3712]{1,0:T(8,128)(2,1)S(1)} %collective-permute-done.11.refs_2_), channel_id=1, source_target_pairs={{0,8},{8,0},{1,9},{9,1},{2,10},{10,2},{3,11},{11,3},{4,12},{12,4},... | collective-permute-start | bytes 712712 | tf_op jit(solution)/shard_map/ppermute | solution.py:148
  31.3 1.6 %collective-permute-start.15 = (bf16[32,3584]{1,0:T(8,128)(2,1)S(1)}, bf16[32,3584]{1,0:T(8,128)(2,1)S(1)}, u32[]{:S(2)}, u32[]{:S(2)}) collective-permute-start(bf16[32,3584]{1,0:T(8,128)(2,1)S(1)} %get-tuple-element.81), channel_id=1, source_target_pairs={{0,8},{8,0},{1,9},{9,1},{2,10},{10,2},{3,11},{11,3},{4,12},{12,4},... | collective-permute-start | bytes 688136 | tf_op jit(solution)/shard_map/ppermute | solution.py:148
  31.5 2.9 %collective-permute-start.16 = (bf16[32,3584]{1,0:T(8,128)(2,1)S(1)}, bf16[32,3584]{1,0:T(8,128)(2,1)S(1)}, u32[]{:S(2)}, u32[]{:S(2)}) collective-permute-start(bf16[32,3584]{1,0:T(8,128)(2,1)S(1)} %get-tuple-element.83), channel_id=1, source_target_pairs={{0,8},{8,0},{1,9},{9,1},{2,10},{10,2},{3,11},{11,3},{4,12},{12,4},... | collective-permute-start | bytes 688136 | tf_op jit(solution)/shard_map/ppermute | solution.py:148
  31.9 7.1 %collective-permute-start.18 = (bf16[32,3584]{1,0:T(8,128)(2,1)S(1)}, bf16[32,3584]{1,0:T(8,128)(2,1)S(1)}, u32[]{:S(2)}, u32[]{:S(2)}) collective-permute-start(bf16[32,3584]{1,0:T(8,128)(2,1)S(1)} %get-tuple-element.91), channel_id=1, source_target_pairs={{0,8},{8,0},{1,9},{9,1},{2,10},{10,2},{3,11},{11,3},{4,12},{12,4},... | collective-permute-start | bytes 688136 | tf_op jit(solution)/shard_map/ppermute | solution.py:148
  32.9 6.1 %collective-permute-start.19 = (bf16[32,3584]{1,0:T(8,128)(2,1)S(1)}, bf16[32,3584]{1,0:T(8,128)(2,1)S(1)}, u32[]{:S(2)}, u32[]{:S(2)}) collective-permute-start(bf16[32,3584]{1,0:T(8,128)(2,1)S(1)} %add_convert_fusion.8), channel_id=1, source_target_pairs={{0,2},{2,4},{4,6},{6,7},{7,5},{5,3},{3,1},{1,0},{10,8},{12,10},{14... | collective-permute-start | bytes 688136 | tf_op jit(solution)/shard_map/ppermute | solution.py:145
  34.5 6.9 %collective-permute-start.26 = (bf16[32,3584]{1,0:T(8,128)(2,1)S(1)}, bf16[32,3584]{1,0:T(8,128)(2,1)S(1)}, u32[]{:S(2)}, u32[]{:S(2)}) collective-permute-start(bf16[32,3584]{1,0:T(8,128)(2,1)S(1)} %add_convert_fusion.7), channel_id=1, source_target_pairs={{0,2},{2,4},{4,6},{6,7},{7,5},{5,3},{3,1},{1,0},{10,8},{12,10},{14... | collective-permute-start | bytes 688136 | tf_op jit(solution)/shard_map/ppermute | solution.py:145
  38.4 3.0 %collective-permute-start.25 = (bf16[32,3584]{1,0:T(8,128)(2,1)S(1)}, bf16[32,3584]{1,0:T(8,128)(2,1)S(1)}, u32[]{:S(2)}, u32[]{:S(2)}) collective-permute-start(bf16[32,3584]{1,0:T(8,128)(2,1)S(1)} %get-tuple-element.100), channel_id=1, source_target_pairs={{0,8},{8,0},{1,9},{9,1},{2,10},{10,2},{3,11},{11,3},{4,12},{12,4},... | collective-permute-start | bytes 688136 | tf_op jit(solution)/shard_map/ppermute | solution.py:148
  38.5 4.6 %collective-permute-start.17 = (bf16[32,3584]{1,0:T(8,128)(2,1)S(1)}, bf16[32,3584]{1,0:T(8,128)(2,1)S(1)}, u32[]{:S(2)}, u32[]{:S(2)}) collective-permute-start(bf16[32,3584]{1,0:T(8,128)(2,1)S(1)} %get-tuple-element.89), channel_id=1, source_target_pairs={{0,8},{8,0},{1,9},{9,1},{2,10},{10,2},{3,11},{11,3},{4,12},{12,4},... | collective-permute-start | bytes 688136 | tf_op jit(solution)/shard_map/ppermute | solution.py:148
  39.1 6.1 %collective-permute-start.20 = (bf16[32,3584]{1,0:T(8,128)(2,1)S(1)}, bf16[32,3584]{1,0:T(8,128)(2,1)S(1)}, u32[]{:S(2)}, u32[]{:S(2)}) collective-permute-start(bf16[32,3584]{1,0:T(8,128)(2,1)S(1)} %add_convert_fusion.6), channel_id=1, source_target_pairs={{0,2},{2,4},{4,6},{6,7},{7,5},{5,3},{3,1},{1,0},{10,8},{12,10},{14... | collective-permute-start | bytes 688136 | tf_op jit(solution)/shard_map/ppermute | solution.py:145
  41.5 6.1 %collective-permute-start.27 = (bf16[32,3584]{1,0:T(8,128)(2,1)S(1)}, bf16[32,3584]{1,0:T(8,128)(2,1)S(1)}, u32[]{:S(2)}, u32[]{:S(2)}) collective-permute-start(bf16[32,3584]{1,0:T(8,128)(2,1)S(1)} %add_convert_fusion.3), channel_id=1, source_target_pairs={{0,2},{2,4},{4,6},{6,7},{7,5},{5,3},{3,1},{1,0},{10,8},{12,10},{14... | collective-permute-start | bytes 688136 | tf_op jit(solution)/shard_map/ppermute | solution.py:145
  45.2 2.4 %collective-permute-start.24 = (bf16[32,3584]{1,0:T(8,128)(2,1)S(1)}, bf16[32,3584]{1,0:T(8,128)(2,1)S(1)}, u32[]{:S(2)}, u32[]{:S(2)}) collective-permute-start(bf16[32,3584]{1,0:T(8,128)(2,1)S(1)} %get-tuple-element.98), channel_id=1, source_target_pairs={{0,8},{8,0},{1,9},{9,1},{2,10},{10,2},{3,11},{11,3},{4,12},{12,4},... | collective-permute-start | bytes 688136 | tf_op jit(solution)/shard_map/ppermute | solution.py:148
  45.3 6.1 %collective-permute-start.22 = (bf16[32,3584]{1,0:T(8,128)(2,1)S(1)}, bf16[32,3584]{1,0:T(8,128)(2,1)S(1)}, u32[]{:S(2)}, u32[]{:S(2)}) collective-permute-start(bf16[32,3584]{1,0:T(8,128)(2,1)S(1)} %add_convert_fusion.5), channel_id=1, source_target_pairs={{0,2},{2,4},{4,6},{6,7},{7,5},{5,3},{3,1},{1,0},{10,8},{12,10},{14... | collective-permute-start | bytes 688136 | tf_op jit(solution)/shard_map/ppermute | solution.py:145
  46.9 2.4 %collective-permute-start.21 = (bf16[32,3584]{1,0:T(8,128)(2,1)S(1)}, bf16[32,3584]{1,0:T(8,128)(2,1)S(1)}, u32[]{:S(2)}, u32[]{:S(2)}) collective-permute-start(bf16[32,3584]{1,0:T(8,128)(2,1)S(1)} %get-tuple-element.92), channel_id=1, source_target_pairs={{0,8},{8,0},{1,9},{9,1},{2,10},{10,2},{3,11},{11,3},{4,12},{12,4},... | collective-permute-start | bytes 688136 | tf_op jit(solution)/shard_map/ppermute | solution.py:148
  47.7 8.1 %collective-permute-start.28 = (bf16[32,3584]{1,0:T(8,128)(2,1)S(1)}, bf16[32,3584]{1,0:T(8,128)(2,1)S(1)}, u32[]{:S(2)}, u32[]{:S(2)}) collective-permute-start(bf16[32,3584]{1,0:T(8,128)(2,1)S(1)} %add_convert_fusion.2), channel_id=1, source_target_pairs={{0,2},{2,4},{4,6},{6,7},{7,5},{5,3},{3,1},{1,0},{10,8},{12,10},{14... | collective-permute-start | bytes 688136 | tf_op jit(solution)/shard_map/ppermute | solution.py:145
  51.5 6.1 %collective-permute-start.23 = (bf16[32,3584]{1,0:T(8,128)(2,1)S(1)}, bf16[32,3584]{1,0:T(8,128)(2,1)S(1)}, u32[]{:S(2)}, u32[]{:S(2)}) collective-permute-start(bf16[32,3584]{1,0:T(8,128)(2,1)S(1)} %add_convert_fusion.4), channel_id=1, source_target_pairs={{0,2},{2,4},{4,6},{6,7},{7,5},{5,3},{3,1},{1,0},{10,8},{12,10},{14... | collective-permute-start | bytes 688136 | tf_op jit(solution)/shard_map/ppermute | solution.py:145
  55.9 1.7 %collective-permute-start.29 = (bf16[32,3584]{1,0:T(8,128)(2,1)S(1)}, bf16[32,3584]{1,0:T(8,128)(2,1)S(1)}, u32[]{:S(2)}, u32[]{:S(2)}) collective-permute-start(bf16[32,3584]{1,0:T(8,128)(2,1)S(1)} %add_convert_fusion.1), channel_id=1, source_target_pairs={{0,8},{8,0},{1,9},{9,1},{2,10},{10,2},{3,11},{11,3},{4,12},{12,4},... | collective-permute-start | bytes 688136 | tf_op jit(solution)/shard_map/ppermute | solution.py:148
